TPU v7x, 32 devices: a whole 2x2x4 slice. The times are simulated.
32 devices in a mesh: dir: 4 (over z), row: 8 (over y, x, core).
Axes of the slice: x: 2, y: 2, z: 4, core: 2. Of those that a mesh axis runs over, the one named last changes fastest.
Arguments:
- influence: bfloat16 [3, 32, 192, 144], P(None, 'row'), may hold values from -0.5 to 0.5
- foot_rows: int32 [4, 3, 32], P('dir', None, 'row'), may hold values from 0 to 31, as said below
- foot_columns: int32 [4, 3, 160], P('dir'), may hold values from 0 to 191
- actuator_codes: int32 [3, 48, 48], replicated, may hold values from 0 to 8191, as said below
- poke_rows: int32 [2048], replicated, may hold values from 0 to 8191, as said below
- subaperture_valid: int32 [4, 16, 80], P('dir', 'row'), may hold values 0 or 1
Outputs:
- interaction: bfloat16 [6912, 4, 2560], P(('dir', 'row'))
Inputs may be any that keep to these rules, and one draw needn't show every extreme that they name: `foot_rows`: for every direction, mirror and pupil row y the surface row lies within 2 rows of y, and in every draw some lie exactly 2 rows above and some exactly 2 rows below their pupil row. `actuator_codes`: all entries are distinct. `poke_rows`: all entries are distinct.
All inputs are finite; a program needn't handle non-finite values. No bound on the sum of `subaperture_valid` on one device may be relied on, other than what follows from the above.
Results may differ from a plain program's by a relative error of at most 0.01.
Values may be sent and summed in bfloat16 or wider, within the bound.
No kernel may reach another device: no remote copies, remote signals or barrier semaphores. Data moves between devices by JAX's collectives and lax.ppermute only.
A program may use at most 64 MiB of HBM per device.

v0:
```python
import jax
import jax.numpy as jnp
from jax import lax
from jax.sharding import PartitionSpec as P

NAR = 48
NA = 48
BAND = 3


def shifted(block, axis, distance):
    devices = range(lax.axis_size(axis))
    route = [(i - distance, i) for i in devices if i - distance in devices]
    return lax.ppermute(block, axis, route)


def parity_sign(code_values, row_values):
    folded = jnp.bitwise_and(code_values, row_values)
    for stride in (16, 8, 4, 2, 1):
        folded = jnp.bitwise_xor(folded, jnp.right_shift(folded, stride))
    return (1 - 2 * jnp.bitwise_and(folded, 1)).astype(jnp.bfloat16)


def pick_codes(code_table, positions):
    return code_table[positions]


def shards(influence, foot_rows, foot_columns, actuator_codes, poke_rows, subaperture_valid):
    mirrors = influence.shape[0]
    shard_rows = influence.shape[1]
    surface_rows = shard_rows * lax.axis_size("row")
    base_row = lax.axis_index("row") * shard_rows
    received = []
    for offset in (1, -1):
        received.append(shifted(influence, "row", offset))
    window = jnp.concatenate([received[0], influence, received[1]], axis=1)
    window_rows = window.shape[1]
    local_rows = foot_rows[0] - base_row + shard_rows
    pick_rows = (
        local_rows[:, :, None] == jnp.arange(window_rows, dtype=jnp.int32)[None, None, :]
    ).astype(jnp.bfloat16)
    flat_window = window.reshape(mirrors, window_rows, -1)
    row_picked = jnp.einsum(
        "kyw,kwz->kyz", pick_rows, flat_window, preferred_element_type=jnp.float32
    ).astype(jnp.bfloat16)
    row_picked = row_picked.reshape(mirrors, shard_rows, window.shape[2], window.shape[3])
    pick_columns = (
        foot_columns[0][:, :, None] == jnp.arange(window.shape[2], dtype=jnp.int32)[None, None, :]
    ).astype(jnp.bfloat16)
    sampled = jnp.einsum(
        "kxc,kyca->kyxa", pick_columns, row_picked, preferred_element_type=jnp.float32
    ).astype(jnp.bfloat16)
    band_start = jnp.clip(foot_rows[0] * NAR // surface_rows - 1, 0, NAR - BAND)
    slot_index = jnp.arange(BAND * NA, dtype=jnp.int32)
    code_index = band_start[:, :, None] * NA + slot_index[None, None, :]
    flat_codes = actuator_codes.reshape(mirrors, -1)
    column_code = jax.vmap(pick_codes)(flat_codes, code_index)
    commands = parity_sign(column_code[..., None], poke_rows[None, None, None, :])
    surface = jnp.einsum(
        "kyxa,kyap->kyxp", sampled, commands, preferred_element_type=jnp.float32
    ).astype(jnp.bfloat16)
    pupil_phase = jnp.sum(surface.astype(jnp.float32), axis=0)
    subaperture_rows = shard_rows // 2
    blocks = pupil_phase.reshape(
        subaperture_rows, 2, pupil_phase.shape[1] // 2, 2, pupil_phase.shape[2]
    )
    slope_across = 0.5 * (
        blocks[:, 0, :, 1] - blocks[:, 0, :, 0] + (blocks[:, 1, :, 1] - blocks[:, 1, :, 0])
    )
    slope_down = 0.5 * (
        blocks[:, 1, :, 0] - blocks[:, 0, :, 0] + (blocks[:, 1, :, 1] - blocks[:, 0, :, 1])
    )
    valid_mask = subaperture_valid[0].astype(jnp.float32)[:, None, :, None]
    slopes = (jnp.stack([slope_across, slope_down], axis=1) * valid_mask).astype(jnp.bfloat16)
    slope_rows = slopes.reshape(-1, slopes.shape[-1])
    norm_factor = poke_rows.shape[0] ** (-0.5)
    all_codes = actuator_codes.reshape(-1)
    block_size = all_codes.shape[0] // lax.axis_size("dir")
    own_codes = lax.dynamic_slice_in_dim(all_codes, lax.axis_index("dir") * block_size, block_size)
    sign_table = parity_sign(own_codes[:, None], poke_rows[None, :])
    partial_value = lax.dot_general(
        sign_table,
        lax.all_gather(slope_rows[None], "dir", axis=0, tiled=True),
        (((1,), (2,)), ((), ())),
        preferred_element_type=jnp.float32,
    )
    gathered = (partial_value * norm_factor).astype(jnp.bfloat16)
    return lax.all_to_all(gathered, "row", split_axis=0, concat_axis=2, tiled=True)


def solution(mesh):
    return jax.shard_map(
        shards,
        mesh=mesh,
        in_specs=(
            P(None, "row", None, None),
            P("dir", None, "row"),
            P("dir", None, None),
            P(),
            P(),
            P("dir", "row", None),
        ),
        out_specs=P(("dir", "row"), None, None),
        check_vma=False,
    )
```

profile of v0, /device:TPU:0, one launch (start us, length us, event | category | flops | bytes accessed | tf_op | source)
XLA Modules:
  0.0 300.5 jit_solution(2168518720678760044)
XLA Ops:
  6.5 0.0 all-gather.2.cloned.1.call-start
  6.5 2.4 collective-permute-start
  8.9 1.3 collective-permute-start.1
  10.3 0.7 convert_bitcast_fusion
  10.9 0.1 mul.93
  11.0 0.7 subtract_add_fusion
  11.7 0.6 copy.97
  12.3 1.3 copy.96
  13.6 0.1 fusion.39
  13.7 0.1 reshape.207
  13.7 1.0 reshape.205
  14.7 0.0 copy-start
  14.8 14.4 %gather_fusion = s32[1728]{0:T(1024)S(1)} fusion(s32[3,2304]{1,0:T(4,128)S(1)} %reshape.205, s32[1728]{0:T(1024)S(1)} %reshape.207), kind=kCustom, calls=%fused_computation | custom fusion | bytes 27648 | tf_op jit(solution)/shard_map/vmap()/gather | solution.py:25
  29.2 0.1 reshape.210
  29.3 0.0 collective-permute-done
  29.3 0.0 collective-permute-done.1
  29.3 0.0 copy-done
  29.3 2.0 pad_maximum_fusion
  31.3 3.4 %copy.46 = bf16[3,12,192,144]{3,2,1,0:T(8,128)(2,1)S(1)} copy(bf16[3,12,192,144]{2,3,1,0:T(8,128)(2,1)} %pad_maximum_fusion) | data formatting | bytes 3981312 | tf_op jit(solution)/shard_map/concatenate | solution.py:36
  34.7 6.7 %reshape.203 = bf16[3,12,27648]{2,1,0:T(8,128)(2,1)} reshape(bf16[3,12,192,144]{3,2,1,0:T(8,128)(2,1)S(1)} %copy.46) | data formatting | bytes 3981312 | tf_op jit(solution)/shard_map/reshape | solution.py:42
  41.3 0.0 copy-start.2
  41.3 0.0 copy-start.3
  41.3 2.4 convolution_convert_fusion
  43.7 2.0 reshape.204
  45.7 0.0 copy-done.2
  45.7 0.0 copy-done.3
  45.7 11.2 %convert_reduce_fusion = f32[4,160,2048]{2,1,0:T(8,128)} fusion(s32[2048]{0:T(1024)S(1)} %copy-done.3, s32[3,4,144]{2,1,0:T(4,128)S(1)} %reshape.210, bf16[3,4,192,144]{3,2,1,0:T(8,128)(2,1)S(1)} %reshape.204, s32[3,160]{1,0:T(4,128)S(1)} %bitcast.73), kind=kOutput, calls=%fused_computation.12 | convolution fusion | flops 1302568960 | bytes 5923456 | tf_op jit(solution)/shard_map/kyxa,kyap->kyxp/dot_general | solution.py:59
  56.9 7.5 %reshape.206 = f32[2,2,80,2,2048]{4,3,2,1,0:T(2,128)} reshape(f32[4,160,2048]{2,1,0:T(8,128)} %convert_reduce_fusion) | data formatting | bytes 10485760 | tf_op jit(solution)/shard_map/reshape | solution.py:64
  64.5 8.1 %fusion.57 = (f32[2,1,80,1,2048]{4,3,2,1,0:T(1,128)S(1)}, f32[2,1,80,1,2048]{4,3,2,1,0:T(1,128)S(1)}, f32[2,1,80,1,2048]{4,3,2,1,0:T(1,128)S(1)}, f32[2,1,80,1,2048]{4,3,2,1,0:T(1,128)S(1)}) fusion(f32[2,2,80,2,2048]{4,3,2,1,0:T(2,128)} %reshape.206), kind=kLoop, calls=%fused_computation.85 | loop fusion | bytes 10485760 | tf_op jit(solution)/shard_map/slice | solution.py:68
  72.6 2.5 fusion.31
  75.1 2.5 multiply_bitcast_fusion
  77.6 0.3 pad_maximum_fusion.1
  77.9 0.0 copy-start.1
  77.9 0.3 copy.56
  78.2 1.3 multiply_convert_fusion.1
  79.4 0.0 all-gather.2.cloned.1.call-update
  79.5 0.0 copy-done.1
  79.5 0.1 reshape.202
  79.6 0.1 dynamic_slice.3
  79.6 102.6 %all-gather.2.cloned.1.call-done = bf16[4,320,2048]{2,1,0:T(8,128)(2,1)} async-done(((bf16[1,320,2048]{2,1,0:T(8,128)(2,1)}), bf16[4,320,2048]{2,1,0:T(8,128)(2,1)}) %all-gather.2.cloned.1.call-update) | async-done | bytes 5242896 | tf_op jit(solution)/shard_map/all_gather | solution.py:83
  182.2 16.6 %multiply_convert_fusion = bf16[1728,4,320]{0,2,1:T(8,128)(2,1)} fusion(bf16[4,320,2048]{2,1,0:T(8,128)(2,1)} %all-gather.2.cloned.1.call-done, s32[2048]{0:T(1024)S(1)} %copy-done.3, s32[1728]{0:T(1024)S(1)} %dynamic_slice.3), kind=kOutput, calls=%fused_computation.21 | convolution fusion | flops 9117204480 | bytes 9681664 | tf_op jit(solution)/shard_map/dot_general | solution.py:81
  198.8 10.1 %copy.57 = bf16[1728,4,320]{2,1,0:T(4,128)(2,1)} copy(bf16[1728,4,320]{0,2,1:T(8,128)(2,1)} %multiply_convert_fusion) | data formatting | bytes 8847360 | tf_op jit(solution)/shard_map/convert_element_type | solution.py:87
  208.9 64.7 %all_to_all.18 = bf16[1728,4,320]{2,1,0:T(4,128)(2,1)S(1)} all-to-all(bf16[1728,4,320]{2,1,0:T(4,128)(2,1)} %copy.57), channel_id=1, replica_groups=mesh['dir'=4,'row'=8] {'row'}, dimensions={0} | all-to-all | bytes 8847360 | tf_op jit(solution)/shard_map/all_to_all | solution.py:88
  273.6 4.4 %copy.95 = bf16[8,216,4,320]{3,0,1,2:T(8,128)(2,1)} copy(bf16[8,216,4,320]{3,2,1,0:T(4,128)(2,1)S(1)} %bitcast.70) | data formatting | bytes 8847360 | tf_op jit(solution)/shard_map/all_to_all | solution.py:88
  277.9 9.1 %all_to_all.16 = bf16[216,4,2560]{2,0,1:T(8,128)(2,1)} reshape(bf16[216,4,8,320]{3,2,0,1:T(8,128)(2,1)} %bitcast.69) | data formatting | bytes 8847360 | tf_op jit(solution)/shard_map/all_to_all | solution.py:88
  287.0 6.6 %copy.59 = bf16[216,4,2560]{2,1,0:T(4,128)(2,1)} copy(bf16[216,4,2560]{2,0,1:T(8,128)(2,1)} %all_to_all.16) | data formatting | bytes 8847360 | tf_op jit(solution)/shard_map/all_to_all | solution.py:88
  (2 shorter events, 0.0 us)
Async XLA Ops:
  6.5 175.7 %all-gather.2.cloned.1.call-start = ((), (), s32[]{:S(2)}) async-start(), calls=%async_computation.1 | async-start | bytes 6553600 | tf_op jit(solution)/shard_map/all_gather | solution.py:83
  6.5 22.7 %collective-permute-start = (bf16[3,4,192,144]{2,3,1,0:T(8,128)(2,1)}, bf16[3,4,192,144]{2,3,1,0:T(8,128)(2,1)S(1)}, u32[]{:S(2)}, u32[]{:S(2)}) collective-permute-start(bf16[3,4,192,144]{2,3,1,0:T(8,128)(2,1)} %param.6), channel_id=1, source_target_pairs={{0,1},{1,2},{2,3},{3,4},{4,5},{5,6},{6,7},{8,9},{9,10},{10,11},{11... | collective-permute-start | bytes 1990664 | tf_op jit(solution)/shard_map/ppermute | solution.py:14
  8.9 20.3 %collective-permute-start.1 = (bf16[3,4,192,144]{2,3,1,0:T(8,128)(2,1)}, bf16[3,4,192,144]{2,3,1,0:T(8,128)(2,1)S(1)}, u32[]{:S(2)}, u32[]{:S(2)}) collective-permute-start(bf16[3,4,192,144]{2,3,1,0:T(8,128)(2,1)} %param.6), channel_id=1, source_target_pairs={{1,0},{2,1},{3,2},{4,3},{5,4},{6,5},{7,6},{9,8},{10,9},{11,10},{12... | collective-permute-start | bytes 1990664 | tf_op jit(solution)/shard_map/ppermute | solution.py:14
  14.7 14.5 %copy-start = (bf16[3,4,192,144]{2,3,1,0:T(8,128)(2,1)S(1)}, bf16[3,4,192,144]{2,3,1,0:T(8,128)(2,1)}, u32[]{:S(2)}) copy-start(bf16[3,4,192,144]{2,3,1,0:T(8,128)(2,1)} %param.6) | copy-start | bytes 1990660
  41.3 4.4 %copy-start.2 = (s32[1,3,160]{2,1,0:T(4,128)S(1)}, s32[1,3,160]{2,1,0:T(4,128)}, u32[]{:S(2)}) copy-start(s32[1,3,160]{2,1,0:T(4,128)} %copy.96) | copy-start | bytes 5764
  41.3 4.4 %copy-start.3 = (s32[2048]{0:T(1024)S(1)}, s32[2048]{0:T(1024)}, u32[]{:S(2)}) copy-start(s32[2048]{0:T(1024)} %param.10) | copy-start | bytes 24580
  77.9 1.6 copy-start.1
Sparse Core Ops, SparseCore 0:
  79.6 102.6 all-gather.1
where the time goes:
time: 301 us; the launch traced here: 300 us
  waiting for transfers between devices  103 us (34%)
  local copies, waits for them, and re-layouts  75.8 us (25%)
  blocking collectives  64.7 us (21%)
  matrix products  30.1 us (10%)
  between operations  13.6 us (5%)
  other arithmetic  10 us (3%)
  starting transfers between devices  3.7 us (1%)
    all_gather x1, waiting for transfers between devices, shards(): lax.all_gather(slope_rows[None], 'dir', axis=0, tiled=True)  103 us
    all_to_all x1, blocking collectives, shards(): lax.all_to_all(gathered, 'row', split_axis=0, concat_axis=2, tiled=True)  64.7 us
    all_to_all x3, local copies, waits for them, and re-layouts, shards(): lax.all_to_all(gathered, 'row', split_axis=0, concat_axis=2, tiled=True)  20 us
    dot_general x1, matrix products, shards(): lax.dot_general(sign_table, lax.all_gather(slope_rows[None], 'dir', axis=...  16.6 us
    gather x3, local copies, waits for them, and re-layouts, pick_codes(): return code_table[positions]  14.6 us
    dot_general x1, matrix products, shards(): jnp.einsum('kyxa,kyap->kyxp', sampled, commands, preferred_element_type=j...  11.2 us
    convert_element_type x1, local copies, waits for them, and re-layouts, shards(): gathered = (partial_value * norm_factor).astype(jnp.bfloat16)  10.1 us
    slice x1, local copies, waits for them, and re-layouts, shards(): blocks[:, 0, :, 1] - blocks[:, 0, :, 0]  8.06 us
  transfers between devices with their start and end apart: 3, of which 1 were waited for; matrix products, arithmetic and copies ran while one was open for 6% of the time, Pallas kernels for 0%

commit v1 on v0

v1 whole, which is shorter than its diff:
```python
import functools
import math

import jax
import jax.numpy as jnp
import numpy as np
from jax import lax
from jax.experimental import pallas as pl
from jax.experimental.pallas import tpu as pltpu
from jax.sharding import PartitionSpec as P

NAR = 48
NA = 48
BAND = 3
LANES = 128
WINDOW = 256
VMEM_BYTES = 56 * 1024 * 1024


def parity(codes, rows):
    return lax.population_count(codes & rows) & 1


def pack_kernel(block_ref, packed_ref):
    mirrors, rows, slots, samples = block_ref.shape
    tail = samples - LANES
    for unit in range(mirrors * rows // 2):
        base = unit * 3 * slots
        tails = []
        for side in range(2):
            k, l = divmod(2 * unit + side, rows)
            packed_ref[pl.ds(base + side * slots, slots), :] = block_ref[k, l, :, :LANES]
            tails.append(block_ref[k, l, :, LANES:])
        packed_ref[pl.ds(base + 2 * slots, slots), :] = jnp.concatenate(tails, axis=1)


def pack(block):
    mirrors, rows, slots, samples = block.shape
    return pl.pallas_call(
        pack_kernel,
        out_shape=jax.ShapeDtypeStruct((mirrors * rows * slots * samples // LANES, LANES), block.dtype),
        in_specs=[pl.BlockSpec(memory_space=pltpu.VMEM)],
        out_specs=pl.BlockSpec(memory_space=pltpu.VMEM),
        compiler_params=pltpu.CompilerParams(vmem_limit_bytes=VMEM_BYTES),
        cost_estimate=pl.CostEstimate(flops=0, bytes_accessed=3 * block.size, transcendentals=0),
        name="pack_influence",
    )(block)


def column_of(row, length):
    return jnp.transpose(jnp.broadcast_to(row, (LANES, length)), (1, 0))


def gram_kernel(own_ref, codes_ref, pokes_ref, gram_ref, poke_columns, own_signs, own_sums):
    pokes = pokes_ref.shape[1]
    own = own_signs.shape[0]

    @pl.when(pl.program_id(0) == 0)
    def _():
        for at in range(0, pokes, LANES):
            poke_columns[pl.ds(at, LANES), :] = column_of(pokes_ref[:, at:at + LANES], LANES)
        own_column = jnp.concatenate(
            [column_of(own_ref[:, at:at + LANES], LANES) for at in range(0, own_ref.shape[1], LANES)], axis=0
        )[:own]
        total = jnp.zeros((own, LANES), jnp.float32)
        for at in range(0, pokes, LANES):
            signs = (1 - 2 * parity(own_column, pokes_ref[:, at:at + LANES])).astype(jnp.float32)
            own_signs[:, at:at + LANES] = signs.astype(jnp.bfloat16)
            total = total + signs
        own_sums[...] = jnp.broadcast_to(jnp.sum(total, axis=1, keepdims=True), own_sums.shape)

    width = codes_ref.shape[1]
    depth = 256
    total = jnp.zeros((own, width), jnp.float32)
    for at in range(0, pokes, depth):
        column = poke_columns[pl.ds(at, depth), :]
        bits = [
            parity(codes_ref[:, lane:lane + LANES], column).astype(jnp.float32).astype(jnp.bfloat16)
            for lane in range(0, width, LANES)
        ]
        total = total + jnp.dot(
            own_signs[:, at:at + depth], jnp.concatenate(bits, axis=1), preferred_element_type=jnp.float32
        )
    sums = jnp.concatenate([own_sums[...]] * (width // LANES), axis=1)
    gram_ref[...] = (sums - 2.0 * total).astype(jnp.bfloat16)


def gram(own_codes, codes, pokes):
    own = own_codes.shape[0]
    padded = -(-own // LANES) * LANES
    own_row = jnp.pad(own_codes, (0, padded - own))[None]
    acts, count = codes.shape[0], pokes.shape[0]
    return pl.pallas_call(
        gram_kernel,
        grid=(acts // WINDOW,),
        out_shape=jax.ShapeDtypeStruct((own, acts), jnp.bfloat16),
        in_specs=[
            pl.BlockSpec((1, padded), lambda s: (0, 0)),
            pl.BlockSpec((1, WINDOW), lambda s: (0, s)),
            pl.BlockSpec((1, count), lambda s: (0, 0)),
        ],
        out_specs=pl.BlockSpec((own, WINDOW), lambda s: (0, s)),
        scratch_shapes=[
            pltpu.VMEM((count, LANES), jnp.int32),
            pltpu.VMEM((own, count), jnp.bfloat16),
            pltpu.VMEM((own, LANES), jnp.float32),
        ],
        compiler_params=pltpu.CompilerParams(vmem_limit_bytes=VMEM_BYTES),
        cost_estimate=pl.CostEstimate(
            flops=2 * own * acts * count, bytes_accessed=2 * own * acts, transcendentals=0
        ),
        name="gram_rows",
    )(own_row, codes[None], pokes[None])


def decode_kernel(
    shard_rows, surface_rows, samples, phases, foot_ref, gram_ref, block_ref, columns_ref, signs_ref, scale_ref,
    out_ref, window, decoded, differences, total
):
    step = pl.program_id(0)
    blocks = surface_rows // shard_rows
    mirrors = decoded.shape[0]
    own = gram_ref.shape[0]
    directions = scale_ref.shape[0]
    slots = BAND * NA
    tail = samples - LANES
    slope_lanes = columns_ref.shape[-1]

    @pl.when(step == 0)
    def _():
        window[...] = jnp.zeros_like(window)

        def build(index, _):
            phase = lax.rem(index, phases)
            for k in range(mirrors):
                first = columns_ref[index, 2 * k:2 * k + 1, :]
                second = columns_ref[index, 2 * k + 1:2 * k + 2, :]
                for y in range(2):
                    plus = signs_ref[phase, 2 * y:2 * y + 1, :]
                    minus = signs_ref[phase, 2 * y + 1:2 * y + 2, :]

                    def piece(start, length):
                        x = start + lax.broadcasted_iota(jnp.int32, (length, slope_lanes), 0)
                        return (
                            jnp.where(x == second, plus, 0.0) + jnp.where(x == first, minus, 0.0)
                        ).astype(jnp.bfloat16)

                    differences[index, pl.ds((2 * k + y) * LANES, LANES), :] = piece(0, LANES)
                    differences[index, pl.ds(2 * mirrors * LANES + k * LANES + y * tail, tail), :] = piece(LANES, tail)
            return 0

        lax.fori_loop(0, directions * phases, build, 0)

    @pl.when(step < blocks)
    def _():
        lane = lax.broadcasted_iota(jnp.int32, (own, LANES), 1)
        for q in range(mirrors * shard_rows):
            k, l = divmod(q, shard_rows)
            r = step * shard_rows + l
            band = jnp.clip(r * NAR // surface_rows - 1, 0, NAR - BAND)
            column = (k * NAR + band) * NA
            base = pl.multiple_of(column // LANES * LANES, LANES)
            shift = pl.multiple_of(column - base, 16)
            unit, side = divmod(q, 2)
            slot = q % window.shape[0]
            window[slot] = jnp.zeros(window.shape[1:], window.dtype)
            at = unit * 3 * slots
            window[slot, pl.ds(shift, slots), :LANES] = block_ref[0, pl.ds(at + side * slots, slots), :]
            window[slot, pl.ds(shift, slots), LANES:] = block_ref[0, pl.ds(at + 2 * slots, slots), :]
            u = jnp.dot(gram_ref[:, pl.ds(base, WINDOW)], window[slot], preferred_element_type=jnp.float32)
            decoded[k, r, :, :LANES] = u[:, :LANES].astype(jnp.bfloat16)
            rest = u[:, LANES:]
            turned = pltpu.roll(rest, LANES // 2, 1)
            low, high = (rest, turned) if side == 0 else (turned, rest)
            decoded[k, r, :, LANES:] = jnp.where(lane < tail, low, high).astype(jnp.bfloat16)

    @pl.when(step >= blocks)
    def _():
        group = step - blocks
        lane = lax.broadcasted_iota(jnp.int32, (own, LANES), 1)

        def one(d, _):
            pieces = []
            for phase in range(phases):
                i = group * phases + phase
                heads, tails = [], []
                for k in range(mirrors):
                    rows = [foot_ref[(d * mirrors + k) * surface_rows + 2 * i + y] for y in range(2)]
                    heads += [decoded[k, row, :, :LANES] for row in rows]
                    tails.append(
                        jnp.where(lane < tail, decoded[k, rows[0], :, LANES:], decoded[k, rows[1], :, LANES:])
                    )
                pieces.append(
                    jnp.dot(
                        jnp.concatenate(heads + tails, axis=1),
                        differences[d * phases + phase],
                        preferred_element_type=jnp.float32,
                    )
                )
            tiles = out_ref.shape[2] // LANES
            for tile in range(tiles):
                value = None
                for phase in range(phases):
                    start = phase * out_ref.shape[2] // phases // LANES
                    if start <= tile < start + slope_lanes // LANES:
                        part = pieces[phase][:, (tile - start) * LANES:(tile - start + 1) * LANES]
                        value = part if value is None else value + part
                value = value * scale_ref[d, :, tile * LANES:(tile + 1) * LANES]
                total[tile, pl.ds(d, own, stride=directions), :] = value
            return 0

        lax.fori_loop(0, directions, one, 0)
        for tile in range(out_ref.shape[2] // LANES):
            value = total[tile].reshape(own, directions, LANES)
            out_ref[:, :, tile * LANES:(tile + 1) * LANES] = value.astype(out_ref.dtype)


def decode(foot_rows, gram_rows, blocks, columns, signs, scale, shard_rows, samples, phases):
    directions, mirrors, surface_rows = foot_rows.shape
    own, acts = gram_rows.shape
    count = blocks.shape[0]
    width = scale.shape[1]
    groups = width // (scale.shape[1] // (surface_rows // 2) * phases)
    lanes = width // groups
    flops = 2 * own * WINDOW * WINDOW * mirrors * surface_rows + 2 * own * mirrors * 3 * LANES * WINDOW * directions * surface_rows // 2
    return pl.pallas_call(
        functools.partial(decode_kernel, shard_rows, surface_rows, samples, phases),
        grid=(count + groups,),
        out_shape=jax.ShapeDtypeStruct((own, directions, width), jnp.bfloat16),
        in_specs=[
            pl.BlockSpec(memory_space=pltpu.SMEM),
            pl.BlockSpec(memory_space=pltpu.VMEM),
            pl.BlockSpec((1,) + blocks.shape[1:], lambda s: (jnp.minimum(s, count - 1), 0, 0)),
            pl.BlockSpec(memory_space=pltpu.VMEM),
            pl.BlockSpec(memory_space=pltpu.VMEM),
            pl.BlockSpec((directions, 1, lanes), lambda s: (0, 0, jnp.maximum(s - count, 0))),
        ],
        out_specs=pl.BlockSpec((own, directions, lanes), lambda s: (0, 0, jnp.maximum(s - count, 0))),
        scratch_shapes=[
            pltpu.VMEM((4, WINDOW, WINDOW), jnp.bfloat16),
            pltpu.VMEM((mirrors, surface_rows, own, WINDOW), jnp.bfloat16),
            pltpu.VMEM((directions * phases, 3 * mirrors * LANES, columns.shape[-1]), jnp.bfloat16),
            pltpu.VMEM((lanes // LANES, own * directions, LANES), jnp.float32),
        ],
        compiler_params=pltpu.CompilerParams(vmem_limit_bytes=VMEM_BYTES),
        cost_estimate=pl.CostEstimate(flops=flops, bytes_accessed=2 * own * directions * width, transcendentals=0),
        name="decode",
    )(foot_rows.reshape(-1), gram_rows, blocks, columns, signs, scale[:, None])


def placed_columns(foot_columns, phases):
    directions, mirrors, pupil = foot_columns.shape
    pairs = foot_columns.reshape(directions, mirrors, pupil // 2, 2).transpose(0, 1, 3, 2)
    both = jnp.concatenate([pairs, pairs], axis=-1)
    placed = []
    for phase in range(phases):
        start = phase * pupil % LANES
        placed.append(
            jnp.pad(both, ((0, 0),) * 3 + ((start, WINDOW - pupil - start),), constant_values=-1)
        )
    return jnp.stack(placed, axis=1).reshape(directions * phases, mirrors * 2, WINDOW)


def placed_signs(pupil, phases):
    signs = np.zeros((phases, 4, WINDOW), np.float32)
    for phase in range(phases):
        start = phase * pupil % LANES
        middle, end = start + pupil // 2, start + pupil
        signs[phase, :, start:middle] = np.array([1, -1, 1, -1])[:, None]
        signs[phase, :, middle:end] = np.array([-1, -1, 1, 1])[:, None]
    return jnp.asarray(signs)


def gather_small(foot_rows, foot_columns, valid):
    directions, devices = lax.axis_size("dir"), lax.axis_size("row")
    own = [foot_rows[0], foot_columns[0], valid[0]]
    flat = jnp.concatenate([piece.reshape(-1) for piece in own])
    every = lax.all_gather(flat, ("dir", "row")).reshape(directions, devices, -1)
    cuts = np.cumsum([piece.size for piece in own])
    rows = every[:, :, :cuts[0]].reshape((directions, devices) + own[0].shape)
    rows = rows.transpose(0, 2, 1, 3).reshape(directions, own[0].shape[0], -1)
    columns = every[:, 0, cuts[0]:cuts[1]].reshape((directions,) + own[1].shape)
    return rows, columns, every[:, :, cuts[1]:].reshape(directions, -1, own[2].shape[1])


def shards(influence, foot_rows, foot_columns, actuator_codes, poke_rows, subaperture_valid):
    mirrors, shard_rows, samples, slots = influence.shape
    pupil = foot_columns.shape[2]
    packed = pack(jnp.swapaxes(influence, 2, 3))
    blocks = lax.all_gather(packed, "row")
    rows, columns, valid = gather_small(foot_rows, foot_columns, subaperture_valid)
    codes = actuator_codes.reshape(-1)
    own = codes.shape[0] // (lax.axis_size("dir") * lax.axis_size("row"))
    device = lax.axis_index("dir") * lax.axis_size("row") + lax.axis_index("row")
    gram_rows = gram(lax.dynamic_slice_in_dim(codes, device * own, own), codes, poke_rows)
    phases = LANES // math.gcd(pupil, LANES)
    norm_factor = 0.5 * poke_rows.shape[0] ** (-0.5)
    scale = valid.astype(jnp.float32) * norm_factor
    scale = jnp.broadcast_to(scale[:, :, None], scale.shape[:2] + (2, scale.shape[2])).reshape(scale.shape[0], -1)
    return decode(
        rows, gram_rows, blocks, placed_columns(columns, phases), placed_signs(pupil, phases), scale,
        shard_rows, samples, phases,
    )


def solution(mesh):
    return jax.shard_map(
        shards,
        mesh=mesh,
        in_specs=(
            P(None, "row", None, None),
            P("dir", None, "row"),
            P("dir", None, None),
            P(),
            P(),
            P("dir", "row", None),
        ),
        out_specs=P(("dir", "row"), None, None),
        check_vma=False,
    )
```

time: 301 us -> 184 us (0.61)
  local copies, waits for them, and re-layouts: 75.8 us -> 8.95 us
  blocking collectives: 64.7 us -> 0 us
  Pallas kernels: 0 us -> 50.6 us
  matrix products: 30.1 us -> 0 us
  other arithmetic: 10 us -> 1.79 us
  starting transfers between devices: 3.7 us -> 0.05 us
    unnamed x1 -> x3, waiting for transfers between devices: 0.02 us -> 105 us
    all_gather x1, waiting for transfers between devices: 103 us -> 0.01 us  [shards(): blocks = lax.all_gather(packed, 'row')]
    all_to_all x1 -> x0, blocking collectives: 64.7 us -> none  [shards(): lax.all_to_all(gathered, 'row', split_axis=0, concat_axis=2, tiled=True)]
    pallas_call x0 -> x3, Pallas kernels: none -> 50.6 us  [the longest x1 29.5 us: decode(): pl.pallas_call(functools.partial(decode_kernel, shard_rows, surface_rows,...]
    dot_general x3 -> x0, matrix products: 30.1 us -> none  [the longest x1 16.6 us: shards(): lax.dot_general(sign_table, lax.all_gather(slope_rows[None], 'dir', axis=...]
    all_to_all x3 -> x0, local copies, waits for them, and re-layouts: 20 us -> none  [shards(): lax.all_to_all(gathered, 'row', split_axis=0, concat_axis=2, tiled=True)]
    gather x3 -> x0, local copies, waits for them, and re-layouts: 14.6 us -> none  [pick_codes(): return code_table[positions]]
    reshape x5 -> x4, local copies, waits for them, and re-layouts: 17.3 us -> 2.79 us  [the longest x1 1.02 us: gather_small(): lax.all_gather(flat, ('dir', 'row')).reshape(directions, devices, -1)]
  transfers between devices with their start and end apart: 3 -> 2, of which waited for: 1 -> 1; matrix products, arithmetic and copies ran while one was open for 6% -> 4% of each run, Pallas kernels for 0% -> 12%
where the time goes in v1:
time: 184 us; the launch traced here: 181 us
  waiting for transfers between devices  105 us (57%)
  Pallas kernels  50.6 us (28%)
  between operations  14.9 us (8%)
  local copies, waits for them, and re-layouts  8.95 us (5%)
    unnamed x3, waiting for transfers between devices  105 us
    pallas_call x1, Pallas kernels, decode(): pl.pallas_call(functools.partial(decode_kernel, shard_rows, surface_rows,...  29.5 us
    pallas_call x1, Pallas kernels, gram(): pl.pallas_call(gram_kernel, grid=(acts // WINDOW,), out_shape=jax.ShapeDt...  18.9 us
  transfers between devices with their start and end apart: 2, of which 1 were waited for; matrix products, arithmetic and copies ran while one was open for 4% of the time, Pallas kernels for 12%

profile of v1, /device:TPU:0, one launch (start us, length us, event | category | flops | bytes accessed | tf_op | source)
XLA Modules:
  0.0 181.3 jit_solution(9837278653301862603)
XLA Ops:
  7.4 0.0 all-reduce.8.cloned.1.call-start
  7.4 0.8 reshape_squeeze.11
  8.1 0.7 reduce
  8.8 0.1 reshape_squeeze.9
  8.9 0.7 reduce.1
  9.6 0.1 reshape_squeeze.10
  9.7 0.2 add_dynamic-update-slice_fusion
  9.9 0.0 copy-start
  9.9 0.6 copy-done
  10.6 0.0 all-reduce.8.cloned.1.call-update
  10.6 0.0 all-gather.4.cloned.1.call-start
  10.6 2.1 %pack_influence.1 = bf16[2592,128]{1,0:T(8,128)(2,1)} custom-call(bf16[3,4,144,192]{3,2,1,0:T(8,128)(2,1)} %bitcast.21), custom_call_target="tpu_custom_call" | custom-call | bytes 995328 | tf_op jit(solution)/shard_map/pack_influence/pallas_call | solution.py:39
  12.8 0.0 all-gather.4.cloned.1.call-update
  12.8 1.6 broadcast_in_dim_reshape.6.codes_ref
  14.4 1.0 reshape.24
  15.4 0.1 dynamic_slice.3
  15.5 0.6 pad.20
  16.1 18.9 %gram_rows.1.gram_ref = bf16[216,6912]{1,0:T(8,128)(2,1)} custom-call(s32[1,256]{1,0:T(1,128)} %bitcast.23, s32[1,6912]{1,0:T(1,128)} %broadcast_in_dim_reshape.6.codes_ref, s32[1,2048]{1,0:T(1,128)} %bitcast.25), custom_call_target="tpu_custom_call" | custom-call | flops 6115295232 | bytes 2985984 | tf_op jit(solution)/shard_map/gram_rows/pallas_call | solution.py:93
  35.0 105.0 %all-reduce.8.cloned.1.call-done = s32[20864]{0:T(1024)} async-done(((s32[20864]{0:T(1024)}), s32[20864]{0:T(1024)}) %all-reduce.8.cloned.1.call-update) | async-done | bytes 83472
  139.9 1.0 reshape.22
  141.0 0.1 slice.13
  141.1 0.1 fusion
  141.1 0.1 mul.23
  141.2 0.1 copy.32
  141.3 0.1 copy.33
  141.5 0.7 reshape_reshape.3.foot_ref
  142.2 0.8 broadcast_in_dim_reshape.7.scale_ref
  143.0 0.1 copy.34
  143.1 0.1 copy.35
  143.3 0.1 pad_add_fusion.1
  143.4 0.1 pad_bitcast_fusion.3
  143.5 0.1 copy.39
  143.6 0.7 reshape.31.columns_ref
  144.3 0.0 all-gather.4.cloned.1.call-done
  144.3 29.5 %decode.1 = bf16[216,4,2560]{2,1,0:T(4,128)(2,1)} custom-call(s32[384]{0:T(512)} %reshape_reshape.3.foot_ref, bf16[216,6912]{1,0:T(8,128)(2,1)} %gram_rows.1.gram_ref, bf16[8,2592,128]{2,1,0:T(8,128)(2,1)} %bitcast.24, s32[16,6,256]{2,1,0:T(8,128)} %reshape.31.columns_ref, f32[4,4,256]{2,1,0:T(4,128)} %constant.22.clone.signs_ref, ...), custom_call_target="tpu_custom_call" | custom-call | flops 10871635968 | bytes 4423680 | tf_op jit(solution)/shard_map/decode/pallas_call | solution.py:226
  (4 shorter events, 0.0 us)
Async XLA Ops:
  7.4 132.6 %all-reduce.8.cloned.1.call-start = ((), (), s32[]{:S(2)}) async-start(), calls=%async_computation.1 | async-start | bytes 172032
  9.9 0.7 copy-start
  10.6 133.7 %all-gather.4.cloned.1.call-start = ((), (), s32[]{:S(2)}) async-start(), calls=%async_computation | async-start | bytes 5971968 | tf_op jit(solution)/shard_map/all_gather | solution.py:290
Sparse Core Ops, SparseCore 0:
  13.8 126.1 all-reduce.7
Sparse Core Ops, SparseCore 1:
  12.9 44.0 all-gather.3

commit v2 on v1

v2 whole, which is shorter than its diff:
```python
import functools
import math

import jax
import jax.numpy as jnp
import numpy as np
from jax import lax
from jax.experimental import pallas as pl
from jax.experimental.pallas import tpu as pltpu
from jax.sharding import PartitionSpec as P

NAR = 48
NA = 48
BAND = 3
LANES = 128
WINDOW = 256
VMEM_BYTES = 56 * 1024 * 1024


def parity(codes, rows):
    return lax.population_count(codes & rows) & 1


def pack_kernel(block_ref, packed_ref):
    mirrors, rows, slots, samples = block_ref.shape
    for unit in range(mirrors * rows // 2):
        base = unit * 3 * slots
        tails = []
        for side in range(2):
            k, l = divmod(2 * unit + side, rows)
            packed_ref[pl.ds(base + side * slots, slots), :] = block_ref[k, l, :, :LANES]
            tails.append(block_ref[k, l, :, LANES:])
        packed_ref[pl.ds(base + 2 * slots, slots), :] = jnp.concatenate(tails, axis=1)


def pack(block):
    mirrors, rows, slots, samples = block.shape
    return pl.pallas_call(
        pack_kernel,
        out_shape=jax.ShapeDtypeStruct((mirrors * rows * slots * samples // LANES, LANES), block.dtype),
        in_specs=[pl.BlockSpec(memory_space=pltpu.VMEM)],
        out_specs=pl.BlockSpec(memory_space=pltpu.VMEM),
        compiler_params=pltpu.CompilerParams(vmem_limit_bytes=VMEM_BYTES),
        cost_estimate=pl.CostEstimate(flops=0, bytes_accessed=3 * block.size, transcendentals=0),
        name="pack_influence",
    )(block)


def column_of(row, length):
    return jnp.transpose(jnp.broadcast_to(row, (LANES, length)), (1, 0))


def gram_kernel(own_ref, codes_ref, pokes_ref, gram_ref, poke_columns, own_signs, own_sums):
    pokes = pokes_ref.shape[1]
    own = own_signs.shape[0]

    @pl.when(pl.program_id(0) == 0)
    def _():
        for at in range(0, pokes, LANES):
            poke_columns[pl.ds(at, LANES), :] = column_of(pokes_ref[:, at:at + LANES], LANES)
        own_column = jnp.concatenate(
            [column_of(own_ref[:, at:at + LANES], LANES) for at in range(0, own_ref.shape[1], LANES)], axis=0
        )[:own]
        total = jnp.zeros((own, LANES), jnp.float32)
        for at in range(0, pokes, LANES):
            signs = (1 - 2 * parity(own_column, pokes_ref[:, at:at + LANES])).astype(jnp.float32)
            own_signs[:, at:at + LANES] = signs.astype(jnp.bfloat16)
            total = total + signs
        own_sums[...] = jnp.broadcast_to(jnp.sum(total, axis=1, keepdims=True), own_sums.shape)

    width = codes_ref.shape[1]
    depth = 256
    total = jnp.zeros((own, width), jnp.float32)
    for at in range(0, pokes, depth):
        column = poke_columns[pl.ds(at, depth), :]
        bits = [
            parity(codes_ref[:, lane:lane + LANES], column).astype(jnp.float32).astype(jnp.bfloat16)
            for lane in range(0, width, LANES)
        ]
        total = total + jnp.dot(
            own_signs[:, at:at + depth], jnp.concatenate(bits, axis=1), preferred_element_type=jnp.float32
        )
    sums = jnp.concatenate([own_sums[...]] * (width // LANES), axis=1)
    gram_ref[...] = (sums - 2.0 * total).astype(jnp.bfloat16)


def gram(own_codes, codes, pokes):
    padded = -(-own_codes.shape[0] // LANES) * LANES
    own_row = jnp.pad(own_codes, (0, padded - own_codes.shape[0]))[None]
    own = -(-own_codes.shape[0] // 16) * 16
    acts, count = codes.shape[0], pokes.shape[0]
    return pl.pallas_call(
        gram_kernel,
        grid=(acts // WINDOW,),
        out_shape=jax.ShapeDtypeStruct((own, acts), jnp.bfloat16),
        in_specs=[
            pl.BlockSpec((1, padded), lambda s: (0, 0)),
            pl.BlockSpec((1, WINDOW), lambda s: (0, s)),
            pl.BlockSpec((1, count), lambda s: (0, 0)),
        ],
        out_specs=pl.BlockSpec((own, WINDOW), lambda s: (0, s)),
        scratch_shapes=[
            pltpu.VMEM((count, LANES), jnp.int32),
            pltpu.VMEM((own, count), jnp.bfloat16),
            pltpu.VMEM((own, LANES), jnp.float32),
        ],
        compiler_params=pltpu.CompilerParams(vmem_limit_bytes=VMEM_BYTES),
        cost_estimate=pl.CostEstimate(
            flops=2 * own * acts * count, bytes_accessed=2 * own * acts, transcendentals=0
        ),
        name="gram_rows",
    )(own_row, codes[None], pokes[None])


def band_product(block_parts, q, row_shape, block, surface_rows, gram_ref, window_ref):
    mirrors, shard_rows, slots, samples = row_shape
    k, l = divmod(q, shard_rows)
    band = jnp.clip((block * shard_rows + l) * NAR // surface_rows - 1, 0, NAR - BAND)
    column = (k * NAR + band) * NA
    base = pl.multiple_of(column // LANES * LANES, LANES)
    shift = pl.multiple_of(column - base, 16)
    unit, side = divmod(q, 2)
    units = mirrors * shard_rows // 2 // len(block_parts)
    part, at = block_parts[unit // units], unit % units * 3 * slots
    window_ref[...] = jnp.zeros(window_ref.shape, window_ref.dtype)
    window_ref[pl.ds(shift, slots), :LANES] = part[pl.ds(at + side * slots, slots), :]
    window_ref[pl.ds(shift, slots), LANES:] = part[pl.ds(at + 2 * slots, slots), :]
    u = jnp.dot(gram_ref[:, pl.ds(base, WINDOW)], window_ref[...], preferred_element_type=jnp.float32)
    rest = u[:, LANES:]
    turned = pltpu.roll(rest, LANES // 2, 1)
    low, high = (rest, turned) if side == 0 else (turned, rest)
    lane = lax.broadcasted_iota(jnp.int32, rest.shape, 1)
    rest = jnp.where(lane < samples - LANES, low, high)
    return u[:, :LANES].astype(jnp.bfloat16), rest.astype(jnp.bfloat16)


def bands_kernel(row_shape, surface_rows, first, counts, own_ref, gram_ref, *refs):
    sources = refs[:len(counts)]
    out_ref, window = refs[-2:]
    step = pl.program_id(0)
    start = 0
    for source, count in zip(sources, counts):
        @pl.when((step >= start) & (step < start + count))
        def _():
            block = (first + step) ^ own_ref[0]
            for q in range(row_shape[0] * row_shape[1]):
                head, rest = band_product(
                    [source.at[0]], q, row_shape, block, surface_rows, gram_ref, window.at[q % window.shape[0]]
                )
                out_ref[0, q, :, :LANES] = head
                out_ref[0, q, :, LANES:] = rest
        start += count


def bands(gram_rows, sources, decoded, first, place, row_shape, surface_rows):
    own = gram_rows.shape[0]
    counts = [source.shape[0] for source in sources]
    starts = np.cumsum([0] + counts)
    total = surface_rows // row_shape[1]
    rows = row_shape[0] * row_shape[1]
    specs = [
        pl.BlockSpec(
            (1,) + source.shape[1:],
            functools.partial(lambda low, high, s: (jnp.clip(s - low, 0, high - 1), 0, 0), int(starts[n]), counts[n]),
        )
        for n, source in enumerate(sources)
    ]
    arguments = [place, gram_rows, *sources]
    in_specs = [pl.BlockSpec(memory_space=pltpu.SMEM), pl.BlockSpec(memory_space=pltpu.VMEM), *specs]
    aliases = {}
    body = functools.partial(bands_kernel, row_shape, surface_rows, first, counts)
    if decoded is not None:
        aliases = {len(arguments): 0}
        arguments.append(decoded)
        in_specs.append(pl.BlockSpec(memory_space=pl.ANY))
    flops = 2 * own * WINDOW * WINDOW * rows * sum(counts)
    return pl.pallas_call(
        body,
        grid=(sum(counts),),
        out_shape=jax.ShapeDtypeStruct((total, rows, own, WINDOW), jnp.bfloat16),
        in_specs=in_specs,
        out_specs=pl.BlockSpec((1, rows, own, WINDOW), lambda s: (first + s, 0, 0, 0)),
        scratch_shapes=[pltpu.VMEM((4, WINDOW, WINDOW), jnp.bfloat16)],
        input_output_aliases=aliases,
        compiler_params=pltpu.CompilerParams(vmem_limit_bytes=VMEM_BYTES),
        cost_estimate=pl.CostEstimate(
            flops=flops, bytes_accessed=2 * own * WINDOW * rows * sum(counts), transcendentals=0
        ),
        name="bands",
    )(*arguments)


def build_differences(columns_ref, signs_ref, differences, mirrors, samples):
    lanes = columns_ref.shape[-1]
    tail = samples - LANES

    def build(d, _):
        for k in range(mirrors):
            first = columns_ref[d, 2 * k:2 * k + 1, :]
            second = columns_ref[d, 2 * k + 1:2 * k + 2, :]
            for y in range(2):
                plus = signs_ref[2 * y:2 * y + 1, :]
                minus = signs_ref[2 * y + 1:2 * y + 2, :]

                def piece(start, length):
                    x = start + lax.broadcasted_iota(jnp.int32, (length, lanes), 0)
                    value = jnp.where(x == second, plus, 0.0) + jnp.where(x == first, minus, 0.0)
                    return value.astype(jnp.bfloat16)

                differences[d, pl.ds((2 * k + y) * LANES, LANES), :] = piece(0, LANES)
                differences[d, pl.ds(2 * mirrors * LANES + k * LANES + y * tail, tail), :] = piece(LANES, tail)
        return 0

    lax.fori_loop(0, differences.shape[0], build, 0)


def decode_kernel(
    row_shape, surface_rows, own, late, place_ref, foot_ref, columns_ref, signs_ref, scale_ref, *refs
):
    mirrors, shard_rows, slots, samples = row_shape
    extras = refs[:late[1] * late[2]]
    gram_ref, decoded_ref, out_ref, decoded, differences, total, window, semaphores = refs[late[1] * late[2]:]
    group = pl.program_id(0)
    directions = differences.shape[0]
    pupil = columns_ref.shape[2]
    phases = out_ref.shape[2] // pupil
    tail = samples - LANES
    ready = late[0]

    @pl.when(group == 0)
    def _():
        copies = [
            pltpu.make_async_copy(decoded_ref.at[block], decoded.at[block], semaphores.at[block])
            for block in range(ready)
        ]
        for copy in copies:
            copy.start()
        build_differences(columns_ref, signs_ref, differences, mirrors, samples)
        for n in range(late[1]):
            block = (ready + n) ^ place_ref[0]
            parts = [extras[n * late[2] + part] for part in range(late[2])]
            for q in range(mirrors * shard_rows):
                head, rest = band_product(
                    parts, q, row_shape, block, surface_rows, gram_ref, window.at[q % window.shape[0]]
                )
                decoded[ready + n, q, :, :LANES] = head
                decoded[ready + n, q, :, LANES:] = rest
        for copy in copies:
            copy.wait()

    lane = lax.broadcasted_iota(jnp.int32, (decoded.shape[2], LANES), 1)

    def one(d, _):
        place = d ^ place_ref[1]
        left = []
        for phase in range(phases):
            i = group * phases + phase
            block = (2 * i // shard_rows) ^ place_ref[0]
            heads, tails = [], []
            for k in range(mirrors):
                picked = []
                for y in range(2):
                    row = foot_ref[((block * directions + place) * mirrors + k) * shard_rows + (2 * i + y) % shard_rows]
                    picked.append(
                        (row // shard_rows ^ place_ref[0], k * shard_rows + row % shard_rows)
                    )
                heads += [decoded[e, q, :, :LANES] for e, q in picked]
                tails.append(
                    jnp.where(lane < tail, *(decoded[e, q, :, LANES:] for e, q in picked))
                )
            left.append(jnp.concatenate(heads + tails, axis=1))
        rows = left[0].shape[0]
        product = jnp.dot(
            jnp.concatenate(left, axis=0), differences[place], preferred_element_type=jnp.float32
        )
        pieces = []
        for phase in range(phases):
            i = group * phases + phase
            block = (2 * i // shard_rows) ^ place_ref[0]
            factor = scale_ref[block, place, pl.ds(i % (shard_rows // 2), 1), :]
            pieces.append(product[phase * rows:phase * rows + own] * factor)
        value = jnp.concatenate(pieces, axis=1)
        for tile in range(out_ref.shape[2] // LANES):
            total[tile, pl.ds(d, own, stride=directions), :] = value[:, tile * LANES:(tile + 1) * LANES]
        return 0

    lax.fori_loop(0, directions, one, 0)
    for tile in range(out_ref.shape[2] // LANES):
        value = total[tile].reshape(own, directions, LANES)
        out_ref[:, :, tile * LANES:(tile + 1) * LANES] = value.astype(out_ref.dtype)


def decode(place, foot_rows, columns, scale, gram_rows, decoded, extras, parts, own, row_shape, surface_rows):
    directions, mirrors = columns.shape[0], row_shape[0]
    pupil = columns.shape[-1]
    padded = gram_rows.shape[0]
    phases = LANES // math.gcd(pupil, LANES)
    width = surface_rows // 2 * pupil
    lanes = phases * pupil
    signs = np.ones((4, pupil), np.float32)
    signs[1, :pupil // 2] = signs[3, :pupil // 2] = signs[0, pupil // 2:] = signs[1, pupil // 2:] = -1
    late = len(extras) // parts
    ready = decoded.shape[0] - late
    flops = 2 * padded * 3 * mirrors * LANES * pupil * directions * surface_rows // 2
    vmem = pl.BlockSpec(memory_space=pltpu.VMEM)
    smem = pl.BlockSpec(memory_space=pltpu.SMEM)
    return pl.pallas_call(
        functools.partial(decode_kernel, row_shape, surface_rows, own, (ready, late, parts)),
        grid=(width // lanes,),
        out_shape=jax.ShapeDtypeStruct((own, directions, width), jnp.bfloat16),
        in_specs=[smem, smem, vmem, vmem, vmem] + [vmem] * len(extras) + [vmem, pl.BlockSpec(memory_space=pl.ANY)],
        out_specs=pl.BlockSpec((own, directions, lanes), lambda s: (0, 0, s)),
        scratch_shapes=[
            pltpu.VMEM(decoded.shape, jnp.bfloat16),
            pltpu.VMEM((directions, 3 * mirrors * LANES, pupil), jnp.bfloat16),
            pltpu.VMEM((lanes // LANES, own * directions, LANES), jnp.float32),
            pltpu.VMEM((4, WINDOW, WINDOW), jnp.bfloat16),
            pltpu.SemaphoreType.DMA((decoded.shape[0],)),
        ],
        compiler_params=pltpu.CompilerParams(vmem_limit_bytes=VMEM_BYTES),
        cost_estimate=pl.CostEstimate(flops=flops, bytes_accessed=2 * own * directions * width, transcendentals=0),
        name="decode",
    )(place, foot_rows.reshape(-1), columns, jnp.asarray(signs), scale, *extras, gram_rows, decoded)


def swap(block, axis, distance):
    return lax.ppermute(block, axis, [(i, i ^ distance) for i in range(lax.axis_size(axis))])


def small_arrays(foot_rows, foot_columns, valid, staged):
    mirrors, shard_rows = foot_rows.shape[1:]
    pupil = foot_columns.shape[2]
    pairs = foot_columns[0].reshape(mirrors, pupil // 2, 2).transpose(0, 2, 1).reshape(2 * mirrors, pupil // 2)
    lines = jnp.concatenate([pairs, valid[0]], axis=0)
    lines = jnp.concatenate([lines, lines], axis=1)
    row_line = jnp.pad(foot_rows[0].reshape(1, -1), ((0, 0), (0, pupil - mirrors * shard_rows)))
    lines = jnp.concatenate([lines, row_line], axis=0)
    if staged:
        directions = lax.axis_size("dir")
        every = jnp.stack([lines] + [swap(lines, "dir", e) for e in range(1, directions)])
        columns, rest = every[:, :2 * mirrors], every[None, :, 2 * mirrors:]
        distance = 1
        while distance < lax.axis_size("row"):
            rest = jnp.concatenate([rest, swap(rest, "row", distance)], axis=0)
            distance *= 2
    else:
        every = lax.all_gather(lax.all_gather(lines, "dir"), "row")
        columns, rest = every[0, :, :2 * mirrors], every[:, :, 2 * mirrors:]
    return rest[:, :, -1, :mirrors * shard_rows], columns, rest[:, :, :-1]


def shards(influence, foot_rows, foot_columns, actuator_codes, poke_rows, subaperture_valid):
    mirrors, shard_rows, samples, slots = influence.shape
    row_shape = (mirrors, shard_rows, slots, samples)
    directions, devices = lax.axis_size("dir"), lax.axis_size("row")
    surface_rows = shard_rows * devices
    staged = devices == 8 and directions & (directions - 1) == 0
    packed = pack(jnp.swapaxes(influence, 2, 3))
    if staged:
        half = packed.shape[0] // 2
        beside, across, sibling = swap(packed, "row", 2), swap(packed, "row", 4), swap(packed, "row", 1)
        upper, lower = swap(beside[:half], "row", 4), swap(across[half:], "row", 2)
        beside_sibling, across_sibling = swap(beside, "row", 1), swap(across, "row", 1)
        late = [upper, lower, swap(upper, "row", 1), swap(lower, "row", 1)]
        early = [[packed, sibling], [beside, beside_sibling, across, across_sibling]]
        place = jnp.stack([lax.axis_index("row"), lax.axis_index("dir")]).astype(jnp.int32)
    else:
        early, late = [[lax.all_gather(packed, "row")]], []
        place = jnp.zeros((2,), jnp.int32)
    rows, columns, valid = small_arrays(foot_rows, foot_columns, subaperture_valid, staged)
    codes = actuator_codes.reshape(-1)
    own = codes.shape[0] // (directions * devices)
    device = lax.axis_index("dir") * devices + lax.axis_index("row")
    gram_rows = gram(lax.dynamic_slice_in_dim(codes, device * own, own), codes, poke_rows)
    scale = valid.astype(jnp.float32) * (0.5 * poke_rows.shape[0] ** (-0.5))
    decoded, first = None, 0
    for sources in early:
        sources = [source if source.ndim == 3 else source[None] for source in sources]
        decoded = bands(gram_rows, sources, decoded, first, place, row_shape, surface_rows)
        first += sum(source.shape[0] for source in sources)
    return decode(place, rows, columns, scale, gram_rows, decoded, late, 2, own, row_shape, surface_rows)


def solution(mesh):
    return jax.shard_map(
        shards,
        mesh=mesh,
        in_specs=(
            P(None, "row", None, None),
            P("dir", None, "row"),
            P("dir", None, None),
            P(),
            P(),
            P("dir", "row", None),
        ),
        out_specs=P(("dir", "row"), None, None),
        check_vma=False,
    )
```

time: 184 us -> 89.4 us (0.49); the launches traced: 181 us -> 88.6 us
  waiting for transfers between devices: 105 us -> 9.89 us
  between operations: 14.9 us -> 0.09 us
  starting transfers between devices: 0.05 us -> 13.3 us
  Pallas kernels: 50.6 us -> 54.9 us
  local copies, waits for them, and re-layouts: 8.95 us -> 6.19 us
  other arithmetic: 1.79 us -> 4.22 us
    unnamed x3 -> x0, waiting for transfers between devices: 105 us -> none
    ppermute x0 -> x15, starting transfers between devices: none -> 13.3 us  [swap(): lax.ppermute(block, axis, [(i, i ^ distance) for i in range(lax.axis_size...]
    ppermute x0 -> x15, waiting for transfers between devices: none -> 9.89 us  [swap(): lax.ppermute(block, axis, [(i, i ^ distance) for i in range(lax.axis_size...]
    pallas_call x1 -> x3, Pallas kernels: 29.5 us -> 33.8 us  [the longest x1 21.6 us: decode(): pl.pallas_call(functools.partial(decode_kernel, row_shape, surface_rows,...]
    another operation x1 -> x3, other arithmetic: 0.01 us -> 2.03 us  [the longest x2 1.44 us: small_arrays(): jnp.stack([lines] + [swap(lines, 'dir', e) for e in range(1, directions)])]
  transfers between devices with their start and end apart: 2 -> 15, of which waited for: 1 -> 4; matrix products, arithmetic and copies ran while one was open for 4% -> 10% of each run, Pallas kernels for 12% -> 35%
where the time goes in v2:
time: 89.4 us; the launch traced here: 88.6 us
  Pallas kernels  54.9 us (61%)
  starting transfers between devices  13.3 us (15%)
  waiting for transfers between devices  9.89 us (11%)
  local copies, waits for them, and re-layouts  6.19 us (7%)
  other arithmetic  4.22 us (5%)
    pallas_call x1, Pallas kernels, decode(): pl.pallas_call(functools.partial(decode_kernel, row_shape, surface_rows,...  21.6 us
    pallas_call x1, Pallas kernels, gram(): pl.pallas_call(gram_kernel, grid=(acts // WINDOW,), out_shape=jax.ShapeDt...  19 us
    ppermute x15, starting transfers between devices, swap(): lax.ppermute(block, axis, [(i, i ^ distance) for i in range(lax.axis_size...  13.3 us
    pallas_call x2, Pallas kernels, bands(): pl.pallas_call(body, grid=(sum(counts),), out_shape=jax.ShapeDtypeStruct(...  12.2 us
    ppermute x15, waiting for transfers between devices, swap(): lax.ppermute(block, axis, [(i, i ^ distance) for i in range(lax.axis_size...  9.89 us
    pallas_call x1, Pallas kernels, pack(): pl.pallas_call(pack_kernel, out_shape=jax.ShapeDtypeStruct((mirrors * row...  2.14 us
    unnamed x10, local copies, waits for them, and re-layouts  1.88 us
  transfers between devices with their start and end apart: 15, of which 4 were waited for; matrix products, arithmetic and copies ran while one was open for 10% of the time, Pallas kernels for 35%

profile of v2, /device:TPU:0, one launch (start us, length us, event | category | flops | bytes accessed | tf_op | source)
XLA Modules:
  0.0 88.6 jit_solution(15572896369001283759)
XLA Ops:
  0.0 2.1 %pack_influence.1 = bf16[2592,128]{1,0:T(8,128)(2,1)} custom-call(bf16[3,4,144,192]{3,2,1,0:T(8,128)(2,1)} %bitcast.23), custom_call_target="tpu_custom_call" | custom-call | bytes 995328 | tf_op jit(solution)/shard_map/pack_influence/pallas_call | solution.py:38
  2.1 2.9 %collective-permute-start.6 = (bf16[2592,128]{1,0:T(8,128)(2,1)}, bf16[2592,128]{1,0:T(8,128)(2,1)S(1)}, u32[]{:S(2)}, u32[]{:S(2)}) collective-permute-start(bf16[2592,128]{1,0:T(8,128)(2,1)} %pack_influence.1), channel_id=1, source_target_pairs={{0,2},{1,3},{2,0},{3,1},{4,6},{5,7},{6,4},{7,5},{8,10},{9,11},{10,... | collective-permute-start | bytes 1990664 | tf_op jit(solution)/shard_map/ppermute | solution.py:327
  5.1 1.5 %collective-permute-start.8 = (bf16[2592,128]{1,0:T(8,128)(2,1)}, bf16[2592,128]{1,0:T(8,128)(2,1)S(1)}, u32[]{:S(2)}, u32[]{:S(2)}) collective-permute-start(bf16[2592,128]{1,0:T(8,128)(2,1)} %pack_influence.1), channel_id=1, source_target_pairs={{0,4},{1,5},{2,6},{3,7},{4,0},{5,1},{6,2},{7,3},{8,12},{9,13},{10,... | collective-permute-start | bytes 1990664 | tf_op jit(solution)/shard_map/ppermute | solution.py:327
  6.6 0.7 reduce
  7.3 0.1 reshape_squeeze.9
  7.4 0.1 copy.10
  7.5 0.7 reduce.1
  8.3 0.1 reshape_squeeze.10
  8.3 0.8 fusion.2
  9.2 1.6 %collective-permute-start = (s32[9,160]{1,0:T(8,128)S(1)}, s32[9,160]{1,0:T(8,128)S(1)}, u32[]{:S(2)}, u32[]{:S(2)}) collective-permute-start(s32[9,160]{1,0:T(8,128)S(1)} %get-tuple-element.6), channel_id=1, source_target_pairs={{0,8},{8,0},{16,24},{24,16},{1,9},{9,1},{17,25},{25,17},{2,10},{10... | collective-permute-start | bytes 17288 | tf_op jit(solution)/shard_map/ppermute | solution.py:327
  10.8 2.6 %collective-permute-start.1 = (s32[9,160]{1,0:T(8,128)S(1)}, s32[9,160]{1,0:T(8,128)S(1)}, u32[]{:S(2)}, u32[]{:S(2)}) collective-permute-start(s32[9,160]{1,0:T(8,128)S(1)} %get-tuple-element.6), channel_id=1, source_target_pairs={{0,16},{8,24},{16,0},{24,8},{1,17},{9,25},{17,1},{25,9},{2,18},{10... | collective-permute-start | bytes 17288 | tf_op jit(solution)/shard_map/ppermute | solution.py:327
  13.4 0.2 collective-permute-start.2
  13.6 1.9 %collective-permute-done.1 = s32[9,160]{1,0:T(8,128)S(1)} collective-permute-done((s32[9,160]{1,0:T(8,128)S(1)}, s32[9,160]{1,0:T(8,128)S(1)}, u32[]{:S(2)}, u32[]{:S(2)}) %collective-permute-start.1) | collective-permute-done | bytes 5792 | tf_op jit(solution)/shard_map/ppermute | solution.py:327
  15.5 3.4 %collective-permute-done.2 = s32[9,160]{1,0:T(8,128)S(1)} collective-permute-done((s32[9,160]{1,0:T(8,128)S(1)}, s32[9,160]{1,0:T(8,128)S(1)}, u32[]{:S(2)}, u32[]{:S(2)}) %collective-permute-start.2) | collective-permute-done | bytes 5792 | tf_op jit(solution)/shard_map/ppermute | solution.py:327
  18.9 0.1 collective-permute-start.3
  19.0 1.2 %collective-permute-done.3 = s32[1,4,3,160]{3,2,1,0:T(4,128)S(1)} collective-permute-done((s32[1,4,3,160]{3,2,1,0:T(4,128)S(1)}, s32[1,4,3,160]{3,2,1,0:T(4,128)S(1)}, u32[]{:S(2)}, u32[]{:S(2)}) %collective-permute-start.3) | collective-permute-done | bytes 7712 | tf_op jit(solution)/shard_map/ppermute | solution.py:327
  20.2 0.6 collective-permute-start.4
  20.8 3.4 %collective-permute-done.4 = s32[2,4,3,160]{3,2,1,0:T(4,128)S(1)} collective-permute-done((s32[2,4,3,160]{3,2,1,0:T(4,128)S(1)}, s32[2,4,3,160]{3,2,1,0:T(4,128)S(1)}, u32[]{:S(2)}, u32[]{:S(2)}) %collective-permute-start.4) | collective-permute-done | bytes 15392 | tf_op jit(solution)/shard_map/ppermute | solution.py:327
  24.2 0.6 collective-permute-start.5
  24.7 0.0 collective-permute-start.14
  24.7 1.0 %reshape.7 = s32[6912]{0:T(1024)S(1)} reshape(s32[3,48,48]{2,1,0:T(8,128)} %param.10) | data formatting | bytes 55296 | tf_op jit(solution)/shard_map/reshape | solution.py:371
  25.7 1.6 %broadcast_in_dim_reshape.3.codes_ref = s32[1,6912]{1,0:T(1,128)} reshape(s32[3,48,48]{2,1,0:T(8,128)} %param.10) | data formatting | bytes 55296 | tf_op jit(solution)/shard_map/broadcast_in_dim;reshape | solution.py:112
  27.3 0.1 dynamic_slice.3
  27.4 0.6 pad.9
  28.0 0.0 collective-permute-done.6
  28.0 1.6 %collective-permute-start.7 = (bf16[1296,128]{1,0:T(8,128)(2,1)S(1)}, bf16[1296,128]{1,0:T(8,128)(2,1)}, u32[]{:S(2)}, u32[]{:S(2)}) collective-permute-start(bf16[1296,128]{1,0:T(8,128)(2,1)S(1)} %slice.24), channel_id=1, source_target_pairs={{0,4},{1,5},{2,6},{3,7},{4,0},{5,1},{6,2},{7,3},{8,12},{9,13},{10,... | collective-permute-start | bytes 995336 | tf_op jit(solution)/shard_map/ppermute | solution.py:327
  29.6 0.6 collective-permute-start.9
  30.2 0.0 collective-permute-start.12
  30.2 0.0 collective-permute-done.5
  30.3 0.5 collective-permute-start.13
  30.8 19.0 %gram_rows.1.gram_ref.refs_4_ = bf16[224,6912]{1,0:T(8,128)(2,1)} custom-call(s32[1,256]{1,0:T(1,128)} %bitcast.35, s32[1,6912]{1,0:T(1,128)} %broadcast_in_dim_reshape.3.codes_ref, s32[1,2048]{1,0:T(1,128)} %bitcast.36), custom_call_target="tpu_custom_call" | custom-call | flops 6341787648 | bytes 3096576 | tf_op jit(solution)/shard_map/gram_rows/pallas_call | solution.py:92
  49.7 0.6 pad_add_fusion.9.own_ref.place_ref
  50.3 0.0 collective-permute-done.7.refs_0_
  50.3 0.0 collective-permute-start.10
  50.3 0.0 collective-permute-done.9.refs_1_
  50.3 0.5 collective-permute-start.11
  50.8 0.6 pad_add_fusion.4.columns_ref
  51.4 0.1 add_reduce_fusion
  51.5 0.7 reshape_squeeze.11.foot_ref
  52.2 0.7 fusion.1.scale_ref
  52.9 0.0 collective-permute-done.14
  52.9 0.8 copy-done.2
  53.7 4.9 %bands.2.refs_4_ = bf16[8,12,224,256]{3,2,1,0:T(8,128)(2,1)} custom-call(s32[2]{0:T(128)} %pad_add_fusion.9.own_ref.place_ref, bf16[224,6912]{1,0:T(8,128)(2,1)} %gram_rows.1.gram_ref.refs_4_, bf16[1,2592,128]{2,1,0:T(8,128)(2,1)} %bitcast.20, bf16[1,2592,128]{2,1,0:T(8,128)(2,1)} %bitcast.24), custom_call_target="tpu_custom_call" | custom-call | flops 704643072 | bytes 2752512 | tf_op jit(solution)/shard_map/bands/pallas_call | solution.py:177
  58.7 0.0 collective-permute-done.13
  58.7 0.8 copy-done.3
  59.5 0.2 copy-done.4
  59.7 7.3 %bands.3.refs_5_ = bf16[8,12,224,256]{3,2,1,0:T(8,128)(2,1)} custom-call(s32[2]{0:T(128)} %pad_add_fusion.9.own_ref.place_ref, bf16[224,6912]{1,0:T(8,128)(2,1)} %gram_rows.1.gram_ref.refs_4_, bf16[1,2592,128]{2,1,0:T(8,128)(2,1)} %bitcast.21, bf16[1,2592,128]{2,1,0:T(8,128)(2,1)} %bitcast.25, ...), custom_call_target="tpu_custom_call", output_to_operand_aliasing={{}: (6, {})} | custom-call | flops 1409286144 | bytes 5505024 | tf_op jit(solution)/shard_map/bands/pallas_call | solution.py:177
  67.0 21.6 %decode.1 = bf16[216,4,2560]{2,1,0:T(4,128)(2,1)} custom-call(s32[2]{0:T(128)} %pad_add_fusion.9.own_ref.place_ref, s32[384]{0:T(512)} %reshape_squeeze.11.foot_ref, s32[4,6,160]{2,1,0:T(8,128)} %pad_add_fusion.4.columns_ref, f32[4,160]{1,0:T(4,128)} %constant.20.clone.signs_ref, f32[8,4,2,160]{3,2,1,0:T(2,128)} %fusion.1.scale_ref, ...), custom_call_target="tpu_custom_call" | custom-call | flops 5284823040 | bytes 4423680 | tf_op jit(solution)/shard_map/decode/pallas_call | solution.py:307
  (18 shorter events, 0.1 us)
Async XLA Ops:
  2.1 25.9 %collective-permute-start.6 = (bf16[2592,128]{1,0:T(8,128)(2,1)}, bf16[2592,128]{1,0:T(8,128)(2,1)S(1)}, u32[]{:S(2)}, u32[]{:S(2)}) collective-permute-start(bf16[2592,128]{1,0:T(8,128)(2,1)} %pack_influence.1), channel_id=1, source_target_pairs={{0,2},{1,3},{2,0},{3,1},{4,6},{5,7},{6,4},{7,5},{8,10},{9,11},{10,... | collective-permute-start | bytes 1990664 | tf_op jit(solution)/shard_map/ppermute | solution.py:327
  5.1 24.5 %collective-permute-start.8 = (bf16[2592,128]{1,0:T(8,128)(2,1)}, bf16[2592,128]{1,0:T(8,128)(2,1)S(1)}, u32[]{:S(2)}, u32[]{:S(2)}) collective-permute-start(bf16[2592,128]{1,0:T(8,128)(2,1)} %pack_influence.1), channel_id=1, source_target_pairs={{0,4},{1,5},{2,6},{3,7},{4,0},{5,1},{6,2},{7,3},{8,12},{9,13},{10,... | collective-permute-start | bytes 1990664 | tf_op jit(solution)/shard_map/ppermute | solution.py:327
  9.2 4.4 %collective-permute-start = (s32[9,160]{1,0:T(8,128)S(1)}, s32[9,160]{1,0:T(8,128)S(1)}, u32[]{:S(2)}, u32[]{:S(2)}) collective-permute-start(s32[9,160]{1,0:T(8,128)S(1)} %get-tuple-element.6), channel_id=1, source_target_pairs={{0,8},{8,0},{16,24},{24,16},{1,9},{9,1},{17,25},{25,17},{2,10},{10... | collective-permute-start | bytes 17288 | tf_op jit(solution)/shard_map/ppermute | solution.py:327
  10.8 4.7 %collective-permute-start.1 = (s32[9,160]{1,0:T(8,128)S(1)}, s32[9,160]{1,0:T(8,128)S(1)}, u32[]{:S(2)}, u32[]{:S(2)}) collective-permute-start(s32[9,160]{1,0:T(8,128)S(1)} %get-tuple-element.6), channel_id=1, source_target_pairs={{0,16},{8,24},{16,0},{24,8},{1,17},{9,25},{17,1},{25,9},{2,18},{10... | collective-permute-start | bytes 17288 | tf_op jit(solution)/shard_map/ppermute | solution.py:327
  13.4 5.5 %collective-permute-start.2 = (s32[9,160]{1,0:T(8,128)S(1)}, s32[9,160]{1,0:T(8,128)S(1)}, u32[]{:S(2)}, u32[]{:S(2)}) collective-permute-start(s32[9,160]{1,0:T(8,128)S(1)} %get-tuple-element.6), channel_id=1, source_target_pairs={{0,24},{8,16},{16,8},{24,0},{1,25},{9,17},{17,9},{25,1},{2,26},{10... | collective-permute-start | bytes 17288 | tf_op jit(solution)/shard_map/ppermute | solution.py:327
  18.9 1.2 %collective-permute-start.3 = (s32[1,4,3,160]{3,2,1,0:T(4,128)S(1)}, s32[1,4,3,160]{3,2,1,0:T(4,128)S(1)}, u32[]{:S(2)}, u32[]{:S(2)}) collective-permute-start(s32[1,4,3,160]{3,2,1,0:T(4,128)S(1)} %add_bitcast_fusion), channel_id=1, source_target_pairs={{0,1},{1,0},{2,3},{3,2},{4,5},{5,4},{6,7},{7,6},{8,9},{9,8},{10,11... | collective-permute-start | bytes 23048 | tf_op jit(solution)/shard_map/ppermute | solution.py:327
  20.2 4.0 %collective-permute-start.4 = (s32[2,4,3,160]{3,2,1,0:T(4,128)S(1)}, s32[2,4,3,160]{3,2,1,0:T(4,128)S(1)}, u32[]{:S(2)}, u32[]{:S(2)}) collective-permute-start(s32[2,4,3,160]{3,2,1,0:T(4,128)S(1)} %pad_add_fusion.7), channel_id=1, source_target_pairs={{0,2},{1,3},{2,0},{3,1},{4,6},{5,7},{6,4},{7,5},{8,10},{9,11},{10,... | collective-permute-start | bytes 46088 | tf_op jit(solution)/shard_map/ppermute | solution.py:327
  24.2 6.1 %collective-permute-start.5 = (s32[4,4,3,160]{3,2,1,0:T(4,128)S(1)}, s32[4,4,3,160]{3,2,1,0:T(4,128)S(1)}, u32[]{:S(2)}, u32[]{:S(2)}) collective-permute-start(s32[4,4,3,160]{3,2,1,0:T(4,128)S(1)} %pad_add_fusion.3), channel_id=1, source_target_pairs={{0,4},{1,5},{2,6},{3,7},{4,0},{5,1},{6,2},{7,3},{8,12},{9,13},{10,... | collective-permute-start | bytes 92168 | tf_op jit(solution)/shard_map/ppermute | solution.py:327
  24.7 28.2 %collective-permute-start.14 = (bf16[2592,128]{1,0:T(8,128)(2,1)}, bf16[2592,128]{1,0:T(8,128)(2,1)S(1)}, u32[]{:S(2)}, u32[]{:S(2)}) collective-permute-start(bf16[2592,128]{1,0:T(8,128)(2,1)} %pack_influence.1), channel_id=1, source_target_pairs={{0,1},{1,0},{2,3},{3,2},{4,5},{5,4},{6,7},{7,6},{8,9},{9,8},{10,11... | collective-permute-start | bytes 1990664 | tf_op jit(solution)/shard_map/ppermute | solution.py:327
  28.0 21.7 %copy-start = (bf16[2592,128]{1,0:T(8,128)(2,1)}, bf16[2592,128]{1,0:T(8,128)(2,1)S(1)}, u32[]{:S(2)}) copy-start(bf16[2592,128]{1,0:T(8,128)(2,1)S(1)} %collective-permute-done.6) | copy-start | bytes 1990660
  28.0 22.3 %collective-permute-start.7 = (bf16[1296,128]{1,0:T(8,128)(2,1)S(1)}, bf16[1296,128]{1,0:T(8,128)(2,1)}, u32[]{:S(2)}, u32[]{:S(2)}) collective-permute-start(bf16[1296,128]{1,0:T(8,128)(2,1)S(1)} %slice.24), channel_id=1, source_target_pairs={{0,4},{1,5},{2,6},{3,7},{4,0},{5,1},{6,2},{7,3},{8,12},{9,13},{10,... | collective-permute-start | bytes 995336 | tf_op jit(solution)/shard_map/ppermute | solution.py:327
  29.6 20.1 %copy-start.1 = (bf16[2592,128]{1,0:T(8,128)(2,1)}, bf16[2592,128]{1,0:T(8,128)(2,1)S(1)}, u32[]{:S(2)}) copy-start(bf16[2592,128]{1,0:T(8,128)(2,1)S(1)} %collective-permute-done.8) | copy-start | bytes 1990660
  29.6 20.7 %collective-permute-start.9 = (bf16[1296,128]{1,0:T(8,128)(2,1)S(1)}, bf16[1296,128]{1,0:T(8,128)(2,1)}, u32[]{:S(2)}, u32[]{:S(2)}) collective-permute-start(bf16[1296,128]{1,0:T(8,128)(2,1)S(1)} %slice.25), channel_id=1, source_target_pairs={{0,2},{1,3},{2,0},{3,1},{4,6},{5,7},{6,4},{7,5},{8,10},{9,11},{10,... | collective-permute-start | bytes 995336 | tf_op jit(solution)/shard_map/ppermute | solution.py:327
  30.2 28.4 %collective-permute-start.12 = (bf16[2592,128]{1,0:T(8,128)(2,1)S(1)}, bf16[2592,128]{1,0:T(8,128)(2,1)S(1)}, u32[]{:S(2)}, u32[]{:S(2)}) collective-permute-start(bf16[2592,128]{1,0:T(8,128)(2,1)S(1)} %collective-permute-done.6), channel_id=1, source_target_pairs={{0,1},{1,0},{2,3},{3,2},{4,5},{5,4},{6,7},{7,6},{8,9},{9,8},{10,11... | collective-permute-start | bytes 1990664 | tf_op jit(solution)/shard_map/ppermute | solution.py:327
  30.3 28.4 %collective-permute-start.13 = (bf16[2592,128]{1,0:T(8,128)(2,1)S(1)}, bf16[2592,128]{1,0:T(8,128)(2,1)S(1)}, u32[]{:S(2)}, u32[]{:S(2)}) collective-permute-start(bf16[2592,128]{1,0:T(8,128)(2,1)S(1)} %collective-permute-done.8), channel_id=1, source_target_pairs={{0,1},{1,0},{2,3},{3,2},{4,5},{5,4},{6,7},{7,6},{8,9},{9,8},{10,11... | collective-permute-start | bytes 1990664 | tf_op jit(solution)/shard_map/ppermute | solution.py:327
  50.3 16.7 %collective-permute-start.10 = (bf16[1296,128]{1,0:T(8,128)(2,1)}, bf16[1296,128]{1,0:T(8,128)(2,1)}, u32[]{:S(2)}, u32[]{:S(2)}) collective-permute-start(bf16[1296,128]{1,0:T(8,128)(2,1)} %collective-permute-done.7.refs_0_), channel_id=1, source_target_pairs={{0,1},{1,0},{2,3},{3,2},{4,5},{5,4},{6,7},{7,6},{8,9},{9,8},{10,11... | collective-permute-start | bytes 995336 | tf_op jit(solution)/shard_map/ppermute | solution.py:327
  50.3 16.6 %collective-permute-start.11 = (bf16[1296,128]{1,0:T(8,128)(2,1)}, bf16[1296,128]{1,0:T(8,128)(2,1)}, u32[]{:S(2)}, u32[]{:S(2)}) collective-permute-start(bf16[1296,128]{1,0:T(8,128)(2,1)} %collective-permute-done.9.refs_1_), channel_id=1, source_target_pairs={{0,1},{1,0},{2,3},{3,2},{4,5},{5,4},{6,7},{7,6},{8,9},{9,8},{10,11... | collective-permute-start | bytes 995336 | tf_op jit(solution)/shard_map/ppermute | solution.py:327
  52.9 0.8 copy-start.2
  58.7 0.8 copy-start.3
  58.7 1.0 %copy-start.4 = (bf16[2592,128]{1,0:T(8,128)(2,1)}, bf16[2592,128]{1,0:T(8,128)(2,1)S(1)}, u32[]{:S(2)}) copy-start(bf16[2592,128]{1,0:T(8,128)(2,1)S(1)} %collective-permute-done.13) | copy-start | bytes 1990660

commit v3 on v2

v3 whole, which is shorter than its diff:
```python
import functools
import math

import jax
import jax.numpy as jnp
import numpy as np
from jax import lax
from jax.experimental import pallas as pl
from jax.experimental.pallas import tpu as pltpu
from jax.sharding import PartitionSpec as P

NAR = 48
NA = 48
BAND = 3
BITS = 13
LANES = 128
WINDOW = 256
VMEM_BYTES = 56 * 1024 * 1024


def parity(codes, rows):
    return lax.population_count(codes & rows) & 1


def pack_kernel(block_ref, rows_ref, columns_ref, valid_ref, packed_ref, lines_ref):
    mirrors, rows, slots, samples = block_ref.shape
    lines_ref[...] = jnp.zeros(lines_ref.shape, lines_ref.dtype)
    lines_ref[:mirrors, :columns_ref.shape[2]] = columns_ref[0]
    lines_ref[mirrors:mirrors + valid_ref.shape[1], :valid_ref.shape[2]] = valid_ref[0]
    lines_ref[mirrors + valid_ref.shape[1]:, :rows] = rows_ref[0]
    for unit in range(mirrors * rows // 2):
        base = unit * 3 * slots
        tails = []
        for side in range(2):
            k, l = divmod(2 * unit + side, rows)
            packed_ref[pl.ds(base + side * slots, slots), :] = block_ref[k, l, :, :LANES]
            tails.append(block_ref[k, l, :, LANES:])
        packed_ref[pl.ds(base + 2 * slots, slots), :] = jnp.concatenate(tails, axis=1)


def pack(block, foot_rows, foot_columns, valid):
    mirrors, rows, slots, samples = block.shape
    vmem = pl.BlockSpec(memory_space=pltpu.VMEM)
    return pl.pallas_call(
        pack_kernel,
        out_shape=[
            jax.ShapeDtypeStruct((mirrors * rows * slots * samples // LANES, LANES), block.dtype),
            jax.ShapeDtypeStruct((2 * mirrors + rows // 2, WINDOW), jnp.int32),
        ],
        in_specs=[vmem] * 4,
        out_specs=[vmem] * 2,
        compiler_params=pltpu.CompilerParams(vmem_limit_bytes=VMEM_BYTES),
        cost_estimate=pl.CostEstimate(flops=0, bytes_accessed=3 * block.size, transcendentals=0),
        name="pack_influence",
    )(block, foot_rows, foot_columns, valid)


def column_of(row):
    return jnp.transpose(jnp.broadcast_to(row, (LANES, LANES)), (1, 0))


def gram_kernel(codes_ref, pokes_ref, gram_ref, words, own_signs, own_sums):
    planes = pokes_ref.shape[0]
    half = LANES // 2
    own = own_signs.shape[0]
    chunks = gram_ref.shape[1] // WINDOW

    @pl.when(pl.program_id(0) == 0)
    def _():
        plane = lax.broadcasted_iota(jnp.int32, pokes_ref.shape, 0)
        for bit in range(BITS):
            low = jnp.sum((pokes_ref[...] >> bit & 1) << plane, axis=0, keepdims=True)
            word = low | pltpu.roll(jnp.broadcast_to(low, (8, LANES)), half, 1)[:1] << planes
            words[bit] = column_of(word)[:half]
        count = codes_ref.shape[0] * LANES // (lax.axis_size("dir") * lax.axis_size("row"))
        first = (lax.axis_index("dir") * lax.axis_size("row") + lax.axis_index("row")) * count
        lane = lax.broadcasted_iota(jnp.int32, (8, LANES), 1)
        shift = first % LANES
        lines = [
            pltpu.roll(
                jnp.broadcast_to(
                    codes_ref[pl.ds(jnp.minimum(first // LANES + n, codes_ref.shape[0] - 1), 1), :], (8, LANES)
                ),
                LANES - shift, 1,
            )
            for n in range(-(-own // LANES) + 1)
        ]
        own_column = jnp.concatenate(
            [
                column_of(jnp.where(lane < LANES - shift, lines[n], lines[n + 1])[:1])
                for n in range(len(lines) - 1)
            ],
            axis=0,
        )[:own]
        lane = lax.broadcasted_iota(jnp.int32, (1, LANES), 1)
        total = jnp.zeros((own, LANES), jnp.float32)
        for at in range(planes):
            signs = (1 - 2 * parity(own_column, pokes_ref[at:at + 1, :])).astype(jnp.float32)
            upper = -(2.0 ** -(at + planes)) if at + planes == 31 else 2.0 ** -(at + planes)
            own_signs[:, at * LANES:(at + 1) * LANES] = (
                signs * jnp.where(lane < half, 2.0 ** -at, upper)
            ).astype(jnp.bfloat16)
            total = total + signs
        own_sums[...] = jnp.broadcast_to(jnp.sum(total, axis=1, keepdims=True), own_sums.shape)

    def chunk(index, _):
        word = []
        for side in range(WINDOW // LANES):
            line = (pl.program_id(0) * chunks + index) * (WINDOW // LANES) + side
            code = jnp.broadcast_to(codes_ref[pl.ds(line, 1), :], (8, LANES))
            value = None
            for bit in range(BITS):
                mask = jnp.concatenate([code << (31 - bit) >> 31] * (half // 8), axis=0)
                part = words[bit] & mask
                value = part if value is None else value ^ part
            word.append(value)
        word = jnp.concatenate(word, axis=1)
        total = jnp.zeros((own, WINDOW), jnp.float32)
        for at in range(0, planes, 2):
            bits = [
                (word & np.int32(np.uint32(1 << plane).view(np.int32))).astype(jnp.float32).astype(jnp.bfloat16)
                for plane in (at, at + planes, at + 1, at + 1 + planes)
            ]
            total = total + jnp.dot(
                own_signs[:, at * LANES:(at + 2) * LANES], jnp.concatenate(bits, axis=0),
                preferred_element_type=jnp.float32,
            )
        sums = jnp.concatenate([own_sums[...]] * (WINDOW // LANES), axis=1)
        gram_ref[:, pl.ds(pl.multiple_of(index * WINDOW, WINDOW), WINDOW)] = (sums - 2.0 * total).astype(jnp.bfloat16)
        return 0

    lax.fori_loop(0, chunks, chunk, 0, unroll=3)


def gram(codes, pokes, own):
    own = -(-own // 16) * 16
    acts, count = codes.size, pokes.shape[0]
    steps = 3
    return pl.pallas_call(
        gram_kernel,
        grid=(steps,),
        out_shape=jax.ShapeDtypeStruct((own, acts), jnp.bfloat16),
        in_specs=[pl.BlockSpec(memory_space=pltpu.VMEM)] * 2,
        out_specs=pl.BlockSpec((own, acts // steps), lambda s: (0, s)),
        scratch_shapes=[
            pltpu.VMEM((BITS, LANES // 2, LANES), jnp.int32),
            pltpu.VMEM((own, count), jnp.bfloat16),
            pltpu.VMEM((own, LANES), jnp.float32),
        ],
        compiler_params=pltpu.CompilerParams(vmem_limit_bytes=VMEM_BYTES),
        cost_estimate=pl.CostEstimate(
            flops=2 * own * acts * count, bytes_accessed=2 * own * acts, transcendentals=0
        ),
        name="gram_rows",
    )(codes.reshape(-1, LANES), pokes.reshape(-1, LANES))


def position(axis, staged):
    return lax.axis_index(axis) if staged else 0


def band_product(block_parts, q, row_shape, block, surface_rows, gram_ref, window_ref):
    mirrors, shard_rows, slots, samples = row_shape
    k, l = divmod(q, shard_rows)
    band = jnp.clip((block * shard_rows + l) * NAR // surface_rows - 1, 0, NAR - BAND)
    column = (k * NAR + band) * NA
    base = pl.multiple_of(column // LANES * LANES, LANES)
    shift = pl.multiple_of(column - base, 16)
    unit, side = divmod(q, 2)
    units = mirrors * shard_rows // 2 // len(block_parts)
    part, at = block_parts[unit // units], unit % units * 3 * slots
    for gap in range(0, WINDOW - slots, 16):
        row = pl.multiple_of((shift + slots + gap) % WINDOW, 16)
        window_ref[pl.ds(row, 16), :] = jnp.zeros((16, WINDOW), window_ref.dtype)
    window_ref[pl.ds(shift, slots), :LANES] = part[pl.ds(at + side * slots, slots), :]
    both = part[pl.ds(at + 2 * slots, slots), :]
    tail = samples - LANES
    mine = both[:, side * tail:(side + 1) * tail]
    window_ref[pl.ds(shift, slots), LANES:] = jnp.concatenate([mine, mine], axis=1)
    u = jnp.dot(gram_ref[:, pl.ds(base, WINDOW)], window_ref[...], preferred_element_type=jnp.float32)
    return u.astype(jnp.bfloat16)


def bands_kernel(row_shape, surface_rows, first, counts, staged, gram_ref, *refs):
    sources = refs[:len(counts)]
    out_ref, window = refs[-2:]
    step = pl.program_id(0)
    start = 0
    for source, count in zip(sources, counts):
        @pl.when((step >= start) & (step < start + count))
        def _():
            block = (first + step) ^ position("row", staged)
            for q in range(row_shape[0] * row_shape[1]):
                out_ref[0, q] = band_product(
                    [source.at[0]], q, row_shape, block, surface_rows, gram_ref, window.at[q % window.shape[0]]
                )
        start += count


def bands(gram_rows, sources, decoded, first, staged, row_shape, surface_rows):
    own = gram_rows.shape[0]
    counts = [source.shape[0] for source in sources]
    starts = np.cumsum([0] + counts)
    total = surface_rows // row_shape[1]
    rows = row_shape[0] * row_shape[1]
    specs = [
        pl.BlockSpec(
            (1,) + source.shape[1:],
            functools.partial(lambda low, high, s: (jnp.clip(s - low, 0, high - 1), 0, 0), int(starts[n]), counts[n]),
        )
        for n, source in enumerate(sources)
    ]
    arguments = [gram_rows, *sources]
    in_specs = [pl.BlockSpec(memory_space=pltpu.VMEM), *specs]
    aliases = {}
    body = functools.partial(bands_kernel, row_shape, surface_rows, first, counts, staged)
    if decoded is not None:
        aliases = {len(arguments): 0}
        arguments.append(decoded)
        in_specs.append(pl.BlockSpec(memory_space=pl.ANY))
    flops = 2 * own * WINDOW * WINDOW * rows * sum(counts)
    return pl.pallas_call(
        body,
        grid=(sum(counts),),
        out_shape=jax.ShapeDtypeStruct((total, rows, own, WINDOW), jnp.bfloat16),
        in_specs=in_specs,
        out_specs=pl.BlockSpec((1, rows, own, WINDOW), lambda s: (first + s, 0, 0, 0)),
        scratch_shapes=[pltpu.VMEM((4, WINDOW, WINDOW), jnp.bfloat16)],
        input_output_aliases=aliases,
        compiler_params=pltpu.CompilerParams(vmem_limit_bytes=VMEM_BYTES),
        cost_estimate=pl.CostEstimate(
            flops=flops, bytes_accessed=2 * own * WINDOW * rows * sum(counts), transcendentals=0
        ),
        name="bands",
    )(*arguments)


def build_differences(lines_ref, differences, mirrors, samples, pupil):
    tail = samples - LANES
    half = pupil // 2
    x = lax.broadcasted_iota(jnp.int32, (pupil, 2 * pupil), 0)
    lane = lax.broadcasted_iota(jnp.int32, (pupil, 2 * pupil), 1)
    spread = (x == lane % half * 2 + lane // pupil).astype(jnp.float32).astype(jnp.bfloat16)
    upper = lax.broadcasted_iota(jnp.int32, (1, pupil), 1) >= half
    for d in range(differences.shape[0]):
        columns = jnp.dot(
            lines_ref[0, d, :, :pupil].astype(jnp.float32).astype(jnp.bfloat16), spread,
            preferred_element_type=jnp.float32,
        ).astype(jnp.int32)
        for k in range(mirrors):
            first, second = columns[k:k + 1, :pupil], columns[k:k + 1, pupil:]

            def pieces(start, length):
                at = start + lax.broadcasted_iota(jnp.int32, (length, pupil), 0)
                ahead, behind = (at == second).astype(jnp.float32), (at == first).astype(jnp.float32)
                across, down = ahead - behind, ahead + behind
                return [jnp.where(upper, sign * down, across).astype(jnp.bfloat16) for sign in (-1.0, 1.0)]

            for y, (head, rest) in enumerate(zip(pieces(0, LANES), pieces(LANES, tail))):
                differences[d, pl.ds((2 * k + y) * LANES, LANES), :] = head
                differences[d, pl.ds(2 * mirrors * LANES + k * LANES + y * tail, tail), :] = rest


def decode_kernel(row_shape, surface_rows, own, late, staged, norm, foot_ref, lines_ref, *refs):
    mirrors, shard_rows, slots, samples = row_shape
    extras = refs[:late[1] * late[2]]
    gram_ref, decoded_ref, out_ref, decoded, differences, total, window, semaphores = refs[late[1] * late[2]:]
    group = pl.program_id(0)
    directions = differences.shape[0]
    pupil = differences.shape[2]
    phases = out_ref.shape[2] // pupil
    tail = samples - LANES
    ready = late[0]
    place = position("row", staged)

    @pl.when(group == 0)
    def _():
        copies = [
            pltpu.make_async_copy(decoded_ref.at[block], decoded.at[block], semaphores.at[block])
            for block in range(ready)
        ]
        for copy in copies:
            copy.start()
        build_differences(lines_ref, differences, mirrors, samples, pupil)
        for n in range(late[1]):
            block = (ready + n) ^ place
            parts = [extras[n * late[2] + part] for part in range(late[2])]
            for q in range(mirrors * shard_rows):
                decoded[ready + n, q] = band_product(
                    parts, q, row_shape, block, surface_rows, gram_ref, window.at[q % window.shape[0]]
                )
        for copy in copies:
            copy.wait()

    lane = lax.broadcasted_iota(jnp.int32, (decoded.shape[2], LANES), 1)
    for d in range(directions):
        held = d ^ position("dir", staged)
        left, factors = [], []
        for phase in range(phases):
            i = group * phases + phase
            block = (2 * i // shard_rows) ^ place
            heads, tails = [], []
            for k in range(mirrors):
                picked = []
                for y in range(2):
                    row = foot_ref[((block * directions + held) * mirrors + k) * shard_rows + (2 * i + y) % shard_rows]
                    picked.append((row // shard_rows ^ place, k * shard_rows + row % shard_rows))
                heads += [decoded[e, q, :, :LANES] for e, q in picked]
                tails.append(
                    jnp.where(lane < tail, *(decoded[e, q, :, LANES:] for e, q in picked))
                )
            left.append(jnp.concatenate(heads + tails, axis=1))
            line = mirrors + phase % (shard_rows // 2)
            valid = lines_ref[block, held, line:line + 1, :pupil // 2]
            factors.append(valid.astype(jnp.float32) * norm)
        rows = left[0].shape[0]
        product = jnp.dot(
            jnp.concatenate(left, axis=0), differences[held], preferred_element_type=jnp.float32
        )
        value = jnp.concatenate([product[phase * rows:phase * rows + own] for phase in range(phases)], axis=1)
        value = value * jnp.concatenate([factor for factor in factors for _ in range(2)], axis=1)
        for tile in range(out_ref.shape[2] // LANES):
            total[tile, pl.ds(d, own, stride=directions), :] = value[:, tile * LANES:(tile + 1) * LANES]
    for tile in range(out_ref.shape[2] // LANES):
        value = total[tile].reshape(own, directions, LANES)
        out_ref[:, :, tile * LANES:(tile + 1) * LANES] = value.astype(out_ref.dtype)


def decode(lines, gram_rows, decoded, extras, parts, own, row_shape, surface_rows, pupil, norm, staged):
    blocks, directions = lines.shape[:2]
    mirrors, shard_rows = row_shape[:2]
    padded = gram_rows.shape[0]
    foot_rows = lines[:, :, mirrors + shard_rows // 2:, :shard_rows].reshape(-1)
    phases = LANES // math.gcd(pupil, LANES)
    width = surface_rows // 2 * pupil
    lanes = phases * pupil
    late = len(extras) // parts
    ready = decoded.shape[0] - late
    flops = 2 * padded * 3 * mirrors * LANES * pupil * directions * surface_rows // 2
    vmem = pl.BlockSpec(memory_space=pltpu.VMEM)
    return pl.pallas_call(
        functools.partial(decode_kernel, row_shape, surface_rows, own, (ready, late, parts), staged, norm),
        grid=(width // lanes,),
        out_shape=jax.ShapeDtypeStruct((own, directions, width), jnp.bfloat16),
        in_specs=[pl.BlockSpec(memory_space=pltpu.SMEM), vmem]
        + [vmem] * len(extras)
        + [vmem, pl.BlockSpec(memory_space=pl.ANY)],
        out_specs=pl.BlockSpec((own, directions, lanes), lambda s: (0, 0, s)),
        scratch_shapes=[
            pltpu.VMEM(decoded.shape, jnp.bfloat16),
            pltpu.VMEM((directions, 3 * mirrors * LANES, pupil), jnp.bfloat16),
            pltpu.VMEM((lanes // LANES, own * directions, LANES), jnp.float32),
            pltpu.VMEM((4, WINDOW, WINDOW), jnp.bfloat16),
            pltpu.SemaphoreType.DMA((decoded.shape[0],)),
        ],
        compiler_params=pltpu.CompilerParams(vmem_limit_bytes=VMEM_BYTES),
        cost_estimate=pl.CostEstimate(flops=flops, bytes_accessed=2 * own * directions * width, transcendentals=0),
        name="decode",
    )(foot_rows, lines, *extras, gram_rows, decoded)


def swap(block, axis, distance):
    return lax.ppermute(block, axis, [(i, i ^ distance) for i in range(lax.axis_size(axis))])


def shards(influence, foot_rows, foot_columns, actuator_codes, poke_rows, subaperture_valid):
    mirrors, shard_rows, samples, slots = influence.shape
    row_shape = (mirrors, shard_rows, slots, samples)
    directions, devices = lax.axis_size("dir"), lax.axis_size("row")
    surface_rows = shard_rows * devices
    pupil = foot_columns.shape[2]
    norm = 0.5 * poke_rows.shape[0] ** (-0.5)
    own = actuator_codes.size // (directions * devices)
    staged = devices == 8 and directions & (directions - 1) == 0
    packed, lines = pack(jnp.swapaxes(influence, 2, 3), foot_rows, foot_columns, subaperture_valid)
    if not staged:
        gram_rows = gram(actuator_codes, poke_rows, own)
        decoded = bands(gram_rows, [lax.all_gather(packed, "row")], None, 0, staged, row_shape, surface_rows)
        lines = lax.all_gather(lax.all_gather(lines, "dir"), "row")
        return decode(lines, gram_rows, decoded, [], 1, own, row_shape, surface_rows, pupil, norm, staged)

    beside, across, sibling = (swap(packed, "row", distance) for distance in (2, 4, 1))
    lines = jnp.stack([lines] + [swap(lines, "dir", e) for e in range(1, directions)])[None]
    gram_rows = gram(actuator_codes, poke_rows, own)
    gram_rows, lines = lax.optimization_barrier((gram_rows, lines))
    lines = jnp.concatenate([lines, swap(lines, "row", 1)], axis=0)
    decoded = bands(gram_rows, [packed[None], sibling[None]], None, 0, staged, row_shape, surface_rows)
    decoded, lines, beside, across = lax.optimization_barrier((decoded, lines, beside, across))
    half = packed.shape[0] // 2
    upper, lower = swap(beside[:half], "row", 4), swap(across[half:], "row", 2)
    beside_sibling, across_sibling = swap(beside, "row", 1), swap(across, "row", 1)
    lines = jnp.concatenate([lines, swap(lines, "row", 2)], axis=0)
    sources = [source[None] for source in (beside, beside_sibling, across, across_sibling)]
    decoded = bands(gram_rows, sources, decoded, 2, staged, row_shape, surface_rows)
    decoded, lines, upper, lower = lax.optimization_barrier((decoded, lines, upper, lower))
    late = [upper, lower, swap(upper, "row", 1), swap(lower, "row", 1)]
    lines = jnp.concatenate([lines, swap(lines, "row", 4)], axis=0)
    return decode(lines, gram_rows, decoded, late, 2, own, row_shape, surface_rows, pupil, norm, staged)


def solution(mesh):
    return jax.shard_map(
        shards,
        mesh=mesh,
        in_specs=(
            P(None, "row", None, None),
            P("dir", None, "row"),
            P("dir", None, None),
            P(),
            P(),
            P("dir", "row", None),
        ),
        out_specs=P(("dir", "row"), None, None),
        check_vma=False,
    )
```

time: 89.4 us -> 86 us (0.962)
  Pallas kernels: 54.9 us -> 48.7 us
  waiting for transfers between devices: 9.89 us -> 14.1 us
  other arithmetic: 4.22 us -> 0.02 us
  local copies, waits for them, and re-layouts: 6.19 us -> 8.3 us
  starting transfers between devices: 13.3 us -> 14.2 us
    pallas_call x2, Pallas kernels: 21.1 us -> 14.7 us  [the longest x1 12.5 us: gram(): pl.pallas_call(gram_kernel, grid=(steps,), out_shape=jax.ShapeDtypeStruct...]
    ppermute x15, waiting for transfers between devices: 9.89 us -> 14.1 us  [swap(): lax.ppermute(block, axis, [(i, i ^ distance) for i in range(lax.axis_size...]
    unnamed x10 -> x25, local copies, waits for them, and re-layouts: 1.88 us -> 5.93 us
    another operation x4 -> x0, local copies, waits for them, and re-layouts: 2.53 us -> none  [the longest x1 1.6 us: gram(): codes[None]]
    another operation x3 -> x0, other arithmetic: 2.03 us -> none  [the longest x2 1.44 us: small_arrays(): jnp.stack([lines] + [swap(lines, 'dir', e) for e in range(1, directions)])]
    unnamed x2 -> x0, other arithmetic: 1.42 us -> none
    reshape x2, local copies, waits for them, and re-layouts: 0.99 us -> 2.3 us  [the longest x1 1.59 us: gram(): codes.reshape(-1, LANES)]
  transfers between devices with their start and end apart: 15 -> 15, of which waited for: 4 -> 3; matrix products, arithmetic and copies ran while one was open for 10% -> 3% of each run, Pallas kernels for 35% -> 30%
where the time goes in v3:
time: 86 us; the launch traced here: 85.7 us
  Pallas kernels  48.7 us (57%)
  starting transfers between devices  14.2 us (17%)
  waiting for transfers between devices  14.1 us (16%)
  local copies, waits for them, and re-layouts  8.3 us (10%)
    pallas_call x1, Pallas kernels, decode(): pl.pallas_call(functools.partial(decode_kernel, row_shape, surface_rows,...  21.3 us
    ppermute x15, starting transfers between devices, swap(): lax.ppermute(block, axis, [(i, i ^ distance) for i in range(lax.axis_size...  14.2 us
    ppermute x15, waiting for transfers between devices, swap(): lax.ppermute(block, axis, [(i, i ^ distance) for i in range(lax.axis_size...  14.1 us
    pallas_call x2, Pallas kernels, bands(): pl.pallas_call(body, grid=(sum(counts),), out_shape=jax.ShapeDtypeStruct(...  12.8 us
    pallas_call x1, Pallas kernels, gram(): pl.pallas_call(gram_kernel, grid=(steps,), out_shape=jax.ShapeDtypeStruct...  12.5 us
    unnamed x25, local copies, waits for them, and re-layouts  5.93 us
    pallas_call x1, Pallas kernels, pack(): pl.pallas_call(pack_kernel, out_shape=[jax.ShapeDtypeStruct((mirrors * ro...  2.15 us
  transfers between devices with their start and end apart: 15, of which 3 were waited for; matrix products, arithmetic and copies ran while one was open for 3% of the time, Pallas kernels for 30%

profile of v3, /device:TPU:0, one launch (start us, length us, event | category | flops | bytes accessed | tf_op | source)
XLA Modules:
  0.0 85.7 jit_solution(16296822998180885974)
XLA Ops:
  0.0 1.3 %copy.10.rows_ref = s32[1,3,4]{2,1,0:T(4,128)} copy(s32[1,3,4]{2,0,1:T(1,128)} %param.7) | data formatting | bytes 96 | tf_op args[1]
  1.3 1.3 %copy.11.columns_ref = s32[1,3,160]{2,1,0:T(4,128)} copy(s32[1,3,160]{2,0,1:T(1,128)} %param.8) | data formatting | bytes 3840 | tf_op args[2]
  2.5 2.2 %pack_influence.1 = (bf16[2592,128]{1,0:T(8,128)(2,1)}, s32[8,256]{1,0:T(8,128)}) custom-call(bf16[3,4,144,192]{3,2,1,0:T(8,128)(2,1)} %bitcast.16, s32[1,3,4]{2,1,0:T(4,128)} %copy.10.rows_ref, s32[1,3,160]{2,1,0:T(4,128)} %copy.11.columns_ref, s32[1,2,80]{2,1,0:T(2,128)} %valid_ref.1), custom_call_target="tpu_custom_call" | custom-call | bytes 995328 | tf_op jit(solution)/shard_map/pack_influence/pallas_call | solution.py:44
  4.7 5.0 %collective-permute-start.2 = (s32[8,256]{1,0:T(8,128)}, s32[8,256]{1,0:T(8,128)S(1)}, u32[]{:S(2)}, u32[]{:S(2)}) collective-permute-start(s32[8,256]{1,0:T(8,128)} %get-tuple-element.17), channel_id=1, source_target_pairs={{0,24},{8,16},{16,8},{24,0},{1,25},{9,17},{17,9},{25,1},{2,26},{10... | collective-permute-start | bytes 24584 | tf_op jit(solution)/shard_map/ppermute | solution.py:363
  9.7 0.0 collective-permute-start.1
  9.8 0.6 collective-permute-start
  10.3 0.0 collective-permute-start.3
  10.3 1.7 %collective-permute-start.5 = (bf16[2592,128]{1,0:T(8,128)(2,1)}, bf16[2592,128]{1,0:T(8,128)(2,1)S(1)}, u32[]{:S(2)}, u32[]{:S(2)}) collective-permute-start(bf16[2592,128]{1,0:T(8,128)(2,1)} %get-tuple-element.19), channel_id=1, source_target_pairs={{0,2},{1,3},{2,0},{3,1},{4,6},{5,7},{6,4},{7,5},{8,10},{9,11},{10,... | collective-permute-start | bytes 1990664 | tf_op jit(solution)/shard_map/ppermute | solution.py:363
  12.0 1.6 %reshape.9.codes_ref = s32[54,128]{1,0:T(8,128)} reshape(s32[3,48,48]{2,1,0:T(8,128)} %param.9) | data formatting | bytes 55296 | tf_op jit(solution)/shard_map/reshape | solution.py:155
  13.6 0.0 collective-permute-done.2
  13.6 1.5 %collective-permute-start.6 = (bf16[2592,128]{1,0:T(8,128)(2,1)}, bf16[2592,128]{1,0:T(8,128)(2,1)S(1)}, u32[]{:S(2)}, u32[]{:S(2)}) collective-permute-start(bf16[2592,128]{1,0:T(8,128)(2,1)} %get-tuple-element.19), channel_id=1, source_target_pairs={{0,4},{1,5},{2,6},{3,7},{4,0},{5,1},{6,2},{7,3},{8,12},{9,13},{10,... | collective-permute-start | bytes 1990664 | tf_op jit(solution)/shard_map/ppermute | solution.py:363
  15.1 12.5 %gram_rows.1.gram_ref.refs_4_ = bf16[224,6912]{1,0:T(8,128)(2,1)} custom-call(s32[54,128]{1,0:T(8,128)} %reshape.9.codes_ref, s32[16,128]{1,0:T(8,128)} %bitcast.25), custom_call_target="tpu_custom_call" | custom-call | flops 6341787648 | bytes 3096576 | tf_op jit(solution)/shard_map/gram_rows/pallas_call | solution.py:139
  27.7 0.0 collective-permute-done.1
  27.7 0.0 collective-permute-done
  27.7 0.1 collective-permute-start.4
  27.8 1.2 %collective-permute-done.4 = s32[1,4,8,256]{3,2,1,0:T(8,128)S(1)} collective-permute-done((s32[1,4,8,256]{3,2,1,0:T(8,128)S(1)}, s32[1,4,8,256]{3,2,1,0:T(8,128)S(1)}, u32[]{:S(2)}, u32[]{:S(2)}) %collective-permute-start.4) | collective-permute-done | bytes 32800 | tf_op jit(solution)/shard_map/ppermute | solution.py:363
  29.0 0.0 collective-permute-done.3
  29.0 0.9 copy-done.3
  29.9 5.2 %bands.2.refs_4_ = bf16[8,12,224,256]{3,2,1,0:T(8,128)(2,1)} custom-call(bf16[224,6912]{1,0:T(8,128)(2,1)} %gram_rows.1.gram_ref.refs_4_, bf16[1,2592,128]{2,1,0:T(8,128)(2,1)} %bitcast.17, bf16[1,2592,128]{2,1,0:T(8,128)(2,1)} %bitcast.18), custom_call_target="tpu_custom_call" | custom-call | flops 704643072 | bytes 2752512 | tf_op jit(solution)/shard_map/bands/pallas_call | solution.py:222
  35.0 0.0 collective-permute-done.5
  35.0 0.0 collective-permute-done.6
  35.1 0.2 collective-permute-start.7
  35.3 0.3 collective-permute-start.8
  35.7 0.6 collective-permute-start.10
  36.3 0.3 collective-permute-start.11
  36.6 1.7 %collective-permute-start.9 = (s32[2,4,8,256]{3,2,1,0:T(8,128)S(1)}, s32[2,4,8,256]{3,2,1,0:T(8,128)S(1)}, u32[]{:S(2)}, u32[]{:S(2)}) collective-permute-start(s32[2,4,8,256]{3,2,1,0:T(8,128)S(1)} %pad_add_fusion.1), channel_id=1, source_target_pairs={{0,2},{1,3},{2,0},{3,1},{4,6},{5,7},{6,4},{7,5},{8,10},{9,11},{10,... | collective-permute-start | bytes 196616 | tf_op jit(solution)/shard_map/ppermute | solution.py:363
  38.3 9.0 %collective-permute-done.9 = s32[2,4,8,256]{3,2,1,0:T(8,128)S(1)} collective-permute-done((s32[2,4,8,256]{3,2,1,0:T(8,128)S(1)}, s32[2,4,8,256]{3,2,1,0:T(8,128)S(1)}, u32[]{:S(2)}, u32[]{:S(2)}) %collective-permute-start.9) | collective-permute-done | bytes 65568 | tf_op jit(solution)/shard_map/ppermute | solution.py:363
  47.3 0.0 collective-permute-done.7
  47.3 0.0 copy-start.4
  47.3 0.0 collective-permute-done.8
  47.3 0.8 copy-done.4
  48.1 0.3 copy-done.5
  48.4 7.6 %bands.3.refs_5_ = bf16[8,12,224,256]{3,2,1,0:T(8,128)(2,1)} custom-call(bf16[224,6912]{1,0:T(8,128)(2,1)} %gram_rows.1.gram_ref.refs_4_, bf16[1,2592,128]{2,1,0:T(8,128)(2,1)} %bitcast.14, bf16[1,2592,128]{2,1,0:T(8,128)(2,1)} %bitcast.19, bf16[1,2592,128]{2,1,0:T(8,128)(2,1)} %bitcast.15, ...), custom_call_target="tpu_custom_call", output_to_operand_aliasing={{}: (5, {})} | custom-call | flops 1409286144 | bytes 5505024 | tf_op jit(solution)/shard_map/bands/pallas_call | solution.py:222
  56.0 0.0 collective-permute-done.10.refs_0_
  56.0 0.0 collective-permute-done.11.refs_1_
  56.0 0.1 collective-permute-start.13
  56.1 0.5 collective-permute-start.14
  56.6 1.5 %collective-permute-start.12 = (s32[4,4,8,256]{3,2,1,0:T(8,128)S(1)}, s32[4,4,8,256]{3,2,1,0:T(8,128)S(1)}, u32[]{:S(2)}, u32[]{:S(2)}) collective-permute-start(s32[4,4,8,256]{3,2,1,0:T(8,128)S(1)} %pad_add_fusion), channel_id=1, source_target_pairs={{0,4},{1,5},{2,6},{3,7},{4,0},{5,1},{6,2},{7,3},{8,12},{9,13},{10,... | collective-permute-start | bytes 393224 | tf_op jit(solution)/shard_map/ppermute | solution.py:363
  58.1 3.9 %collective-permute-done.12 = s32[4,4,8,256]{3,2,1,0:T(8,128)S(1)} collective-permute-done((s32[4,4,8,256]{3,2,1,0:T(8,128)S(1)}, s32[4,4,8,256]{3,2,1,0:T(8,128)S(1)}, u32[]{:S(2)}, u32[]{:S(2)}) %collective-permute-start.12) | collective-permute-done | bytes 131104 | tf_op jit(solution)/shard_map/ppermute | solution.py:363
  62.1 0.7 reshape.11.foot_ref
  62.8 0.0 collective-permute-done.13.refs_2_
  62.8 0.0 collective-permute-done.14.refs_3_
  62.8 0.0 copy-done.6
  62.8 0.0 copy-done.7
  62.8 0.0 copy-done.2
  62.8 0.7 copy-done.8
  63.6 0.7 copy-done.9
  64.3 21.3 %decode.1 = bf16[216,4,2560]{2,1,0:T(4,128)(2,1)} custom-call(s32[384]{0:T(512)} %reshape.11.foot_ref, s32[8,4,8,256]{3,2,1,0:T(8,128)} %copy-done.2, bf16[1296,128]{1,0:T(8,128)(2,1)} %copy-done.6, bf16[1296,128]{1,0:T(8,128)(2,1)} %copy-done.7, bf16[1296,128]{1,0:T(8,128)(2,1)} %copy-done.8, bf16[1296,128]{1,0:T(8,128)(2,1)} %copy-done.9, ...), custom_call_target="tpu_custom_call" | custom-call | flops 5284823040 | bytes 4423680 | tf_op jit(solution)/shard_map/decode/pallas_call | solution.py:341
  (21 shorter events, 0.1 us)
Async XLA Ops:
  4.7 8.9 %collective-permute-start.2 = (s32[8,256]{1,0:T(8,128)}, s32[8,256]{1,0:T(8,128)S(1)}, u32[]{:S(2)}, u32[]{:S(2)}) collective-permute-start(s32[8,256]{1,0:T(8,128)} %get-tuple-element.17), channel_id=1, source_target_pairs={{0,24},{8,16},{16,8},{24,0},{1,25},{9,17},{17,9},{25,1},{2,26},{10... | collective-permute-start | bytes 24584 | tf_op jit(solution)/shard_map/ppermute | solution.py:363
  9.7 17.9 %collective-permute-start.1 = (s32[8,256]{1,0:T(8,128)}, s32[8,256]{1,0:T(8,128)S(1)}, u32[]{:S(2)}, u32[]{:S(2)}) collective-permute-start(s32[8,256]{1,0:T(8,128)} %get-tuple-element.17), channel_id=1, source_target_pairs={{0,16},{8,24},{16,0},{24,8},{1,17},{9,25},{17,1},{25,9},{2,18},{10... | collective-permute-start | bytes 24584 | tf_op jit(solution)/shard_map/ppermute | solution.py:363
  9.8 17.9 %collective-permute-start = (s32[8,256]{1,0:T(8,128)}, s32[8,256]{1,0:T(8,128)S(1)}, u32[]{:S(2)}, u32[]{:S(2)}) collective-permute-start(s32[8,256]{1,0:T(8,128)} %get-tuple-element.17), channel_id=1, source_target_pairs={{0,8},{8,0},{16,24},{24,16},{1,9},{9,1},{17,25},{25,17},{2,10},{10... | collective-permute-start | bytes 24584 | tf_op jit(solution)/shard_map/ppermute | solution.py:363
  10.3 18.7 %collective-permute-start.3 = (bf16[2592,128]{1,0:T(8,128)(2,1)}, bf16[2592,128]{1,0:T(8,128)(2,1)S(1)}, u32[]{:S(2)}, u32[]{:S(2)}) collective-permute-start(bf16[2592,128]{1,0:T(8,128)(2,1)} %get-tuple-element.19), channel_id=1, source_target_pairs={{0,1},{1,0},{2,3},{3,2},{4,5},{5,4},{6,7},{7,6},{8,9},{9,8},{10,11... | collective-permute-start | bytes 1990664 | tf_op jit(solution)/shard_map/ppermute | solution.py:363
  10.3 24.7 %collective-permute-start.5 = (bf16[2592,128]{1,0:T(8,128)(2,1)}, bf16[2592,128]{1,0:T(8,128)(2,1)S(1)}, u32[]{:S(2)}, u32[]{:S(2)}) collective-permute-start(bf16[2592,128]{1,0:T(8,128)(2,1)} %get-tuple-element.19), channel_id=1, source_target_pairs={{0,2},{1,3},{2,0},{3,1},{4,6},{5,7},{6,4},{7,5},{8,10},{9,11},{10,... | collective-permute-start | bytes 1990664 | tf_op jit(solution)/shard_map/ppermute | solution.py:363
  13.6 21.4 %collective-permute-start.6 = (bf16[2592,128]{1,0:T(8,128)(2,1)}, bf16[2592,128]{1,0:T(8,128)(2,1)S(1)}, u32[]{:S(2)}, u32[]{:S(2)}) collective-permute-start(bf16[2592,128]{1,0:T(8,128)(2,1)} %get-tuple-element.19), channel_id=1, source_target_pairs={{0,4},{1,5},{2,6},{3,7},{4,0},{5,1},{6,2},{7,3},{8,12},{9,13},{10,... | collective-permute-start | bytes 1990664 | tf_op jit(solution)/shard_map/ppermute | solution.py:363
  15.1 12.6 %copy-start.10 = (s32[8,256]{1,0:T(8,128)S(1)}, s32[8,256]{1,0:T(8,128)}, u32[]{:S(2)}) copy-start(s32[8,256]{1,0:T(8,128)} %get-tuple-element.17) | copy-start | bytes 24580
  27.7 1.3 %collective-permute-start.4 = (s32[1,4,8,256]{3,2,1,0:T(8,128)S(1)}, s32[1,4,8,256]{3,2,1,0:T(8,128)S(1)}, u32[]{:S(2)}, u32[]{:S(2)}) collective-permute-start(s32[1,4,8,256]{3,2,1,0:T(8,128)S(1)} %add_bitcast_fusion), channel_id=1, source_target_pairs={{0,1},{1,0},{2,3},{3,2},{4,5},{5,4},{6,7},{7,6},{8,9},{9,8},{10,11... | collective-permute-start | bytes 98312 | tf_op jit(solution)/shard_map/ppermute | solution.py:363
  29.0 0.9 %copy-start.3 = (bf16[2592,128]{1,0:T(8,128)(2,1)}, bf16[2592,128]{1,0:T(8,128)(2,1)S(1)}, u32[]{:S(2)}) copy-start(bf16[2592,128]{1,0:T(8,128)(2,1)S(1)} %collective-permute-done.3) | copy-start | bytes 1990660
  35.0 12.3 %copy-start = (bf16[2592,128]{1,0:T(8,128)(2,1)}, bf16[2592,128]{1,0:T(8,128)(2,1)S(1)}, u32[]{:S(2)}) copy-start(bf16[2592,128]{1,0:T(8,128)(2,1)S(1)} %collective-permute-done.5) | copy-start | bytes 1990660
  35.0 12.3 %copy-start.1 = (bf16[2592,128]{1,0:T(8,128)(2,1)}, bf16[2592,128]{1,0:T(8,128)(2,1)S(1)}, u32[]{:S(2)}) copy-start(bf16[2592,128]{1,0:T(8,128)(2,1)S(1)} %collective-permute-done.6) | copy-start | bytes 1990660
  35.1 12.2 %collective-permute-start.7 = (bf16[2592,128]{1,0:T(8,128)(2,1)S(1)}, bf16[2592,128]{1,0:T(8,128)(2,1)S(1)}, u32[]{:S(2)}, u32[]{:S(2)}) collective-permute-start(bf16[2592,128]{1,0:T(8,128)(2,1)S(1)} %collective-permute-done.5), channel_id=1, source_target_pairs={{0,1},{1,0},{2,3},{3,2},{4,5},{5,4},{6,7},{7,6},{8,9},{9,8},{10,11... | collective-permute-start | bytes 1990664 | tf_op jit(solution)/shard_map/ppermute | solution.py:363
  35.3 12.0 %collective-permute-start.8 = (bf16[2592,128]{1,0:T(8,128)(2,1)S(1)}, bf16[2592,128]{1,0:T(8,128)(2,1)S(1)}, u32[]{:S(2)}, u32[]{:S(2)}) collective-permute-start(bf16[2592,128]{1,0:T(8,128)(2,1)S(1)} %collective-permute-done.6), channel_id=1, source_target_pairs={{0,1},{1,0},{2,3},{3,2},{4,5},{5,4},{6,7},{7,6},{8,9},{9,8},{10,11... | collective-permute-start | bytes 1990664 | tf_op jit(solution)/shard_map/ppermute | solution.py:363
  35.7 20.3 %collective-permute-start.10 = (bf16[1296,128]{1,0:T(8,128)(2,1)S(1)}, bf16[1296,128]{1,0:T(8,128)(2,1)S(1)}, u32[]{:S(2)}, u32[]{:S(2)}) collective-permute-start(bf16[1296,128]{1,0:T(8,128)(2,1)S(1)} %slice.9), channel_id=1, source_target_pairs={{0,4},{1,5},{2,6},{3,7},{4,0},{5,1},{6,2},{7,3},{8,12},{9,13},{10,... | collective-permute-start | bytes 995336 | tf_op jit(solution)/shard_map/ppermute | solution.py:363
  36.3 19.7 %collective-permute-start.11 = (bf16[1296,128]{1,0:T(8,128)(2,1)S(1)}, bf16[1296,128]{1,0:T(8,128)(2,1)S(1)}, u32[]{:S(2)}, u32[]{:S(2)}) collective-permute-start(bf16[1296,128]{1,0:T(8,128)(2,1)S(1)} %slice.10), channel_id=1, source_target_pairs={{0,2},{1,3},{2,0},{3,1},{4,6},{5,7},{6,4},{7,5},{8,10},{9,11},{10,... | collective-permute-start | bytes 995336 | tf_op jit(solution)/shard_map/ppermute | solution.py:363
  36.6 10.7 %collective-permute-start.9 = (s32[2,4,8,256]{3,2,1,0:T(8,128)S(1)}, s32[2,4,8,256]{3,2,1,0:T(8,128)S(1)}, u32[]{:S(2)}, u32[]{:S(2)}) collective-permute-start(s32[2,4,8,256]{3,2,1,0:T(8,128)S(1)} %pad_add_fusion.1), channel_id=1, source_target_pairs={{0,2},{1,3},{2,0},{3,1},{4,6},{5,7},{6,4},{7,5},{8,10},{9,11},{10,... | collective-permute-start | bytes 196616 | tf_op jit(solution)/shard_map/ppermute | solution.py:363
  47.3 0.8 copy-start.4
  47.3 1.1 %copy-start.5 = (bf16[2592,128]{1,0:T(8,128)(2,1)}, bf16[2592,128]{1,0:T(8,128)(2,1)S(1)}, u32[]{:S(2)}) copy-start(bf16[2592,128]{1,0:T(8,128)(2,1)S(1)} %collective-permute-done.8) | copy-start | bytes 1990660
  56.0 6.9 %copy-start.6 = (bf16[1296,128]{1,0:T(8,128)(2,1)}, bf16[1296,128]{1,0:T(8,128)(2,1)S(1)}, u32[]{:S(2)}) copy-start(bf16[1296,128]{1,0:T(8,128)(2,1)S(1)} %collective-permute-done.10.refs_0_) | copy-start | bytes 995332
  56.0 6.8 %copy-start.7 = (bf16[1296,128]{1,0:T(8,128)(2,1)}, bf16[1296,128]{1,0:T(8,128)(2,1)S(1)}, u32[]{:S(2)}) copy-start(bf16[1296,128]{1,0:T(8,128)(2,1)S(1)} %collective-permute-done.11.refs_1_) | copy-start | bytes 995332
  56.0 6.8 %collective-permute-start.13 = (bf16[1296,128]{1,0:T(8,128)(2,1)S(1)}, bf16[1296,128]{1,0:T(8,128)(2,1)S(1)}, u32[]{:S(2)}, u32[]{:S(2)}) collective-permute-start(bf16[1296,128]{1,0:T(8,128)(2,1)S(1)} %collective-permute-done.10.refs_0_), channel_id=1, source_target_pairs={{0,1},{1,0},{2,3},{3,2},{4,5},{5,4},{6,7},{7,6},{8,9},{9,8},{10,11... | collective-permute-start | bytes 995336 | tf_op jit(solution)/shard_map/ppermute | solution.py:363
  56.1 6.7 %collective-permute-start.14 = (bf16[1296,128]{1,0:T(8,128)(2,1)S(1)}, bf16[1296,128]{1,0:T(8,128)(2,1)S(1)}, u32[]{:S(2)}, u32[]{:S(2)}) collective-permute-start(bf16[1296,128]{1,0:T(8,128)(2,1)S(1)} %collective-permute-done.11.refs_1_), channel_id=1, source_target_pairs={{0,1},{1,0},{2,3},{3,2},{4,5},{5,4},{6,7},{7,6},{8,9},{9,8},{10,11... | collective-permute-start | bytes 995336 | tf_op jit(solution)/shard_map/ppermute | solution.py:363
  56.6 5.5 %collective-permute-start.12 = (s32[4,4,8,256]{3,2,1,0:T(8,128)S(1)}, s32[4,4,8,256]{3,2,1,0:T(8,128)S(1)}, u32[]{:S(2)}, u32[]{:S(2)}) collective-permute-start(s32[4,4,8,256]{3,2,1,0:T(8,128)S(1)} %pad_add_fusion), channel_id=1, source_target_pairs={{0,4},{1,5},{2,6},{3,7},{4,0},{5,1},{6,2},{7,3},{8,12},{9,13},{10,... | collective-permute-start | bytes 393224 | tf_op jit(solution)/shard_map/ppermute | solution.py:363
  62.1 0.8 copy-start.2
  62.8 0.7 copy-start.8
  63.5 0.7 copy-start.9

commit v4 on v3

v4 whole, which is shorter than its diff:
```python
import functools
import math

import jax
import jax.numpy as jnp
import numpy as np
from jax import lax
from jax.experimental import pallas as pl
from jax.experimental.pallas import tpu as pltpu
from jax.sharding import PartitionSpec as P

NAR = 48
NA = 48
BAND = 3
BITS = 13
LANES = 128
WINDOW = 256
VMEM_BYTES = 56 * 1024 * 1024


def parity(codes, rows):
    return lax.population_count(codes & rows) & 1


def lines_kernel(rows_ref, columns_ref, valid_ref, lines_ref):
    mirrors, rows = rows_ref.shape[0], rows_ref.shape[2]
    lines_ref[...] = jnp.zeros(lines_ref.shape, lines_ref.dtype)
    lines_ref[mirrors:mirrors + valid_ref.shape[1], :valid_ref.shape[2]] = valid_ref[0]
    for k in range(mirrors):
        lines_ref[k:k + 1, :columns_ref.shape[2]] = columns_ref[k]
        lines_ref[mirrors + valid_ref.shape[1]:mirrors + valid_ref.shape[1] + 1, k * rows:(k + 1) * rows] = rows_ref[k]


def small_lines(foot_rows, foot_columns, valid):
    vmem = pl.BlockSpec(memory_space=pltpu.VMEM)
    count = foot_rows.shape[1] + valid.shape[1] + 1
    return pl.pallas_call(
        lines_kernel,
        out_shape=jax.ShapeDtypeStruct((-(-count // 8) * 8, WINDOW), jnp.int32),
        in_specs=[vmem] * 3,
        out_specs=vmem,
        name="small_lines",
    )(jnp.swapaxes(foot_rows, 0, 1), jnp.swapaxes(foot_columns, 0, 1), valid)


def pack_kernel(block_ref, *refs):
    lines_refs, packed_ref = refs[:-1], refs[-1]
    mirrors, rows, slots, samples = block_ref.shape
    for unit in range(mirrors * rows // 2):
        base = unit * 3 * slots
        tails = []
        for side in range(2):
            k, l = divmod(2 * unit + side, rows)
            packed_ref[pl.ds(base + side * slots, slots), :] = block_ref[k, l, :, :LANES]
            tails.append(block_ref[k, l, :, LANES:])
        packed_ref[pl.ds(base + 2 * slots, slots), :] = jnp.concatenate(tails, axis=1)
    count = rows // 2 + 1
    lines = [ref[n, mirrors:mirrors + count, :LANES] for ref in lines_refs for n in range(ref.shape[0])]
    extra = packed_ref.shape[0] - mirrors * rows * slots * samples // LANES
    lines.append(jnp.zeros((extra - count * len(lines), LANES), jnp.int32))
    packed_ref[pl.ds(packed_ref.shape[0] - extra, extra), :] = (
        jnp.concatenate(lines, axis=0).astype(jnp.float32).astype(jnp.bfloat16)
    )


def pack(block, lines):
    mirrors, rows, slots, samples = block.shape
    vmem = pl.BlockSpec(memory_space=pltpu.VMEM)
    extra = -(-sum(line.shape[0] for line in lines) * (rows // 2 + 1) // 16) * 16
    return pl.pallas_call(
        pack_kernel,
        out_shape=jax.ShapeDtypeStruct((mirrors * rows * slots * samples // LANES + extra, LANES), block.dtype),
        in_specs=[vmem] * (1 + len(lines)),
        out_specs=vmem,
        compiler_params=pltpu.CompilerParams(vmem_limit_bytes=VMEM_BYTES),
        cost_estimate=pl.CostEstimate(flops=0, bytes_accessed=3 * block.size, transcendentals=0),
        name="pack_influence",
    )(block, *lines)


def column_of(row):
    return jnp.transpose(jnp.broadcast_to(row, (LANES, LANES)), (1, 0))


def gram_kernel(codes_ref, pokes_ref, gram_ref, words, own_signs, own_sums):
    planes = pokes_ref.shape[0]
    half = LANES // 2
    own = own_signs.shape[0]
    chunks = gram_ref.shape[1] // WINDOW

    @pl.when(pl.program_id(0) == 0)
    def _():
        plane = lax.broadcasted_iota(jnp.int32, pokes_ref.shape, 0)
        for bit in range(BITS):
            low = jnp.sum((pokes_ref[...] >> bit & 1) << plane, axis=0, keepdims=True)
            word = low | pltpu.roll(jnp.broadcast_to(low, (8, LANES)), half, 1)[:1] << planes
            words[bit] = column_of(word)[:half]
        count = codes_ref.shape[0] * LANES // (lax.axis_size("dir") * lax.axis_size("row"))
        first = (lax.axis_index("dir") * lax.axis_size("row") + lax.axis_index("row")) * count
        lane = lax.broadcasted_iota(jnp.int32, (8, LANES), 1)
        shift = first % LANES
        lines = [
            pltpu.roll(
                jnp.broadcast_to(
                    codes_ref[pl.ds(jnp.minimum(first // LANES + n, codes_ref.shape[0] - 1), 1), :], (8, LANES)
                ),
                LANES - shift, 1,
            )
            for n in range(-(-own // LANES) + 1)
        ]
        own_column = jnp.concatenate(
            [
                column_of(jnp.where(lane < LANES - shift, lines[n], lines[n + 1])[:1])
                for n in range(len(lines) - 1)
            ],
            axis=0,
        )[:own]
        lane = lax.broadcasted_iota(jnp.int32, (1, LANES), 1)
        total = jnp.zeros((own, LANES), jnp.float32)
        for at in range(planes):
            signs = (1 - 2 * parity(own_column, pokes_ref[at:at + 1, :])).astype(jnp.float32)
            upper = -(2.0 ** -(at + planes)) if at + planes == 31 else 2.0 ** -(at + planes)
            own_signs[:, at * LANES:(at + 1) * LANES] = (
                signs * jnp.where(lane < half, 2.0 ** -at, upper)
            ).astype(jnp.bfloat16)
            total = total + signs
        own_sums[...] = jnp.broadcast_to(jnp.sum(total, axis=1, keepdims=True), own_sums.shape)

    def chunk(index, _):
        word = []
        for side in range(WINDOW // LANES):
            line = (pl.program_id(0) * chunks + index) * (WINDOW // LANES) + side
            code = jnp.broadcast_to(codes_ref[pl.ds(line, 1), :], (8, LANES))
            value = None
            for bit in range(BITS):
                mask = jnp.concatenate([code << (31 - bit) >> 31] * (half // 8), axis=0)
                part = words[bit] & mask
                value = part if value is None else value ^ part
            word.append(value)
        word = jnp.concatenate(word, axis=1)
        total = jnp.zeros((own, WINDOW), jnp.float32)
        for at in range(0, planes, 2):
            bits = [
                (word & np.int32(np.uint32(1 << plane).view(np.int32))).astype(jnp.float32).astype(jnp.bfloat16)
                for plane in (at, at + planes, at + 1, at + 1 + planes)
            ]
            total = total + jnp.dot(
                own_signs[:, at * LANES:(at + 2) * LANES], jnp.concatenate(bits, axis=0),
                preferred_element_type=jnp.float32,
            )
        sums = jnp.concatenate([own_sums[...]] * (WINDOW // LANES), axis=1)
        gram_ref[:, pl.ds(pl.multiple_of(index * WINDOW, WINDOW), WINDOW)] = (sums - 2.0 * total).astype(jnp.bfloat16)
        return 0

    lax.fori_loop(0, chunks, chunk, 0, unroll=3)


def gram(codes, pokes, own):
    own = -(-own // 16) * 16
    acts, count = codes.size, pokes.shape[0]
    steps = 3
    return pl.pallas_call(
        gram_kernel,
        grid=(steps,),
        out_shape=jax.ShapeDtypeStruct((own, acts), jnp.bfloat16),
        in_specs=[pl.BlockSpec(memory_space=pltpu.VMEM)] * 2,
        out_specs=pl.BlockSpec((own, acts // steps), lambda s: (0, s)),
        scratch_shapes=[
            pltpu.VMEM((BITS, LANES // 2, LANES), jnp.int32),
            pltpu.VMEM((own, count), jnp.bfloat16),
            pltpu.VMEM((own, LANES), jnp.float32),
        ],
        compiler_params=pltpu.CompilerParams(vmem_limit_bytes=VMEM_BYTES),
        cost_estimate=pl.CostEstimate(
            flops=2 * own * acts * count, bytes_accessed=2 * own * acts, transcendentals=0
        ),
        name="gram_rows",
    )(codes.reshape(-1, LANES), pokes.reshape(-1, LANES))


def position(axis, staged):
    return lax.axis_index(axis) if staged else 0


def band_products(parts, row_shape, block, surface_rows, gram_ref, window_ref, out_ref):
    mirrors, shard_rows, slots, samples = row_shape
    tail = samples - LANES
    bases = []
    for q in range(mirrors * shard_rows):
        k, l = divmod(q, shard_rows)
        band = jnp.clip((block * shard_rows + l) * NAR // surface_rows - 1, 0, NAR - BAND)
        column = (k * NAR + band) * NA
        bases.append(pl.multiple_of(column // LANES * LANES, LANES))
        shift = pl.multiple_of(column - bases[-1], 16)
        unit, side = divmod(q, 2)
        units = mirrors * shard_rows // 2 // len(parts)
        part, at = parts[unit // units], unit % units * 3 * slots
        for gap in range(0, WINDOW - slots, 16):
            row = pl.multiple_of((shift + slots + gap) % WINDOW, 16)
            window_ref[q, pl.ds(row, 16), :] = jnp.zeros((16, WINDOW), window_ref.dtype)
        window_ref[q, pl.ds(shift, slots), :LANES] = part[pl.ds(at + side * slots, slots), :]
        window_ref[q, pl.ds(shift, slots), LANES:] = part[pl.ds(at + 2 * slots, slots), :]
    for q, base in enumerate(bases):
        u = jnp.dot(gram_ref[:, pl.ds(base, WINDOW)], window_ref[q], preferred_element_type=jnp.float32)
        out_ref[q, :LANES] = jnp.transpose(u[:, :LANES]).astype(jnp.bfloat16)
        rest = jnp.transpose(u[:, LANES:])[q % 2 * tail:(q % 2 + 1) * tail]
        out_ref[q, LANES:] = rest.astype(jnp.bfloat16)


def bands_kernel(row_shape, surface_rows, first, counts, staged, gram_ref, *refs):
    sources = refs[:len(counts)]
    out_ref, window = refs[-2:]
    step = pl.program_id(0)
    start = 0
    for source, count in zip(sources, counts):
        @pl.when((step >= start) & (step < start + count))
        def _():
            block = (first + step) ^ position("row", staged)
            band_products([source.at[0]], row_shape, block, surface_rows, gram_ref, window, out_ref.at[0])
        start += count


def bands(gram_rows, sources, decoded, first, staged, row_shape, surface_rows):
    own = gram_rows.shape[0]
    counts = [source.shape[0] for source in sources]
    starts = np.cumsum([0] + counts)
    total = surface_rows // row_shape[1]
    rows = row_shape[0] * row_shape[1]
    specs = [
        pl.BlockSpec(
            (1,) + source.shape[1:],
            functools.partial(lambda low, high, s: (jnp.clip(s - low, 0, high - 1), 0, 0), int(starts[n]), counts[n]),
        )
        for n, source in enumerate(sources)
    ]
    arguments = [gram_rows, *sources]
    in_specs = [pl.BlockSpec(memory_space=pltpu.VMEM), *specs]
    aliases = {}
    body = functools.partial(bands_kernel, row_shape, surface_rows, first, counts, staged)
    if decoded is not None:
        aliases = {len(arguments): 0}
        arguments.append(decoded)
        in_specs.append(pl.BlockSpec(memory_space=pl.ANY))
    flops = 2 * own * WINDOW * WINDOW * rows * sum(counts)
    return pl.pallas_call(
        body,
        grid=(sum(counts),),
        out_shape=jax.ShapeDtypeStruct((total, rows, row_shape[3], own), jnp.bfloat16),
        in_specs=in_specs,
        out_specs=pl.BlockSpec((1, rows, row_shape[3], own), lambda s: (first + s, 0, 0, 0)),
        scratch_shapes=[pltpu.VMEM((rows, WINDOW, WINDOW), jnp.bfloat16)],
        input_output_aliases=aliases,
        compiler_params=pltpu.CompilerParams(vmem_limit_bytes=VMEM_BYTES),
        cost_estimate=pl.CostEstimate(
            flops=flops, bytes_accessed=2 * own * WINDOW * rows * sum(counts), transcendentals=0
        ),
        name="bands",
    )(*arguments)


def build_differences(columns, differences, mirrors, samples, pupil):
    half = pupil // 2
    slope = lax.broadcasted_iota(jnp.int32, (pupil, pupil), 0)
    lane = lax.broadcasted_iota(jnp.int32, (pupil, pupil), 1)
    upper = lax.broadcasted_iota(jnp.int32, (pupil, samples), 0) >= half
    at = lax.broadcasted_iota(jnp.int32, (pupil, samples), 1)
    for d, lines in enumerate(columns):
        for k in range(mirrors):
            line = jnp.broadcast_to(lines[k:k + 1], (pupil, pupil))
            sides = [
                jnp.sum(jnp.where(lane == slope % half * 2 + side, line, 0), axis=1, keepdims=True) for side in range(2)
            ]
            behind, ahead = ((at == side).astype(jnp.float32) for side in sides)
            across, down = ahead - behind, ahead + behind
            value = jnp.concatenate([jnp.where(upper, -down, across), jnp.where(upper, down, across)], axis=1)
            differences[d, :, 2 * k * samples:2 * (k + 1) * samples] = value.astype(jnp.bfloat16)


def decode_kernel(row_shape, surface_rows, own, late, staged, norm, counts, *refs):
    mirrors, shard_rows, slots, samples = row_shape
    columns_refs, refs = refs[:counts[0]], refs[counts[0]:]
    lines_refs, refs = refs[:counts[1]], refs[counts[1]:]
    late_refs, refs = refs[:counts[2]], refs[counts[2]:]
    gram_ref, decoded_ref, out_ref, decoded, differences, total, window, lines, scalars, semaphores = refs
    group = pl.program_id(0)
    directions, pupil = differences.shape[:2]
    phases = out_ref.shape[2] // pupil
    place = position("row", staged)
    blocks = surface_rows // shard_rows
    ready = blocks - late
    width = shard_rows // 2 + 1

    @pl.when(group == 0)
    def _():
        copies = [
            pltpu.make_async_copy(decoded_ref.at[block], decoded.at[block], semaphores.at[block])
            for block in range(ready)
        ]
        for copy in copies:
            copy.start()
        extra = lines.shape[1]
        ends = [ref.at[n] for ref in lines_refs for n in range(ref.shape[0])]
        parts = [late_refs[n * counts[2] // max(late, 1):(n + 1) * counts[2] // max(late, 1)] for n in range(late)]
        ends += [part[-1].at[pl.ds(part[-1].shape[0] - extra, extra)] for part in parts]
        for block, end in enumerate(ends):
            lines[block] = end[...].astype(jnp.float32).astype(jnp.int32)
        to_scalars = pltpu.make_async_copy(lines, scalars, semaphores.at[blocks])
        to_scalars.start()
        columns = [ref[n, :, :pupil] for ref in columns_refs for n in range(ref.shape[0])]
        build_differences(columns, differences, mirrors, samples, pupil)
        for n, part in enumerate(parts):
            band_products(
                part, row_shape, (ready + n) ^ place, surface_rows, gram_ref, window, decoded.at[ready + n]
            )
        to_scalars.wait()
        for copy in copies:
            copy.wait()

    for d in range(directions):
        held = d ^ position("dir", staged)
        products, factors = [], []
        for phase in range(phases):
            i = group * phases + phase
            block = (2 * i // shard_rows) ^ place
            picked = []
            for k in range(mirrors):
                for y in range(2):
                    row = scalars[block, held * width + width - 1, k * shard_rows + (2 * phase + y) % shard_rows]
                    picked.append(decoded[row // shard_rows ^ place, k * shard_rows + row % shard_rows])
            products.append(
                jnp.dot(differences[held], jnp.concatenate(picked, axis=0), preferred_element_type=jnp.float32)
            )
            valid = lines[block, pl.ds(held * width + phase % (shard_rows // 2), 1), :][:, :pupil // 2]
            factors += [valid.astype(jnp.float32) * norm] * 2
        product = jnp.concatenate(products, axis=0)
        factor = jnp.concatenate(factors, axis=1)
        for tile in range(out_ref.shape[2] // LANES):
            at = tile * LANES
            value = jnp.transpose(product[at:at + LANES])[:own] * factor[:, at:at + LANES]
            total[tile, pl.ds(d, own, stride=directions), :] = value
    for tile in range(out_ref.shape[2] // LANES):
        value = total[tile].reshape(own, directions, LANES)
        out_ref[:, :, tile * LANES:(tile + 1) * LANES] = value.astype(out_ref.dtype)


def decode(columns, sources, late_parts, late, gram_rows, decoded, own, row_shape, surface_rows, pupil, norm, staged):
    blocks = decoded.shape[0]
    mirrors, shard_rows, slots, samples = row_shape
    padded = gram_rows.shape[0]
    directions = sum(line.shape[0] for line in columns)
    extra = -(-directions * (shard_rows // 2 + 1) // 16) * 16
    phases = LANES // math.gcd(pupil, LANES)
    width = surface_rows // 2 * pupil
    lanes = phases * pupil
    flops = 2 * padded * 2 * mirrors * samples * pupil * directions * surface_rows // 2
    vmem = pl.BlockSpec(memory_space=pltpu.VMEM)
    ends = [
        pl.BlockSpec(
            (source.shape[0], extra, LANES),
            functools.partial(lambda last, s: (0, last, 0), source.shape[1] // extra - 1),
        )
        for source in sources
    ]
    counts = (len(columns), len(sources), len(late_parts))
    return pl.pallas_call(
        functools.partial(decode_kernel, row_shape, surface_rows, own, late, staged, norm, counts),
        grid=(width // lanes,),
        out_shape=jax.ShapeDtypeStruct((own, directions, width), jnp.bfloat16),
        in_specs=[vmem] * len(columns) + ends + [vmem] * len(late_parts) + [vmem, pl.BlockSpec(memory_space=pl.ANY)],
        out_specs=pl.BlockSpec((own, directions, lanes), lambda s: (0, 0, s)),
        scratch_shapes=[
            pltpu.VMEM(decoded.shape, jnp.bfloat16),
            pltpu.VMEM((directions, pupil, 2 * mirrors * samples), jnp.bfloat16),
            pltpu.VMEM((lanes // LANES, own * directions, LANES), jnp.float32),
            pltpu.VMEM((mirrors * shard_rows, WINDOW, WINDOW), jnp.bfloat16),
            pltpu.VMEM((blocks, extra, LANES), jnp.int32),
            pltpu.SMEM((blocks, extra, LANES), jnp.int32),
            pltpu.SemaphoreType.DMA((blocks + 1,)),
        ],
        compiler_params=pltpu.CompilerParams(vmem_limit_bytes=VMEM_BYTES),
        cost_estimate=pl.CostEstimate(flops=flops, bytes_accessed=2 * own * directions * width, transcendentals=0),
        name="decode",
    )(*columns, *sources, *late_parts, gram_rows, decoded)


def swap(block, axis, distance):
    return lax.ppermute(block, axis, [(i, i ^ distance) for i in range(lax.axis_size(axis))])


def shards(influence, foot_rows, foot_columns, actuator_codes, poke_rows, subaperture_valid):
    mirrors, shard_rows, samples, slots = influence.shape
    row_shape = (mirrors, shard_rows, slots, samples)
    directions, devices = lax.axis_size("dir"), lax.axis_size("row")
    surface_rows = shard_rows * devices
    pupil = foot_columns.shape[2]
    norm = 0.5 * poke_rows.shape[0] ** (-0.5)
    own = actuator_codes.size // (directions * devices)
    staged = devices == 8 and directions & (directions - 1) == 0
    turned = jnp.swapaxes(influence, 2, 3)
    lines = small_lines(foot_rows, foot_columns, subaperture_valid)
    if not staged:
        lines = [lax.all_gather(lines, "dir")]
        every = lax.all_gather(pack(turned, lines), "row")
        gram_rows = gram(actuator_codes, poke_rows, own)
        decoded = bands(gram_rows, [every], None, 0, staged, row_shape, surface_rows)
        return decode(
            lines, [every], [], 0, gram_rows, decoded, own, row_shape, surface_rows, pupil, norm, staged
        )

    lines = [lines[None]] + [swap(lines, "dir", e)[None] for e in range(1, directions)]
    packed = pack(turned, lines)
    beside, across, sibling = (swap(packed, "row", distance) for distance in (2, 4, 1))
    gram_rows = gram(actuator_codes, poke_rows, own)
    decoded = bands(gram_rows, [packed[None], sibling[None]], None, 0, staged, row_shape, surface_rows)
    decoded, beside, across = lax.optimization_barrier((decoded, beside, across))
    half = mirrors * shard_rows * slots * samples // LANES // 2
    upper, lower = swap(beside[:half], "row", 4), swap(across[half:], "row", 2)
    beside_sibling, across_sibling = swap(beside, "row", 1), swap(across, "row", 1)
    sources = [source[None] for source in (beside, beside_sibling, across, across_sibling)]
    decoded = bands(gram_rows, sources, decoded, 2, staged, row_shape, surface_rows)
    decoded, upper, lower = lax.optimization_barrier((decoded, upper, lower))
    late = [upper, lower, swap(upper, "row", 1), swap(lower, "row", 1)]
    return decode(
        lines, [packed[None], sibling[None], *sources], late, 2, gram_rows, decoded, own, row_shape, surface_rows,
        pupil, norm, staged,
    )


def solution(mesh):
    return jax.shard_map(
        shards,
        mesh=mesh,
        in_specs=(
            P(None, "row", None, None),
            P("dir", None, "row"),
            P("dir", None, None),
            P(),
            P(),
            P("dir", "row", None),
        ),
        out_specs=P(("dir", "row"), None, None),
        check_vma=False,
    )
```

time: 86 us -> 75.4 us (0.88)
  waiting for transfers between devices: 14.1 us -> 8.6 us
  starting transfers between devices: 14.2 us -> 10.9 us
  local copies, waits for them, and re-layouts: 8.3 us -> 5.38 us
  Pallas kernels: 48.7 us -> 49.9 us
    ppermute x15 -> x12, waiting for transfers between devices: 14.1 us -> 8.6 us  [swap(): lax.ppermute(block, axis, [(i, i ^ distance) for i in range(lax.axis_size...]
    ppermute x15 -> x12, starting transfers between devices: 14.2 us -> 10.9 us  [swap(): lax.ppermute(block, axis, [(i, i ^ distance) for i in range(lax.axis_size...]
    unnamed x25 -> x24, local copies, waits for them, and re-layouts: 5.93 us -> 3.75 us
    pallas_call x1 -> x2, Pallas kernels: 2.15 us -> 3.64 us  [the longest x1 2.25 us: pack(): pl.pallas_call(pack_kernel, out_shape=jax.ShapeDtypeStruct((mirrors * row...]
    pallas_call x1, Pallas kernels: 21.3 us -> 19.9 us  [decode(): pl.pallas_call(functools.partial(decode_kernel, row_shape, surface_rows,...]
    pallas_call x2, Pallas kernels: 12.8 us -> 13.9 us  [bands(): pl.pallas_call(body, grid=(sum(counts),), out_shape=jax.ShapeDtypeStruct(...]
  transfers between devices with their start and end apart: 15 -> 12, of which waited for: 3 -> 5; matrix products, arithmetic and copies ran while one was open for 3% -> 2% of each run, Pallas kernels for 30% -> 35%
where the time goes in v4:
time: 75.4 us; the launch traced here: 75.1 us
  Pallas kernels  49.9 us (66%)
  starting transfers between devices  10.9 us (14%)
  waiting for transfers between devices  8.6 us (11%)
  local copies, waits for them, and re-layouts  5.38 us (7%)
    pallas_call x1, Pallas kernels, decode(): pl.pallas_call(functools.partial(decode_kernel, row_shape, surface_rows,...  19.9 us
    pallas_call x2, Pallas kernels, bands(): pl.pallas_call(body, grid=(sum(counts),), out_shape=jax.ShapeDtypeStruct(...  13.9 us
    pallas_call x1, Pallas kernels, gram(): pl.pallas_call(gram_kernel, grid=(steps,), out_shape=jax.ShapeDtypeStruct...  12.5 us
    ppermute x12, starting transfers between devices, swap(): lax.ppermute(block, axis, [(i, i ^ distance) for i in range(lax.axis_size...  10.9 us
    ppermute x12, waiting for transfers between devices, swap(): lax.ppermute(block, axis, [(i, i ^ distance) for i in range(lax.axis_size...  8.6 us
    unnamed x24, local copies, waits for them, and re-layouts  3.75 us
    pallas_call x1, Pallas kernels, pack(): pl.pallas_call(pack_kernel, out_shape=jax.ShapeDtypeStruct((mirrors * row...  2.25 us
    reshape x1, local copies, waits for them, and re-layouts, gram(): codes.reshape(-1, LANES)  1.59 us
  transfers between devices with their start and end apart: 12, of which 5 were waited for; matrix products, arithmetic and copies ran while one was open for 2% of the time, Pallas kernels for 35%

profile of v4, /device:TPU:0, one launch (start us, length us, event | category | flops | bytes accessed | tf_op | source)
XLA Modules:
  0.0 75.1 jit_solution(8367304579993642640)
XLA Ops:
  0.0 1.4 %small_lines.1 = s32[8,256]{1,0:T(8,128)} custom-call(s32[3,1,4]{2,1,0:T(1,128)} %bitcast.36, s32[3,1,160]{2,1,0:T(1,128)} %bitcast.35, s32[1,2,80]{2,1,0:T(2,128)} %valid_ref.1), custom_call_target="tpu_custom_call" | custom-call | tf_op jit(solution)/shard_map/small_lines/pallas_call | solution.py:37
  1.4 3.0 %collective-permute-start = (s32[8,256]{1,0:T(8,128)}, s32[8,256]{1,0:T(8,128)S(1)}, u32[]{:S(2)}, u32[]{:S(2)}) collective-permute-start(s32[8,256]{1,0:T(8,128)} %small_lines.1), channel_id=1, source_target_pairs={{0,8},{8,0},{16,24},{24,16},{1,9},{9,1},{17,25},{25,17},{2,10},{10... | collective-permute-start | bytes 24584 | tf_op jit(solution)/shard_map/ppermute | solution.py:387
  4.4 2.6 %collective-permute-start.1 = (s32[8,256]{1,0:T(8,128)}, s32[8,256]{1,0:T(8,128)S(1)}, u32[]{:S(2)}, u32[]{:S(2)}) collective-permute-start(s32[8,256]{1,0:T(8,128)} %small_lines.1), channel_id=1, source_target_pairs={{0,16},{8,24},{16,0},{24,8},{1,17},{9,25},{17,1},{25,9},{2,18},{10... | collective-permute-start | bytes 24584 | tf_op jit(solution)/shard_map/ppermute | solution.py:387
  7.0 0.0 collective-permute-start.2
  7.0 0.0 collective-permute-done
  7.0 0.0 copy-start.9
  7.0 2.2 %collective-permute-done.1 = s32[8,256]{1,0:T(8,128)S(1)} collective-permute-done((s32[8,256]{1,0:T(8,128)}, s32[8,256]{1,0:T(8,128)S(1)}, u32[]{:S(2)}, u32[]{:S(2)}) %collective-permute-start.1) | collective-permute-done | bytes 8224 | tf_op jit(solution)/shard_map/ppermute | solution.py:387
  9.2 0.0 copy-start.10
  9.2 3.5 %collective-permute-done.2 = s32[8,256]{1,0:T(8,128)S(1)} collective-permute-done((s32[8,256]{1,0:T(8,128)}, s32[8,256]{1,0:T(8,128)S(1)}, u32[]{:S(2)}, u32[]{:S(2)}) %collective-permute-start.2) | collective-permute-done | bytes 8224 | tf_op jit(solution)/shard_map/ppermute | solution.py:387
  12.7 0.0 copy-start.11
  12.7 0.0 copy-done.9
  12.7 0.0 copy-done.10
  12.7 0.6 copy-done.11
  13.3 2.3 %pack_influence.1 = bf16[2608,128]{1,0:T(8,128)(2,1)} custom-call(bf16[3,4,144,192]{3,2,1,0:T(8,128)(2,1)} %bitcast.26, s32[1,8,256]{2,1,0:T(8,128)} %bitcast.27, s32[1,8,256]{2,1,0:T(8,128)} %bitcast.29, s32[1,8,256]{2,1,0:T(8,128)} %bitcast.31, s32[1,8,256]{2,1,0:T(8,128)} %bitcast.33), custom_call_target="tpu_custom_call" | custom-call | bytes 995328 | tf_op jit(solution)/shard_map/pack_influence/pallas_call | solution.py:70
  15.5 0.0 collective-permute-start.3
  15.5 1.5 %collective-permute-start.4 = (bf16[2608,128]{1,0:T(8,128)(2,1)}, bf16[2608,128]{1,0:T(8,128)(2,1)S(1)}, u32[]{:S(2)}, u32[]{:S(2)}) collective-permute-start(bf16[2608,128]{1,0:T(8,128)(2,1)} %pack_influence.1), channel_id=1, source_target_pairs={{0,2},{1,3},{2,0},{3,1},{4,6},{5,7},{6,4},{7,5},{8,10},{9,11},{10,... | collective-permute-start | bytes 2002952 | tf_op jit(solution)/shard_map/ppermute | solution.py:387
  17.0 1.5 %collective-permute-start.5 = (bf16[2608,128]{1,0:T(8,128)(2,1)}, bf16[2608,128]{1,0:T(8,128)(2,1)S(1)}, u32[]{:S(2)}, u32[]{:S(2)}) collective-permute-start(bf16[2608,128]{1,0:T(8,128)(2,1)} %pack_influence.1), channel_id=1, source_target_pairs={{0,4},{1,5},{2,6},{3,7},{4,0},{5,1},{6,2},{7,3},{8,12},{9,13},{10,... | collective-permute-start | bytes 2002952 | tf_op jit(solution)/shard_map/ppermute | solution.py:387
  18.5 1.6 %reshape.6.codes_ref = s32[54,128]{1,0:T(8,128)} reshape(s32[3,48,48]{2,1,0:T(8,128)} %param.9) | data formatting | bytes 55296 | tf_op jit(solution)/shard_map/reshape | solution.py:178
  20.1 12.5 %gram_rows.1.gram_ref.refs_14_ = bf16[224,6912]{1,0:T(8,128)(2,1)} custom-call(s32[54,128]{1,0:T(8,128)} %reshape.6.codes_ref, s32[16,128]{1,0:T(8,128)} %bitcast.37), custom_call_target="tpu_custom_call" | custom-call | flops 6341787648 | bytes 3096576 | tf_op jit(solution)/shard_map/gram_rows/pallas_call | solution.py:162
  32.6 0.0 collective-permute-done.3
  32.6 0.8 %copy-done.2 = bf16[2608,128]{1,0:T(8,128)(2,1)} copy-done((bf16[2608,128]{1,0:T(8,128)(2,1)}, bf16[2608,128]{1,0:T(8,128)(2,1)S(1)}, u32[]{:S(2)}) %copy-start.2) | copy-done | bytes 667672
  33.5 5.6 %bands.2.refs_4_ = bf16[8,12,192,224]{3,2,1,0:T(8,128)(2,1)} custom-call(bf16[224,6912]{1,0:T(8,128)(2,1)} %gram_rows.1.gram_ref.refs_14_, bf16[1,2608,128]{2,1,0:T(8,128)(2,1)} %bitcast.14, bf16[1,2608,128]{2,1,0:T(8,128)(2,1)} %bitcast.20), custom_call_target="tpu_custom_call" | custom-call | flops 704643072 | bytes 2752512 | tf_op jit(solution)/shard_map/bands/pallas_call | solution.py:245
  39.0 0.0 collective-permute-done.4
  39.0 0.0 collective-permute-done.5
  39.0 0.0 copy-start
  39.0 0.1 collective-permute-start.6
  39.1 0.5 collective-permute-start.7
  39.6 0.6 collective-permute-start.9
  40.3 0.6 collective-permute-start.8
  40.8 0.4 collective-permute-done.6
  41.2 1.0 %collective-permute-done.7 = bf16[2608,128]{1,0:T(8,128)(2,1)S(1)} collective-permute-done((bf16[2608,128]{1,0:T(8,128)(2,1)S(1)}, bf16[2608,128]{1,0:T(8,128)(2,1)S(1)}, u32[]{:S(2)}, u32[]{:S(2)}) %collective-permute-start.7) | collective-permute-done | bytes 667680 | tf_op jit(solution)/shard_map/ppermute | solution.py:387
  42.2 0.0 copy-done.1
  42.2 0.0 copy-done
  42.2 0.0 copy-done.3
  42.2 0.8 %copy-done.4 = bf16[2608,128]{1,0:T(8,128)(2,1)} copy-done((bf16[2608,128]{1,0:T(8,128)(2,1)}, bf16[2608,128]{1,0:T(8,128)(2,1)S(1)}, u32[]{:S(2)}) %copy-start.4) | copy-done | bytes 667672
  43.0 8.3 %bands.3.refs_15_ = bf16[8,12,192,224]{3,2,1,0:T(8,128)(2,1)} custom-call(bf16[224,6912]{1,0:T(8,128)(2,1)} %gram_rows.1.gram_ref.refs_14_, bf16[1,2608,128]{2,1,0:T(8,128)(2,1)} %bitcast.18, bf16[1,2608,128]{2,1,0:T(8,128)(2,1)} %bitcast.22, bf16[1,2608,128]{2,1,0:T(8,128)(2,1)} %bitcast.16, ...), custom_call_target="tpu_custom_call", output_to_operand_aliasing={{}: (5, {})} | custom-call | flops 1409286144 | bytes 5505024 | tf_op jit(solution)/shard_map/bands/pallas_call | solution.py:245
  51.4 0.0 collective-permute-done.8.refs_10_
  51.4 0.0 collective-permute-done.9.refs_11_
  51.4 0.0 copy-start.5
  51.4 0.2 collective-permute-start.11
  51.6 0.4 collective-permute-start.10
  52.0 1.6 %collective-permute-done.10.refs_12_ = bf16[1296,128]{1,0:T(8,128)(2,1)S(1)} collective-permute-done((bf16[1296,128]{1,0:T(8,128)(2,1)S(1)}, bf16[1296,128]{1,0:T(8,128)(2,1)S(1)}, u32[]{:S(2)}, u32[]{:S(2)}) %collective-permute-start.10) | collective-permute-done | bytes 331808 | tf_op jit(solution)/shard_map/ppermute | solution.py:387
  53.6 0.0 collective-permute-done.11.refs_13_
  53.6 0.0 copy-done.7
  53.6 0.0 copy-done.5
  53.6 0.7 copy-done.8
  54.3 0.7 copy-done.6
  55.1 19.9 %decode.1 = bf16[216,4,2560]{2,1,0:T(4,128)(2,1)} custom-call(s32[1,8,256]{2,1,0:T(8,128)} %bitcast.28, s32[1,8,256]{2,1,0:T(8,128)} %bitcast.30, s32[1,8,256]{2,1,0:T(8,128)} %bitcast.32, s32[1,8,256]{2,1,0:T(8,128)} %bitcast.34, bf16[1,2608,128]{2,1,0:T(8,128)(2,1)} %bitcast.15, bf16[1,2608,128]{2,1,0:T(8,128)(2,1)} %bitcast.21, ...), custom_call_target="tpu_custom_call" | custom-call | flops 5284823040 | bytes 4423680 | tf_op jit(solution)/shard_map/decode/pallas_call | solution.py:365
  (9 shorter events, 0.1 us)
Async XLA Ops:
  1.4 5.6 %collective-permute-start = (s32[8,256]{1,0:T(8,128)}, s32[8,256]{1,0:T(8,128)S(1)}, u32[]{:S(2)}, u32[]{:S(2)}) collective-permute-start(s32[8,256]{1,0:T(8,128)} %small_lines.1), channel_id=1, source_target_pairs={{0,8},{8,0},{16,24},{24,16},{1,9},{9,1},{17,25},{25,17},{2,10},{10... | collective-permute-start | bytes 24584 | tf_op jit(solution)/shard_map/ppermute | solution.py:387
  4.4 4.8 %collective-permute-start.1 = (s32[8,256]{1,0:T(8,128)}, s32[8,256]{1,0:T(8,128)S(1)}, u32[]{:S(2)}, u32[]{:S(2)}) collective-permute-start(s32[8,256]{1,0:T(8,128)} %small_lines.1), channel_id=1, source_target_pairs={{0,16},{8,24},{16,0},{24,8},{1,17},{9,25},{17,1},{25,9},{2,18},{10... | collective-permute-start | bytes 24584 | tf_op jit(solution)/shard_map/ppermute | solution.py:387
  7.0 5.7 %collective-permute-start.2 = (s32[8,256]{1,0:T(8,128)}, s32[8,256]{1,0:T(8,128)S(1)}, u32[]{:S(2)}, u32[]{:S(2)}) collective-permute-start(s32[8,256]{1,0:T(8,128)} %small_lines.1), channel_id=1, source_target_pairs={{0,24},{8,16},{16,8},{24,0},{1,25},{9,17},{17,9},{25,1},{2,26},{10... | collective-permute-start | bytes 24584 | tf_op jit(solution)/shard_map/ppermute | solution.py:387
  7.0 5.7 %copy-start.9 = (s32[8,256]{1,0:T(8,128)}, s32[8,256]{1,0:T(8,128)S(1)}, u32[]{:S(2)}) copy-start(s32[8,256]{1,0:T(8,128)S(1)} %collective-permute-done) | copy-start | bytes 24580
  9.2 3.5 %copy-start.10 = (s32[8,256]{1,0:T(8,128)}, s32[8,256]{1,0:T(8,128)S(1)}, u32[]{:S(2)}) copy-start(s32[8,256]{1,0:T(8,128)S(1)} %collective-permute-done.1) | copy-start | bytes 24580
  12.7 0.6 copy-start.11
  15.5 17.1 %collective-permute-start.3 = (bf16[2608,128]{1,0:T(8,128)(2,1)}, bf16[2608,128]{1,0:T(8,128)(2,1)S(1)}, u32[]{:S(2)}, u32[]{:S(2)}) collective-permute-start(bf16[2608,128]{1,0:T(8,128)(2,1)} %pack_influence.1), channel_id=1, source_target_pairs={{0,1},{1,0},{2,3},{3,2},{4,5},{5,4},{6,7},{7,6},{8,9},{9,8},{10,11... | collective-permute-start | bytes 2002952 | tf_op jit(solution)/shard_map/ppermute | solution.py:387
  15.5 23.5 %collective-permute-start.4 = (bf16[2608,128]{1,0:T(8,128)(2,1)}, bf16[2608,128]{1,0:T(8,128)(2,1)S(1)}, u32[]{:S(2)}, u32[]{:S(2)}) collective-permute-start(bf16[2608,128]{1,0:T(8,128)(2,1)} %pack_influence.1), channel_id=1, source_target_pairs={{0,2},{1,3},{2,0},{3,1},{4,6},{5,7},{6,4},{7,5},{8,10},{9,11},{10,... | collective-permute-start | bytes 2002952 | tf_op jit(solution)/shard_map/ppermute | solution.py:387
  17.0 22.0 %collective-permute-start.5 = (bf16[2608,128]{1,0:T(8,128)(2,1)}, bf16[2608,128]{1,0:T(8,128)(2,1)S(1)}, u32[]{:S(2)}, u32[]{:S(2)}) collective-permute-start(bf16[2608,128]{1,0:T(8,128)(2,1)} %pack_influence.1), channel_id=1, source_target_pairs={{0,4},{1,5},{2,6},{3,7},{4,0},{5,1},{6,2},{7,3},{8,12},{9,13},{10,... | collective-permute-start | bytes 2002952 | tf_op jit(solution)/shard_map/ppermute | solution.py:387
  32.6 0.8 %copy-start.2 = (bf16[2608,128]{1,0:T(8,128)(2,1)}, bf16[2608,128]{1,0:T(8,128)(2,1)S(1)}, u32[]{:S(2)}) copy-start(bf16[2608,128]{1,0:T(8,128)(2,1)S(1)} %collective-permute-done.3) | copy-start | bytes 2002948
  39.0 3.2 %copy-start.1 = (bf16[2608,128]{1,0:T(8,128)(2,1)}, bf16[2608,128]{1,0:T(8,128)(2,1)S(1)}, u32[]{:S(2)}) copy-start(bf16[2608,128]{1,0:T(8,128)(2,1)S(1)} %collective-permute-done.4) | copy-start | bytes 2002948
  39.0 3.2 %copy-start = (bf16[2608,128]{1,0:T(8,128)(2,1)}, bf16[2608,128]{1,0:T(8,128)(2,1)S(1)}, u32[]{:S(2)}) copy-start(bf16[2608,128]{1,0:T(8,128)(2,1)S(1)} %collective-permute-done.5) | copy-start | bytes 2002948
  39.0 2.2 %collective-permute-start.6 = (bf16[2608,128]{1,0:T(8,128)(2,1)S(1)}, bf16[2608,128]{1,0:T(8,128)(2,1)S(1)}, u32[]{:S(2)}, u32[]{:S(2)}) collective-permute-start(bf16[2608,128]{1,0:T(8,128)(2,1)S(1)} %collective-permute-done.4), channel_id=1, source_target_pairs={{0,1},{1,0},{2,3},{3,2},{4,5},{5,4},{6,7},{7,6},{8,9},{9,8},{10,11... | collective-permute-start | bytes 2002952 | tf_op jit(solution)/shard_map/ppermute | solution.py:387
  39.1 3.1 %collective-permute-start.7 = (bf16[2608,128]{1,0:T(8,128)(2,1)S(1)}, bf16[2608,128]{1,0:T(8,128)(2,1)S(1)}, u32[]{:S(2)}, u32[]{:S(2)}) collective-permute-start(bf16[2608,128]{1,0:T(8,128)(2,1)S(1)} %collective-permute-done.5), channel_id=1, source_target_pairs={{0,1},{1,0},{2,3},{3,2},{4,5},{5,4},{6,7},{7,6},{8,9},{9,8},{10,11... | collective-permute-start | bytes 2002952 | tf_op jit(solution)/shard_map/ppermute | solution.py:387
  39.6 11.7 %collective-permute-start.9 = (bf16[1312,128]{1,0:T(8,128)(2,1)S(1)}, bf16[1312,128]{1,0:T(8,128)(2,1)S(1)}, u32[]{:S(2)}, u32[]{:S(2)}) collective-permute-start(bf16[1312,128]{1,0:T(8,128)(2,1)S(1)} %slice.7), channel_id=1, source_target_pairs={{0,2},{1,3},{2,0},{3,1},{4,6},{5,7},{6,4},{7,5},{8,10},{9,11},{10,... | collective-permute-start | bytes 1007624 | tf_op jit(solution)/shard_map/ppermute | solution.py:387
  40.3 11.1 %collective-permute-start.8 = (bf16[1296,128]{1,0:T(8,128)(2,1)S(1)}, bf16[1296,128]{1,0:T(8,128)(2,1)S(1)}, u32[]{:S(2)}, u32[]{:S(2)}) collective-permute-start(bf16[1296,128]{1,0:T(8,128)(2,1)S(1)} %slice.6), channel_id=1, source_target_pairs={{0,4},{1,5},{2,6},{3,7},{4,0},{5,1},{6,2},{7,3},{8,12},{9,13},{10,... | collective-permute-start | bytes 995336 | tf_op jit(solution)/shard_map/ppermute | solution.py:387
  41.2 1.0 %copy-start.3 = (bf16[2608,128]{1,0:T(8,128)(2,1)}, bf16[2608,128]{1,0:T(8,128)(2,1)S(1)}, u32[]{:S(2)}) copy-start(bf16[2608,128]{1,0:T(8,128)(2,1)S(1)} %collective-permute-done.6) | copy-start | bytes 2002948
  42.2 0.8 %copy-start.4 = (bf16[2608,128]{1,0:T(8,128)(2,1)}, bf16[2608,128]{1,0:T(8,128)(2,1)S(1)}, u32[]{:S(2)}) copy-start(bf16[2608,128]{1,0:T(8,128)(2,1)S(1)} %collective-permute-done.7) | copy-start | bytes 2002948
  51.4 2.2 %copy-start.7 = (bf16[1296,128]{1,0:T(8,128)(2,1)}, bf16[1296,128]{1,0:T(8,128)(2,1)S(1)}, u32[]{:S(2)}) copy-start(bf16[1296,128]{1,0:T(8,128)(2,1)S(1)} %collective-permute-done.8.refs_10_) | copy-start | bytes 995332
  51.4 2.2 %copy-start.5 = (bf16[1312,128]{1,0:T(8,128)(2,1)}, bf16[1312,128]{1,0:T(8,128)(2,1)S(1)}, u32[]{:S(2)}) copy-start(bf16[1312,128]{1,0:T(8,128)(2,1)S(1)} %collective-permute-done.9.refs_11_) | copy-start | bytes 1007620
  51.4 2.2 %collective-permute-start.11 = (bf16[1312,128]{1,0:T(8,128)(2,1)S(1)}, bf16[1312,128]{1,0:T(8,128)(2,1)S(1)}, u32[]{:S(2)}, u32[]{:S(2)}) collective-permute-start(bf16[1312,128]{1,0:T(8,128)(2,1)S(1)} %collective-permute-done.9.refs_11_), channel_id=1, source_target_pairs={{0,1},{1,0},{2,3},{3,2},{4,5},{5,4},{6,7},{7,6},{8,9},{9,8},{10,11... | collective-permute-start | bytes 1007624 | tf_op jit(solution)/shard_map/ppermute | solution.py:387
  51.6 2.0 %collective-permute-start.10 = (bf16[1296,128]{1,0:T(8,128)(2,1)S(1)}, bf16[1296,128]{1,0:T(8,128)(2,1)S(1)}, u32[]{:S(2)}, u32[]{:S(2)}) collective-permute-start(bf16[1296,128]{1,0:T(8,128)(2,1)S(1)} %collective-permute-done.8.refs_10_), channel_id=1, source_target_pairs={{0,1},{1,0},{2,3},{3,2},{4,5},{5,4},{6,7},{7,6},{8,9},{9,8},{10,11... | collective-permute-start | bytes 995336 | tf_op jit(solution)/shard_map/ppermute | solution.py:387
  53.6 0.7 copy-start.8
  54.3 0.7 copy-start.6

commit v5 on v4

--- a/solution.py
+++ b/solution.py
@@ -46,17 +46,25 @@
 def pack_kernel(block_ref, *refs):
     lines_refs, packed_ref = refs[:-1], refs[-1]
     mirrors, rows, slots, samples = block_ref.shape
-    for unit in range(mirrors * rows // 2):
-        base = unit * 3 * slots
+    groups = mirrors * rows // 2
+    identity = (
+        lax.broadcasted_iota(jnp.int32, (samples, samples), 0) == lax.broadcasted_iota(jnp.int32, (samples, samples), 1)
+    ).astype(jnp.float32).astype(jnp.bfloat16)
+    for part in range(2):
+        base = part * (groups + 1) * samples
         tails = []
-        for side in range(2):
-            k, l = divmod(2 * unit + side, rows)
-            packed_ref[pl.ds(base + side * slots, slots), :] = block_ref[k, l, :, :LANES]
-            tails.append(block_ref[k, l, :, LANES:])
-        packed_ref[pl.ds(base + 2 * slots, slots), :] = jnp.concatenate(tails, axis=1)
+        for group in range(groups):
+            k, l = divmod(part * groups + group, rows)
+            turned = lax.dot_general(
+                identity, block_ref[k, l], (((1,), (1,)), ((), ())), preferred_element_type=jnp.float32
+            ).astype(jnp.bfloat16)
+            packed_ref[pl.ds(base + group * samples, samples), :] = turned[:, :LANES]
+            tails.append(turned[:, LANES:])
+        tails.append(jnp.zeros((samples, LANES - groups * (slots - LANES)), jnp.bfloat16))
+        packed_ref[pl.ds(base + groups * samples, samples), :] = jnp.concatenate(tails, axis=1)
     count = rows // 2 + 1
     lines = [ref[n, mirrors:mirrors + count, :LANES] for ref in lines_refs for n in range(ref.shape[0])]
-    extra = packed_ref.shape[0] - mirrors * rows * slots * samples // LANES
+    extra = packed_ref.shape[0] - 2 * (groups + 1) * samples
     lines.append(jnp.zeros((extra - count * len(lines), LANES), jnp.int32))
     packed_ref[pl.ds(packed_ref.shape[0] - extra, extra), :] = (
         jnp.concatenate(lines, axis=0).astype(jnp.float32).astype(jnp.bfloat16)
@@ -69,7 +77,7 @@
     extra = -(-sum(line.shape[0] for line in lines) * (rows // 2 + 1) // 16) * 16
     return pl.pallas_call(
         pack_kernel,
-        out_shape=jax.ShapeDtypeStruct((mirrors * rows * slots * samples // LANES + extra, LANES), block.dtype),
+        out_shape=jax.ShapeDtypeStruct(((mirrors * rows + 2) * samples + extra, LANES), block.dtype),
         in_specs=[vmem] * (1 + len(lines)),
         out_specs=vmem,
         compiler_params=pltpu.CompilerParams(vmem_limit_bytes=VMEM_BYTES),
@@ -82,49 +90,66 @@
     return jnp.transpose(jnp.broadcast_to(row, (LANES, LANES)), (1, 0))
 
 
-def gram_kernel(codes_ref, pokes_ref, gram_ref, words, own_signs, own_sums):
+def signs_kernel(codes_ref, pokes_ref, words, own_signs, own_sums):
     planes = pokes_ref.shape[0]
     half = LANES // 2
     own = own_signs.shape[0]
-    chunks = gram_ref.shape[1] // WINDOW
-
-    @pl.when(pl.program_id(0) == 0)
-    def _():
-        plane = lax.broadcasted_iota(jnp.int32, pokes_ref.shape, 0)
-        for bit in range(BITS):
-            low = jnp.sum((pokes_ref[...] >> bit & 1) << plane, axis=0, keepdims=True)
-            word = low | pltpu.roll(jnp.broadcast_to(low, (8, LANES)), half, 1)[:1] << planes
-            words[bit] = column_of(word)[:half]
-        count = codes_ref.shape[0] * LANES // (lax.axis_size("dir") * lax.axis_size("row"))
-        first = (lax.axis_index("dir") * lax.axis_size("row") + lax.axis_index("row")) * count
-        lane = lax.broadcasted_iota(jnp.int32, (8, LANES), 1)
-        shift = first % LANES
-        lines = [
-            pltpu.roll(
-                jnp.broadcast_to(
-                    codes_ref[pl.ds(jnp.minimum(first // LANES + n, codes_ref.shape[0] - 1), 1), :], (8, LANES)
-                ),
-                LANES - shift, 1,
-            )
-            for n in range(-(-own // LANES) + 1)
-        ]
-        own_column = jnp.concatenate(
-            [
-                column_of(jnp.where(lane < LANES - shift, lines[n], lines[n + 1])[:1])
-                for n in range(len(lines) - 1)
-            ],
-            axis=0,
-        )[:own]
-        lane = lax.broadcasted_iota(jnp.int32, (1, LANES), 1)
-        total = jnp.zeros((own, LANES), jnp.float32)
-        for at in range(planes):
-            signs = (1 - 2 * parity(own_column, pokes_ref[at:at + 1, :])).astype(jnp.float32)
-            upper = -(2.0 ** -(at + planes)) if at + planes == 31 else 2.0 ** -(at + planes)
-            own_signs[:, at * LANES:(at + 1) * LANES] = (
-                signs * jnp.where(lane < half, 2.0 ** -at, upper)
-            ).astype(jnp.bfloat16)
-            total = total + signs
-        own_sums[...] = jnp.broadcast_to(jnp.sum(total, axis=1, keepdims=True), own_sums.shape)
+    plane = lax.broadcasted_iota(jnp.int32, pokes_ref.shape, 0)
+    for bit in range(BITS):
+        low = jnp.sum((pokes_ref[...] >> bit & 1) << plane, axis=0, keepdims=True)
+        word = low | pltpu.roll(jnp.broadcast_to(low, (8, LANES)), half, 1)[:1] << planes
+        words[bit] = column_of(word)[:half]
+    count = codes_ref.shape[0] * LANES // (lax.axis_size("dir") * lax.axis_size("row"))
+    first = (lax.axis_index("dir") * lax.axis_size("row") + lax.axis_index("row")) * count
+    lane = lax.broadcasted_iota(jnp.int32, (8, LANES), 1)
+    shift = first % LANES
+    lines = [
+        pltpu.roll(
+            jnp.broadcast_to(
+                codes_ref[pl.ds(jnp.minimum(first // LANES + n, codes_ref.shape[0] - 1), 1), :], (8, LANES)
+            ),
+            LANES - shift, 1,
+        )
+        for n in range(-(-own // LANES) + 1)
+    ]
+    own_column = jnp.concatenate(
+        [column_of(jnp.where(lane < LANES - shift, lines[n], lines[n + 1])[:1]) for n in range(len(lines) - 1)],
+        axis=0,
+    )[:own]
+    lane = lax.broadcasted_iota(jnp.int32, (1, LANES), 1)
+    total = jnp.zeros((own, LANES), jnp.float32)
+    for at in range(planes):
+        signs = (1 - 2 * parity(own_column, pokes_ref[at:at + 1, :])).astype(jnp.float32)
+        upper = -(2.0 ** -(at + planes)) if at + planes == 31 else 2.0 ** -(at + planes)
+        own_signs[:, at * LANES:(at + 1) * LANES] = (
+            signs * jnp.where(lane < half, 2.0 ** -at, upper)
+        ).astype(jnp.bfloat16)
+        total = total + signs
+    own_sums[...] = jnp.broadcast_to(jnp.sum(total, axis=1, keepdims=True), own_sums.shape)
+
+
+def own_side(codes, pokes, own):
+    own = -(-own // 16) * 16
+    vmem = pl.BlockSpec(memory_space=pltpu.VMEM)
+    return pl.pallas_call(
+        signs_kernel,
+        out_shape=[
+            jax.ShapeDtypeStruct((BITS, LANES // 2, LANES), jnp.int32),
+            jax.ShapeDtypeStruct((own, pokes.size), jnp.bfloat16),
+            jax.ShapeDtypeStruct((own, LANES), jnp.float32),
+        ],
+        in_specs=[vmem] * 2,
+        out_specs=[vmem] * 3,
+        compiler_params=pltpu.CompilerParams(vmem_limit_bytes=VMEM_BYTES),
+        name="own_signs",
+    )(codes, pokes)
+
+
+def gram_kernel(codes_ref, words, own_signs, own_sums, gram_ref):
+    half = LANES // 2
+    own, pokes = own_signs.shape
+    planes = pokes // LANES
+    chunks = gram_ref.shape[0] // WINDOW
 
     def chunk(index, _):
         word = []
@@ -149,79 +174,75 @@
                 preferred_element_type=jnp.float32,
             )
         sums = jnp.concatenate([own_sums[...]] * (WINDOW // LANES), axis=1)
-        gram_ref[:, pl.ds(pl.multiple_of(index * WINDOW, WINDOW), WINDOW)] = (sums - 2.0 * total).astype(jnp.bfloat16)
+        turned = jnp.transpose(sums - 2.0 * total)
+        gram_ref[pl.ds(pl.multiple_of(index * WINDOW, WINDOW), WINDOW), :] = turned.astype(jnp.bfloat16)
         return 0
 
     lax.fori_loop(0, chunks, chunk, 0, unroll=3)
 
 
-def gram(codes, pokes, own):
-    own = -(-own // 16) * 16
-    acts, count = codes.size, pokes.shape[0]
+def gram(codes, words, own_signs, own_sums):
+    acts, (own, count) = codes.size, own_signs.shape
     steps = 3
+    vmem = pl.BlockSpec(memory_space=pltpu.VMEM)
     return pl.pallas_call(
         gram_kernel,
         grid=(steps,),
-        out_shape=jax.ShapeDtypeStruct((own, acts), jnp.bfloat16),
-        in_specs=[pl.BlockSpec(memory_space=pltpu.VMEM)] * 2,
-        out_specs=pl.BlockSpec((own, acts // steps), lambda s: (0, s)),
-        scratch_shapes=[
-            pltpu.VMEM((BITS, LANES // 2, LANES), jnp.int32),
-            pltpu.VMEM((own, count), jnp.bfloat16),
-            pltpu.VMEM((own, LANES), jnp.float32),
-        ],
+        out_shape=jax.ShapeDtypeStruct((acts, own), jnp.bfloat16),
+        in_specs=[vmem] * 4,
+        out_specs=pl.BlockSpec((acts // steps, own), lambda s: (s, 0)),
         compiler_params=pltpu.CompilerParams(vmem_limit_bytes=VMEM_BYTES),
         cost_estimate=pl.CostEstimate(
             flops=2 * own * acts * count, bytes_accessed=2 * own * acts, transcendentals=0
         ),
         name="gram_rows",
-    )(codes.reshape(-1, LANES), pokes.reshape(-1, LANES))
+    )(codes, words, own_signs, own_sums)
 
 
 def position(axis, staged):
     return lax.axis_index(axis) if staged else 0
 
 
-def band_products(parts, row_shape, block, surface_rows, gram_ref, window_ref, out_ref):
+def band_products(parts, row_shape, block, surface_rows, gram_ref, out_ref):
     mirrors, shard_rows, slots, samples = row_shape
-    tail = samples - LANES
-    bases = []
+    groups = mirrors * shard_rows // 2
+    own = gram_ref.shape[1]
+    narrow = slots - LANES
     for q in range(mirrors * shard_rows):
         k, l = divmod(q, shard_rows)
         band = jnp.clip((block * shard_rows + l) * NAR // surface_rows - 1, 0, NAR - BAND)
-        column = (k * NAR + band) * NA
-        bases.append(pl.multiple_of(column // LANES * LANES, LANES))
-        shift = pl.multiple_of(column - bases[-1], 16)
-        unit, side = divmod(q, 2)
-        units = mirrors * shard_rows // 2 // len(parts)
-        part, at = parts[unit // units], unit % units * 3 * slots
-        for gap in range(0, WINDOW - slots, 16):
-            row = pl.multiple_of((shift + slots + gap) % WINDOW, 16)
-            window_ref[q, pl.ds(row, 16), :] = jnp.zeros((16, WINDOW), window_ref.dtype)
-        window_ref[q, pl.ds(shift, slots), :LANES] = part[pl.ds(at + side * slots, slots), :]
-        window_ref[q, pl.ds(shift, slots), LANES:] = part[pl.ds(at + 2 * slots, slots), :]
-    for q, base in enumerate(bases):
-        u = jnp.dot(gram_ref[:, pl.ds(base, WINDOW)], window_ref[q], preferred_element_type=jnp.float32)
-        out_ref[q, :LANES] = jnp.transpose(u[:, :LANES]).astype(jnp.bfloat16)
-        rest = jnp.transpose(u[:, LANES:])[q % 2 * tail:(q % 2 + 1) * tail]
-        out_ref[q, LANES:] = rest.astype(jnp.bfloat16)
+        column = pl.multiple_of((k * NAR + band) * NA, 16)
+        part, group = divmod(q, groups)
+        source, base = (parts[0], part * (groups + 1) * samples) if len(parts) == 1 else (parts[part], 0)
+        left = jnp.concatenate(
+            [source[pl.ds(base + group * samples, samples), :], source[pl.ds(base + groups * samples, samples), :]],
+            axis=1,
+        )
+        right = [gram_ref[pl.ds(column, LANES), :]]
+        if group:
+            right.append(jnp.zeros((group * narrow, own), jnp.bfloat16))
+        right.append(gram_ref[pl.ds(column + LANES, narrow), :])
+        right.append(jnp.zeros((LANES - (group + 1) * narrow, own), jnp.bfloat16))
+        out_ref[q] = jnp.dot(
+            left, jnp.concatenate(right, axis=0), preferred_element_type=jnp.float32
+        ).astype(jnp.bfloat16)
 
 
 def bands_kernel(row_shape, surface_rows, first, counts, staged, gram_ref, *refs):
     sources = refs[:len(counts)]
-    out_ref, window = refs[-2:]
+    out_ref = refs[-1]
     step = pl.program_id(0)
     start = 0
     for source, count in zip(sources, counts):
         @pl.when((step >= start) & (step < start + count))
         def _():
             block = (first + step) ^ position("row", staged)
-            band_products([source.at[0]], row_shape, block, surface_rows, gram_ref, window, out_ref.at[0])
+            band_products([source.at[0]], row_shape, block, surface_rows, gram_ref, out_ref.at[0])
         start += count
 
 
 def bands(gram_rows, sources, decoded, first, staged, row_shape, surface_rows):
-    own = gram_rows.shape[0]
+    own = gram_rows.shape[1]
     counts = [source.shape[0] for source in sources]
     starts = np.cumsum([0] + counts)
     total = surface_rows // row_shape[1]
@@ -248,7 +269,6 @@
         out_shape=jax.ShapeDtypeStruct((total, rows, row_shape[3], own), jnp.bfloat16),
         in_specs=in_specs,
         out_specs=pl.BlockSpec((1, rows, row_shape[3], own), lambda s: (first + s, 0, 0, 0)),
-        scratch_shapes=[pltpu.VMEM((rows, WINDOW, WINDOW), jnp.bfloat16)],
         input_output_aliases=aliases,
         compiler_params=pltpu.CompilerParams(vmem_limit_bytes=VMEM_BYTES),
         cost_estimate=pl.CostEstimate(
@@ -260,20 +280,21 @@
 
 def build_differences(columns, differences, mirrors, samples, pupil):
     half = pupil // 2
-    slope = lax.broadcasted_iota(jnp.int32, (pupil, pupil), 0)
-    lane = lax.broadcasted_iota(jnp.int32, (pupil, pupil), 1)
-    upper = lax.broadcasted_iota(jnp.int32, (pupil, samples), 0) >= half
-    at = lax.broadcasted_iota(jnp.int32, (pupil, samples), 1)
+    slope = lax.broadcasted_iota(jnp.int32, (half, pupil), 0)
+    lane = lax.broadcasted_iota(jnp.int32, (half, pupil), 1)
+    at = lax.broadcasted_iota(jnp.int32, (half, mirrors * samples), 1)
     for d, lines in enumerate(columns):
-        for k in range(mirrors):
-            line = jnp.broadcast_to(lines[k:k + 1], (pupil, pupil))
-            sides = [
-                jnp.sum(jnp.where(lane == slope % half * 2 + side, line, 0), axis=1, keepdims=True) for side in range(2)
-            ]
-            behind, ahead = ((at == side).astype(jnp.float32) for side in sides)
-            across, down = ahead - behind, ahead + behind
-            value = jnp.concatenate([jnp.where(upper, -down, across), jnp.where(upper, down, across)], axis=1)
-            differences[d, :, 2 * k * samples:2 * (k + 1) * samples] = value.astype(jnp.bfloat16)
+        sides = []
+        for side in range(2):
+            hit = None
+            for k in range(mirrors):
+                line = jnp.broadcast_to(lines[k:k + 1], (half, pupil))
+                column = jnp.sum(jnp.where(lane == slope * 2 + side, line, 0), axis=1, keepdims=True)
+                here = (at == column + k * samples).astype(jnp.float32)
+                hit = here if hit is None else hit + here
+            sides.append(hit)
+        differences[d, 0] = (sides[1] - sides[0]).astype(jnp.bfloat16)
+        differences[d, 1] = (sides[1] + sides[0]).astype(jnp.bfloat16)
 
 
 def decode_kernel(row_shape, surface_rows, own, late, staged, norm, counts, *refs):
@@ -281,9 +302,9 @@
     columns_refs, refs = refs[:counts[0]], refs[counts[0]:]
     lines_refs, refs = refs[:counts[1]], refs[counts[1]:]
     late_refs, refs = refs[:counts[2]], refs[counts[2]:]
-    gram_ref, decoded_ref, out_ref, decoded, differences, total, window, lines, scalars, semaphores = refs
+    gram_ref, decoded_ref, out_ref, decoded, differences, total, lines, scalars, semaphores = refs
     group = pl.program_id(0)
-    directions, pupil = differences.shape[:2]
+    directions, pupil = differences.shape[0], 2 * differences.shape[2]
     phases = out_ref.shape[2] // pupil
     place = position("row", staged)
     blocks = surface_rows // shard_rows
@@ -309,9 +330,7 @@
         columns = [ref[n, :, :pupil] for ref in columns_refs for n in range(ref.shape[0])]
         build_differences(columns, differences, mirrors, samples, pupil)
         for n, part in enumerate(parts):
-            band_products(
-                part, row_shape, (ready + n) ^ place, surface_rows, gram_ref, window, decoded.at[ready + n]
-            )
+            band_products(part, row_shape, (ready + n) ^ place, surface_rows, gram_ref, decoded.at[ready + n])
         to_scalars.wait()
         for copy in copies:
             copy.wait()
@@ -322,14 +341,20 @@
         for phase in range(phases):
             i = group * phases + phase
             block = (2 * i // shard_rows) ^ place
-            picked = []
+            sums, changes = [], []
             for k in range(mirrors):
+                picked = []
                 for y in range(2):
                     row = scalars[block, held * width + width - 1, k * shard_rows + (2 * phase + y) % shard_rows]
                     picked.append(decoded[row // shard_rows ^ place, k * shard_rows + row % shard_rows])
-            products.append(
-                jnp.dot(differences[held], jnp.concatenate(picked, axis=0), preferred_element_type=jnp.float32)
-            )
+                sums.append(picked[0] + picked[1])
+                changes.append(picked[1] - picked[0])
+            for kind, rows in enumerate((sums, changes)):
+                products.append(
+                    jnp.dot(
+                        differences[held, kind], jnp.concatenate(rows, axis=0), preferred_element_type=jnp.float32
+                    )
+                )
             valid = lines[block, pl.ds(held * width + phase % (shard_rows // 2), 1), :][:, :pupil // 2]
             factors += [valid.astype(jnp.float32) * norm] * 2
         product = jnp.concatenate(products, axis=0)
@@ -346,7 +371,7 @@
 def decode(columns, sources, late_parts, late, gram_rows, decoded, own, row_shape, surface_rows, pupil, norm, staged):
     blocks = decoded.shape[0]
     mirrors, shard_rows, slots, samples = row_shape
-    padded = gram_rows.shape[0]
+    padded = gram_rows.shape[1]
     directions = sum(line.shape[0] for line in columns)
     extra = -(-directions * (shard_rows // 2 + 1) // 16) * 16
     phases = LANES // math.gcd(pupil, LANES)
@@ -370,9 +395,8 @@
         out_specs=pl.BlockSpec((own, directions, lanes), lambda s: (0, 0, s)),
         scratch_shapes=[
             pltpu.VMEM(decoded.shape, jnp.bfloat16),
-            pltpu.VMEM((directions, pupil, 2 * mirrors * samples), jnp.bfloat16),
+            pltpu.VMEM((directions, 2, pupil // 2, mirrors * samples), jnp.bfloat16),
             pltpu.VMEM((lanes // LANES, own * directions, LANES), jnp.float32),
-            pltpu.VMEM((mirrors * shard_rows, WINDOW, WINDOW), jnp.bfloat16),
             pltpu.VMEM((blocks, extra, LANES), jnp.int32),
             pltpu.SMEM((blocks, extra, LANES), jnp.int32),
             pltpu.SemaphoreType.DMA((blocks + 1,)),
@@ -397,23 +421,26 @@
     own = actuator_codes.size // (directions * devices)
     staged = devices == 8 and directions & (directions - 1) == 0
     turned = jnp.swapaxes(influence, 2, 3)
+    codes, pokes = actuator_codes.reshape(-1, LANES), poke_rows.reshape(-1, LANES)
     lines = small_lines(foot_rows, foot_columns, subaperture_valid)
     if not staged:
         lines = [lax.all_gather(lines, "dir")]
         every = lax.all_gather(pack(turned, lines), "row")
-        gram_rows = gram(actuator_codes, poke_rows, own)
+        gram_rows = gram(codes, *own_side(codes, pokes, own))
         decoded = bands(gram_rows, [every], None, 0, staged, row_shape, surface_rows)
         return decode(
             lines, [every], [], 0, gram_rows, decoded, own, row_shape, surface_rows, pupil, norm, staged
         )
 
     lines = [lines[None]] + [swap(lines, "dir", e)[None] for e in range(1, directions)]
+    sides = own_side(codes, pokes, own)
+    lines, sides = lax.optimization_barrier((lines, sides))
     packed = pack(turned, lines)
     beside, across, sibling = (swap(packed, "row", distance) for distance in (2, 4, 1))
-    gram_rows = gram(actuator_codes, poke_rows, own)
+    gram_rows = gram(codes, *sides)
     decoded = bands(gram_rows, [packed[None], sibling[None]], None, 0, staged, row_shape, surface_rows)
     decoded, beside, across = lax.optimization_barrier((decoded, beside, across))
-    half = mirrors * shard_rows * slots * samples // LANES // 2
+    half = (mirrors * shard_rows + 2) * samples // 2
     upper, lower = swap(beside[:half], "row", 4), swap(across[half:], "row", 2)
     beside_sibling, across_sibling = swap(beside, "row", 1), swap(across, "row", 1)
     sources = [source[None] for source in (beside, beside_sibling, across, across_sibling)]

time: 75.4 us -> 68.6 us (0.910)
  waiting for transfers between devices: 8.6 us -> 5.03 us
  Pallas kernels: 49.9 us -> 46.8 us
    pallas_call x1, Pallas kernels: 19.9 us -> 16.2 us  [decode(): pl.pallas_call(functools.partial(decode_kernel, row_shape, surface_rows,...]
    ppermute x12, waiting for transfers between devices: 8.6 us -> 5.03 us  [swap(): lax.ppermute(block, axis, [(i, i ^ distance) for i in range(lax.axis_size...]
    pallas_call x1 -> x2, Pallas kernels: 2.25 us -> 5.3 us  [the longest x1 2.67 us: own_side(): pl.pallas_call(signs_kernel, out_shape=[jax.ShapeDtypeStruct((BITS, LANES...]
    pallas_call x2, Pallas kernels: 13.9 us -> 10.9 us  [bands(): pl.pallas_call(body, grid=(sum(counts),), out_shape=jax.ShapeDtypeStruct(...]
  transfers between devices with their start and end apart: 12 -> 12, of which waited for: 5 -> 5; matrix products, arithmetic and copies ran while one was open for 2% -> 2% of each run, Pallas kernels for 35% -> 39%
where the time goes in v5:
time: 68.6 us; the launch traced here: 68.3 us
  Pallas kernels  46.8 us (68%)
  starting transfers between devices  10.9 us (16%)
  local copies, waits for them, and re-layouts  5.4 us (8%)
  waiting for transfers between devices  5.03 us (7%)
    pallas_call x1, Pallas kernels, decode(): pl.pallas_call(functools.partial(decode_kernel, row_shape, surface_rows,...  16.2 us
    pallas_call x1, Pallas kernels, gram(): pl.pallas_call(gram_kernel, grid=(steps,), out_shape=jax.ShapeDtypeStruct...  13.2 us
    ppermute x12, starting transfers between devices, swap(): lax.ppermute(block, axis, [(i, i ^ distance) for i in range(lax.axis_size...  10.9 us
    pallas_call x2, Pallas kernels, bands(): pl.pallas_call(body, grid=(sum(counts),), out_shape=jax.ShapeDtypeStruct(...  10.9 us
    ppermute x12, waiting for transfers between devices, swap(): lax.ppermute(block, axis, [(i, i ^ distance) for i in range(lax.axis_size...  5.03 us
    unnamed x24, local copies, waits for them, and re-layouts  3.77 us
    pallas_call x1, Pallas kernels, own_side(): pl.pallas_call(signs_kernel, out_shape=[jax.ShapeDtypeStruct((BITS, LANES...  2.67 us
    pallas_call x1, Pallas kernels, pack(): pl.pallas_call(pack_kernel, out_shape=jax.ShapeDtypeStruct(((mirrors * ro...  2.63 us
  transfers between devices with their start and end apart: 12, of which 5 were waited for; matrix products, arithmetic and copies ran while one was open for 2% of the time, Pallas kernels for 39%

profile of v5, /device:TPU:0, one launch (start us, length us, event | category | flops | bytes accessed | tf_op | source)
XLA Modules:
  0.0 68.3 jit_solution(2799754494306786400)
XLA Ops:
  0.0 1.4 %small_lines.1 = s32[8,256]{1,0:T(8,128)} custom-call(s32[3,1,4]{2,1,0:T(1,128)} %bitcast.37, s32[3,1,160]{2,1,0:T(1,128)} %bitcast.36, s32[1,2,80]{2,1,0:T(2,128)} %valid_ref.1), custom_call_target="tpu_custom_call" | custom-call | tf_op jit(solution)/shard_map/small_lines/pallas_call | solution.py:37
  1.4 3.0 %collective-permute-start = (s32[8,256]{1,0:T(8,128)}, s32[8,256]{1,0:T(8,128)S(1)}, u32[]{:S(2)}, u32[]{:S(2)}) collective-permute-start(s32[8,256]{1,0:T(8,128)} %small_lines.1), channel_id=1, source_target_pairs={{0,8},{8,0},{16,24},{24,16},{1,9},{9,1},{17,25},{25,17},{2,10},{10... | collective-permute-start | bytes 24584 | tf_op jit(solution)/shard_map/ppermute | solution.py:411
  4.4 2.6 %collective-permute-start.1 = (s32[8,256]{1,0:T(8,128)}, s32[8,256]{1,0:T(8,128)S(1)}, u32[]{:S(2)}, u32[]{:S(2)}) collective-permute-start(s32[8,256]{1,0:T(8,128)} %small_lines.1), channel_id=1, source_target_pairs={{0,16},{8,24},{16,0},{24,8},{1,17},{9,25},{17,1},{25,9},{2,18},{10... | collective-permute-start | bytes 24584 | tf_op jit(solution)/shard_map/ppermute | solution.py:411
  7.0 0.0 collective-permute-start.2
  7.0 1.6 %reshape.6.codes_ref = s32[54,128]{1,0:T(8,128)} reshape(s32[3,48,48]{2,1,0:T(8,128)} %param.9) | data formatting | bytes 55296 | tf_op jit(solution)/shard_map/reshape | solution.py:424
  8.6 2.7 %own_signs.1 = (s32[13,64,128]{2,1,0:T(8,128)}, bf16[224,2048]{1,0:T(8,128)(2,1)}, f32[224,128]{1,0:T(8,128)}) custom-call(s32[54,128]{1,0:T(8,128)} %reshape.6.codes_ref, s32[16,128]{1,0:T(8,128)} %bitcast.35), custom_call_target="tpu_custom_call" | custom-call | tf_op jit(solution)/shard_map/own_signs/pallas_call | solution.py:134
  11.2 0.0 collective-permute-done
  11.2 0.0 copy-start.9
  11.2 0.0 collective-permute-done.1
  11.2 0.0 copy-start.10
  11.3 1.4 %collective-permute-done.2 = s32[8,256]{1,0:T(8,128)S(1)} collective-permute-done((s32[8,256]{1,0:T(8,128)}, s32[8,256]{1,0:T(8,128)S(1)}, u32[]{:S(2)}, u32[]{:S(2)}) %collective-permute-start.2) | collective-permute-done | bytes 8224 | tf_op jit(solution)/shard_map/ppermute | solution.py:411
  12.6 0.0 copy-start.11
  12.6 0.0 copy-done.9
  12.7 0.0 copy-done.10
  12.7 0.6 copy-done.11
  13.2 2.6 %pack_influence.1 = bf16[2704,128]{1,0:T(8,128)(2,1)} custom-call(bf16[3,4,144,192]{3,2,1,0:T(8,128)(2,1)} %bitcast.26, s32[1,8,256]{2,1,0:T(8,128)} %bitcast.27, s32[1,8,256]{2,1,0:T(8,128)} %bitcast.29, s32[1,8,256]{2,1,0:T(8,128)} %bitcast.31, s32[1,8,256]{2,1,0:T(8,128)} %bitcast.33), custom_call_target="tpu_custom_call" | custom-call | bytes 995328 | tf_op jit(solution)/shard_map/pack_influence/pallas_call | solution.py:78
  15.9 0.0 collective-permute-start.3
  15.9 1.5 %collective-permute-start.4 = (bf16[2704,128]{1,0:T(8,128)(2,1)}, bf16[2704,128]{1,0:T(8,128)(2,1)S(1)}, u32[]{:S(2)}, u32[]{:S(2)}) collective-permute-start(bf16[2704,128]{1,0:T(8,128)(2,1)} %pack_influence.1), channel_id=1, source_target_pairs={{0,2},{1,3},{2,0},{3,1},{4,6},{5,7},{6,4},{7,5},{8,10},{9,11},{10,... | collective-permute-start | bytes 2076680 | tf_op jit(solution)/shard_map/ppermute | solution.py:411
  17.4 1.5 %collective-permute-start.5 = (bf16[2704,128]{1,0:T(8,128)(2,1)}, bf16[2704,128]{1,0:T(8,128)(2,1)S(1)}, u32[]{:S(2)}, u32[]{:S(2)}) collective-permute-start(bf16[2704,128]{1,0:T(8,128)(2,1)} %pack_influence.1), channel_id=1, source_target_pairs={{0,4},{1,5},{2,6},{3,7},{4,0},{5,1},{6,2},{7,3},{8,12},{9,13},{10,... | collective-permute-start | bytes 2076680 | tf_op jit(solution)/shard_map/ppermute | solution.py:411
  18.9 13.2 %gram_rows.1.gram_ref.refs_14_ = bf16[6912,224]{1,0:T(8,128)(2,1)} custom-call(s32[54,128]{1,0:T(8,128)} %reshape.6.codes_ref, s32[13,64,128]{2,1,0:T(8,128)} %get-tuple-element.28.words, bf16[224,2048]{1,0:T(8,128)(2,1)} %get-tuple-element.29.own_signs, f32[224,128]{1,0:T(8,128)} %get-tuple-element.30.own_sums), custom_call_target="tpu_custom_call" | custom-call | flops 6341787648 | bytes 3096576 | tf_op jit(solution)/shard_map/gram_rows/pallas_call | solution.py:188
  32.0 0.0 collective-permute-done.3
  32.0 0.9 %copy-done.2 = bf16[2704,128]{1,0:T(8,128)(2,1)} copy-done((bf16[2704,128]{1,0:T(8,128)(2,1)}, bf16[2704,128]{1,0:T(8,128)(2,1)S(1)}, u32[]{:S(2)}) %copy-start.2) | copy-done | bytes 692248
  32.9 4.4 %bands.2.refs_4_ = bf16[8,12,192,224]{3,2,1,0:T(8,128)(2,1)} custom-call(bf16[6912,224]{1,0:T(8,128)(2,1)} %gram_rows.1.gram_ref.refs_14_, bf16[1,2704,128]{2,1,0:T(8,128)(2,1)} %bitcast.14, bf16[1,2704,128]{2,1,0:T(8,128)(2,1)} %bitcast.20), custom_call_target="tpu_custom_call" | custom-call | flops 704643072 | bytes 2752512 | tf_op jit(solution)/shard_map/bands/pallas_call | solution.py:266
  37.3 0.0 collective-permute-done.4
  37.4 0.0 collective-permute-done.5
  37.4 0.0 copy-start
  37.4 0.1 collective-permute-start.6
  37.5 0.5 collective-permute-start.7
  38.0 0.6 collective-permute-start.9
  38.6 0.6 collective-permute-start.8
  39.2 0.4 collective-permute-done.6
  39.6 1.0 %collective-permute-done.7 = bf16[2704,128]{1,0:T(8,128)(2,1)S(1)} collective-permute-done((bf16[2704,128]{1,0:T(8,128)(2,1)S(1)}, bf16[2704,128]{1,0:T(8,128)(2,1)S(1)}, u32[]{:S(2)}, u32[]{:S(2)}) %collective-permute-start.7) | collective-permute-done | bytes 692256 | tf_op jit(solution)/shard_map/ppermute | solution.py:411
  40.6 0.0 copy-done.1
  40.6 0.0 copy-done
  40.6 0.0 copy-done.3
  40.6 0.8 %copy-done.4 = bf16[2704,128]{1,0:T(8,128)(2,1)} copy-done((bf16[2704,128]{1,0:T(8,128)(2,1)}, bf16[2704,128]{1,0:T(8,128)(2,1)S(1)}, u32[]{:S(2)}) %copy-start.4) | copy-done | bytes 692248
  41.4 6.4 %bands.3.refs_15_ = bf16[8,12,192,224]{3,2,1,0:T(8,128)(2,1)} custom-call(bf16[6912,224]{1,0:T(8,128)(2,1)} %gram_rows.1.gram_ref.refs_14_, bf16[1,2704,128]{2,1,0:T(8,128)(2,1)} %bitcast.18, bf16[1,2704,128]{2,1,0:T(8,128)(2,1)} %bitcast.22, bf16[1,2704,128]{2,1,0:T(8,128)(2,1)} %bitcast.16, ...), custom_call_target="tpu_custom_call", output_to_operand_aliasing={{}: (5, {})} | custom-call | flops 1409286144 | bytes 5505024 | tf_op jit(solution)/shard_map/bands/pallas_call | solution.py:266
  47.9 0.6 collective-permute-done.8.refs_10_
  48.5 0.0 collective-permute-done.9.refs_11_
  48.5 0.1 collective-permute-start.11
  48.5 0.5 collective-permute-start.10
  49.0 1.6 %collective-permute-done.10.refs_12_ = bf16[1344,128]{1,0:T(8,128)(2,1)S(1)} collective-permute-done((bf16[1344,128]{1,0:T(8,128)(2,1)S(1)}, bf16[1344,128]{1,0:T(8,128)(2,1)S(1)}, u32[]{:S(2)}, u32[]{:S(2)}) %collective-permute-start.10) | collective-permute-done | bytes 344096 | tf_op jit(solution)/shard_map/ppermute | solution.py:411
  50.7 0.0 collective-permute-done.11.refs_13_
  50.7 0.0 copy-done.7
  50.7 0.0 copy-done.5
  50.7 0.7 %copy-done.8 = bf16[1344,128]{1,0:T(8,128)(2,1)} copy-done((bf16[1344,128]{1,0:T(8,128)(2,1)}, bf16[1344,128]{1,0:T(8,128)(2,1)S(1)}, u32[]{:S(2)}) %copy-start.8) | copy-done | bytes 344088
  51.4 0.7 %copy-done.6 = bf16[1360,128]{1,0:T(8,128)(2,1)} copy-done((bf16[1360,128]{1,0:T(8,128)(2,1)}, bf16[1360,128]{1,0:T(8,128)(2,1)S(1)}, u32[]{:S(2)}) %copy-start.6) | copy-done | bytes 348184
  52.2 16.2 %decode.1 = bf16[216,4,2560]{2,1,0:T(4,128)(2,1)} custom-call(s32[1,8,256]{2,1,0:T(8,128)} %bitcast.28, s32[1,8,256]{2,1,0:T(8,128)} %bitcast.30, s32[1,8,256]{2,1,0:T(8,128)} %bitcast.32, s32[1,8,256]{2,1,0:T(8,128)} %bitcast.34, bf16[1,2704,128]{2,1,0:T(8,128)(2,1)} %bitcast.15, bf16[1,2704,128]{2,1,0:T(8,128)(2,1)} %bitcast.21, ...), custom_call_target="tpu_custom_call" | custom-call | flops 5284823040 | bytes 4423680 | tf_op jit(solution)/shard_map/decode/pallas_call | solution.py:390
  (10 shorter events, 0.1 us)
Async XLA Ops:
  1.4 9.9 %collective-permute-start = (s32[8,256]{1,0:T(8,128)}, s32[8,256]{1,0:T(8,128)S(1)}, u32[]{:S(2)}, u32[]{:S(2)}) collective-permute-start(s32[8,256]{1,0:T(8,128)} %small_lines.1), channel_id=1, source_target_pairs={{0,8},{8,0},{16,24},{24,16},{1,9},{9,1},{17,25},{25,17},{2,10},{10... | collective-permute-start | bytes 24584 | tf_op jit(solution)/shard_map/ppermute | solution.py:411
  4.4 6.8 %collective-permute-start.1 = (s32[8,256]{1,0:T(8,128)}, s32[8,256]{1,0:T(8,128)S(1)}, u32[]{:S(2)}, u32[]{:S(2)}) collective-permute-start(s32[8,256]{1,0:T(8,128)} %small_lines.1), channel_id=1, source_target_pairs={{0,16},{8,24},{16,0},{24,8},{1,17},{9,25},{17,1},{25,9},{2,18},{10... | collective-permute-start | bytes 24584 | tf_op jit(solution)/shard_map/ppermute | solution.py:411
  7.0 5.7 %collective-permute-start.2 = (s32[8,256]{1,0:T(8,128)}, s32[8,256]{1,0:T(8,128)S(1)}, u32[]{:S(2)}, u32[]{:S(2)}) collective-permute-start(s32[8,256]{1,0:T(8,128)} %small_lines.1), channel_id=1, source_target_pairs={{0,24},{8,16},{16,8},{24,0},{1,25},{9,17},{17,9},{25,1},{2,26},{10... | collective-permute-start | bytes 24584 | tf_op jit(solution)/shard_map/ppermute | solution.py:411
  11.2 1.4 %copy-start.9 = (s32[8,256]{1,0:T(8,128)}, s32[8,256]{1,0:T(8,128)S(1)}, u32[]{:S(2)}) copy-start(s32[8,256]{1,0:T(8,128)S(1)} %collective-permute-done) | copy-start | bytes 24580
  11.2 1.4 %copy-start.10 = (s32[8,256]{1,0:T(8,128)}, s32[8,256]{1,0:T(8,128)S(1)}, u32[]{:S(2)}) copy-start(s32[8,256]{1,0:T(8,128)S(1)} %collective-permute-done.1) | copy-start | bytes 24580
  12.6 0.6 copy-start.11
  15.9 16.2 %collective-permute-start.3 = (bf16[2704,128]{1,0:T(8,128)(2,1)}, bf16[2704,128]{1,0:T(8,128)(2,1)S(1)}, u32[]{:S(2)}, u32[]{:S(2)}) collective-permute-start(bf16[2704,128]{1,0:T(8,128)(2,1)} %pack_influence.1), channel_id=1, source_target_pairs={{0,1},{1,0},{2,3},{3,2},{4,5},{5,4},{6,7},{7,6},{8,9},{9,8},{10,11... | collective-permute-start | bytes 2076680 | tf_op jit(solution)/shard_map/ppermute | solution.py:411
  15.9 21.5 %collective-permute-start.4 = (bf16[2704,128]{1,0:T(8,128)(2,1)}, bf16[2704,128]{1,0:T(8,128)(2,1)S(1)}, u32[]{:S(2)}, u32[]{:S(2)}) collective-permute-start(bf16[2704,128]{1,0:T(8,128)(2,1)} %pack_influence.1), channel_id=1, source_target_pairs={{0,2},{1,3},{2,0},{3,1},{4,6},{5,7},{6,4},{7,5},{8,10},{9,11},{10,... | collective-permute-start | bytes 2076680 | tf_op jit(solution)/shard_map/ppermute | solution.py:411
  17.4 20.0 %collective-permute-start.5 = (bf16[2704,128]{1,0:T(8,128)(2,1)}, bf16[2704,128]{1,0:T(8,128)(2,1)S(1)}, u32[]{:S(2)}, u32[]{:S(2)}) collective-permute-start(bf16[2704,128]{1,0:T(8,128)(2,1)} %pack_influence.1), channel_id=1, source_target_pairs={{0,4},{1,5},{2,6},{3,7},{4,0},{5,1},{6,2},{7,3},{8,12},{9,13},{10,... | collective-permute-start | bytes 2076680 | tf_op jit(solution)/shard_map/ppermute | solution.py:411
  32.0 0.9 %copy-start.2 = (bf16[2704,128]{1,0:T(8,128)(2,1)}, bf16[2704,128]{1,0:T(8,128)(2,1)S(1)}, u32[]{:S(2)}) copy-start(bf16[2704,128]{1,0:T(8,128)(2,1)S(1)} %collective-permute-done.3) | copy-start | bytes 2076676
  37.3 3.2 %copy-start.1 = (bf16[2704,128]{1,0:T(8,128)(2,1)}, bf16[2704,128]{1,0:T(8,128)(2,1)S(1)}, u32[]{:S(2)}) copy-start(bf16[2704,128]{1,0:T(8,128)(2,1)S(1)} %collective-permute-done.4) | copy-start | bytes 2076676
  37.4 3.2 %copy-start = (bf16[2704,128]{1,0:T(8,128)(2,1)}, bf16[2704,128]{1,0:T(8,128)(2,1)S(1)}, u32[]{:S(2)}) copy-start(bf16[2704,128]{1,0:T(8,128)(2,1)S(1)} %collective-permute-done.5) | copy-start | bytes 2076676
  37.4 2.2 %collective-permute-start.6 = (bf16[2704,128]{1,0:T(8,128)(2,1)S(1)}, bf16[2704,128]{1,0:T(8,128)(2,1)S(1)}, u32[]{:S(2)}, u32[]{:S(2)}) collective-permute-start(bf16[2704,128]{1,0:T(8,128)(2,1)S(1)} %collective-permute-done.4), channel_id=1, source_target_pairs={{0,1},{1,0},{2,3},{3,2},{4,5},{5,4},{6,7},{7,6},{8,9},{9,8},{10,11... | collective-permute-start | bytes 2076680 | tf_op jit(solution)/shard_map/ppermute | solution.py:411
  37.5 3.1 %collective-permute-start.7 = (bf16[2704,128]{1,0:T(8,128)(2,1)S(1)}, bf16[2704,128]{1,0:T(8,128)(2,1)S(1)}, u32[]{:S(2)}, u32[]{:S(2)}) collective-permute-start(bf16[2704,128]{1,0:T(8,128)(2,1)S(1)} %collective-permute-done.5), channel_id=1, source_target_pairs={{0,1},{1,0},{2,3},{3,2},{4,5},{5,4},{6,7},{7,6},{8,9},{9,8},{10,11... | collective-permute-start | bytes 2076680 | tf_op jit(solution)/shard_map/ppermute | solution.py:411
  38.0 10.5 %collective-permute-start.9 = (bf16[1360,128]{1,0:T(8,128)(2,1)S(1)}, bf16[1360,128]{1,0:T(8,128)(2,1)S(1)}, u32[]{:S(2)}, u32[]{:S(2)}) collective-permute-start(bf16[1360,128]{1,0:T(8,128)(2,1)S(1)} %slice.7), channel_id=1, source_target_pairs={{0,2},{1,3},{2,0},{3,1},{4,6},{5,7},{6,4},{7,5},{8,10},{9,11},{10,... | collective-permute-start | bytes 1044488 | tf_op jit(solution)/shard_map/ppermute | solution.py:411
  38.6 9.8 %collective-permute-start.8 = (bf16[1344,128]{1,0:T(8,128)(2,1)S(1)}, bf16[1344,128]{1,0:T(8,128)(2,1)S(1)}, u32[]{:S(2)}, u32[]{:S(2)}) collective-permute-start(bf16[1344,128]{1,0:T(8,128)(2,1)S(1)} %slice.6), channel_id=1, source_target_pairs={{0,4},{1,5},{2,6},{3,7},{4,0},{5,1},{6,2},{7,3},{8,12},{9,13},{10,... | collective-permute-start | bytes 1032200 | tf_op jit(solution)/shard_map/ppermute | solution.py:411
  39.6 1.0 %copy-start.3 = (bf16[2704,128]{1,0:T(8,128)(2,1)}, bf16[2704,128]{1,0:T(8,128)(2,1)S(1)}, u32[]{:S(2)}) copy-start(bf16[2704,128]{1,0:T(8,128)(2,1)S(1)} %collective-permute-done.6) | copy-start | bytes 2076676
  40.6 0.9 %copy-start.4 = (bf16[2704,128]{1,0:T(8,128)(2,1)}, bf16[2704,128]{1,0:T(8,128)(2,1)S(1)}, u32[]{:S(2)}) copy-start(bf16[2704,128]{1,0:T(8,128)(2,1)S(1)} %collective-permute-done.7) | copy-start | bytes 2076676
  48.5 2.2 %copy-start.7 = (bf16[1344,128]{1,0:T(8,128)(2,1)}, bf16[1344,128]{1,0:T(8,128)(2,1)S(1)}, u32[]{:S(2)}) copy-start(bf16[1344,128]{1,0:T(8,128)(2,1)S(1)} %collective-permute-done.8.refs_10_) | copy-start | bytes 1032196
  48.5 2.2 %copy-start.5 = (bf16[1360,128]{1,0:T(8,128)(2,1)}, bf16[1360,128]{1,0:T(8,128)(2,1)S(1)}, u32[]{:S(2)}) copy-start(bf16[1360,128]{1,0:T(8,128)(2,1)S(1)} %collective-permute-done.9.refs_11_) | copy-start | bytes 1044484
  48.5 2.2 %collective-permute-start.11 = (bf16[1360,128]{1,0:T(8,128)(2,1)S(1)}, bf16[1360,128]{1,0:T(8,128)(2,1)S(1)}, u32[]{:S(2)}, u32[]{:S(2)}) collective-permute-start(bf16[1360,128]{1,0:T(8,128)(2,1)S(1)} %collective-permute-done.9.refs_11_), channel_id=1, source_target_pairs={{0,1},{1,0},{2,3},{3,2},{4,5},{5,4},{6,7},{7,6},{8,9},{9,8},{10,11... | collective-permute-start | bytes 1044488 | tf_op jit(solution)/shard_map/ppermute | solution.py:411
  48.5 2.1 %collective-permute-start.10 = (bf16[1344,128]{1,0:T(8,128)(2,1)S(1)}, bf16[1344,128]{1,0:T(8,128)(2,1)S(1)}, u32[]{:S(2)}, u32[]{:S(2)}) collective-permute-start(bf16[1344,128]{1,0:T(8,128)(2,1)S(1)} %collective-permute-done.8.refs_10_), channel_id=1, source_target_pairs={{0,1},{1,0},{2,3},{3,2},{4,5},{5,4},{6,7},{7,6},{8,9},{9,8},{10,11... | collective-permute-start | bytes 1032200 | tf_op jit(solution)/shard_map/ppermute | solution.py:411
  50.7 0.7 %copy-start.8 = (bf16[1344,128]{1,0:T(8,128)(2,1)}, bf16[1344,128]{1,0:T(8,128)(2,1)S(1)}, u32[]{:S(2)}) copy-start(bf16[1344,128]{1,0:T(8,128)(2,1)S(1)} %collective-permute-done.10.refs_12_) | copy-start | bytes 1032196
  51.4 0.7 %copy-start.6 = (bf16[1360,128]{1,0:T(8,128)(2,1)}, bf16[1360,128]{1,0:T(8,128)(2,1)S(1)}, u32[]{:S(2)}) copy-start(bf16[1360,128]{1,0:T(8,128)(2,1)S(1)} %collective-permute-done.11.refs_13_) | copy-start | bytes 1044484

commit v6 on v5

v6 whole, which is shorter than its diff:
```python
import functools
import math

import jax
import jax.numpy as jnp
import numpy as np
from jax import lax
from jax.experimental import pallas as pl
from jax.experimental.pallas import tpu as pltpu
from jax.sharding import PartitionSpec as P

NAR = 48
NA = 48
BAND = 3
BITS = 13
SCALE = 7
NARROW = jnp.float8_e5m2
LANES = 128
WINDOW = 256
VMEM_BYTES = 56 * 1024 * 1024


def parity(codes, rows):
    return lax.population_count(codes & rows) & 1


def lines_kernel(rows_ref, columns_ref, valid_ref, lines_ref):
    mirrors, rows = rows_ref.shape[0], rows_ref.shape[2]
    lines_ref[...] = jnp.zeros(lines_ref.shape, lines_ref.dtype)
    lines_ref[mirrors:mirrors + valid_ref.shape[1], :valid_ref.shape[2]] = valid_ref[0]
    for k in range(mirrors):
        lines_ref[k:k + 1, :columns_ref.shape[2]] = columns_ref[k]
        lines_ref[mirrors + valid_ref.shape[1]:mirrors + valid_ref.shape[1] + 1, k * rows:(k + 1) * rows] = rows_ref[k]


def small_lines(foot_rows, foot_columns, valid):
    vmem = pl.BlockSpec(memory_space=pltpu.VMEM)
    count = foot_rows.shape[1] + valid.shape[1] + 1
    return pl.pallas_call(
        lines_kernel,
        out_shape=jax.ShapeDtypeStruct((-(-count // 8) * 8, WINDOW), jnp.int32),
        in_specs=[vmem] * 3,
        out_specs=vmem,
        name="small_lines",
    )(jnp.swapaxes(foot_rows, 0, 1), jnp.swapaxes(foot_columns, 0, 1), valid)


def pack_kernel(block_ref, *refs):
    lines_refs, packed_ref = refs[:-1], refs[-1]
    mirrors, rows, slots, samples = block_ref.shape
    groups = mirrors * rows // 2
    identity = (
        lax.broadcasted_iota(jnp.int32, (samples, samples), 0) == lax.broadcasted_iota(jnp.int32, (samples, samples), 1)
    ).astype(jnp.float32).astype(jnp.bfloat16)
    for part in range(2):
        base = part * (groups + 1) * samples
        tails = []
        for group in range(groups):
            k, l = divmod(part * groups + group, rows)
            turned = lax.dot_general(
                identity, block_ref[k, l], (((1,), (1,)), ((), ())), preferred_element_type=jnp.float32
            ).astype(jnp.bfloat16)
            packed_ref[pl.ds(base + group * samples, samples), :] = turned[:, :LANES]
            tails.append(turned[:, LANES:])
        tails.append(jnp.zeros((samples, LANES - groups * (slots - LANES)), jnp.bfloat16))
        packed_ref[pl.ds(base + groups * samples, samples), :] = jnp.concatenate(tails, axis=1)
    count = rows // 2 + 1
    lines = [ref[n, mirrors:mirrors + count, :LANES] for ref in lines_refs for n in range(ref.shape[0])]
    extra = packed_ref.shape[0] - 2 * (groups + 1) * samples
    lines.append(jnp.zeros((extra - count * len(lines), LANES), jnp.int32))
    packed_ref[pl.ds(packed_ref.shape[0] - extra, extra), :] = (
        jnp.concatenate(lines, axis=0).astype(jnp.float32).astype(jnp.bfloat16)
    )


def pack(block, lines):
    mirrors, rows, slots, samples = block.shape
    vmem = pl.BlockSpec(memory_space=pltpu.VMEM)
    extra = -(-sum(line.shape[0] for line in lines) * (rows // 2 + 1) // 16) * 16
    return pl.pallas_call(
        pack_kernel,
        out_shape=jax.ShapeDtypeStruct(((mirrors * rows + 2) * samples + extra, LANES), block.dtype),
        in_specs=[vmem] * (1 + len(lines)),
        out_specs=vmem,
        compiler_params=pltpu.CompilerParams(vmem_limit_bytes=VMEM_BYTES),
        cost_estimate=pl.CostEstimate(flops=0, bytes_accessed=3 * block.size, transcendentals=0),
        name="pack_influence",
    )(block, *lines)


def column_of(row):
    return jnp.transpose(jnp.broadcast_to(row, (LANES, LANES)), (1, 0))


def signs_kernel(table_ref, pokes_ref, codes_ref, words, own_signs, own_sums):
    planes = pokes_ref.shape[0]
    mirrors, rows, columns = table_ref.shape
    for line in range(codes_ref.shape[0]):
        pieces, at = [], line * LANES
        while at < (line + 1) * LANES:
            row, lane = divmod(at, columns)
            length = min(columns - lane, (line + 1) * LANES - at)
            pieces.append(table_ref[row // rows, row % rows:row % rows + 1, lane:lane + length])
            at += length
        codes_ref[line:line + 1, :] = jnp.concatenate(pieces, axis=1)
    half = LANES // 2
    own = own_signs.shape[0]
    plane = lax.broadcasted_iota(jnp.int32, pokes_ref.shape, 0)
    for bit in range(BITS):
        low = jnp.sum((pokes_ref[...] >> bit & 1) << plane, axis=0, keepdims=True)
        word = low | pltpu.roll(jnp.broadcast_to(low, (8, LANES)), half, 1)[:1] << planes
        words[bit] = column_of(word)[:half]
    count = codes_ref.shape[0] * LANES // (lax.axis_size("dir") * lax.axis_size("row"))
    first = (lax.axis_index("dir") * lax.axis_size("row") + lax.axis_index("row")) * count
    lane = lax.broadcasted_iota(jnp.int32, (8, LANES), 1)
    shift = first % LANES
    lines = [
        pltpu.roll(
            jnp.broadcast_to(
                codes_ref[pl.ds(jnp.minimum(first // LANES + n, codes_ref.shape[0] - 1), 1), :], (8, LANES)
            ),
            LANES - shift, 1,
        )
        for n in range(-(-own // LANES) + 1)
    ]
    own_column = jnp.concatenate(
        [column_of(jnp.where(lane < LANES - shift, lines[n], lines[n + 1])[:1]) for n in range(len(lines) - 1)],
        axis=0,
    )[:own]
    total = jnp.zeros((own, LANES), jnp.float32)
    for at in range(planes):
        signs = (1 - 2 * parity(own_column, pokes_ref[at:at + 1, :])).astype(jnp.float32)
        own_signs[:, at * LANES:(at + 1) * LANES] = (signs * 2.0 ** (SCALE - at)).astype(NARROW)
        total = total + signs
    own_sums[...] = jnp.broadcast_to(jnp.sum(total, axis=1, keepdims=True), own_sums.shape)


def own_side(table, pokes, own):
    own = -(-own // 32) * 32
    vmem = pl.BlockSpec(memory_space=pltpu.VMEM)
    return pl.pallas_call(
        signs_kernel,
        out_shape=[
            jax.ShapeDtypeStruct((table.size // LANES, LANES), jnp.int32),
            jax.ShapeDtypeStruct((BITS, LANES // 2, LANES), jnp.int32),
            jax.ShapeDtypeStruct((own, pokes.size), NARROW),
            jax.ShapeDtypeStruct((own, LANES), jnp.float32),
        ],
        in_specs=[vmem] * 2,
        out_specs=[vmem] * 4,
        compiler_params=pltpu.CompilerParams(vmem_limit_bytes=VMEM_BYTES),
        name="own_signs",
    )(table, pokes)


def gram_kernel(row_shape, surface_rows, codes_ref, words, own_signs, own_sums, packed_ref, gram_out, first_ref, gram_ref, semaphores):
    mirror = pl.program_id(0)
    half = LANES // 2
    own, pokes = own_signs.shape
    planes = pokes // LANES
    lines = codes_ref.shape[0] // row_shape[0]
    height = gram_ref.shape[0] // row_shape[0]

    def chunk(index, _):
        word = []
        for side in range(WINDOW // LANES):
            line = mirror * lines + index * (WINDOW // LANES) + side
            code = jnp.broadcast_to(codes_ref[pl.ds(line, 1), :], (8, LANES))
            value = None
            for bit in range(BITS):
                mask = jnp.concatenate([code << (31 - bit) >> 31] * (half // 8), axis=0)
                part = words[bit] & mask
                value = part if value is None else value ^ part
            word.append(value)
        word = jnp.concatenate(word, axis=1)
        words_of = (word, word >> planes)
        total = jnp.zeros((own, WINDOW), jnp.float32)
        for at in range(0, planes, 2):
            bits = [
                (side & (1 << plane)).astype(jnp.float32).astype(NARROW)
                for plane in (at, at + 1) for side in words_of
            ]
            total = total + jnp.dot(
                own_signs[:, at * LANES:(at + 2) * LANES], jnp.concatenate(bits, axis=0),
                preferred_element_type=jnp.float32,
            )
        sums = jnp.concatenate([own_sums[...]] * (WINDOW // LANES), axis=1)
        turned = jnp.transpose(sums - 2.0 ** (1 - SCALE) * total)
        at = pl.multiple_of(mirror * height + index * WINDOW, WINDOW)
        gram_ref[pl.ds(at, WINDOW), :] = turned.astype(jnp.bfloat16)
        return 0

    lax.fori_loop(0, height // WINDOW, chunk, 0, unroll=3)

    def send(k):
        part = pl.ds(pl.multiple_of(k * height, height), height)
        return pltpu.make_async_copy(gram_ref.at[part], gram_out.at[part], semaphores.at[k])

    send(mirror).start()
    block = lax.axis_index("row")
    for l in range(row_shape[1]):
        for k in range(row_shape[0]):
            @pl.when(mirror == k)
            def _():
                first_ref[0, l] = band_product(
                    [packed_ref], k * row_shape[1] + l, row_shape, block, surface_rows, gram_ref
                )

    @pl.when(mirror == pl.num_programs(0) - 1)
    def _():
        for k in range(row_shape[0]):
            send(k).wait()


def gram(codes, words, own_signs, own_sums, packed, row_shape, surface_rows):
    acts, (own, count) = codes.size, own_signs.shape
    mirrors, shard_rows, slots, samples = row_shape
    vmem = pl.BlockSpec(memory_space=pltpu.VMEM)
    return pl.pallas_call(
        functools.partial(gram_kernel, row_shape, surface_rows),
        grid=(mirrors,),
        out_shape=[
            jax.ShapeDtypeStruct((acts, own), jnp.bfloat16),
            jax.ShapeDtypeStruct((1, mirrors * shard_rows, samples, own), jnp.bfloat16),
        ],
        in_specs=[vmem] * 5,
        out_specs=[
            pl.BlockSpec(memory_space=pl.ANY),
            pl.BlockSpec((1, shard_rows, samples, own), lambda s: (0, s, 0, 0)),
        ],
        scratch_shapes=[pltpu.VMEM((acts, own), jnp.bfloat16), pltpu.SemaphoreType.DMA((mirrors,))],
        compiler_params=pltpu.CompilerParams(vmem_limit_bytes=VMEM_BYTES),
        cost_estimate=pl.CostEstimate(
            flops=2 * own * acts * count, bytes_accessed=2 * own * acts, transcendentals=0
        ),
        name="gram_rows",
    )(codes, words, own_signs, own_sums, packed)


def position(axis, staged):
    return lax.axis_index(axis) if staged else 0


def row_block(place, staged):
    if not staged:
        return place
    return (place ^ 7 if place in (3, 4) else place) ^ lax.axis_index("row")


def row_place(block, staged):
    if not staged:
        return block
    place = block ^ lax.axis_index("row")
    return jnp.where((place == 3) | (place == 4), place ^ 7, place)


def band_product(parts, q, row_shape, block, surface_rows, gram_ref):
    mirrors, shard_rows, slots, samples = row_shape
    groups = mirrors * shard_rows // 2
    own = gram_ref.shape[1]
    narrow = slots - LANES
    k, l = divmod(q, shard_rows)
    band = jnp.clip((block * shard_rows + l) * NAR // surface_rows - 1, 0, NAR - BAND)
    column = pl.multiple_of((k * NAR + band) * NA, 16)
    part, group = divmod(q, groups)
    source, base = (parts[0], part * (groups + 1) * samples) if len(parts) == 1 else (parts[part], 0)
    left = jnp.concatenate(
        [source[pl.ds(base + group * samples, samples), :], source[pl.ds(base + groups * samples, samples), :]],
        axis=1,
    )
    right = [gram_ref[pl.ds(column, LANES), :]]
    if group:
        right.append(jnp.zeros((group * narrow, own), jnp.bfloat16))
    right.append(gram_ref[pl.ds(column + LANES, narrow), :])
    right.append(jnp.zeros((LANES - (group + 1) * narrow, own), jnp.bfloat16))
    return jnp.dot(left, jnp.concatenate(right, axis=0), preferred_element_type=jnp.float32).astype(jnp.bfloat16)


def fetch_gram(gram_any, gram_ref, semaphores, mirrors):
    height = gram_ref.shape[0] // mirrors
    return [
        pltpu.make_async_copy(
            gram_any.at[pl.ds(k * height, height)], gram_ref.at[pl.ds(k * height, height)], semaphores.at[k]
        )
        for k in range(mirrors)
    ]


def bands_kernel(row_shape, surface_rows, first, counts, staged, gram_any, *refs):
    mirrors, shard_rows = row_shape[:2]
    sources = [ref.at[n] for ref, count in zip(refs, counts) for n in range(count)]
    out_ref, gram_ref, blocks, gram_semaphores, block_semaphores = refs[len(counts):]
    step = pl.program_id(0)
    gram_copies = fetch_gram(gram_any, gram_ref, gram_semaphores, mirrors)

    def fetch(n):
        return pltpu.make_async_copy(sources[n], blocks.at[n], block_semaphores.at[n])

    @pl.when(step == 0)
    def _():
        fetch(0).start()
        for copy in gram_copies:
            copy.start()
        for n in range(1, len(sources)):
            fetch(n).start()

    for n in range(len(sources)):
        @pl.when(step == n)
        def _():
            fetch(n).wait()
            block = row_block(first + n, staged)
            for q in range(mirrors * shard_rows):
                if n == 0 and q % shard_rows == 0:
                    gram_copies[q // shard_rows].wait()
                out_ref[0, q] = band_product([blocks.at[n]], q, row_shape, block, surface_rows, gram_ref)


def bands(gram_rows, sources, first, staged, row_shape, surface_rows):
    acts, own = gram_rows.shape
    counts = [source.shape[0] for source in sources]
    rows = row_shape[0] * row_shape[1]
    flops = 2 * own * WINDOW * row_shape[3] * rows * sum(counts)
    return pl.pallas_call(
        functools.partial(bands_kernel, row_shape, surface_rows, first, counts, staged),
        grid=(sum(counts),),
        out_shape=jax.ShapeDtypeStruct((sum(counts), rows, row_shape[3], own), jnp.bfloat16),
        in_specs=[pl.BlockSpec(memory_space=pl.ANY)] * (1 + len(sources)),
        out_specs=pl.BlockSpec((1, rows, row_shape[3], own), lambda s: (s, 0, 0, 0)),
        scratch_shapes=[
            pltpu.VMEM((acts, own), jnp.bfloat16),
            pltpu.VMEM((sum(counts),) + sources[0].shape[1:], jnp.bfloat16),
            pltpu.SemaphoreType.DMA((row_shape[0],)),
            pltpu.SemaphoreType.DMA((sum(counts),)),
        ],
        compiler_params=pltpu.CompilerParams(vmem_limit_bytes=VMEM_BYTES),
        cost_estimate=pl.CostEstimate(
            flops=flops, bytes_accessed=2 * own * WINDOW * rows * sum(counts), transcendentals=0
        ),
        name="bands",
    )(gram_rows, *sources)


def build_differences(columns, differences, mirrors, samples, pupil):
    half = pupil // 2
    slope = lax.broadcasted_iota(jnp.int32, (half, pupil), 0)
    lane = lax.broadcasted_iota(jnp.int32, (half, pupil), 1)
    at = lax.broadcasted_iota(jnp.int32, (half, mirrors * samples), 1)
    for d, lines in enumerate(columns):
        sides = []
        for side in range(2):
            hit = None
            for k in range(mirrors):
                line = jnp.broadcast_to(lines[k:k + 1], (half, pupil))
                column = jnp.sum(jnp.where(lane == slope * 2 + side, line, 0), axis=1, keepdims=True)
                here = (at == column + k * samples).astype(jnp.float32)
                hit = here if hit is None else hit + here
            sides.append(hit)
        differences[d, 0] = (sides[1] - sides[0]).astype(jnp.bfloat16)
        differences[d, 1] = (sides[1] + sides[0]).astype(jnp.bfloat16)


def decode_kernel(row_shape, surface_rows, own, staged, norm, counts, late_parts, *refs):
    mirrors, shard_rows, slots, samples = row_shape
    columns_refs, refs = refs[:counts[0]], refs[counts[0]:]
    lines_refs, refs = refs[:counts[1]], refs[counts[1]:]
    late_refs, refs = refs[:counts[2]], refs[counts[2]:]
    ready_refs, refs = refs[:counts[3]], refs[counts[3]:]
    (gram_any, out_ref, gram_ref, decoded, differences, total, packed_lines, lines, scalars, *refs) = refs
    late_blocks, refs = refs[:counts[2]], refs[counts[2]:]
    gram_semaphores, ready_semaphores, line_semaphores, late_semaphores, scalar_semaphore = refs
    group = pl.program_id(0)
    directions, pupil = differences.shape[0], 2 * differences.shape[2]
    phases = out_ref.shape[2] // pupil
    blocks = surface_rows // shard_rows
    late = len(late_parts)
    ready = blocks - late
    width = shard_rows // 2 + 1
    extra = lines.shape[1]

    @pl.when(group == 0)
    def _():
        def started(copies):
            for copy in copies:
                copy.start()
            return copies

        ends = [ref.at[n, pl.ds(ref.shape[1] - extra, extra)] for ref in lines_refs for n in range(ref.shape[0])]
        line_copies = started([
            pltpu.make_async_copy(end, packed_lines.at[n], line_semaphores.at[n]) for n, end in enumerate(ends)
        ])
        late_copies = started([
            pltpu.make_async_copy(late_refs[n], late_blocks[n], late_semaphores.at[n]) for n in range(counts[2])
        ])
        gram_copies = started(fetch_gram(gram_any, gram_ref, gram_semaphores, mirrors)) if late else []
        ready_copies = started([
            pltpu.make_async_copy(block, decoded.at[n], ready_semaphores.at[n])
            for n, block in enumerate([ref.at[m] for ref in ready_refs for m in range(ref.shape[0])])
        ])
        columns = [ref[n, :, :pupil] for ref in columns_refs for n in range(ref.shape[0])]
        build_differences(columns, differences, mirrors, samples, pupil)
        for copy in line_copies + late_copies:
            copy.wait()
        held = [packed_lines[n] for n in range(len(ends))]
        at = 0
        for part in late_parts:
            at += part
            last = late_blocks[at - 1]
            held.append(last[pl.ds(last.shape[0] - extra, extra), :])
        for n, value in enumerate(held):
            lines[n] = value.astype(jnp.float32).astype(jnp.int32)
        to_scalars = pltpu.make_async_copy(lines, scalars, scalar_semaphore.at[0])
        to_scalars.start()
        at = 0
        for n, part in enumerate(late_parts):
            parts, at = late_blocks[at:at + part], at + part
            for q in range(mirrors * shard_rows):
                if n == 0 and q % shard_rows == 0:
                    gram_copies[q // shard_rows].wait()
                decoded[ready + n, q] = band_product(
                    parts, q, row_shape, row_block(ready + n, staged), surface_rows, gram_ref
                )
        to_scalars.wait()
        for copy in ready_copies:
            copy.wait()

    for d in range(directions):
        held = d ^ position("dir", staged)
        products, factors = [], []
        for phase in range(phases):
            i = group * phases + phase
            block = row_place(2 * i // shard_rows, staged)
            sums, changes = [], []
            for k in range(mirrors):
                picked = []
                for y in range(2):
                    row = scalars[block, held * width + width - 1, k * shard_rows + (2 * phase + y) % shard_rows]
                    picked.append(decoded[row_place(row // shard_rows, staged), k * shard_rows + row % shard_rows])
                sums.append(picked[0] + picked[1])
                changes.append(picked[1] - picked[0])
            for kind, rows in enumerate((sums, changes)):
                products.append(
                    jnp.dot(
                        differences[held, kind], jnp.concatenate(rows, axis=0), preferred_element_type=jnp.float32
                    )
                )
            valid = lines[block, pl.ds(held * width + phase % (shard_rows // 2), 1), :][:, :pupil // 2]
            factors += [valid.astype(jnp.float32) * norm] * 2
        product = jnp.concatenate(products, axis=0)
        factor = jnp.concatenate(factors, axis=1)
        for tile in range(out_ref.shape[2] // LANES):
            at = tile * LANES
            value = jnp.transpose(product[at:at + LANES])[:own] * factor[:, at:at + LANES]
            total[tile, pl.ds(d, own, stride=directions), :] = value
    for tile in range(out_ref.shape[2] // LANES):
        value = total[tile].reshape(own, directions, LANES)
        out_ref[:, :, tile * LANES:(tile + 1) * LANES] = value.astype(out_ref.dtype)


def decode(columns, sources, late, ready, gram_rows, own, row_shape, surface_rows, pupil, norm, staged):
    mirrors, shard_rows, slots, samples = row_shape
    acts, padded = gram_rows.shape
    directions = sum(line.shape[0] for line in columns)
    blocks = surface_rows // shard_rows
    extra = -(-directions * (shard_rows // 2 + 1) // 16) * 16
    phases = LANES // math.gcd(pupil, LANES)
    width = surface_rows // 2 * pupil
    lanes = phases * pupil
    flops = 2 * padded * mirrors * samples * pupil * directions * surface_rows // 2
    vmem, anywhere = pl.BlockSpec(memory_space=pltpu.VMEM), pl.BlockSpec(memory_space=pl.ANY)
    parts = [part for block in late for part in block]
    counts = (len(columns), len(sources), len(parts), len(ready))
    semaphores = [mirrors, blocks, blocks, max(len(parts), 1), 1]
    return pl.pallas_call(
        functools.partial(
            decode_kernel, row_shape, surface_rows, own, staged, norm, counts, [len(block) for block in late]
        ),
        grid=(width // lanes,),
        out_shape=jax.ShapeDtypeStruct((own, directions, width), jnp.bfloat16),
        in_specs=[vmem] * counts[0] + [anywhere] * (sum(counts[1:]) + 1),
        out_specs=pl.BlockSpec((own, directions, lanes), lambda s: (0, 0, s)),
        scratch_shapes=[
            pltpu.VMEM((acts, padded), jnp.bfloat16),
            pltpu.VMEM((blocks, mirrors * shard_rows, samples, padded), jnp.bfloat16),
            pltpu.VMEM((directions, 2, pupil // 2, mirrors * samples), jnp.bfloat16),
            pltpu.VMEM((lanes // LANES, own * directions, LANES), jnp.float32),
            pltpu.VMEM((blocks, extra, LANES), jnp.bfloat16),
            pltpu.VMEM((blocks, extra, LANES), jnp.int32),
            pltpu.SMEM((blocks, extra, LANES), jnp.int32),
            *[pltpu.VMEM(part.shape, part.dtype) for part in parts],
            *[pltpu.SemaphoreType.DMA((count,)) for count in semaphores],
        ],
        compiler_params=pltpu.CompilerParams(vmem_limit_bytes=VMEM_BYTES),
        cost_estimate=pl.CostEstimate(flops=flops, bytes_accessed=2 * own * directions * width, transcendentals=0),
        name="decode",
    )(*columns, *sources, *parts, *ready, gram_rows)


def swap(block, axis, distance):
    return lax.ppermute(block, axis, [(i, i ^ distance) for i in range(lax.axis_size(axis))])


def shards(influence, foot_rows, foot_columns, actuator_codes, poke_rows, subaperture_valid):
    mirrors, shard_rows, samples, slots = influence.shape
    row_shape = (mirrors, shard_rows, slots, samples)
    directions, devices = lax.axis_size("dir"), lax.axis_size("row")
    surface_rows = shard_rows * devices
    pupil = foot_columns.shape[2]
    norm = 0.5 * poke_rows.shape[0] ** (-0.5)
    own = actuator_codes.size // (directions * devices)
    staged = devices == 8 and directions & (directions - 1) == 0
    turned = jnp.swapaxes(influence, 2, 3)
    pokes = poke_rows.reshape(-1, LANES)
    lines = small_lines(foot_rows, foot_columns, subaperture_valid)
    if not staged:
        lines = [lax.all_gather(lines, "dir")]
        packed = pack(turned, lines)
        every = lax.all_gather(packed, "row")
        gram_rows, _ = gram(*own_side(actuator_codes, pokes, own), packed, row_shape, surface_rows)
        ready = [bands(gram_rows, [every], 0, staged, row_shape, surface_rows)]
        return decode(lines, [every], [], ready, gram_rows, own, row_shape, surface_rows, pupil, norm, staged)

    lines = [lines[None]] + [swap(lines, "dir", e)[None] for e in range(1, directions)]
    sides = own_side(actuator_codes, pokes, own)
    lines, sides = lax.optimization_barrier((lines, sides))
    packed = pack(turned, lines)
    beside, across, sibling = (swap(packed, "row", distance) for distance in (2, 4, 1))
    gram_rows, first = gram(*sides, packed, row_shape, surface_rows)
    gram_rows, beside, across = lax.optimization_barrier((gram_rows, beside, across))
    half = (mirrors * shard_rows + 2) * samples // 2
    upper, lower = swap(beside[:half], "row", 4), swap(across[half:], "row", 2)
    beside_sibling, across_sibling = swap(beside, "row", 1), swap(across, "row", 1)
    sources = [source[None] for source in (sibling, beside, across)]
    ready = bands(gram_rows, sources, 1, staged, row_shape, surface_rows)
    ready, upper, lower = lax.optimization_barrier((ready, upper, lower))
    late = [[beside_sibling], [across_sibling], [upper, lower], [swap(upper, "row", 1), swap(lower, "row", 1)]]
    return decode(
        lines, [packed[None], *sources], late, [first, ready], gram_rows, own, row_shape, surface_rows, pupil, norm,
        staged,
    )


def solution(mesh):
    return jax.shard_map(
        shards,
        mesh=mesh,
        in_specs=(
            P(None, "row", None, None),
            P("dir", None, "row"),
            P("dir", None, None),
            P(),
            P(),
            P("dir", "row", None),
        ),
        out_specs=P(("dir", "row"), None, None),
        check_vma=False,
    )
```

time: 68.6 us -> 62.7 us (0.914)
  Pallas kernels: 46.8 us -> 42.9 us
  local copies, waits for them, and re-layouts: 5.4 us -> 2.34 us
  starting transfers between devices: 10.9 us -> 11.8 us
    pallas_call x4 -> x3, Pallas kernels: 26.7 us -> 22.2 us  [the longest x1 14.2 us: gram(): pl.pallas_call(functools.partial(gram_kernel, row_shape, surface_rows), g...]
    reshape x1 -> x0, local copies, waits for them, and re-layouts: 1.58 us -> none  [shards(): actuator_codes.reshape(-1, LANES)]
    unnamed x24, local copies, waits for them, and re-layouts: 3.77 us -> 2.3 us
    ppermute x12, starting transfers between devices: 10.9 us -> 11.8 us  [swap(): lax.ppermute(block, axis, [(i, i ^ distance) for i in range(lax.axis_size...]
  transfers between devices with their start and end apart: 12 -> 12, of which waited for: 5 -> 3; matrix products, arithmetic and copies ran while one was open for 2% -> 0% of each run, Pallas kernels for 39% -> 36%
where the time goes in v6:
time: 62.7 us; the launch traced here: 62.4 us
  Pallas kernels  42.9 us (68%)
  starting transfers between devices  11.8 us (19%)
  waiting for transfers between devices  5.17 us (8%)
  local copies, waits for them, and re-layouts  2.34 us (4%)
    pallas_call x1, Pallas kernels, decode(): pl.pallas_call(functools.partial(decode_kernel, row_shape, surface_rows,...  16.7 us
    pallas_call x1, Pallas kernels, gram(): pl.pallas_call(functools.partial(gram_kernel, row_shape, surface_rows), g...  14.2 us
    ppermute x12, starting transfers between devices, swap(): lax.ppermute(block, axis, [(i, i ^ distance) for i in range(lax.axis_size...  11.8 us
    pallas_call x1, Pallas kernels, bands(): pl.pallas_call(functools.partial(bands_kernel, row_shape, surface_rows, f...  5.25 us
    ppermute x12, waiting for transfers between devices, swap(): lax.ppermute(block, axis, [(i, i ^ distance) for i in range(lax.axis_size...  5.17 us
    pallas_call x1, Pallas kernels, own_side(): pl.pallas_call(signs_kernel, out_shape=[jax.ShapeDtypeStruct((table.size...  2.78 us
    pallas_call x1, Pallas kernels, pack(): pl.pallas_call(pack_kernel, out_shape=jax.ShapeDtypeStruct(((mirrors * ro...  2.67 us
    unnamed x24, local copies, waits for them, and re-layouts  2.3 us
  transfers between devices with their start and end apart: 12, of which 3 were waited for; matrix products, arithmetic and copies ran while one was open for 0% of the time, Pallas kernels for 36%

profile of v6, /device:TPU:0, one launch (start us, length us, event | category | flops | bytes accessed | tf_op | source)
XLA Modules:
  0.0 62.4 jit_solution(6218282018656510389)
XLA Ops:
  0.0 1.4 %small_lines.1 = s32[8,256]{1,0:T(8,128)} custom-call(s32[3,1,4]{2,1,0:T(1,128)} %bitcast.30, s32[3,1,160]{2,1,0:T(1,128)} %bitcast.29, s32[1,2,80]{2,1,0:T(2,128)} %valid_ref.1), custom_call_target="tpu_custom_call" | custom-call | tf_op jit(solution)/shard_map/small_lines/pallas_call | solution.py:39
  1.4 5.0 %collective-permute-start.2 = (s32[8,256]{1,0:T(8,128)}, s32[8,256]{1,0:T(8,128)S(1)}, u32[]{:S(2)}, u32[]{:S(2)}) collective-permute-start(s32[8,256]{1,0:T(8,128)} %small_lines.1), channel_id=1, source_target_pairs={{0,24},{8,16},{16,8},{24,0},{1,25},{9,17},{17,9},{25,1},{2,26},{10... | collective-permute-start | bytes 24584 | tf_op jit(solution)/shard_map/ppermute | solution.py:499
  6.4 0.0 collective-permute-start.1
  6.4 0.6 collective-permute-start
  7.0 2.8 %own_signs.1 = (s32[54,128]{1,0:T(8,128)}, s32[13,64,128]{2,1,0:T(8,128)}, f8e5m2[224,2048]{1,0:T(32,128)(4,1)}, f32[224,128]{1,0:T(8,128)}) custom-call(s32[3,48,48]{2,1,0:T(8,128)} %table_ref.1, s32[16,128]{1,0:T(8,128)} %bitcast.28), custom_call_target="tpu_custom_call" | custom-call | tf_op jit(solution)/shard_map/own_signs/pallas_call | solution.py:141
  9.8 0.0 collective-permute-done.2
  9.8 0.0 copy-start.9
  9.8 1.4 %collective-permute-done.1 = s32[8,256]{1,0:T(8,128)S(1)} collective-permute-done((s32[8,256]{1,0:T(8,128)}, s32[8,256]{1,0:T(8,128)S(1)}, u32[]{:S(2)}, u32[]{:S(2)}) %collective-permute-start.1) | collective-permute-done | bytes 8224 | tf_op jit(solution)/shard_map/ppermute | solution.py:499
  11.2 0.0 copy-start.10
  11.2 0.0 collective-permute-done
  11.2 0.0 copy-start.11
  11.2 0.0 copy-done.9
  11.2 0.6 copy-done.10
  11.8 0.0 copy-done.11
  11.8 2.7 %pack_influence.1.packed_ref = bf16[2704,128]{1,0:T(8,128)(2,1)} custom-call(bf16[3,4,144,192]{3,2,1,0:T(8,128)(2,1)} %bitcast.19, s32[1,8,256]{2,1,0:T(8,128)} %bitcast.20, s32[1,8,256]{2,1,0:T(8,128)} %bitcast.26, s32[1,8,256]{2,1,0:T(8,128)} %bitcast.24, s32[1,8,256]{2,1,0:T(8,128)} %bitcast.22), custom_call_target="tpu_custom_call" | custom-call | bytes 995328 | tf_op jit(solution)/shard_map/pack_influence/pallas_call | solution.py:80
  14.5 1.5 %collective-permute-start.5 = (bf16[2704,128]{1,0:T(8,128)(2,1)}, bf16[2704,128]{1,0:T(8,128)(2,1)S(1)}, u32[]{:S(2)}, u32[]{:S(2)}) collective-permute-start(bf16[2704,128]{1,0:T(8,128)(2,1)} %pack_influence.1.packed_ref), channel_id=1, source_target_pairs={{0,4},{1,5},{2,6},{3,7},{4,0},{5,1},{6,2},{7,3},{8,12},{9,13},{10,... | collective-permute-start | bytes 2076680 | tf_op jit(solution)/shard_map/ppermute | solution.py:499
  16.0 1.5 %collective-permute-start.4 = (bf16[2704,128]{1,0:T(8,128)(2,1)}, bf16[2704,128]{1,0:T(8,128)(2,1)S(1)}, u32[]{:S(2)}, u32[]{:S(2)}) collective-permute-start(bf16[2704,128]{1,0:T(8,128)(2,1)} %pack_influence.1.packed_ref), channel_id=1, source_target_pairs={{0,2},{1,3},{2,0},{3,1},{4,6},{5,7},{6,4},{7,5},{8,10},{9,11},{10,... | collective-permute-start | bytes 2076680 | tf_op jit(solution)/shard_map/ppermute | solution.py:499
  17.5 0.0 collective-permute-start.3
  17.5 14.2 %gram_rows.1 = (bf16[6912,224]{1,0:T(8,128)(2,1)}, bf16[1,12,192,224]{3,2,1,0:T(8,128)(2,1)}) custom-call(s32[54,128]{1,0:T(8,128)} %get-tuple-element.33.codes_ref, s32[13,64,128]{2,1,0:T(8,128)} %get-tuple-element.34.words, f8e5m2[224,2048]{1,0:T(32,128)(4,1)} %get-tuple-element.35.own_signs, f32[224,128]{1,0:T(8,128)} %get-tuple-element.36.own_sums, ...), custom_call_target="tpu_custom_call" | custom-call | flops 6341787648 | bytes 3096576 | tf_op jit(solution)/shard_map/gram_rows/pallas_call | solution.py:219
  31.7 0.0 collective-permute-done.5
  31.7 0.0 copy-start
  31.7 0.0 collective-permute-done.4
  31.8 0.0 copy-start.1
  31.8 1.6 %collective-permute-start.9 = (bf16[1360,128]{1,0:T(8,128)(2,1)S(1)}, bf16[1360,128]{1,0:T(8,128)(2,1)S(1)}, u32[]{:S(2)}, u32[]{:S(2)}) collective-permute-start(bf16[1360,128]{1,0:T(8,128)(2,1)S(1)} %slice.7), channel_id=1, source_target_pairs={{0,2},{1,3},{2,0},{3,1},{4,6},{5,7},{6,4},{7,5},{8,10},{9,11},{10,... | collective-permute-start | bytes 1044488 | tf_op jit(solution)/shard_map/ppermute | solution.py:499
  33.4 0.6 collective-permute-start.8
  33.9 0.0 collective-permute-start.6
  33.9 0.5 collective-permute-start.7
  34.5 0.0 collective-permute-done.3
  34.5 0.0 copy-done
  34.5 0.0 copy-done.1
  34.5 0.8 %copy-done.2 = bf16[2704,128]{1,0:T(8,128)(2,1)} copy-done((bf16[2704,128]{1,0:T(8,128)(2,1)}, bf16[2704,128]{1,0:T(8,128)(2,1)S(1)}, u32[]{:S(2)}) %copy-start.2) | copy-done | bytes 692248
  35.3 5.2 %bands.1.refs_15_ = bf16[3,12,192,224]{3,2,1,0:T(8,128)(2,1)} custom-call(bf16[6912,224]{1,0:T(8,128)(2,1)} %get-tuple-element.40.gram_any.refs_16_, bf16[1,2704,128]{2,1,0:T(8,128)(2,1)} %bitcast.17, bf16[1,2704,128]{2,1,0:T(8,128)(2,1)} %bitcast.14, bf16[1,2704,128]{2,1,0:T(8,128)(2,1)} %bitcast.12), custom_call_target="tpu_custom_call" | custom-call | flops 792723456 | bytes 4128768 | tf_op jit(solution)/shard_map/bands/pallas_call | solution.py:323
  40.6 2.1 %collective-permute-done.8.refs_10_ = bf16[1344,128]{1,0:T(8,128)(2,1)S(1)} collective-permute-done((bf16[1344,128]{1,0:T(8,128)(2,1)S(1)}, bf16[1344,128]{1,0:T(8,128)(2,1)S(1)}, u32[]{:S(2)}, u32[]{:S(2)}) %collective-permute-start.8) | collective-permute-done | bytes 344096 | tf_op jit(solution)/shard_map/ppermute | solution.py:499
  42.7 0.0 collective-permute-done.9.refs_11_
  42.7 0.1 collective-permute-start.11
  42.8 0.5 collective-permute-start.10
  43.2 0.0 collective-permute-done.6.refs_8_
  43.3 0.0 collective-permute-done.7.refs_9_
  43.3 0.0 copy-start.4
  43.3 1.6 %collective-permute-done.10.refs_12_ = bf16[1344,128]{1,0:T(8,128)(2,1)S(1)} collective-permute-done((bf16[1344,128]{1,0:T(8,128)(2,1)S(1)}, bf16[1344,128]{1,0:T(8,128)(2,1)S(1)}, u32[]{:S(2)}, u32[]{:S(2)}) %collective-permute-start.10) | collective-permute-done | bytes 344096 | tf_op jit(solution)/shard_map/ppermute | solution.py:499
  44.9 0.0 collective-permute-done.11.refs_13_
  44.9 0.0 copy-done.7
  44.9 0.0 copy-done.5
  44.9 0.0 copy-done.3
  44.9 0.0 copy-done.4
  44.9 0.7 %copy-done.8 = bf16[1344,128]{1,0:T(8,128)(2,1)} copy-done((bf16[1344,128]{1,0:T(8,128)(2,1)}, bf16[1344,128]{1,0:T(8,128)(2,1)S(1)}, u32[]{:S(2)}) %copy-start.8) | copy-done | bytes 344088
  45.6 0.1 copy-done.6
  45.8 16.7 %decode.1 = bf16[216,4,2560]{2,1,0:T(4,128)(2,1)} custom-call(s32[1,8,256]{2,1,0:T(8,128)} %bitcast.21, s32[1,8,256]{2,1,0:T(8,128)} %bitcast.27, s32[1,8,256]{2,1,0:T(8,128)} %bitcast.25, s32[1,8,256]{2,1,0:T(8,128)} %bitcast.23, bf16[1,2704,128]{2,1,0:T(8,128)(2,1)} %bitcast.16, bf16[1,2704,128]{2,1,0:T(8,128)(2,1)} %bitcast.18, ...), custom_call_target="tpu_custom_call" | custom-call | flops 2642411520 | bytes 4423680 | tf_op jit(solution)/shard_map/decode/pallas_call | solution.py:473
  (8 shorter events, 0.1 us)
Async XLA Ops:
  1.4 8.4 %collective-permute-start.2 = (s32[8,256]{1,0:T(8,128)}, s32[8,256]{1,0:T(8,128)S(1)}, u32[]{:S(2)}, u32[]{:S(2)}) collective-permute-start(s32[8,256]{1,0:T(8,128)} %small_lines.1), channel_id=1, source_target_pairs={{0,24},{8,16},{16,8},{24,0},{1,25},{9,17},{17,9},{25,1},{2,26},{10... | collective-permute-start | bytes 24584 | tf_op jit(solution)/shard_map/ppermute | solution.py:499
  6.4 4.8 %collective-permute-start.1 = (s32[8,256]{1,0:T(8,128)}, s32[8,256]{1,0:T(8,128)S(1)}, u32[]{:S(2)}, u32[]{:S(2)}) collective-permute-start(s32[8,256]{1,0:T(8,128)} %small_lines.1), channel_id=1, source_target_pairs={{0,16},{8,24},{16,0},{24,8},{1,17},{9,25},{17,1},{25,9},{2,18},{10... | collective-permute-start | bytes 24584 | tf_op jit(solution)/shard_map/ppermute | solution.py:499
  6.4 4.8 %collective-permute-start = (s32[8,256]{1,0:T(8,128)}, s32[8,256]{1,0:T(8,128)S(1)}, u32[]{:S(2)}, u32[]{:S(2)}) collective-permute-start(s32[8,256]{1,0:T(8,128)} %small_lines.1), channel_id=1, source_target_pairs={{0,8},{8,0},{16,24},{24,16},{1,9},{9,1},{17,25},{25,17},{2,10},{10... | collective-permute-start | bytes 24584 | tf_op jit(solution)/shard_map/ppermute | solution.py:499
  9.8 1.4 %copy-start.9 = (s32[8,256]{1,0:T(8,128)}, s32[8,256]{1,0:T(8,128)S(1)}, u32[]{:S(2)}) copy-start(s32[8,256]{1,0:T(8,128)S(1)} %collective-permute-done.2) | copy-start | bytes 24580
  11.2 0.6 copy-start.10
  11.2 0.6 copy-start.11
  14.5 17.2 %collective-permute-start.5 = (bf16[2704,128]{1,0:T(8,128)(2,1)}, bf16[2704,128]{1,0:T(8,128)(2,1)S(1)}, u32[]{:S(2)}, u32[]{:S(2)}) collective-permute-start(bf16[2704,128]{1,0:T(8,128)(2,1)} %pack_influence.1.packed_ref), channel_id=1, source_target_pairs={{0,4},{1,5},{2,6},{3,7},{4,0},{5,1},{6,2},{7,3},{8,12},{9,13},{10,... | collective-permute-start | bytes 2076680 | tf_op jit(solution)/shard_map/ppermute | solution.py:499
  16.0 15.8 %collective-permute-start.4 = (bf16[2704,128]{1,0:T(8,128)(2,1)}, bf16[2704,128]{1,0:T(8,128)(2,1)S(1)}, u32[]{:S(2)}, u32[]{:S(2)}) collective-permute-start(bf16[2704,128]{1,0:T(8,128)(2,1)} %pack_influence.1.packed_ref), channel_id=1, source_target_pairs={{0,2},{1,3},{2,0},{3,1},{4,6},{5,7},{6,4},{7,5},{8,10},{9,11},{10,... | collective-permute-start | bytes 2076680 | tf_op jit(solution)/shard_map/ppermute | solution.py:499
  17.5 17.0 %collective-permute-start.3 = (bf16[2704,128]{1,0:T(8,128)(2,1)}, bf16[2704,128]{1,0:T(8,128)(2,1)S(1)}, u32[]{:S(2)}, u32[]{:S(2)}) collective-permute-start(bf16[2704,128]{1,0:T(8,128)(2,1)} %pack_influence.1.packed_ref), channel_id=1, source_target_pairs={{0,1},{1,0},{2,3},{3,2},{4,5},{5,4},{6,7},{7,6},{8,9},{9,8},{10,11... | collective-permute-start | bytes 2076680 | tf_op jit(solution)/shard_map/ppermute | solution.py:499
  31.7 2.7 %copy-start = (bf16[2704,128]{1,0:T(8,128)(2,1)}, bf16[2704,128]{1,0:T(8,128)(2,1)S(1)}, u32[]{:S(2)}) copy-start(bf16[2704,128]{1,0:T(8,128)(2,1)S(1)} %collective-permute-done.5) | copy-start | bytes 2076676
  31.8 2.7 %copy-start.1 = (bf16[2704,128]{1,0:T(8,128)(2,1)}, bf16[2704,128]{1,0:T(8,128)(2,1)S(1)}, u32[]{:S(2)}) copy-start(bf16[2704,128]{1,0:T(8,128)(2,1)S(1)} %collective-permute-done.4) | copy-start | bytes 2076676
  31.8 10.9 %collective-permute-start.9 = (bf16[1360,128]{1,0:T(8,128)(2,1)S(1)}, bf16[1360,128]{1,0:T(8,128)(2,1)S(1)}, u32[]{:S(2)}, u32[]{:S(2)}) collective-permute-start(bf16[1360,128]{1,0:T(8,128)(2,1)S(1)} %slice.7), channel_id=1, source_target_pairs={{0,2},{1,3},{2,0},{3,1},{4,6},{5,7},{6,4},{7,5},{8,10},{9,11},{10,... | collective-permute-start | bytes 1044488 | tf_op jit(solution)/shard_map/ppermute | solution.py:499
  33.4 9.3 %collective-permute-start.8 = (bf16[1344,128]{1,0:T(8,128)(2,1)S(1)}, bf16[1344,128]{1,0:T(8,128)(2,1)S(1)}, u32[]{:S(2)}, u32[]{:S(2)}) collective-permute-start(bf16[1344,128]{1,0:T(8,128)(2,1)S(1)} %slice.6), channel_id=1, source_target_pairs={{0,4},{1,5},{2,6},{3,7},{4,0},{5,1},{6,2},{7,3},{8,12},{9,13},{10,... | collective-permute-start | bytes 1032200 | tf_op jit(solution)/shard_map/ppermute | solution.py:499
  33.9 9.3 %collective-permute-start.6 = (bf16[2704,128]{1,0:T(8,128)(2,1)S(1)}, bf16[2704,128]{1,0:T(8,128)(2,1)S(1)}, u32[]{:S(2)}, u32[]{:S(2)}) collective-permute-start(bf16[2704,128]{1,0:T(8,128)(2,1)S(1)} %collective-permute-done.4), channel_id=1, source_target_pairs={{0,1},{1,0},{2,3},{3,2},{4,5},{5,4},{6,7},{7,6},{8,9},{9,8},{10,11... | collective-permute-start | bytes 2076680 | tf_op jit(solution)/shard_map/ppermute | solution.py:499
  33.9 9.3 %collective-permute-start.7 = (bf16[2704,128]{1,0:T(8,128)(2,1)S(1)}, bf16[2704,128]{1,0:T(8,128)(2,1)S(1)}, u32[]{:S(2)}, u32[]{:S(2)}) collective-permute-start(bf16[2704,128]{1,0:T(8,128)(2,1)S(1)} %collective-permute-done.5), channel_id=1, source_target_pairs={{0,1},{1,0},{2,3},{3,2},{4,5},{5,4},{6,7},{7,6},{8,9},{9,8},{10,11... | collective-permute-start | bytes 2076680 | tf_op jit(solution)/shard_map/ppermute | solution.py:499
  34.5 0.8 %copy-start.2 = (bf16[2704,128]{1,0:T(8,128)(2,1)}, bf16[2704,128]{1,0:T(8,128)(2,1)S(1)}, u32[]{:S(2)}) copy-start(bf16[2704,128]{1,0:T(8,128)(2,1)S(1)} %collective-permute-done.3) | copy-start | bytes 2076676
  42.7 2.2 %copy-start.7 = (bf16[1344,128]{1,0:T(8,128)(2,1)}, bf16[1344,128]{1,0:T(8,128)(2,1)S(1)}, u32[]{:S(2)}) copy-start(bf16[1344,128]{1,0:T(8,128)(2,1)S(1)} %collective-permute-done.8.refs_10_) | copy-start | bytes 1032196
  42.7 2.2 %copy-start.5 = (bf16[1360,128]{1,0:T(8,128)(2,1)}, bf16[1360,128]{1,0:T(8,128)(2,1)S(1)}, u32[]{:S(2)}) copy-start(bf16[1360,128]{1,0:T(8,128)(2,1)S(1)} %collective-permute-done.9.refs_11_) | copy-start | bytes 1044484
  42.7 2.2 %collective-permute-start.11 = (bf16[1360,128]{1,0:T(8,128)(2,1)S(1)}, bf16[1360,128]{1,0:T(8,128)(2,1)S(1)}, u32[]{:S(2)}, u32[]{:S(2)}) collective-permute-start(bf16[1360,128]{1,0:T(8,128)(2,1)S(1)} %collective-permute-done.9.refs_11_), channel_id=1, source_target_pairs={{0,1},{1,0},{2,3},{3,2},{4,5},{5,4},{6,7},{7,6},{8,9},{9,8},{10,11... | collective-permute-start | bytes 1044488 | tf_op jit(solution)/shard_map/ppermute | solution.py:499
  42.8 2.1 %collective-permute-start.10 = (bf16[1344,128]{1,0:T(8,128)(2,1)S(1)}, bf16[1344,128]{1,0:T(8,128)(2,1)S(1)}, u32[]{:S(2)}, u32[]{:S(2)}) collective-permute-start(bf16[1344,128]{1,0:T(8,128)(2,1)S(1)} %collective-permute-done.8.refs_10_), channel_id=1, source_target_pairs={{0,1},{1,0},{2,3},{3,2},{4,5},{5,4},{6,7},{7,6},{8,9},{9,8},{10,11... | collective-permute-start | bytes 1032200 | tf_op jit(solution)/shard_map/ppermute | solution.py:499
  43.3 1.7 %copy-start.3 = (bf16[2704,128]{1,0:T(8,128)(2,1)}, bf16[2704,128]{1,0:T(8,128)(2,1)S(1)}, u32[]{:S(2)}) copy-start(bf16[2704,128]{1,0:T(8,128)(2,1)S(1)} %collective-permute-done.6.refs_8_) | copy-start | bytes 2076676
  43.3 1.7 %copy-start.4 = (bf16[2704,128]{1,0:T(8,128)(2,1)}, bf16[2704,128]{1,0:T(8,128)(2,1)S(1)}, u32[]{:S(2)}) copy-start(bf16[2704,128]{1,0:T(8,128)(2,1)S(1)} %collective-permute-done.7.refs_9_) | copy-start | bytes 2076676
  44.9 0.7 %copy-start.8 = (bf16[1344,128]{1,0:T(8,128)(2,1)}, bf16[1344,128]{1,0:T(8,128)(2,1)S(1)}, u32[]{:S(2)}) copy-start(bf16[1344,128]{1,0:T(8,128)(2,1)S(1)} %collective-permute-done.10.refs_12_) | copy-start | bytes 1032196
  44.9 0.9 %copy-start.6 = (bf16[1360,128]{1,0:T(8,128)(2,1)}, bf16[1360,128]{1,0:T(8,128)(2,1)S(1)}, u32[]{:S(2)}) copy-start(bf16[1360,128]{1,0:T(8,128)(2,1)S(1)} %collective-permute-done.11.refs_13_) | copy-start | bytes 1044484

commit v7 on v6

--- a/solution.py
+++ b/solution.py
@@ -13,42 +13,24 @@
 NA = 48
 BAND = 3
 BITS = 13
-SCALE = 7
 NARROW = jnp.float8_e5m2
 LANES = 128
 WINDOW = 256
-VMEM_BYTES = 56 * 1024 * 1024
+VMEM_BYTES = 63 * 1024 * 1024
 
 
 def parity(codes, rows):
     return lax.population_count(codes & rows) & 1
 
 
-def lines_kernel(rows_ref, columns_ref, valid_ref, lines_ref):
-    mirrors, rows = rows_ref.shape[0], rows_ref.shape[2]
+def pack_kernel(block_ref, rows_ref, columns_ref, valid_ref, packed_ref, lines_ref):
+    mirrors, rows, slots, samples = block_ref.shape
+    groups = mirrors * rows // 2
     lines_ref[...] = jnp.zeros(lines_ref.shape, lines_ref.dtype)
     lines_ref[mirrors:mirrors + valid_ref.shape[1], :valid_ref.shape[2]] = valid_ref[0]
     for k in range(mirrors):
         lines_ref[k:k + 1, :columns_ref.shape[2]] = columns_ref[k]
         lines_ref[mirrors + valid_ref.shape[1]:mirrors + valid_ref.shape[1] + 1, k * rows:(k + 1) * rows] = rows_ref[k]
-
-
-def small_lines(foot_rows, foot_columns, valid):
-    vmem = pl.BlockSpec(memory_space=pltpu.VMEM)
-    count = foot_rows.shape[1] + valid.shape[1] + 1
-    return pl.pallas_call(
-        lines_kernel,
-        out_shape=jax.ShapeDtypeStruct((-(-count // 8) * 8, WINDOW), jnp.int32),
-        in_specs=[vmem] * 3,
-        out_specs=vmem,
-        name="small_lines",
-    )(jnp.swapaxes(foot_rows, 0, 1), jnp.swapaxes(foot_columns, 0, 1), valid)
-
-
-def pack_kernel(block_ref, *refs):
-    lines_refs, packed_ref = refs[:-1], refs[-1]
-    mirrors, rows, slots, samples = block_ref.shape
-    groups = mirrors * rows // 2
     identity = (
         lax.broadcasted_iota(jnp.int32, (samples, samples), 0) == lax.broadcasted_iota(jnp.int32, (samples, samples), 1)
     ).astype(jnp.float32).astype(jnp.bfloat16)
@@ -64,28 +46,24 @@
             tails.append(turned[:, LANES:])
         tails.append(jnp.zeros((samples, LANES - groups * (slots - LANES)), jnp.bfloat16))
         packed_ref[pl.ds(base + groups * samples, samples), :] = jnp.concatenate(tails, axis=1)
-    count = rows // 2 + 1
-    lines = [ref[n, mirrors:mirrors + count, :LANES] for ref in lines_refs for n in range(ref.shape[0])]
-    extra = packed_ref.shape[0] - 2 * (groups + 1) * samples
-    lines.append(jnp.zeros((extra - count * len(lines), LANES), jnp.int32))
-    packed_ref[pl.ds(packed_ref.shape[0] - extra, extra), :] = (
-        jnp.concatenate(lines, axis=0).astype(jnp.float32).astype(jnp.bfloat16)
-    )
-
-
-def pack(block, lines):
+
+
+def pack(block, foot_rows, foot_columns, valid):
     mirrors, rows, slots, samples = block.shape
     vmem = pl.BlockSpec(memory_space=pltpu.VMEM)
-    extra = -(-sum(line.shape[0] for line in lines) * (rows // 2 + 1) // 16) * 16
+    count = mirrors + valid.shape[1] + 1
     return pl.pallas_call(
         pack_kernel,
-        out_shape=jax.ShapeDtypeStruct(((mirrors * rows + 2) * samples + extra, LANES), block.dtype),
-        in_specs=[vmem] * (1 + len(lines)),
-        out_specs=vmem,
+        out_shape=[
+            jax.ShapeDtypeStruct(((mirrors * rows + 2) * samples, LANES), block.dtype),
+            jax.ShapeDtypeStruct((-(-count // 8) * 8, WINDOW), jnp.int32),
+        ],
+        in_specs=[vmem] * 4,
+        out_specs=[vmem] * 2,
         compiler_params=pltpu.CompilerParams(vmem_limit_bytes=VMEM_BYTES),
         cost_estimate=pl.CostEstimate(flops=0, bytes_accessed=3 * block.size, transcendentals=0),
         name="pack_influence",
-    )(block, *lines)
+    )(block, jnp.swapaxes(foot_rows, 0, 1), jnp.swapaxes(foot_columns, 0, 1), valid)
 
 
 def column_of(row):
@@ -130,7 +108,7 @@
     total = jnp.zeros((own, LANES), jnp.float32)
     for at in range(planes):
         signs = (1 - 2 * parity(own_column, pokes_ref[at:at + 1, :])).astype(jnp.float32)
-        own_signs[:, at * LANES:(at + 1) * LANES] = (signs * 2.0 ** (SCALE - at)).astype(NARROW)
+        own_signs[:, at * LANES:(at + 1) * LANES] = signs.astype(NARROW)
         total = total + signs
     own_sums[...] = jnp.broadcast_to(jnp.sum(total, axis=1, keepdims=True), own_sums.shape)
 
@@ -173,21 +151,18 @@
                 value = part if value is None else value ^ part
             word.append(value)
         word = jnp.concatenate(word, axis=1)
-        words_of = (word, word >> planes)
-        total = jnp.zeros((own, WINDOW), jnp.float32)
-        for at in range(0, planes, 2):
-            bits = [
-                (side & (1 << plane)).astype(jnp.float32).astype(NARROW)
-                for plane in (at, at + 1) for side in words_of
-            ]
-            total = total + jnp.dot(
-                own_signs[:, at * LANES:(at + 2) * LANES], jnp.concatenate(bits, axis=0),
-                preferred_element_type=jnp.float32,
-            )
+        bits = [None] * (2 * planes)
+        for byte in range(0, 2 * planes, 8):
+            part = (word >> byte).astype(jnp.int8)
+            for bit in range(8):
+                at = byte + bit
+                hit = (part & np.uint8(1 << bit).astype(np.int8)) != 0
+                bits[at % planes * 2 + at // planes] = jnp.where(hit, NARROW(1.0), NARROW(0.0))
+        total = jnp.dot(own_signs[...], jnp.concatenate(bits, axis=0), preferred_element_type=jnp.float32)
         sums = jnp.concatenate([own_sums[...]] * (WINDOW // LANES), axis=1)
-        turned = jnp.transpose(sums - 2.0 ** (1 - SCALE) * total)
+        turned = jnp.transpose((sums - 2.0 * total).astype(jnp.bfloat16))
         at = pl.multiple_of(mirror * height + index * WINDOW, WINDOW)
-        gram_ref[pl.ds(at, WINDOW), :] = turned.astype(jnp.bfloat16)
+        gram_ref[pl.ds(at, WINDOW), :] = turned
         return 0
 
     lax.fori_loop(0, height // WINDOW, chunk, 0, unroll=3)
@@ -361,21 +336,19 @@
 
 def decode_kernel(row_shape, surface_rows, own, staged, norm, counts, late_parts, *refs):
     mirrors, shard_rows, slots, samples = row_shape
-    columns_refs, refs = refs[:counts[0]], refs[counts[0]:]
-    lines_refs, refs = refs[:counts[1]], refs[counts[1]:]
-    late_refs, refs = refs[:counts[2]], refs[counts[2]:]
-    ready_refs, refs = refs[:counts[3]], refs[counts[3]:]
-    (gram_any, out_ref, gram_ref, decoded, differences, total, packed_lines, lines, scalars, *refs) = refs
-    late_blocks, refs = refs[:counts[2]], refs[counts[2]:]
-    gram_semaphores, ready_semaphores, line_semaphores, late_semaphores, scalar_semaphore = refs
+    lines_ref, *refs = refs
+    late_refs, refs = refs[:counts[0]], refs[counts[0]:]
+    ready_refs, refs = refs[:counts[1]], refs[counts[1]:]
+    (gram_any, out_ref, gram_ref, decoded, differences, total, foot_rows, scalars, *refs) = refs
+    late_blocks, refs = refs[:counts[0]], refs[counts[0]:]
+    gram_semaphores, ready_semaphores, late_semaphores, scalar_semaphore = refs
     group = pl.program_id(0)
     directions, pupil = differences.shape[0], 2 * differences.shape[2]
     phases = out_ref.shape[2] // pupil
     blocks = surface_rows // shard_rows
     late = len(late_parts)
     ready = blocks - late
-    width = shard_rows // 2 + 1
-    extra = lines.shape[1]
+    foot_line = mirrors + shard_rows // 2
 
     @pl.when(group == 0)
     def _():
@@ -384,32 +357,23 @@
                 copy.start()
             return copies
 
-        ends = [ref.at[n, pl.ds(ref.shape[1] - extra, extra)] for ref in lines_refs for n in range(ref.shape[0])]
-        line_copies = started([
-            pltpu.make_async_copy(end, packed_lines.at[n], line_semaphores.at[n]) for n, end in enumerate(ends)
-        ])
+        for block in range(blocks):
+            for d in range(directions):
+                foot_rows[block, d:d + 1] = lines_ref[block, d, foot_line:foot_line + 1, :LANES]
+        to_scalars = pltpu.make_async_copy(foot_rows, scalars, scalar_semaphore.at[0])
+        to_scalars.start()
         late_copies = started([
-            pltpu.make_async_copy(late_refs[n], late_blocks[n], late_semaphores.at[n]) for n in range(counts[2])
+            pltpu.make_async_copy(late_refs[n], late_blocks[n], late_semaphores.at[n]) for n in range(counts[0])
         ])
         gram_copies = started(fetch_gram(gram_any, gram_ref, gram_semaphores, mirrors)) if late else []
         ready_copies = started([
             pltpu.make_async_copy(block, decoded.at[n], ready_semaphores.at[n])
             for n, block in enumerate([ref.at[m] for ref in ready_refs for m in range(ref.shape[0])])
         ])
-        columns = [ref[n, :, :pupil] for ref in columns_refs for n in range(ref.shape[0])]
+        columns = [lines_ref[0, d, :, :pupil] for d in range(directions)]
         build_differences(columns, differences, mirrors, samples, pupil)
-        for copy in line_copies + late_copies:
+        for copy in late_copies:
             copy.wait()
-        held = [packed_lines[n] for n in range(len(ends))]
-        at = 0
-        for part in late_parts:
-            at += part
-            last = late_blocks[at - 1]
-            held.append(last[pl.ds(last.shape[0] - extra, extra), :])
-        for n, value in enumerate(held):
-            lines[n] = value.astype(jnp.float32).astype(jnp.int32)
-        to_scalars = pltpu.make_async_copy(lines, scalars, scalar_semaphore.at[0])
-        to_scalars.start()
         at = 0
         for n, part in enumerate(late_parts):
             parts, at = late_blocks[at:at + part], at + part
@@ -428,12 +392,12 @@
         products, factors = [], []
         for phase in range(phases):
             i = group * phases + phase
-            block = row_place(2 * i // shard_rows, staged)
+            block = (2 * i // shard_rows) ^ position("row", staged)
             sums, changes = [], []
             for k in range(mirrors):
                 picked = []
                 for y in range(2):
-                    row = scalars[block, held * width + width - 1, k * shard_rows + (2 * phase + y) % shard_rows]
+                    row = scalars[block, held, k * shard_rows + (2 * phase + y) % shard_rows]
                     picked.append(decoded[row_place(row // shard_rows, staged), k * shard_rows + row % shard_rows])
                 sums.append(picked[0] + picked[1])
                 changes.append(picked[1] - picked[0])
@@ -443,7 +407,8 @@
                         differences[held, kind], jnp.concatenate(rows, axis=0), preferred_element_type=jnp.float32
                     )
                 )
-            valid = lines[block, pl.ds(held * width + phase % (shard_rows // 2), 1), :][:, :pupil // 2]
+            line = mirrors + phase % (shard_rows // 2)
+            valid = lines_ref[block, held, line:line + 1, :pupil // 2]
             factors += [valid.astype(jnp.float32) * norm] * 2
         product = jnp.concatenate(products, axis=0)
         factor = jnp.concatenate(factors, axis=1)
@@ -456,43 +421,40 @@
         out_ref[:, :, tile * LANES:(tile + 1) * LANES] = value.astype(out_ref.dtype)
 
 
-def decode(columns, sources, late, ready, gram_rows, own, row_shape, surface_rows, pupil, norm, staged):
+def decode(lines, late, ready, gram_rows, own, row_shape, surface_rows, pupil, norm, staged):
     mirrors, shard_rows, slots, samples = row_shape
     acts, padded = gram_rows.shape
-    directions = sum(line.shape[0] for line in columns)
-    blocks = surface_rows // shard_rows
-    extra = -(-directions * (shard_rows // 2 + 1) // 16) * 16
+    blocks, directions = lines.shape[:2]
     phases = LANES // math.gcd(pupil, LANES)
     width = surface_rows // 2 * pupil
     lanes = phases * pupil
     flops = 2 * padded * mirrors * samples * pupil * directions * surface_rows // 2
     vmem, anywhere = pl.BlockSpec(memory_space=pltpu.VMEM), pl.BlockSpec(memory_space=pl.ANY)
     parts = [part for block in late for part in block]
-    counts = (len(columns), len(sources), len(parts), len(ready))
-    semaphores = [mirrors, blocks, blocks, max(len(parts), 1), 1]
+    counts = (len(parts), len(ready))
+    semaphores = [mirrors, blocks, max(len(parts), 1), 1]
     return pl.pallas_call(
         functools.partial(
             decode_kernel, row_shape, surface_rows, own, staged, norm, counts, [len(block) for block in late]
         ),
         grid=(width // lanes,),
         out_shape=jax.ShapeDtypeStruct((own, directions, width), jnp.bfloat16),
-        in_specs=[vmem] * counts[0] + [anywhere] * (sum(counts[1:]) + 1),
+        in_specs=[vmem] + [anywhere] * (sum(counts) + 1),
         out_specs=pl.BlockSpec((own, directions, lanes), lambda s: (0, 0, s)),
         scratch_shapes=[
             pltpu.VMEM((acts, padded), jnp.bfloat16),
             pltpu.VMEM((blocks, mirrors * shard_rows, samples, padded), jnp.bfloat16),
             pltpu.VMEM((directions, 2, pupil // 2, mirrors * samples), jnp.bfloat16),
             pltpu.VMEM((lanes // LANES, own * directions, LANES), jnp.float32),
-            pltpu.VMEM((blocks, extra, LANES), jnp.bfloat16),
-            pltpu.VMEM((blocks, extra, LANES), jnp.int32),
-            pltpu.SMEM((blocks, extra, LANES), jnp.int32),
+            pltpu.VMEM((blocks, -(-directions // 8) * 8, LANES), jnp.int32),
+            pltpu.SMEM((blocks, -(-directions // 8) * 8, LANES), jnp.int32),
             *[pltpu.VMEM(part.shape, part.dtype) for part in parts],
             *[pltpu.SemaphoreType.DMA((count,)) for count in semaphores],
         ],
         compiler_params=pltpu.CompilerParams(vmem_limit_bytes=VMEM_BYTES),
         cost_estimate=pl.CostEstimate(flops=flops, bytes_accessed=2 * own * directions * width, transcendentals=0),
         name="decode",
-    )(*columns, *sources, *parts, *ready, gram_rows)
+    )(lines, *parts, *ready, gram_rows)
 
 
 def swap(block, axis, distance):
@@ -510,33 +472,33 @@
     staged = devices == 8 and directions & (directions - 1) == 0
     turned = jnp.swapaxes(influence, 2, 3)
     pokes = poke_rows.reshape(-1, LANES)
-    lines = small_lines(foot_rows, foot_columns, subaperture_valid)
+    packed, lines = pack(turned, foot_rows, foot_columns, subaperture_valid)
     if not staged:
-        lines = [lax.all_gather(lines, "dir")]
-        packed = pack(turned, lines)
         every = lax.all_gather(packed, "row")
+        lines = lax.all_gather(lax.all_gather(lines, "dir"), "row")
         gram_rows, _ = gram(*own_side(actuator_codes, pokes, own), packed, row_shape, surface_rows)
         ready = [bands(gram_rows, [every], 0, staged, row_shape, surface_rows)]
-        return decode(lines, [every], [], ready, gram_rows, own, row_shape, surface_rows, pupil, norm, staged)
-
-    lines = [lines[None]] + [swap(lines, "dir", e)[None] for e in range(1, directions)]
+        return decode(lines, [], ready, gram_rows, own, row_shape, surface_rows, pupil, norm, staged)
+
+    beside, across, sibling = (swap(packed, "row", distance) for distance in (2, 4, 1))
+    lines = jnp.stack([lines] + [swap(lines, "dir", e) for e in range(1, directions)])[None]
     sides = own_side(actuator_codes, pokes, own)
     lines, sides = lax.optimization_barrier((lines, sides))
-    packed = pack(turned, lines)
-    beside, across, sibling = (swap(packed, "row", distance) for distance in (2, 4, 1))
+    more = swap(lines, "row", 1)
     gram_rows, first = gram(*sides, packed, row_shape, surface_rows)
-    gram_rows, beside, across = lax.optimization_barrier((gram_rows, beside, across))
-    half = (mirrors * shard_rows + 2) * samples // 2
+    gram_rows, beside, across, more = lax.optimization_barrier((gram_rows, beside, across, more))
+    lines = jnp.concatenate([lines, more], axis=0)
+    more = swap(lines, "row", 2)
+    half = packed.shape[0] // 2
     upper, lower = swap(beside[:half], "row", 4), swap(across[half:], "row", 2)
     beside_sibling, across_sibling = swap(beside, "row", 1), swap(across, "row", 1)
     sources = [source[None] for source in (sibling, beside, across)]
     ready = bands(gram_rows, sources, 1, staged, row_shape, surface_rows)
-    ready, upper, lower = lax.optimization_barrier((ready, upper, lower))
+    ready, upper, lower, more = lax.optimization_barrier((ready, upper, lower, more))
+    lines = jnp.concatenate([lines, more], axis=0)
+    lines = jnp.concatenate([lines, swap(lines, "row", 4)], axis=0)
     late = [[beside_sibling], [across_sibling], [upper, lower], [swap(upper, "row", 1), swap(lower, "row", 1)]]
-    return decode(
-        lines, [packed[None], *sources], late, [first, ready], gram_rows, own, row_shape, surface_rows, pupil, norm,
-        staged,
-    )
+    return decode(lines, late, [first, ready], gram_rows, own, row_shape, surface_rows, pupil, norm, staged)
 
 
 def solution(mesh):

time: 62.7 us -> 68.1 us (1.086)
  waiting for transfers between devices: 5.17 us -> 12.2 us
  Pallas kernels: 42.9 us -> 38.8 us
  other arithmetic: 0 us -> 1.43 us
  starting transfers between devices: 11.8 us -> 12.7 us
    ppermute x12 -> x15, waiting for transfers between devices: 5.17 us -> 12.2 us  [swap(): lax.ppermute(block, axis, [(i, i ^ distance) for i in range(lax.axis_size...]
    pallas_call x1, Pallas kernels: 14.2 us -> 11.3 us  [gram(): pl.pallas_call(functools.partial(gram_kernel, row_shape, surface_rows), g...]
    unnamed x24 -> x2, local copies, waits for them, and re-layouts: 2.3 us -> 0.01 us
    slice x1, local copies, waits for them, and re-layouts: 0.02 us -> 1.74 us  [shards(): beside[:half]]
    pallas_call x2 -> x1, Pallas kernels: 4.05 us -> 2.58 us  [pack(): pl.pallas_call(pack_kernel, out_shape=[jax.ShapeDtypeStruct(((mirrors * r...]
    ppermute x12 -> x15, starting transfers between devices: 11.8 us -> 12.7 us  [swap(): lax.ppermute(block, axis, [(i, i ^ distance) for i in range(lax.axis_size...]
    slice x1, local copies, waits for them, and re-layouts: 0.02 us -> 0.79 us  [shards(): across[half:]]
    concatenate x0 -> x3, other arithmetic: none -> 0.73 us  [the longest x1 0.72 us: shards(): lines = jnp.concatenate([lines, swap(lines, 'row', 4)], axis=0)]
  transfers between devices with their start and end apart: 12 -> 15, of which waited for: 3 -> 3; matrix products, arithmetic and copies ran while one was open for 0% -> 6% of each run, Pallas kernels for 36% -> 29%
where the time goes in v7:
time: 68.1 us; the launch traced here: 67.7 us
  Pallas kernels  38.8 us (57%)
  starting transfers between devices  12.7 us (19%)
  waiting for transfers between devices  12.2 us (18%)
  local copies, waits for them, and re-layouts  2.54 us (4%)
  other arithmetic  1.43 us (2%)
    pallas_call x1, Pallas kernels, decode(): pl.pallas_call(functools.partial(decode_kernel, row_shape, surface_rows,...  16.8 us
    ppermute x15, starting transfers between devices, swap(): lax.ppermute(block, axis, [(i, i ^ distance) for i in range(lax.axis_size...  12.7 us
    ppermute x15, waiting for transfers between devices, swap(): lax.ppermute(block, axis, [(i, i ^ distance) for i in range(lax.axis_size...  12.2 us
    pallas_call x1, Pallas kernels, gram(): pl.pallas_call(functools.partial(gram_kernel, row_shape, surface_rows), g...  11.3 us
    pallas_call x1, Pallas kernels, bands(): pl.pallas_call(functools.partial(bands_kernel, row_shape, surface_rows, f...  5.29 us
    pallas_call x1, Pallas kernels, own_side(): pl.pallas_call(signs_kernel, out_shape=[jax.ShapeDtypeStruct((table.size...  2.77 us
    pallas_call x1, Pallas kernels, pack(): pl.pallas_call(pack_kernel, out_shape=[jax.ShapeDtypeStruct(((mirrors * r...  2.58 us
    slice x1, local copies, waits for them, and re-layouts, shards(): beside[:half]  1.74 us
  transfers between devices with their start and end apart: 15, of which 3 were waited for; matrix products, arithmetic and copies ran while one was open for 6% of the time, Pallas kernels for 29%

profile of v7, /device:TPU:0, one launch (start us, length us, event | category | flops | bytes accessed | tf_op | source)
XLA Modules:
  0.0 67.7 jit_solution(7408918292410245598)
XLA Ops:
  0.0 2.6 %pack_influence.1 = (bf16[2688,128]{1,0:T(8,128)(2,1)}, s32[8,256]{1,0:T(8,128)}) custom-call(bf16[3,4,144,192]{3,2,1,0:T(8,128)(2,1)} %bitcast.14, s32[3,1,4]{2,1,0:T(1,128)} %bitcast.21, s32[3,1,160]{2,1,0:T(1,128)} %bitcast.20, s32[1,2,80]{2,1,0:T(2,128)} %valid_ref.1), custom_call_target="tpu_custom_call" | custom-call | bytes 995328 | tf_op jit(solution)/shard_map/pack_influence/pallas_call | solution.py:55
  2.6 5.1 %collective-permute-start.2 = (s32[8,256]{1,0:T(8,128)}, s32[8,256]{1,0:T(8,128)S(1)}, u32[]{:S(2)}, u32[]{:S(2)}) collective-permute-start(s32[8,256]{1,0:T(8,128)} %get-tuple-element.26), channel_id=1, source_target_pairs={{0,24},{8,16},{16,8},{24,0},{1,25},{9,17},{17,9},{25,1},{2,26},{10... | collective-permute-start | bytes 24584 | tf_op jit(solution)/shard_map/ppermute | solution.py:461
  7.6 0.0 collective-permute-start.1
  7.6 0.6 collective-permute-start
  8.2 0.0 collective-permute-start.6
  8.2 1.7 %collective-permute-start.4 = (bf16[2688,128]{1,0:T(8,128)(2,1)}, bf16[2688,128]{1,0:T(8,128)(2,1)S(1)}, u32[]{:S(2)}, u32[]{:S(2)}) collective-permute-start(bf16[2688,128]{1,0:T(8,128)(2,1)} %get-tuple-element.36.packed_ref), channel_id=1, source_target_pairs={{0,4},{1,5},{2,6},{3,7},{4,0},{5,1},{6,2},{7,3},{8,12},{9,13},{10,... | collective-permute-start | bytes 2064392 | tf_op jit(solution)/shard_map/ppermute | solution.py:461
  9.9 2.8 %own_signs.1 = (s32[54,128]{1,0:T(8,128)}, s32[13,64,128]{2,1,0:T(8,128)}, f8e5m2[224,2048]{1,0:T(32,128)(4,1)}, f32[224,128]{1,0:T(8,128)}) custom-call(s32[3,48,48]{2,1,0:T(8,128)} %table_ref.1, s32[16,128]{1,0:T(8,128)} %bitcast.15), custom_call_target="tpu_custom_call" | custom-call | tf_op jit(solution)/shard_map/own_signs/pallas_call | solution.py:119
  12.7 0.0 collective-permute-done.2
  12.7 1.5 %collective-permute-start.3 = (bf16[2688,128]{1,0:T(8,128)(2,1)}, bf16[2688,128]{1,0:T(8,128)(2,1)}, u32[]{:S(2)}, u32[]{:S(2)}) collective-permute-start(bf16[2688,128]{1,0:T(8,128)(2,1)} %get-tuple-element.36.packed_ref), channel_id=1, source_target_pairs={{0,2},{1,3},{2,0},{3,1},{4,6},{5,7},{6,4},{7,5},{8,10},{9,11},{10,... | collective-permute-start | bytes 2064392 | tf_op jit(solution)/shard_map/ppermute | solution.py:461
  14.2 0.0 collective-permute-done.1
  14.2 0.0 collective-permute-done
  14.2 0.7 %add_bitcast_fusion = s32[1,4,8,256]{3,2,1,0:T(8,128)S(1)} fusion(s32[1,8,256]{2,1,0:T(8,128)S(1)} %bitcast.17, s32[1,8,256]{2,1,0:T(8,128)S(1)} %bitcast.18, s32[1,8,256]{2,1,0:T(8,128)S(1)} %bitcast.19, s32[1,8,256]{2,1,0:T(8,128)} %bitcast.16), kind=kLoop, calls=%fused_computation.3 | loop fusion | flops 24576 | bytes 65536 | tf_op jit(solution)/shard_map/broadcast_in_dim | solution.py:484
  14.9 0.0 collective-permute-start.5
  14.9 11.3 %gram_rows.1 = (bf16[6912,224]{1,0:T(8,128)(2,1)}, bf16[1,12,192,224]{3,2,1,0:T(8,128)(2,1)}) custom-call(s32[54,128]{1,0:T(8,128)} %get-tuple-element.32.codes_ref, s32[13,64,128]{2,1,0:T(8,128)} %get-tuple-element.33.words, f8e5m2[224,2048]{1,0:T(32,128)(4,1)} %get-tuple-element.34.own_signs, f32[224,128]{1,0:T(8,128)} %get-tuple-element.35.own_sums, ...), custom_call_target="tpu_custom_call" | custom-call | flops 6341787648 | bytes 3096576 | tf_op jit(solution)/shard_map/gram_rows/pallas_call | solution.py:194
  26.2 0.0 collective-permute-done.5
  26.3 0.0 collective-permute-done.4
  26.3 0.0 copy-start
  26.3 4.3 %collective-permute-done.3 = bf16[2688,128]{1,0:T(8,128)(2,1)} collective-permute-done((bf16[2688,128]{1,0:T(8,128)(2,1)}, bf16[2688,128]{1,0:T(8,128)(2,1)}, u32[]{:S(2)}, u32[]{:S(2)}) %collective-permute-start.3) | collective-permute-done | bytes 688160 | tf_op jit(solution)/shard_map/ppermute | solution.py:461
  30.6 1.7 %slice.6 = bf16[1344,128]{1,0:T(8,128)(2,1)} slice(bf16[2688,128]{1,0:T(8,128)(2,1)} %collective-permute-done.3), slice={[0:1344], [0:128]} | slice | bytes 688128 | tf_op jit(solution)/shard_map/slice | solution.py:493
  32.3 0.8 %slice.7 = bf16[1344,128]{1,0:T(8,128)(2,1)} slice(bf16[2688,128]{1,0:T(8,128)(2,1)S(1)} %collective-permute-done.4), slice={[1344:2688], [0:128]} | slice | bytes 688128 | tf_op jit(solution)/shard_map/slice | solution.py:493
  33.1 1.5 %collective-permute-start.8 = (bf16[1344,128]{1,0:T(8,128)(2,1)}, bf16[1344,128]{1,0:T(8,128)(2,1)}, u32[]{:S(2)}, u32[]{:S(2)}) collective-permute-start(bf16[1344,128]{1,0:T(8,128)(2,1)} %slice.7), channel_id=1, source_target_pairs={{0,2},{1,3},{2,0},{3,1},{4,6},{5,7},{6,4},{7,5},{8,10},{9,11},{10,... | collective-permute-start | bytes 1032200 | tf_op jit(solution)/shard_map/ppermute | solution.py:461
  34.6 0.5 collective-permute-start.7
  35.1 0.0 collective-permute-start.11
  35.1 0.5 collective-permute-start.12
  35.7 0.0 collective-permute-done.6
  35.7 0.4 collective-permute-start.9
  36.0 0.0 copy-done
  36.0 5.3 %bands.1.refs_8_ = bf16[3,12,192,224]{3,2,1,0:T(8,128)(2,1)} custom-call(bf16[6912,224]{1,0:T(8,128)(2,1)} %get-tuple-element.39.gram_any.refs_9_, bf16[1,2688,128]{2,1,0:T(8,128)(2,1)} %bitcast.9.refs_0_, bf16[1,2688,128]{2,1,0:T(8,128)(2,1)} %bitcast.10.refs_1_, bf16[1,2688,128]{2,1,0:T(8,128)(2,1)} %bitcast.13), custom_call_target="tpu_custom_call" | custom-call | flops 792723456 | bytes 4128768 | tf_op jit(solution)/shard_map/bands/pallas_call | solution.py:298
  41.3 2.8 %collective-permute-done.9 = s32[2,4,8,256]{3,2,1,0:T(8,128)S(1)} collective-permute-done((s32[2,4,8,256]{3,2,1,0:T(8,128)S(1)}, s32[2,4,8,256]{3,2,1,0:T(8,128)S(1)}, u32[]{:S(2)}, u32[]{:S(2)}) %collective-permute-start.9) | collective-permute-done | bytes 65568 | tf_op jit(solution)/shard_map/ppermute | solution.py:461
  44.1 0.0 collective-permute-done.8.refs_4_
  44.1 0.0 collective-permute-done.7.refs_3_
  44.1 0.0 collective-permute-start.13
  44.1 0.5 collective-permute-start.14
  44.7 0.5 collective-permute-start.10
  45.1 5.1 %collective-permute-done.10 = s32[4,4,8,256]{3,2,1,0:T(8,128)S(1)} collective-permute-done((s32[4,4,8,256]{3,2,1,0:T(8,128)S(1)}, s32[4,4,8,256]{3,2,1,0:T(8,128)S(1)}, u32[]{:S(2)}, u32[]{:S(2)}) %collective-permute-start.10) | collective-permute-done | bytes 131104 | tf_op jit(solution)/shard_map/ppermute | solution.py:461
  50.2 0.7 %pad_add_fusion.refs_0_ = s32[8,4,8,256]{3,2,1,0:T(8,128)} fusion(s32[4,4,8,256]{3,2,1,0:T(8,128)S(1)} %collective-permute-done.10, s32[2,4,8,256]{3,2,1,0:T(8,128)S(1)} %collective-permute-done.9, s32[1,4,8,256]{3,2,1,0:T(8,128)S(1)} %collective-permute-done.5, s32[1,4,8,256]{3,2,1,0:T(8,128)S(1)} %add_bitcast_fusion), kind=kLoop, calls=%fused_computation | loop fusion | flops 196608 | bytes 524288 | tf_op jit(solution)/shard_map/concatenate | solution.py:499
  50.9 0.0 collective-permute-done.11.refs_1_
  50.9 0.0 collective-permute-done.12.refs_2_
  50.9 0.0 collective-permute-done.13.refs_5_
  50.9 0.0 collective-permute-done.14.refs_6_
  50.9 16.8 %decode.1 = bf16[216,4,2560]{2,1,0:T(4,128)(2,1)} custom-call(s32[8,4,8,256]{3,2,1,0:T(8,128)} %pad_add_fusion.refs_0_, bf16[2688,128]{1,0:T(8,128)(2,1)} %collective-permute-done.11.refs_1_, bf16[2688,128]{1,0:T(8,128)(2,1)} %collective-permute-done.12.refs_2_, bf16[1344,128]{1,0:T(8,128)(2,1)} %collective-permute-done.7.refs_3_, ...), custom_call_target="tpu_custom_call" | custom-call | flops 2642411520 | bytes 4423680 | tf_op jit(solution)/shard_map/decode/pallas_call | solution.py:436
  (2 shorter events, 0.0 us)
Async XLA Ops:
  2.6 10.1 %collective-permute-start.2 = (s32[8,256]{1,0:T(8,128)}, s32[8,256]{1,0:T(8,128)S(1)}, u32[]{:S(2)}, u32[]{:S(2)}) collective-permute-start(s32[8,256]{1,0:T(8,128)} %get-tuple-element.26), channel_id=1, source_target_pairs={{0,24},{8,16},{16,8},{24,0},{1,25},{9,17},{17,9},{25,1},{2,26},{10... | collective-permute-start | bytes 24584 | tf_op jit(solution)/shard_map/ppermute | solution.py:461
  7.6 6.6 %collective-permute-start.1 = (s32[8,256]{1,0:T(8,128)}, s32[8,256]{1,0:T(8,128)S(1)}, u32[]{:S(2)}, u32[]{:S(2)}) collective-permute-start(s32[8,256]{1,0:T(8,128)} %get-tuple-element.26), channel_id=1, source_target_pairs={{0,16},{8,24},{16,0},{24,8},{1,17},{9,25},{17,1},{25,9},{2,18},{10... | collective-permute-start | bytes 24584 | tf_op jit(solution)/shard_map/ppermute | solution.py:461
  7.6 6.6 %collective-permute-start = (s32[8,256]{1,0:T(8,128)}, s32[8,256]{1,0:T(8,128)S(1)}, u32[]{:S(2)}, u32[]{:S(2)}) collective-permute-start(s32[8,256]{1,0:T(8,128)} %get-tuple-element.26), channel_id=1, source_target_pairs={{0,8},{8,0},{16,24},{24,16},{1,9},{9,1},{17,25},{25,17},{2,10},{10... | collective-permute-start | bytes 24584 | tf_op jit(solution)/shard_map/ppermute | solution.py:461
  8.2 27.5 %collective-permute-start.6 = (bf16[2688,128]{1,0:T(8,128)(2,1)}, bf16[2688,128]{1,0:T(8,128)(2,1)}, u32[]{:S(2)}, u32[]{:S(2)}) collective-permute-start(bf16[2688,128]{1,0:T(8,128)(2,1)} %get-tuple-element.36.packed_ref), channel_id=1, source_target_pairs={{0,1},{1,0},{2,3},{3,2},{4,5},{5,4},{6,7},{7,6},{8,9},{9,8},{10,11... | collective-permute-start | bytes 2064392 | tf_op jit(solution)/shard_map/ppermute | solution.py:461
  8.2 18.1 %collective-permute-start.4 = (bf16[2688,128]{1,0:T(8,128)(2,1)}, bf16[2688,128]{1,0:T(8,128)(2,1)S(1)}, u32[]{:S(2)}, u32[]{:S(2)}) collective-permute-start(bf16[2688,128]{1,0:T(8,128)(2,1)} %get-tuple-element.36.packed_ref), channel_id=1, source_target_pairs={{0,4},{1,5},{2,6},{3,7},{4,0},{5,1},{6,2},{7,3},{8,12},{9,13},{10,... | collective-permute-start | bytes 2064392 | tf_op jit(solution)/shard_map/ppermute | solution.py:461
  12.7 17.9 %collective-permute-start.3 = (bf16[2688,128]{1,0:T(8,128)(2,1)}, bf16[2688,128]{1,0:T(8,128)(2,1)}, u32[]{:S(2)}, u32[]{:S(2)}) collective-permute-start(bf16[2688,128]{1,0:T(8,128)(2,1)} %get-tuple-element.36.packed_ref), channel_id=1, source_target_pairs={{0,2},{1,3},{2,0},{3,1},{4,6},{5,7},{6,4},{7,5},{8,10},{9,11},{10,... | collective-permute-start | bytes 2064392 | tf_op jit(solution)/shard_map/ppermute | solution.py:461
  14.9 11.3 %collective-permute-start.5 = (s32[1,4,8,256]{3,2,1,0:T(8,128)S(1)}, s32[1,4,8,256]{3,2,1,0:T(8,128)S(1)}, u32[]{:S(2)}, u32[]{:S(2)}) collective-permute-start(s32[1,4,8,256]{3,2,1,0:T(8,128)S(1)} %add_bitcast_fusion), channel_id=1, source_target_pairs={{0,1},{1,0},{2,3},{3,2},{4,5},{5,4},{6,7},{7,6},{8,9},{9,8},{10,11... | collective-permute-start | bytes 98312 | tf_op jit(solution)/shard_map/ppermute | solution.py:461
  26.3 9.8 %copy-start = (bf16[2688,128]{1,0:T(8,128)(2,1)}, bf16[2688,128]{1,0:T(8,128)(2,1)S(1)}, u32[]{:S(2)}) copy-start(bf16[2688,128]{1,0:T(8,128)(2,1)S(1)} %collective-permute-done.4) | copy-start | bytes 2064388
  33.1 11.0 %collective-permute-start.8 = (bf16[1344,128]{1,0:T(8,128)(2,1)}, bf16[1344,128]{1,0:T(8,128)(2,1)}, u32[]{:S(2)}, u32[]{:S(2)}) collective-permute-start(bf16[1344,128]{1,0:T(8,128)(2,1)} %slice.7), channel_id=1, source_target_pairs={{0,2},{1,3},{2,0},{3,1},{4,6},{5,7},{6,4},{7,5},{8,10},{9,11},{10,... | collective-permute-start | bytes 1032200 | tf_op jit(solution)/shard_map/ppermute | solution.py:461
  34.6 9.5 %collective-permute-start.7 = (bf16[1344,128]{1,0:T(8,128)(2,1)}, bf16[1344,128]{1,0:T(8,128)(2,1)}, u32[]{:S(2)}, u32[]{:S(2)}) collective-permute-start(bf16[1344,128]{1,0:T(8,128)(2,1)} %slice.6), channel_id=1, source_target_pairs={{0,4},{1,5},{2,6},{3,7},{4,0},{5,1},{6,2},{7,3},{8,12},{9,13},{10,... | collective-permute-start | bytes 1032200 | tf_op jit(solution)/shard_map/ppermute | solution.py:461
  35.1 15.8 %collective-permute-start.11 = (bf16[2688,128]{1,0:T(8,128)(2,1)}, bf16[2688,128]{1,0:T(8,128)(2,1)}, u32[]{:S(2)}, u32[]{:S(2)}) collective-permute-start(bf16[2688,128]{1,0:T(8,128)(2,1)} %collective-permute-done.3), channel_id=1, source_target_pairs={{0,1},{1,0},{2,3},{3,2},{4,5},{5,4},{6,7},{7,6},{8,9},{9,8},{10,11... | collective-permute-start | bytes 2064392 | tf_op jit(solution)/shard_map/ppermute | solution.py:461
  35.1 15.8 %collective-permute-start.12 = (bf16[2688,128]{1,0:T(8,128)(2,1)S(1)}, bf16[2688,128]{1,0:T(8,128)(2,1)}, u32[]{:S(2)}, u32[]{:S(2)}) collective-permute-start(bf16[2688,128]{1,0:T(8,128)(2,1)S(1)} %collective-permute-done.4), channel_id=1, source_target_pairs={{0,1},{1,0},{2,3},{3,2},{4,5},{5,4},{6,7},{7,6},{8,9},{9,8},{10,11... | collective-permute-start | bytes 2064392 | tf_op jit(solution)/shard_map/ppermute | solution.py:461
  35.7 8.5 %collective-permute-start.9 = (s32[2,4,8,256]{3,2,1,0:T(8,128)S(1)}, s32[2,4,8,256]{3,2,1,0:T(8,128)S(1)}, u32[]{:S(2)}, u32[]{:S(2)}) collective-permute-start(s32[2,4,8,256]{3,2,1,0:T(8,128)S(1)} %pad_add_fusion.2), channel_id=1, source_target_pairs={{0,2},{1,3},{2,0},{3,1},{4,6},{5,7},{6,4},{7,5},{8,10},{9,11},{10,... | collective-permute-start | bytes 196616 | tf_op jit(solution)/shard_map/ppermute | solution.py:461
  44.1 6.8 %collective-permute-start.13 = (bf16[1344,128]{1,0:T(8,128)(2,1)}, bf16[1344,128]{1,0:T(8,128)(2,1)}, u32[]{:S(2)}, u32[]{:S(2)}) collective-permute-start(bf16[1344,128]{1,0:T(8,128)(2,1)} %collective-permute-done.7.refs_3_), channel_id=1, source_target_pairs={{0,1},{1,0},{2,3},{3,2},{4,5},{5,4},{6,7},{7,6},{8,9},{9,8},{10,11... | collective-permute-start | bytes 1032200 | tf_op jit(solution)/shard_map/ppermute | solution.py:461
  44.1 6.8 %collective-permute-start.14 = (bf16[1344,128]{1,0:T(8,128)(2,1)}, bf16[1344,128]{1,0:T(8,128)(2,1)}, u32[]{:S(2)}, u32[]{:S(2)}) collective-permute-start(bf16[1344,128]{1,0:T(8,128)(2,1)} %collective-permute-done.8.refs_4_), channel_id=1, source_target_pairs={{0,1},{1,0},{2,3},{3,2},{4,5},{5,4},{6,7},{7,6},{8,9},{9,8},{10,11... | collective-permute-start | bytes 1032200 | tf_op jit(solution)/shard_map/ppermute | solution.py:461
  44.7 5.5 %collective-permute-start.10 = (s32[4,4,8,256]{3,2,1,0:T(8,128)S(1)}, s32[4,4,8,256]{3,2,1,0:T(8,128)S(1)}, u32[]{:S(2)}, u32[]{:S(2)}) collective-permute-start(s32[4,4,8,256]{3,2,1,0:T(8,128)S(1)} %pad_add_fusion.1), channel_id=1, source_target_pairs={{0,4},{1,5},{2,6},{3,7},{4,0},{5,1},{6,2},{7,3},{8,12},{9,13},{10,... | collective-permute-start | bytes 393224 | tf_op jit(solution)/shard_map/ppermute | solution.py:461

commit v8 on v7

--- a/solution.py
+++ b/solution.py
@@ -131,19 +131,21 @@
     )(table, pokes)
 
 
-def gram_kernel(row_shape, surface_rows, codes_ref, words, own_signs, own_sums, packed_ref, gram_out, first_ref, gram_ref, semaphores):
-    mirror = pl.program_id(0)
+def gram_kernel(
+    row_shape, surface_rows, codes_ref, words, own_signs, own_sums, packed_ref, gram_out, first_ref, gram_ref,
+    even_bits, odd_bits, even_sums, odd_sums, semaphores
+):
     half = LANES // 2
     own, pokes = own_signs.shape
     planes = pokes // LANES
-    lines = codes_ref.shape[0] // row_shape[0]
-    height = gram_ref.shape[0] // row_shape[0]
-
-    def chunk(index, _):
+    chunks = gram_ref.shape[0] // WINDOW
+    pieces = 4
+    depth = pokes // pieces
+
+    def word_bytes(index):
         word = []
         for side in range(WINDOW // LANES):
-            line = mirror * lines + index * (WINDOW // LANES) + side
-            code = jnp.broadcast_to(codes_ref[pl.ds(line, 1), :], (8, LANES))
+            code = jnp.broadcast_to(codes_ref[pl.ds(index * (WINDOW // LANES) + side, 1), :], (8, LANES))
             value = None
             for bit in range(BITS):
                 mask = jnp.concatenate([code << (31 - bit) >> 31] * (half // 8), axis=0)
@@ -151,40 +153,65 @@
                 value = part if value is None else value ^ part
             word.append(value)
         word = jnp.concatenate(word, axis=1)
-        bits = [None] * (2 * planes)
-        for byte in range(0, 2 * planes, 8):
-            part = (word >> byte).astype(jnp.int8)
-            for bit in range(8):
-                at = byte + bit
-                hit = (part & np.uint8(1 << bit).astype(np.int8)) != 0
-                bits[at % planes * 2 + at // planes] = jnp.where(hit, NARROW(1.0), NARROW(0.0))
-        total = jnp.dot(own_signs[...], jnp.concatenate(bits, axis=0), preferred_element_type=jnp.float32)
-        sums = jnp.concatenate([own_sums[...]] * (WINDOW // LANES), axis=1)
-        turned = jnp.transpose((sums - 2.0 * total).astype(jnp.bfloat16))
-        at = pl.multiple_of(mirror * height + index * WINDOW, WINDOW)
-        gram_ref[pl.ds(at, WINDOW), :] = turned
+        return [(word >> byte).astype(jnp.int8) for byte in range(0, 2 * planes, 8)]
+
+    def make_bits(parts, piece, bits_ref):
+        for at in range(piece * planes // pieces, (piece + 1) * planes // pieces):
+            for upper in range(2):
+                plane = at + upper * planes
+                hit = (parts[plane // 8] & np.uint8(1 << plane % 8).astype(np.int8)) != 0
+                bits_ref[pl.ds((2 * at + upper) * half, half), :] = jnp.where(hit, NARROW(1.0), NARROW(0.0))
+
+    def finish(index, sums_ref, side):
+        lanes = slice(side * LANES, (side + 1) * LANES)
+        value = (own_sums[...] - 2.0 * sums_ref[:, lanes]).astype(jnp.bfloat16)
+        at = pl.multiple_of(index * WINDOW + side * LANES, LANES)
+        gram_ref[pl.ds(at, LANES), :] = jnp.transpose(value)
+
+    def product(index, bits_ref, sums_ref, next_bits, before, before_sums):
+        parts = None if next_bits is None else word_bytes(index + 1)
+        total = None
+        for piece in range(pieces):
+            part = jnp.dot(
+                own_signs[:, piece * depth:(piece + 1) * depth], bits_ref[pl.ds(piece * depth, depth), :],
+                preferred_element_type=jnp.float32,
+            )
+            total = part if total is None else total + part
+            if parts is not None:
+                make_bits(parts, piece, next_bits)
+            if before is not None and piece % 2 == 0:
+                finish(before, before_sums, piece // 2)
+        sums_ref[...] = total
+
+    parts = word_bytes(0)
+    for piece in range(pieces):
+        make_bits(parts, piece, even_bits)
+    product(0, even_bits, even_sums, odd_bits, None, None)
+
+    def pair(step, _):
+        index = 2 * step + 1
+        product(index, odd_bits, odd_sums, even_bits, index - 1, even_sums)
+        product(index + 1, even_bits, even_sums, odd_bits, index, odd_sums)
         return 0
 
-    lax.fori_loop(0, height // WINDOW, chunk, 0, unroll=3)
-
-    def send(k):
-        part = pl.ds(pl.multiple_of(k * height, height), height)
-        return pltpu.make_async_copy(gram_ref.at[part], gram_out.at[part], semaphores.at[k])
-
-    send(mirror).start()
+    pairs = (chunks - 2) // 2
+    lax.fori_loop(0, pairs, pair, 0)
+    buffers = [(even_bits, even_sums), (odd_bits, odd_sums)]
+    for index in range(2 * pairs + 1, chunks):
+        bits_ref, sums_ref = buffers[index % 2]
+        next_bits = buffers[(index + 1) % 2][0] if index + 1 < chunks else None
+        product(index, bits_ref, sums_ref, next_bits, index - 1, buffers[(index - 1) % 2][1])
+    for side in range(WINDOW // LANES):
+        finish(chunks - 1, buffers[(chunks - 1) % 2][1], side)
+
+    copies = fetch_gram(gram_ref, gram_out, semaphores, row_shape[0])
+    for copy in copies:
+        copy.start()
     block = lax.axis_index("row")
-    for l in range(row_shape[1]):
-        for k in range(row_shape[0]):
-            @pl.when(mirror == k)
-            def _():
-                first_ref[0, l] = band_product(
-                    [packed_ref], k * row_shape[1] + l, row_shape, block, surface_rows, gram_ref
-                )
-
-    @pl.when(mirror == pl.num_programs(0) - 1)
-    def _():
-        for k in range(row_shape[0]):
-            send(k).wait()
+    for q in range(row_shape[0] * row_shape[1]):
+        first_ref[0, q] = band_product([packed_ref], q, row_shape, block, surface_rows, gram_ref)
+    for copy in copies:
+        copy.wait()
 
 
 def gram(codes, words, own_signs, own_sums, packed, row_shape, surface_rows):
@@ -193,17 +220,20 @@
     vmem = pl.BlockSpec(memory_space=pltpu.VMEM)
     return pl.pallas_call(
         functools.partial(gram_kernel, row_shape, surface_rows),
-        grid=(mirrors,),
         out_shape=[
             jax.ShapeDtypeStruct((acts, own), jnp.bfloat16),
             jax.ShapeDtypeStruct((1, mirrors * shard_rows, samples, own), jnp.bfloat16),
         ],
         in_specs=[vmem] * 5,
-        out_specs=[
-            pl.BlockSpec(memory_space=pl.ANY),
-            pl.BlockSpec((1, shard_rows, samples, own), lambda s: (0, s, 0, 0)),
+        out_specs=[pl.BlockSpec(memory_space=pl.ANY), vmem],
+        scratch_shapes=[
+            pltpu.VMEM((acts, own), jnp.bfloat16),
+            pltpu.VMEM((count, WINDOW), NARROW),
+            pltpu.VMEM((count, WINDOW), NARROW),
+            pltpu.VMEM((own, WINDOW), jnp.float32),
+            pltpu.VMEM((own, WINDOW), jnp.float32),
+            pltpu.SemaphoreType.DMA((mirrors,)),
         ],
-        scratch_shapes=[pltpu.VMEM((acts, own), jnp.bfloat16), pltpu.SemaphoreType.DMA((mirrors,))],
         compiler_params=pltpu.CompilerParams(vmem_limit_bytes=VMEM_BYTES),
         cost_estimate=pl.CostEstimate(
             flops=2 * own * acts * count, bytes_accessed=2 * own * acts, transcendentals=0
@@ -219,14 +249,28 @@
 def row_block(place, staged):
     if not staged:
         return place
-    return (place ^ 7 if place in (3, 4) else place) ^ lax.axis_index("row")
+    row = lax.axis_index("row")
+    core = row & 1
+    return row ^ [0, 1, 2 << core, 4 >> core, (4 >> core) | 1, (2 << core) | 1, 6, 7][place]
 
 
 def row_place(block, staged):
     if not staged:
         return block
-    place = block ^ lax.axis_index("row")
-    return jnp.where((place == 3) | (place == 4), place ^ 7, place)
+    row = lax.axis_index("row")
+    core = row & 1
+    distance = block ^ row
+    near = jnp.where(distance == 2 << core, 2, 3)
+    far = jnp.where(distance == (4 >> core) | 1, 4, 5)
+    middle = jnp.where(distance & 1 == 0, near, far)
+    return jnp.where((distance >= 2) & (distance < 6), middle, distance)
+
+
+def lines_place(block, staged):
+    if not staged:
+        return block
+    distance = block ^ lax.axis_index("row")
+    return (distance >> 1 & 1) * 4 + (distance >> 2) * 2 + (distance & 1)
 
 
 def band_product(parts, q, row_shape, block, surface_rows, gram_ref):
@@ -343,6 +387,7 @@
     late_blocks, refs = refs[:counts[0]], refs[counts[0]:]
     gram_semaphores, ready_semaphores, late_semaphores, scalar_semaphore = refs
     group = pl.program_id(0)
+    groups = pl.num_programs(0) - 1
     directions, pupil = differences.shape[0], 2 * differences.shape[2]
     phases = out_ref.shape[2] // pupil
     blocks = surface_rows // shard_rows
@@ -387,38 +432,62 @@
         for copy in ready_copies:
             copy.wait()
 
-    for d in range(directions):
-        held = d ^ position("dir", staged)
-        products, factors = [], []
-        for phase in range(phases):
-            i = group * phases + phase
-            block = (2 * i // shard_rows) ^ position("row", staged)
-            sums, changes = [], []
-            for k in range(mirrors):
-                picked = []
-                for y in range(2):
-                    row = scalars[block, held, k * shard_rows + (2 * phase + y) % shard_rows]
-                    picked.append(decoded[row_place(row // shard_rows, staged), k * shard_rows + row % shard_rows])
-                sums.append(picked[0] + picked[1])
-                changes.append(picked[1] - picked[0])
-            for kind, rows in enumerate((sums, changes)):
-                products.append(
-                    jnp.dot(
-                        differences[held, kind], jnp.concatenate(rows, axis=0), preferred_element_type=jnp.float32
+    tiles = out_ref.shape[2] // LANES
+
+    def relayout(slot, tile):
+        value = total[slot, tile].reshape(own, directions, LANES)
+        out_ref[:, :, tile * LANES:(tile + 1) * LANES] = value.astype(out_ref.dtype)
+
+    @pl.when(group < groups)
+    def _():
+        slot = lax.rem(group, 2)
+        waiting = []
+        for d in range(directions):
+            held = d ^ position("dir", staged)
+            products, factors = [], []
+            for phase in range(phases):
+                i = group * phases + phase
+                block = lines_place(2 * i // shard_rows, staged)
+                sums, changes = [], []
+                for k in range(mirrors):
+                    picked = []
+                    for y in range(2):
+                        row = scalars[block, held, k * shard_rows + (2 * phase + y) % shard_rows]
+                        picked.append(decoded[row_place(row // shard_rows, staged), k * shard_rows + row % shard_rows])
+                    sums.append(picked[0] + picked[1])
+                    changes.append(picked[1] - picked[0])
+                for kind, rows in enumerate((sums, changes)):
+                    products.append(
+                        jnp.dot(
+                            differences[held, kind], jnp.concatenate(rows, axis=0), preferred_element_type=jnp.float32
+                        )
                     )
-                )
-            line = mirrors + phase % (shard_rows // 2)
-            valid = lines_ref[block, held, line:line + 1, :pupil // 2]
-            factors += [valid.astype(jnp.float32) * norm] * 2
-        product = jnp.concatenate(products, axis=0)
-        factor = jnp.concatenate(factors, axis=1)
-        for tile in range(out_ref.shape[2] // LANES):
-            at = tile * LANES
-            value = jnp.transpose(product[at:at + LANES])[:own] * factor[:, at:at + LANES]
-            total[tile, pl.ds(d, own, stride=directions), :] = value
-    for tile in range(out_ref.shape[2] // LANES):
-        value = total[tile].reshape(own, directions, LANES)
-        out_ref[:, :, tile * LANES:(tile + 1) * LANES] = value.astype(out_ref.dtype)
+                line = mirrors + phase % (shard_rows // 2)
+                valid = lines_ref[block, held, line:line + 1, :pupil // 2]
+                factors += [valid.astype(jnp.float32) * norm] * 2
+                for _ in range(-(-len(waiting) // (phases - phase))):
+                    waiting.pop(0)()
+            product = jnp.concatenate(products, axis=0)
+            factor = jnp.concatenate(factors, axis=1)
+
+            def turn(tile, d, product, factor):
+                at = tile * LANES
+                value = jnp.transpose(product[at:at + LANES])[:own] * factor[:, at:at + LANES]
+                total[slot, tile, pl.ds(d, own, stride=directions), :] = value
+
+            waiting = [functools.partial(turn, tile, d, product, factor) for tile in range(tiles)]
+            if d < directions - 1:
+                waiting += [
+                    functools.partial(relayout, 1 - slot, tile)
+                    for tile in range(d * tiles // (directions - 1), (d + 1) * tiles // (directions - 1))
+                ]
+        for last in waiting:
+            last()
+
+    @pl.when(group == groups)
+    def _():
+        for tile in range(tiles):
+            relayout(lax.rem(group + 1, 2), tile)
 
 
 def decode(lines, late, ready, gram_rows, own, row_shape, surface_rows, pupil, norm, staged):
@@ -437,15 +506,15 @@
         functools.partial(
             decode_kernel, row_shape, surface_rows, own, staged, norm, counts, [len(block) for block in late]
         ),
-        grid=(width // lanes,),
+        grid=(width // lanes + 1,),
         out_shape=jax.ShapeDtypeStruct((own, directions, width), jnp.bfloat16),
         in_specs=[vmem] + [anywhere] * (sum(counts) + 1),
-        out_specs=pl.BlockSpec((own, directions, lanes), lambda s: (0, 0, s)),
+        out_specs=pl.BlockSpec((own, directions, lanes), lambda s: (0, 0, jnp.maximum(s - 1, 0))),
         scratch_shapes=[
             pltpu.VMEM((acts, padded), jnp.bfloat16),
             pltpu.VMEM((blocks, mirrors * shard_rows, samples, padded), jnp.bfloat16),
             pltpu.VMEM((directions, 2, pupil // 2, mirrors * samples), jnp.bfloat16),
-            pltpu.VMEM((lanes // LANES, own * directions, LANES), jnp.float32),
+            pltpu.VMEM((2, lanes // LANES, own * directions, LANES), jnp.float32),
             pltpu.VMEM((blocks, -(-directions // 8) * 8, LANES), jnp.int32),
             pltpu.SMEM((blocks, -(-directions // 8) * 8, LANES), jnp.int32),
             *[pltpu.VMEM(part.shape, part.dtype) for part in parts],
@@ -459,6 +528,12 @@
 
 def swap(block, axis, distance):
     return lax.ppermute(block, axis, [(i, i ^ distance) for i in range(lax.axis_size(axis))])
+
+
+def turn(block, even, odd):
+    return lax.ppermute(
+        block, "row", [(i, i ^ (odd if i % 2 else even)) for i in range(lax.axis_size("row"))]
+    )
 
 
 def shards(influence, foot_rows, foot_columns, actuator_codes, poke_rows, subaperture_valid):
@@ -480,25 +555,24 @@
         ready = [bands(gram_rows, [every], 0, staged, row_shape, surface_rows)]
         return decode(lines, [], ready, gram_rows, own, row_shape, surface_rows, pupil, norm, staged)
 
-    beside, across, sibling = (swap(packed, "row", distance) for distance in (2, 4, 1))
+    first, second = turn(packed, 2, 4), turn(packed, 4, 2)
+    sibling = swap(packed, "row", 1)
     lines = jnp.stack([lines] + [swap(lines, "dir", e) for e in range(1, directions)])[None]
     sides = own_side(actuator_codes, pokes, own)
     lines, sides = lax.optimization_barrier((lines, sides))
-    more = swap(lines, "row", 1)
-    gram_rows, first = gram(*sides, packed, row_shape, surface_rows)
-    gram_rows, beside, across, more = lax.optimization_barrier((gram_rows, beside, across, more))
+    lines = [lines] + [swap(lines, "row", distance) for distance in (1, 4, 5)]
+    gram_rows, own_rows = gram(*sides, packed, row_shape, surface_rows)
+    gram_rows, first, second, lines = lax.optimization_barrier((gram_rows, first, second, lines))
+    lines = jnp.concatenate(lines, axis=0)
+    diagonal = turn(first, 4, 2)
+    first_sibling, second_sibling = swap(first, "row", 1), swap(second, "row", 1)
+    more = swap(lines, "row", 2)
+    sources = [source[None] for source in (sibling, first, second)]
+    ready = bands(gram_rows, sources, 1, staged, row_shape, surface_rows)
+    ready, diagonal, more = lax.optimization_barrier((ready, diagonal, more))
     lines = jnp.concatenate([lines, more], axis=0)
-    more = swap(lines, "row", 2)
-    half = packed.shape[0] // 2
-    upper, lower = swap(beside[:half], "row", 4), swap(across[half:], "row", 2)
-    beside_sibling, across_sibling = swap(beside, "row", 1), swap(across, "row", 1)
-    sources = [source[None] for source in (sibling, beside, across)]
-    ready = bands(gram_rows, sources, 1, staged, row_shape, surface_rows)
-    ready, upper, lower, more = lax.optimization_barrier((ready, upper, lower, more))
-    lines = jnp.concatenate([lines, more], axis=0)
-    lines = jnp.concatenate([lines, swap(lines, "row", 4)], axis=0)
-    late = [[beside_sibling], [across_sibling], [upper, lower], [swap(upper, "row", 1), swap(lower, "row", 1)]]
-    return decode(lines, late, [first, ready], gram_rows, own, row_shape, surface_rows, pupil, norm, staged)
+    late = [[block] for block in (first_sibling, second_sibling, diagonal, swap(diagonal, "row", 1))]
+    return decode(lines, late, [own_rows, ready], gram_rows, own, row_shape, surface_rows, pupil, norm, staged)
 
 
 def solution(mesh):

time: 68.1 us -> 74.2 us (1.090)
  starting transfers between devices: 12.7 us -> 16.5 us
  local copies, waits for them, and re-layouts: 2.54 us -> 3.88 us
  Pallas kernels: 38.8 us -> 39.6 us
    ppermute x0 -> x3, starting transfers between devices: none -> 4.82 us  [turn(): lax.ppermute(block, 'row', [(i, i ^ (odd if i % 2 else even)) for i in ra...]
    ppermute x0 -> x3, waiting for transfers between devices: none -> 3.21 us  [turn(): lax.ppermute(block, 'row', [(i, i ^ (odd if i % 2 else even)) for i in ra...]
    unnamed x2 -> x16, local copies, waits for them, and re-layouts: 0.01 us -> 2.96 us
    ppermute x15 -> x11, waiting for transfers between devices: 12.2 us -> 9.6 us  [swap(): lax.ppermute(block, axis, [(i, i ^ distance) for i in range(lax.axis_size...]
    slice x2 -> x0, local copies, waits for them, and re-layouts: 2.54 us -> none  [the longest x1 1.74 us: shards(): beside[:half]]
    ppermute x15 -> x11, starting transfers between devices: 12.7 us -> 11.7 us  [swap(): lax.ppermute(block, axis, [(i, i ^ distance) for i in range(lax.axis_size...]
    concatenate x0 -> x1, local copies, waits for them, and re-layouts: none -> 0.91 us  [shards(): lines = jnp.concatenate([lines, more], axis=0)]
  transfers between devices with their start and end apart: 15 -> 14, of which waited for: 3 -> 3; matrix products, arithmetic and copies ran while one was open for 6% -> 5% of each run, Pallas kernels for 29% -> 27%
where the time goes in v8:
time: 74.2 us; the launch traced here: 73.7 us
  Pallas kernels  39.6 us (53%)
  starting transfers between devices  16.5 us (22%)
  waiting for transfers between devices  12.8 us (17%)
  local copies, waits for them, and re-layouts  3.88 us (5%)
    pallas_call x1, Pallas kernels, decode(): pl.pallas_call(functools.partial(decode_kernel, row_shape, surface_rows,...  17.5 us
    ppermute x11, starting transfers between devices, swap(): lax.ppermute(block, axis, [(i, i ^ distance) for i in range(lax.axis_size...  11.7 us
    pallas_call x1, Pallas kernels, gram(): pl.pallas_call(functools.partial(gram_kernel, row_shape, surface_rows), o...  11.5 us
    ppermute x11, waiting for transfers between devices, swap(): lax.ppermute(block, axis, [(i, i ^ distance) for i in range(lax.axis_size...  9.6 us
    pallas_call x1, Pallas kernels, bands(): pl.pallas_call(functools.partial(bands_kernel, row_shape, surface_rows, f...  5.26 us
    ppermute x3, starting transfers between devices, turn(): lax.ppermute(block, 'row', [(i, i ^ (odd if i % 2 else even)) for i in ra...  4.82 us
    ppermute x3, waiting for transfers between devices, turn(): lax.ppermute(block, 'row', [(i, i ^ (odd if i % 2 else even)) for i in ra...  3.21 us
    unnamed x16, local copies, waits for them, and re-layouts  2.96 us
  transfers between devices with their start and end apart: 14, of which 3 were waited for; matrix products, arithmetic and copies ran while one was open for 5% of the time, Pallas kernels for 27%

profile of v8, /device:TPU:0, one launch (start us, length us, event | category | flops | bytes accessed | tf_op | source)
XLA Modules:
  0.0 73.7 jit_solution(265307623875563733)
XLA Ops:
  0.0 2.6 %pack_influence.1 = (bf16[2688,128]{1,0:T(8,128)(2,1)}, s32[8,256]{1,0:T(8,128)}) custom-call(bf16[3,4,144,192]{3,2,1,0:T(8,128)(2,1)} %bitcast.13, s32[3,1,4]{2,1,0:T(1,128)} %bitcast.21, s32[3,1,160]{2,1,0:T(1,128)} %bitcast.20, s32[1,2,80]{2,1,0:T(2,128)} %valid_ref.1), custom_call_target="tpu_custom_call" | custom-call | bytes 995328 | tf_op jit(solution)/shard_map/pack_influence/pallas_call | solution.py:55
  2.6 5.1 %collective-permute-start.2 = (s32[8,256]{1,0:T(8,128)}, s32[8,256]{1,0:T(8,128)S(1)}, u32[]{:S(2)}, u32[]{:S(2)}) collective-permute-start(s32[8,256]{1,0:T(8,128)} %get-tuple-element.28), channel_id=1, source_target_pairs={{0,24},{8,16},{16,8},{24,0},{1,25},{9,17},{17,9},{25,1},{2,26},{10... | collective-permute-start | bytes 24584 | tf_op jit(solution)/shard_map/ppermute | solution.py:530
  7.6 0.0 collective-permute-start.1
  7.6 0.6 collective-permute-start
  8.2 1.7 %collective-permute-start.4 = (bf16[2688,128]{1,0:T(8,128)(2,1)}, bf16[2688,128]{1,0:T(8,128)(2,1)S(1)}, u32[]{:S(2)}, u32[]{:S(2)}) collective-permute-start(bf16[2688,128]{1,0:T(8,128)(2,1)} %get-tuple-element.37.packed_ref), channel_id=1, source_target_pairs={{0,4},{1,3},{2,6},{3,1},{4,0},{5,7},{6,2},{7,5},{8,12},{9,11},{10,... | collective-permute-start | bytes 2064392 | tf_op jit(solution)/shard_map/ppermute | solution.py:534
  9.9 1.5 %collective-permute-start.3 = (bf16[2688,128]{1,0:T(8,128)(2,1)}, bf16[2688,128]{1,0:T(8,128)(2,1)}, u32[]{:S(2)}, u32[]{:S(2)}) collective-permute-start(bf16[2688,128]{1,0:T(8,128)(2,1)} %get-tuple-element.37.packed_ref), channel_id=1, source_target_pairs={{0,2},{1,5},{2,0},{3,7},{4,6},{5,1},{6,4},{7,3},{8,10},{9,13},{10,... | collective-permute-start | bytes 2064392 | tf_op jit(solution)/shard_map/ppermute | solution.py:534
  11.4 2.8 %own_signs.1 = (s32[54,128]{1,0:T(8,128)}, s32[13,64,128]{2,1,0:T(8,128)}, f8e5m2[224,2048]{1,0:T(32,128)(4,1)}, f32[224,128]{1,0:T(8,128)}) custom-call(s32[3,48,48]{2,1,0:T(8,128)} %table_ref.1, s32[16,128]{1,0:T(8,128)} %bitcast.15), custom_call_target="tpu_custom_call" | custom-call | tf_op jit(solution)/shard_map/own_signs/pallas_call | solution.py:119
  14.2 0.0 collective-permute-done.2
  14.2 0.0 collective-permute-done.1
  14.2 0.0 collective-permute-done
  14.2 0.7 add_bitcast_fusion
  14.9 0.0 collective-permute-start.7
  14.9 0.6 collective-permute-start.8
  15.5 1.5 %collective-permute-start.6 = (s32[1,4,8,256]{3,2,1,0:T(8,128)S(1)}, s32[1,4,8,256]{3,2,1,0:T(8,128)S(1)}, u32[]{:S(2)}, u32[]{:S(2)}) collective-permute-start(s32[1,4,8,256]{3,2,1,0:T(8,128)S(1)} %add_bitcast_fusion), channel_id=1, source_target_pairs={{0,4},{1,5},{2,6},{3,7},{4,0},{5,1},{6,2},{7,3},{8,12},{9,13},{10,... | collective-permute-start | bytes 98312 | tf_op jit(solution)/shard_map/ppermute | solution.py:530
  17.1 9.5 %collective-permute-done.7 = s32[1,4,8,256]{3,2,1,0:T(8,128)S(1)} collective-permute-done((s32[1,4,8,256]{3,2,1,0:T(8,128)S(1)}, s32[1,4,8,256]{3,2,1,0:T(8,128)S(1)}, u32[]{:S(2)}, u32[]{:S(2)}) %collective-permute-start.7) | collective-permute-done | bytes 32800 | tf_op jit(solution)/shard_map/ppermute | solution.py:530
  26.5 0.6 collective-permute-start.5
  27.1 11.5 %gram_rows.1 = (bf16[6912,224]{1,0:T(8,128)(2,1)}, bf16[1,12,192,224]{3,2,1,0:T(8,128)(2,1)}) custom-call(s32[54,128]{1,0:T(8,128)} %get-tuple-element.33.codes_ref, s32[13,64,128]{2,1,0:T(8,128)} %get-tuple-element.34.words, f8e5m2[224,2048]{1,0:T(32,128)(4,1)} %get-tuple-element.35.own_signs, f32[224,128]{1,0:T(8,128)} %get-tuple-element.36.own_sums, ...), custom_call_target="tpu_custom_call" | custom-call | flops 6341787648 | bytes 3096576 | tf_op jit(solution)/shard_map/gram_rows/pallas_call | solution.py:221
  38.6 0.0 collective-permute-done.6
  38.6 0.0 copy-start.4
  38.7 0.0 collective-permute-done.5
  38.7 0.0 copy-start.5
  38.7 0.0 collective-permute-done.4
  38.7 0.0 copy-start
  38.7 0.0 collective-permute-done.3
  38.7 1.6 %collective-permute-start.9 = (bf16[2688,128]{1,0:T(8,128)(2,1)}, bf16[2688,128]{1,0:T(8,128)(2,1)}, u32[]{:S(2)}, u32[]{:S(2)}) collective-permute-start(bf16[2688,128]{1,0:T(8,128)(2,1)} %collective-permute-done.3), channel_id=1, source_target_pairs={{0,4},{1,3},{2,6},{3,1},{4,0},{5,7},{6,2},{7,5},{8,12},{9,11},{10,... | collective-permute-start | bytes 2064392 | tf_op jit(solution)/shard_map/ppermute | solution.py:534
  40.3 0.0 copy-done.3
  40.3 0.0 copy-done.4
  40.3 0.0 copy-done.5
  40.3 0.6 collective-permute-start.10
  40.9 0.0 collective-permute-start.11
  40.9 0.5 collective-permute-start.12
  41.4 0.0 collective-permute-done.8
  41.4 0.0 copy-done
  41.4 5.3 %bands.1.refs_6_ = bf16[3,12,192,224]{3,2,1,0:T(8,128)(2,1)} custom-call(bf16[6912,224]{1,0:T(8,128)(2,1)} %get-tuple-element.44.gram_any.refs_7_, bf16[1,2688,128]{2,1,0:T(8,128)(2,1)} %bitcast.9.refs_0_, bf16[1,2688,128]{2,1,0:T(8,128)(2,1)} %bitcast.10.refs_1_, bf16[1,2688,128]{2,1,0:T(8,128)(2,1)} %bitcast.14), custom_call_target="tpu_custom_call" | custom-call | flops 792723456 | bytes 4128768 | tf_op jit(solution)/shard_map/bands/pallas_call | solution.py:342
  46.7 0.1 collective-permute-done.10
  46.8 3.2 %collective-permute-done.9.refs_3_ = bf16[2688,128]{1,0:T(8,128)(2,1)} collective-permute-done((bf16[2688,128]{1,0:T(8,128)(2,1)}, bf16[2688,128]{1,0:T(8,128)(2,1)}, u32[]{:S(2)}, u32[]{:S(2)}) %collective-permute-start.9) | collective-permute-done | bytes 688160 | tf_op jit(solution)/shard_map/ppermute | solution.py:534
  50.0 0.0 copy-done.2
  50.0 2.2 %collective-permute-start.13 = (bf16[2688,128]{1,0:T(8,128)(2,1)}, bf16[2688,128]{1,0:T(8,128)(2,1)}, u32[]{:S(2)}, u32[]{:S(2)}) collective-permute-start(bf16[2688,128]{1,0:T(8,128)(2,1)} %collective-permute-done.9.refs_3_), channel_id=1, source_target_pairs={{0,1},{1,0},{2,3},{3,2},{4,5},{5,4},{6,7},{7,6},{8,9},{9,8},{10,11... | collective-permute-start | bytes 2064392 | tf_op jit(solution)/shard_map/ppermute | solution.py:530
  52.3 0.8 %constant_dynamic-update-slice_fusion.3 = s32[8,4,8,256]{3,2,1,0:T(8,128)S(1)} fusion(s32[8,4,8,256]{3,2,1,0:T(8,128)S(1)} %constant_dynamic-update-slice_fusion.4, s32[1,4,8,256]{3,2,1,0:T(8,128)} %copy-done.5), kind=kLoop, calls=%fused_computation.5 | loop fusion | bytes 65536
  53.0 0.8 %constant_dynamic-update-slice_fusion.2 = s32[8,4,8,256]{3,2,1,0:T(8,128)S(1)} fusion(s32[8,4,8,256]{3,2,1,0:T(8,128)S(1)} %constant_dynamic-update-slice_fusion.3, s32[1,4,8,256]{3,2,1,0:T(8,128)} %copy-done.4), kind=kLoop, calls=%fused_computation.4 | loop fusion | bytes 65536
  53.8 0.8 %constant_dynamic-update-slice_fusion.1 = s32[8,4,8,256]{3,2,1,0:T(8,128)S(1)} fusion(s32[8,4,8,256]{3,2,1,0:T(8,128)S(1)} %constant_dynamic-update-slice_fusion.2, s32[1,4,8,256]{3,2,1,0:T(8,128)} %copy-done.3), kind=kLoop, calls=%fused_computation.3 | loop fusion | bytes 65536
  54.5 0.9 %constant_dynamic-update-slice_fusion.refs_0_ = s32[8,4,8,256]{3,2,1,0:T(8,128)S(1)} fusion(s32[8,4,8,256]{3,2,1,0:T(8,128)S(1)} %constant_dynamic-update-slice_fusion.1, s32[4,4,8,256]{3,2,1,0:T(8,128)} %copy-done.2), kind=kLoop, calls=%fused_computation.2 | loop fusion | bytes 262144 | tf_op jit(solution)/shard_map/concatenate | solution.py:573
  55.5 0.0 copy-start.1
  55.5 0.0 collective-permute-done.12.refs_2_
  55.5 0.0 collective-permute-done.11.refs_1_
  55.5 0.0 collective-permute-done.13.refs_4_
  55.5 0.7 copy-done.1
  56.2 17.5 %decode.1 = bf16[216,4,2560]{2,1,0:T(4,128)(2,1)} custom-call(s32[8,4,8,256]{3,2,1,0:T(8,128)} %copy-done.1, bf16[2688,128]{1,0:T(8,128)(2,1)} %collective-permute-done.11.refs_1_, bf16[2688,128]{1,0:T(8,128)(2,1)} %collective-permute-done.12.refs_2_, bf16[2688,128]{1,0:T(8,128)(2,1)} %collective-permute-done.9.refs_3_, ...), custom_call_target="tpu_custom_call" | custom-call | flops 2642411520 | bytes 4423680 | tf_op jit(solution)/shard_map/decode/pallas_call | solution.py:505
  (4 shorter events, 0.0 us)
Async XLA Ops:
  2.6 11.6 %collective-permute-start.2 = (s32[8,256]{1,0:T(8,128)}, s32[8,256]{1,0:T(8,128)S(1)}, u32[]{:S(2)}, u32[]{:S(2)}) collective-permute-start(s32[8,256]{1,0:T(8,128)} %get-tuple-element.28), channel_id=1, source_target_pairs={{0,24},{8,16},{16,8},{24,0},{1,25},{9,17},{17,9},{25,1},{2,26},{10... | collective-permute-start | bytes 24584 | tf_op jit(solution)/shard_map/ppermute | solution.py:530
  7.6 6.6 %collective-permute-start.1 = (s32[8,256]{1,0:T(8,128)}, s32[8,256]{1,0:T(8,128)S(1)}, u32[]{:S(2)}, u32[]{:S(2)}) collective-permute-start(s32[8,256]{1,0:T(8,128)} %get-tuple-element.28), channel_id=1, source_target_pairs={{0,16},{8,24},{16,0},{24,8},{1,17},{9,25},{17,1},{25,9},{2,18},{10... | collective-permute-start | bytes 24584 | tf_op jit(solution)/shard_map/ppermute | solution.py:530
  7.6 6.6 %collective-permute-start = (s32[8,256]{1,0:T(8,128)}, s32[8,256]{1,0:T(8,128)S(1)}, u32[]{:S(2)}, u32[]{:S(2)}) collective-permute-start(s32[8,256]{1,0:T(8,128)} %get-tuple-element.28), channel_id=1, source_target_pairs={{0,8},{8,0},{16,24},{24,16},{1,9},{9,1},{17,25},{25,17},{2,10},{10... | collective-permute-start | bytes 24584 | tf_op jit(solution)/shard_map/ppermute | solution.py:530
  8.2 30.5 %collective-permute-start.4 = (bf16[2688,128]{1,0:T(8,128)(2,1)}, bf16[2688,128]{1,0:T(8,128)(2,1)S(1)}, u32[]{:S(2)}, u32[]{:S(2)}) collective-permute-start(bf16[2688,128]{1,0:T(8,128)(2,1)} %get-tuple-element.37.packed_ref), channel_id=1, source_target_pairs={{0,4},{1,3},{2,6},{3,1},{4,0},{5,7},{6,2},{7,5},{8,12},{9,11},{10,... | collective-permute-start | bytes 2064392 | tf_op jit(solution)/shard_map/ppermute | solution.py:534
  9.9 28.8 %collective-permute-start.3 = (bf16[2688,128]{1,0:T(8,128)(2,1)}, bf16[2688,128]{1,0:T(8,128)(2,1)}, u32[]{:S(2)}, u32[]{:S(2)}) collective-permute-start(bf16[2688,128]{1,0:T(8,128)(2,1)} %get-tuple-element.37.packed_ref), channel_id=1, source_target_pairs={{0,2},{1,5},{2,0},{3,7},{4,6},{5,1},{6,4},{7,3},{8,10},{9,13},{10,... | collective-permute-start | bytes 2064392 | tf_op jit(solution)/shard_map/ppermute | solution.py:534
  14.9 11.6 %collective-permute-start.7 = (s32[1,4,8,256]{3,2,1,0:T(8,128)S(1)}, s32[1,4,8,256]{3,2,1,0:T(8,128)S(1)}, u32[]{:S(2)}, u32[]{:S(2)}) collective-permute-start(s32[1,4,8,256]{3,2,1,0:T(8,128)S(1)} %add_bitcast_fusion), channel_id=1, source_target_pairs={{0,5},{1,4},{2,7},{3,6},{4,1},{5,0},{6,3},{7,2},{8,13},{9,12},{10,... | collective-permute-start | bytes 98312 | tf_op jit(solution)/shard_map/ppermute | solution.py:530
  14.9 26.5 %collective-permute-start.8 = (bf16[2688,128]{1,0:T(8,128)(2,1)}, bf16[2688,128]{1,0:T(8,128)(2,1)}, u32[]{:S(2)}, u32[]{:S(2)}) collective-permute-start(bf16[2688,128]{1,0:T(8,128)(2,1)} %get-tuple-element.37.packed_ref), channel_id=1, source_target_pairs={{0,1},{1,0},{2,3},{3,2},{4,5},{5,4},{6,7},{7,6},{8,9},{9,8},{10,11... | collective-permute-start | bytes 2064392 | tf_op jit(solution)/shard_map/ppermute | solution.py:530
  15.5 23.1 %collective-permute-start.6 = (s32[1,4,8,256]{3,2,1,0:T(8,128)S(1)}, s32[1,4,8,256]{3,2,1,0:T(8,128)S(1)}, u32[]{:S(2)}, u32[]{:S(2)}) collective-permute-start(s32[1,4,8,256]{3,2,1,0:T(8,128)S(1)} %add_bitcast_fusion), channel_id=1, source_target_pairs={{0,4},{1,5},{2,6},{3,7},{4,0},{5,1},{6,2},{7,3},{8,12},{9,13},{10,... | collective-permute-start | bytes 98312 | tf_op jit(solution)/shard_map/ppermute | solution.py:530
  26.5 13.8 %copy-start.3 = (s32[1,4,8,256]{3,2,1,0:T(8,128)}, s32[1,4,8,256]{3,2,1,0:T(8,128)S(1)}, u32[]{:S(2)}) copy-start(s32[1,4,8,256]{3,2,1,0:T(8,128)S(1)} %collective-permute-done.7) | copy-start | bytes 98308
  26.5 12.1 %collective-permute-start.5 = (s32[1,4,8,256]{3,2,1,0:T(8,128)S(1)}, s32[1,4,8,256]{3,2,1,0:T(8,128)S(1)}, u32[]{:S(2)}, u32[]{:S(2)}) collective-permute-start(s32[1,4,8,256]{3,2,1,0:T(8,128)S(1)} %add_bitcast_fusion), channel_id=1, source_target_pairs={{0,1},{1,0},{2,3},{3,2},{4,5},{5,4},{6,7},{7,6},{8,9},{9,8},{10,11... | collective-permute-start | bytes 98312 | tf_op jit(solution)/shard_map/ppermute | solution.py:530
  38.6 1.7 %copy-start.4 = (s32[1,4,8,256]{3,2,1,0:T(8,128)}, s32[1,4,8,256]{3,2,1,0:T(8,128)S(1)}, u32[]{:S(2)}) copy-start(s32[1,4,8,256]{3,2,1,0:T(8,128)S(1)} %collective-permute-done.6) | copy-start | bytes 98308
  38.7 1.6 %copy-start.5 = (s32[1,4,8,256]{3,2,1,0:T(8,128)}, s32[1,4,8,256]{3,2,1,0:T(8,128)S(1)}, u32[]{:S(2)}) copy-start(s32[1,4,8,256]{3,2,1,0:T(8,128)S(1)} %collective-permute-done.5) | copy-start | bytes 98308
  38.7 2.7 %copy-start = (bf16[2688,128]{1,0:T(8,128)(2,1)}, bf16[2688,128]{1,0:T(8,128)(2,1)S(1)}, u32[]{:S(2)}) copy-start(bf16[2688,128]{1,0:T(8,128)(2,1)S(1)} %collective-permute-done.4) | copy-start | bytes 2064388
  38.7 11.3 %collective-permute-start.9 = (bf16[2688,128]{1,0:T(8,128)(2,1)}, bf16[2688,128]{1,0:T(8,128)(2,1)}, u32[]{:S(2)}, u32[]{:S(2)}) collective-permute-start(bf16[2688,128]{1,0:T(8,128)(2,1)} %collective-permute-done.3), channel_id=1, source_target_pairs={{0,4},{1,3},{2,6},{3,1},{4,0},{5,7},{6,2},{7,5},{8,12},{9,11},{10,... | collective-permute-start | bytes 2064392 | tf_op jit(solution)/shard_map/ppermute | solution.py:534
  40.3 6.5 %collective-permute-start.10 = (s32[4,4,8,256]{3,2,1,0:T(8,128)S(1)}, s32[4,4,8,256]{3,2,1,0:T(8,128)S(1)}, u32[]{:S(2)}, u32[]{:S(2)}) collective-permute-start(s32[4,4,8,256]{3,2,1,0:T(8,128)S(1)} %pad_add_fusion), channel_id=1, source_target_pairs={{0,2},{1,3},{2,0},{3,1},{4,6},{5,7},{6,4},{7,5},{8,10},{9,11},{10,... | collective-permute-start | bytes 393224 | tf_op jit(solution)/shard_map/ppermute | solution.py:530
  40.9 14.6 %collective-permute-start.11 = (bf16[2688,128]{1,0:T(8,128)(2,1)}, bf16[2688,128]{1,0:T(8,128)(2,1)}, u32[]{:S(2)}, u32[]{:S(2)}) collective-permute-start(bf16[2688,128]{1,0:T(8,128)(2,1)} %collective-permute-done.3), channel_id=1, source_target_pairs={{0,1},{1,0},{2,3},{3,2},{4,5},{5,4},{6,7},{7,6},{8,9},{9,8},{10,11... | collective-permute-start | bytes 2064392 | tf_op jit(solution)/shard_map/ppermute | solution.py:530
  40.9 14.5 %collective-permute-start.12 = (bf16[2688,128]{1,0:T(8,128)(2,1)S(1)}, bf16[2688,128]{1,0:T(8,128)(2,1)}, u32[]{:S(2)}, u32[]{:S(2)}) collective-permute-start(bf16[2688,128]{1,0:T(8,128)(2,1)S(1)} %collective-permute-done.4), channel_id=1, source_target_pairs={{0,1},{1,0},{2,3},{3,2},{4,5},{5,4},{6,7},{7,6},{8,9},{9,8},{10,11... | collective-permute-start | bytes 2064392 | tf_op jit(solution)/shard_map/ppermute | solution.py:530
  46.8 3.2 %copy-start.2 = (s32[4,4,8,256]{3,2,1,0:T(8,128)}, s32[4,4,8,256]{3,2,1,0:T(8,128)S(1)}, u32[]{:S(2)}) copy-start(s32[4,4,8,256]{3,2,1,0:T(8,128)S(1)} %collective-permute-done.10) | copy-start | bytes 393220
  50.0 5.5 %collective-permute-start.13 = (bf16[2688,128]{1,0:T(8,128)(2,1)}, bf16[2688,128]{1,0:T(8,128)(2,1)}, u32[]{:S(2)}, u32[]{:S(2)}) collective-permute-start(bf16[2688,128]{1,0:T(8,128)(2,1)} %collective-permute-done.9.refs_3_), channel_id=1, source_target_pairs={{0,1},{1,0},{2,3},{3,2},{4,5},{5,4},{6,7},{7,6},{8,9},{9,8},{10,11... | collective-permute-start | bytes 2064392 | tf_op jit(solution)/shard_map/ppermute | solution.py:530
  55.5 0.7 copy-start.1

commit v9 on v6

--- a/solution.py
+++ b/solution.py
@@ -13,11 +13,10 @@
 NA = 48
 BAND = 3
 BITS = 13
-SCALE = 7
-NARROW = jnp.float8_e5m2
+NARROW = jnp.float8_e4m3fn
 LANES = 128
 WINDOW = 256
-VMEM_BYTES = 56 * 1024 * 1024
+VMEM_BYTES = 63 * 1024 * 1024
 
 
 def parity(codes, rows):
@@ -130,7 +129,7 @@
     total = jnp.zeros((own, LANES), jnp.float32)
     for at in range(planes):
         signs = (1 - 2 * parity(own_column, pokes_ref[at:at + 1, :])).astype(jnp.float32)
-        own_signs[:, at * LANES:(at + 1) * LANES] = (signs * 2.0 ** (SCALE - at)).astype(NARROW)
+        own_signs[:, at * LANES:(at + 1) * LANES] = signs.astype(NARROW)
         total = total + signs
     own_sums[...] = jnp.broadcast_to(jnp.sum(total, axis=1, keepdims=True), own_sums.shape)
 
@@ -173,21 +172,18 @@
                 value = part if value is None else value ^ part
             word.append(value)
         word = jnp.concatenate(word, axis=1)
-        words_of = (word, word >> planes)
-        total = jnp.zeros((own, WINDOW), jnp.float32)
-        for at in range(0, planes, 2):
-            bits = [
-                (side & (1 << plane)).astype(jnp.float32).astype(NARROW)
-                for plane in (at, at + 1) for side in words_of
-            ]
-            total = total + jnp.dot(
-                own_signs[:, at * LANES:(at + 2) * LANES], jnp.concatenate(bits, axis=0),
-                preferred_element_type=jnp.float32,
-            )
+        bits = [None] * (2 * planes)
+        for byte in range(0, 2 * planes, 8):
+            part = (word >> byte).astype(jnp.int8)
+            for bit in range(8):
+                at = byte + bit
+                hit = (part & np.uint8(1 << bit).astype(np.int8)) != 0
+                bits[at % planes * 2 + at // planes] = jnp.where(hit, NARROW(1.0), NARROW(0.0))
+        total = jnp.dot(own_signs[...], jnp.concatenate(bits, axis=0), preferred_element_type=jnp.float32)
         sums = jnp.concatenate([own_sums[...]] * (WINDOW // LANES), axis=1)
-        turned = jnp.transpose(sums - 2.0 ** (1 - SCALE) * total)
+        turned = jnp.transpose((sums - 2.0 * total).astype(jnp.bfloat16))
         at = pl.multiple_of(mirror * height + index * WINDOW, WINDOW)
-        gram_ref[pl.ds(at, WINDOW), :] = turned.astype(jnp.bfloat16)
+        gram_ref[pl.ds(at, WINDOW), :] = turned
         return 0
 
     lax.fori_loop(0, height // WINDOW, chunk, 0, unroll=3)
@@ -244,14 +240,21 @@
 def row_block(place, staged):
     if not staged:
         return place
-    return (place ^ 7 if place in (3, 4) else place) ^ lax.axis_index("row")
+    row = lax.axis_index("row")
+    core = row & 1
+    return row ^ [0, 1, 2 << core, 4 >> core, (4 >> core) | 1, (2 << core) | 1, 6, 7][place]
 
 
 def row_place(block, staged):
     if not staged:
         return block
-    place = block ^ lax.axis_index("row")
-    return jnp.where((place == 3) | (place == 4), place ^ 7, place)
+    row = lax.axis_index("row")
+    core = row & 1
+    distance = block ^ row
+    near = jnp.where(distance == 2 << core, 2, 3)
+    far = jnp.where(distance == (4 >> core) | 1, 4, 5)
+    middle = jnp.where(distance & 1 == 0, near, far)
+    return jnp.where((distance >= 2) & (distance < 6), middle, distance)
 
 
 def band_product(parts, q, row_shape, block, surface_rows, gram_ref):
@@ -287,9 +290,15 @@
 
 
 def bands_kernel(row_shape, surface_rows, first, counts, staged, gram_any, *refs):
-    mirrors, shard_rows = row_shape[:2]
+    mirrors, shard_rows, slots, samples = row_shape
     sources = [ref.at[n] for ref, count in zip(refs, counts) for n in range(count)]
-    out_ref, gram_ref, blocks, gram_semaphores, block_semaphores = refs[len(counts):]
+    refs = refs[len(counts):]
+    columns_ref = None
+    if len(refs) == 8:
+        columns_ref, out_ref, whole_ref, rest_ref, *refs = refs
+    else:
+        out_ref, *refs = refs
+    gram_ref, blocks, gram_semaphores, block_semaphores = refs
     step = pl.program_id(0)
     gram_copies = fetch_gram(gram_any, gram_ref, gram_semaphores, mirrors)
 
@@ -303,6 +312,8 @@
             copy.start()
         for n in range(1, len(sources)):
             fetch(n).start()
+        if columns_ref is not None:
+            build_differences(columns_ref, whole_ref, rest_ref, mirrors, samples)
 
     for n in range(len(sources)):
         @pl.when(step == n)
@@ -315,21 +326,36 @@
                 out_ref[0, q] = band_product([blocks.at[n]], q, row_shape, block, surface_rows, gram_ref)
 
 
-def bands(gram_rows, sources, first, staged, row_shape, surface_rows):
+def bands(gram_rows, sources, first, staged, row_shape, surface_rows, columns=None, pupil=None):
     acts, own = gram_rows.shape
+    mirrors, shard_rows, slots, samples = row_shape
     counts = [source.shape[0] for source in sources]
-    rows = row_shape[0] * row_shape[1]
-    flops = 2 * own * WINDOW * row_shape[3] * rows * sum(counts)
+    rows = mirrors * shard_rows
+    flops = 2 * own * WINDOW * samples * rows * sum(counts)
+    vmem, anywhere = pl.BlockSpec(memory_space=pltpu.VMEM), pl.BlockSpec(memory_space=pl.ANY)
+    out_shape = [jax.ShapeDtypeStruct((sum(counts), rows, samples, own), jnp.bfloat16)]
+    out_specs = [pl.BlockSpec((1, rows, samples, own), lambda s: (s, 0, 0, 0))]
+    arguments, in_specs = [gram_rows, *sources], [anywhere] * (1 + len(sources))
+    if columns is not None:
+        depth = mirrors * samples // WINDOW * WINDOW
+        rest = 2 * (mirrors * samples - depth)
+        out_shape += [
+            jax.ShapeDtypeStruct((columns.shape[0], 2, pupil // 2, depth), jnp.bfloat16),
+            jax.ShapeDtypeStruct((columns.shape[0], pupil, rest), jnp.bfloat16),
+        ]
+        out_specs += [vmem] * 2
+        arguments.append(columns)
+        in_specs.append(vmem)
     return pl.pallas_call(
         functools.partial(bands_kernel, row_shape, surface_rows, first, counts, staged),
         grid=(sum(counts),),
-        out_shape=jax.ShapeDtypeStruct((sum(counts), rows, row_shape[3], own), jnp.bfloat16),
-        in_specs=[pl.BlockSpec(memory_space=pl.ANY)] * (1 + len(sources)),
-        out_specs=pl.BlockSpec((1, rows, row_shape[3], own), lambda s: (s, 0, 0, 0)),
+        out_shape=out_shape,
+        in_specs=in_specs,
+        out_specs=out_specs,
         scratch_shapes=[
             pltpu.VMEM((acts, own), jnp.bfloat16),
             pltpu.VMEM((sum(counts),) + sources[0].shape[1:], jnp.bfloat16),
-            pltpu.SemaphoreType.DMA((row_shape[0],)),
+            pltpu.SemaphoreType.DMA((mirrors,)),
             pltpu.SemaphoreType.DMA((sum(counts),)),
         ],
         compiler_params=pltpu.CompilerParams(vmem_limit_bytes=VMEM_BYTES),
@@ -337,39 +363,47 @@
             flops=flops, bytes_accessed=2 * own * WINDOW * rows * sum(counts), transcendentals=0
         ),
         name="bands",
-    )(gram_rows, *sources)
-
-
-def build_differences(columns, differences, mirrors, samples, pupil):
-    half = pupil // 2
+    )(*arguments)
+
+
+def build_differences(columns_ref, whole_ref, rest_ref, mirrors, samples):
+    half = whole_ref.shape[2]
+    pupil, depth = 2 * half, whole_ref.shape[3]
+    remainder = mirrors * samples - depth
     slope = lax.broadcasted_iota(jnp.int32, (half, pupil), 0)
     lane = lax.broadcasted_iota(jnp.int32, (half, pupil), 1)
     at = lax.broadcasted_iota(jnp.int32, (half, mirrors * samples), 1)
-    for d, lines in enumerate(columns):
+    for d in range(columns_ref.shape[0]):
         sides = []
         for side in range(2):
             hit = None
             for k in range(mirrors):
-                line = jnp.broadcast_to(lines[k:k + 1], (half, pupil))
+                line = jnp.broadcast_to(columns_ref[d, k:k + 1, :pupil], (half, pupil))
                 column = jnp.sum(jnp.where(lane == slope * 2 + side, line, 0), axis=1, keepdims=True)
                 here = (at == column + k * samples).astype(jnp.float32)
                 hit = here if hit is None else hit + here
             sides.append(hit)
-        differences[d, 0] = (sides[1] - sides[0]).astype(jnp.bfloat16)
-        differences[d, 1] = (sides[1] + sides[0]).astype(jnp.bfloat16)
+        across, down = sides[1] - sides[0], sides[1] + sides[0]
+        whole_ref[d, 0] = across[:, :depth].astype(jnp.bfloat16)
+        whole_ref[d, 1] = down[:, :depth].astype(jnp.bfloat16)
+        blank = jnp.zeros((half, remainder), jnp.float32)
+        upper = jnp.concatenate([across[:, depth:], blank], axis=1)
+        lower = jnp.concatenate([blank, down[:, depth:]], axis=1)
+        rest_ref[d] = jnp.concatenate([upper, lower], axis=0).astype(jnp.bfloat16)
 
 
 def decode_kernel(row_shape, surface_rows, own, staged, norm, counts, late_parts, *refs):
     mirrors, shard_rows, slots, samples = row_shape
-    columns_refs, refs = refs[:counts[0]], refs[counts[0]:]
-    lines_refs, refs = refs[:counts[1]], refs[counts[1]:]
-    late_refs, refs = refs[:counts[2]], refs[counts[2]:]
-    ready_refs, refs = refs[:counts[3]], refs[counts[3]:]
-    (gram_any, out_ref, gram_ref, decoded, differences, total, packed_lines, lines, scalars, *refs) = refs
-    late_blocks, refs = refs[:counts[2]], refs[counts[2]:]
+    whole_ref, rest_ref, *refs = refs
+    lines_refs, refs = refs[:counts[0]], refs[counts[0]:]
+    late_refs, refs = refs[:counts[1]], refs[counts[1]:]
+    ready_refs, refs = refs[:counts[2]], refs[counts[2]:]
+    (gram_any, out_ref, gram_ref, decoded, total, packed_lines, lines, scalars, *refs) = refs
+    late_blocks, refs = refs[:counts[1]], refs[counts[1]:]
     gram_semaphores, ready_semaphores, line_semaphores, late_semaphores, scalar_semaphore = refs
     group = pl.program_id(0)
-    directions, pupil = differences.shape[0], 2 * differences.shape[2]
+    directions, pupil = whole_ref.shape[0], 2 * whole_ref.shape[2]
+    depth = whole_ref.shape[3]
     phases = out_ref.shape[2] // pupil
     blocks = surface_rows // shard_rows
     late = len(late_parts)
@@ -389,15 +423,13 @@
             pltpu.make_async_copy(end, packed_lines.at[n], line_semaphores.at[n]) for n, end in enumerate(ends)
         ])
         late_copies = started([
-            pltpu.make_async_copy(late_refs[n], late_blocks[n], late_semaphores.at[n]) for n in range(counts[2])
+            pltpu.make_async_copy(late_refs[n], late_blocks[n], late_semaphores.at[n]) for n in range(counts[1])
         ])
         gram_copies = started(fetch_gram(gram_any, gram_ref, gram_semaphores, mirrors)) if late else []
         ready_copies = started([
             pltpu.make_async_copy(block, decoded.at[n], ready_semaphores.at[n])
             for n, block in enumerate([ref.at[m] for ref in ready_refs for m in range(ref.shape[0])])
         ])
-        columns = [ref[n, :, :pupil] for ref in columns_refs for n in range(ref.shape[0])]
-        build_differences(columns, differences, mirrors, samples, pupil)
         for copy in line_copies + late_copies:
             copy.wait()
         held = [packed_lines[n] for n in range(len(ends))]
@@ -424,7 +456,7 @@
             copy.wait()
 
     for d in range(directions):
-        held = d ^ position("dir", staged)
+        held = d
         products, factors = [], []
         for phase in range(phases):
             i = group * phases + phase
@@ -437,12 +469,12 @@
                     picked.append(decoded[row_place(row // shard_rows, staged), k * shard_rows + row % shard_rows])
                 sums.append(picked[0] + picked[1])
                 changes.append(picked[1] - picked[0])
-            for kind, rows in enumerate((sums, changes)):
-                products.append(
-                    jnp.dot(
-                        differences[held, kind], jnp.concatenate(rows, axis=0), preferred_element_type=jnp.float32
-                    )
-                )
+            right = [jnp.concatenate(rows, axis=0) for rows in (sums, changes)]
+            mixed = jnp.concatenate([rows[depth:] for rows in right], axis=0)
+            rest = jnp.dot(rest_ref[held], mixed, preferred_element_type=jnp.float32)
+            for kind, rows in enumerate(right):
+                whole = jnp.dot(whole_ref[held, kind], rows[:depth], preferred_element_type=jnp.float32)
+                products.append(whole + rest[kind * pupil // 2:(kind + 1) * pupil // 2])
             valid = lines[block, pl.ds(held * width + phase % (shard_rows // 2), 1), :][:, :pupil // 2]
             factors += [valid.astype(jnp.float32) * norm] * 2
         product = jnp.concatenate(products, axis=0)
@@ -456,10 +488,10 @@
         out_ref[:, :, tile * LANES:(tile + 1) * LANES] = value.astype(out_ref.dtype)
 
 
-def decode(columns, sources, late, ready, gram_rows, own, row_shape, surface_rows, pupil, norm, staged):
+def decode(differences, sources, late, ready, gram_rows, own, row_shape, surface_rows, pupil, norm, staged):
     mirrors, shard_rows, slots, samples = row_shape
     acts, padded = gram_rows.shape
-    directions = sum(line.shape[0] for line in columns)
+    directions = differences[0].shape[0]
     blocks = surface_rows // shard_rows
     extra = -(-directions * (shard_rows // 2 + 1) // 16) * 16
     phases = LANES // math.gcd(pupil, LANES)
@@ -468,7 +500,7 @@
     flops = 2 * padded * mirrors * samples * pupil * directions * surface_rows // 2
     vmem, anywhere = pl.BlockSpec(memory_space=pltpu.VMEM), pl.BlockSpec(memory_space=pl.ANY)
     parts = [part for block in late for part in block]
-    counts = (len(columns), len(sources), len(parts), len(ready))
+    counts = (len(sources), len(parts), len(ready))
     semaphores = [mirrors, blocks, blocks, max(len(parts), 1), 1]
     return pl.pallas_call(
         functools.partial(
@@ -476,12 +508,11 @@
         ),
         grid=(width // lanes,),
         out_shape=jax.ShapeDtypeStruct((own, directions, width), jnp.bfloat16),
-        in_specs=[vmem] * counts[0] + [anywhere] * (sum(counts[1:]) + 1),
+        in_specs=[vmem] * 2 + [anywhere] * (sum(counts) + 1),
         out_specs=pl.BlockSpec((own, directions, lanes), lambda s: (0, 0, s)),
         scratch_shapes=[
             pltpu.VMEM((acts, padded), jnp.bfloat16),
             pltpu.VMEM((blocks, mirrors * shard_rows, samples, padded), jnp.bfloat16),
-            pltpu.VMEM((directions, 2, pupil // 2, mirrors * samples), jnp.bfloat16),
             pltpu.VMEM((lanes // LANES, own * directions, LANES), jnp.float32),
             pltpu.VMEM((blocks, extra, LANES), jnp.bfloat16),
             pltpu.VMEM((blocks, extra, LANES), jnp.int32),
@@ -492,11 +523,17 @@
         compiler_params=pltpu.CompilerParams(vmem_limit_bytes=VMEM_BYTES),
         cost_estimate=pl.CostEstimate(flops=flops, bytes_accessed=2 * own * directions * width, transcendentals=0),
         name="decode",
-    )(*columns, *sources, *parts, *ready, gram_rows)
+    )(*differences, *sources, *parts, *ready, gram_rows)
 
 
 def swap(block, axis, distance):
     return lax.ppermute(block, axis, [(i, i ^ distance) for i in range(lax.axis_size(axis))])
+
+
+def turn(block, even, odd):
+    return lax.ppermute(
+        block, "row", [(i, i ^ (odd if i % 2 else even)) for i in range(lax.axis_size("row"))]
+    )
 
 
 def shards(influence, foot_rows, foot_columns, actuator_codes, poke_rows, subaperture_valid):
@@ -512,30 +549,34 @@
     pokes = poke_rows.reshape(-1, LANES)
     lines = small_lines(foot_rows, foot_columns, subaperture_valid)
     if not staged:
-        lines = [lax.all_gather(lines, "dir")]
-        packed = pack(turned, lines)
+        lines = lax.all_gather(lines, "dir")
+        packed = pack(turned, [lines])
         every = lax.all_gather(packed, "row")
         gram_rows, _ = gram(*own_side(actuator_codes, pokes, own), packed, row_shape, surface_rows)
-        ready = [bands(gram_rows, [every], 0, staged, row_shape, surface_rows)]
-        return decode(lines, [every], [], ready, gram_rows, own, row_shape, surface_rows, pupil, norm, staged)
-
-    lines = [lines[None]] + [swap(lines, "dir", e)[None] for e in range(1, directions)]
-    sides = own_side(actuator_codes, pokes, own)
-    lines, sides = lax.optimization_barrier((lines, sides))
-    packed = pack(turned, lines)
-    beside, across, sibling = (swap(packed, "row", distance) for distance in (2, 4, 1))
-    gram_rows, first = gram(*sides, packed, row_shape, surface_rows)
-    gram_rows, beside, across = lax.optimization_barrier((gram_rows, beside, across))
-    half = (mirrors * shard_rows + 2) * samples // 2
-    upper, lower = swap(beside[:half], "row", 4), swap(across[half:], "row", 2)
-    beside_sibling, across_sibling = swap(beside, "row", 1), swap(across, "row", 1)
-    sources = [source[None] for source in (sibling, beside, across)]
-    ready = bands(gram_rows, sources, 1, staged, row_shape, surface_rows)
-    ready, upper, lower = lax.optimization_barrier((ready, upper, lower))
-    late = [[beside_sibling], [across_sibling], [upper, lower], [swap(upper, "row", 1), swap(lower, "row", 1)]]
+        ready, *differences = bands(gram_rows, [every], 0, staged, row_shape, surface_rows, lines, pupil)
+        return decode(
+            differences, [every], [], [ready], gram_rows, own, row_shape, surface_rows, pupil, norm, staged
+        )
+
+    lines = lax.all_to_all(jnp.broadcast_to(lines, (directions,) + lines.shape), "dir", 0, 0, tiled=True)
+    packed = pack(turned, [lines])
+    packed, pokes = lax.optimization_barrier((packed, pokes))
+    first, second = turn(packed, 2, 4), turn(packed, 4, 2)
+    sibling = swap(packed, "row", 1)
+    gram_rows, own_rows = gram(*own_side(actuator_codes, pokes, own), packed, row_shape, surface_rows)
+    gram_rows, first, second = lax.optimization_barrier((gram_rows, first, second))
+    first_sibling, second_sibling = swap(first, "row", 1), swap(second, "row", 1)
+    diagonal = turn(first, 4, 2)
+    sources = [source[None] for source in (sibling, first, second)]
+    near, *differences = bands(gram_rows, sources, 1, staged, row_shape, surface_rows, lines, pupil)
+    near, first_sibling, second_sibling = lax.optimization_barrier((near, first_sibling, second_sibling))
+    others = [first_sibling[None], second_sibling[None]]
+    far, = bands(gram_rows, others, 4, staged, row_shape, surface_rows)
+    far, diagonal = lax.optimization_barrier((far, diagonal))
+    late = [[diagonal], [swap(diagonal, "row", 1)]]
     return decode(
-        lines, [packed[None], *sources], late, [first, ready], gram_rows, own, row_shape, surface_rows, pupil, norm,
-        staged,
+        differences, [packed[None], *sources, *others], late, [own_rows, near, far], gram_rows, own, row_shape,
+        surface_rows, pupil, norm, staged,
     )
 
 

time: 62.7 us -> 66.8 us (1.065)
  blocking collectives: 0 us -> 11.9 us
  starting transfers between devices: 11.8 us -> 5.11 us
  waiting for transfers between devices: 5.17 us -> 2.64 us
  Pallas kernels: 42.9 us -> 45.1 us
  local copies, waits for them, and re-layouts: 2.34 us -> 1.57 us
    all_to_all x0 -> x1, blocking collectives: none -> 11.9 us  [shards(): lax.all_to_all(jnp.broadcast_to(lines, (directions,) + lines.shape), 'dir...]
    ppermute x12 -> x4, starting transfers between devices: 11.8 us -> 0.58 us  [swap(): lax.ppermute(block, axis, [(i, i ^ distance) for i in range(lax.axis_size...]
    pallas_call x1 -> x2, Pallas kernels: 5.25 us -> 11.1 us  [bands(): pl.pallas_call(functools.partial(bands_kernel, row_shape, surface_rows, f...]
    ppermute x0 -> x3, starting transfers between devices: none -> 4.53 us  [turn(): lax.ppermute(block, 'row', [(i, i ^ (odd if i % 2 else even)) for i in ra...]
    pallas_call x1, Pallas kernels: 14.2 us -> 11.2 us  [gram(): pl.pallas_call(functools.partial(gram_kernel, row_shape, surface_rows), g...]
    ppermute x12 -> x4, waiting for transfers between devices: 5.17 us -> 2.36 us  [swap(): lax.ppermute(block, axis, [(i, i ^ distance) for i in range(lax.axis_size...]
    unnamed x24 -> x4, local copies, waits for them, and re-layouts: 2.3 us -> 0.87 us
    broadcast_in_dim x0 -> x1, local copies, waits for them, and re-layouts: none -> 0.7 us  [shards(): jnp.broadcast_to(lines, (directions,) + lines.shape)]
  transfers between devices with their start and end apart: 12 -> 7, of which waited for: 3 -> 2; matrix products, arithmetic and copies ran while one was open for 0% -> 0% of each run, Pallas kernels for 36% -> 38%
where the time goes in v9:
time: 66.8 us; the launch traced here: 66.4 us
  Pallas kernels  45.1 us (68%)
  blocking collectives  11.9 us (18%)
  starting transfers between devices  5.11 us (8%)
  waiting for transfers between devices  2.64 us (4%)
  local copies, waits for them, and re-layouts  1.57 us (2%)
    pallas_call x1, Pallas kernels, decode(): pl.pallas_call(functools.partial(decode_kernel, row_shape, surface_rows,...  16 us
    all_to_all x1, blocking collectives, shards(): lax.all_to_all(jnp.broadcast_to(lines, (directions,) + lines.shape), 'dir...  11.9 us
    pallas_call x1, Pallas kernels, gram(): pl.pallas_call(functools.partial(gram_kernel, row_shape, surface_rows), g...  11.2 us
    pallas_call x2, Pallas kernels, bands(): pl.pallas_call(functools.partial(bands_kernel, row_shape, surface_rows, f...  11.1 us
    ppermute x3, starting transfers between devices, turn(): lax.ppermute(block, 'row', [(i, i ^ (odd if i % 2 else even)) for i in ra...  4.53 us
    pallas_call x1, Pallas kernels, own_side(): pl.pallas_call(signs_kernel, out_shape=[jax.ShapeDtypeStruct((table.size...  2.74 us
    pallas_call x1, Pallas kernels, pack(): pl.pallas_call(pack_kernel, out_shape=jax.ShapeDtypeStruct(((mirrors * ro...  2.59 us
    ppermute x4, waiting for transfers between devices, swap(): lax.ppermute(block, axis, [(i, i ^ distance) for i in range(lax.axis_size...  2.36 us
  transfers between devices with their start and end apart: 7, of which 2 were waited for; matrix products, arithmetic and copies ran while one was open for 0% of the time, Pallas kernels for 38%

profile of v9, /device:TPU:0, one launch (start us, length us, event | category | flops | bytes accessed | tf_op | source)
XLA Modules:
  0.0 66.4 jit_solution(6588942587222287437)
XLA Ops:
  0.0 1.4 %small_lines.1 = s32[8,256]{1,0:T(8,128)} custom-call(s32[3,1,4]{2,1,0:T(1,128)} %bitcast.16, s32[3,1,160]{2,1,0:T(1,128)} %bitcast.15, s32[1,2,80]{2,1,0:T(2,128)} %valid_ref.1), custom_call_target="tpu_custom_call" | custom-call | tf_op jit(solution)/shard_map/small_lines/pallas_call | solution.py:38
  1.4 0.7 %broadcast_in_dim.21 = s32[4,8,256]{2,1,0:T(8,128)S(1)} broadcast(s32[8,256]{1,0:T(8,128)} %small_lines.1), dimensions={1,2} | broadcast | bytes 40960 | tf_op jit(solution)/shard_map/broadcast_in_dim | solution.py:561
  2.1 11.9 %all_to_all.5.refs_0_.refs_3_ = s32[4,8,256]{2,1,0:T(8,128)} all-to-all(s32[4,8,256]{2,1,0:T(8,128)S(1)} %broadcast_in_dim.21), channel_id=1, replica_groups=mesh['dir'=4,'row'=8] {'dir'}, dimensions={0} | all-to-all | bytes 65536 | tf_op jit(solution)/shard_map/all_to_all | solution.py:561
  13.9 2.6 %pack_influence.1.packed_ref = bf16[2704,128]{1,0:T(8,128)(2,1)} custom-call(bf16[3,4,144,192]{3,2,1,0:T(8,128)(2,1)} %bitcast.13, s32[4,8,256]{2,1,0:T(8,128)} %all_to_all.5.refs_0_.refs_3_), custom_call_target="tpu_custom_call" | custom-call | bytes 995328 | tf_op jit(solution)/shard_map/pack_influence/pallas_call | solution.py:79
  16.5 1.5 %collective-permute-start.1 = (bf16[2704,128]{1,0:T(8,128)(2,1)}, bf16[2704,128]{1,0:T(8,128)(2,1)S(1)}, u32[]{:S(2)}, u32[]{:S(2)}) collective-permute-start(bf16[2704,128]{1,0:T(8,128)(2,1)} %pack_influence.1.packed_ref), channel_id=1, source_target_pairs={{0,4},{1,3},{2,6},{3,1},{4,0},{5,7},{6,2},{7,5},{8,12},{9,11},{10,... | collective-permute-start | bytes 2076680 | tf_op jit(solution)/shard_map/ppermute | solution.py:534
  18.1 1.5 %collective-permute-start = (bf16[2704,128]{1,0:T(8,128)(2,1)}, bf16[2704,128]{1,0:T(8,128)(2,1)}, u32[]{:S(2)}, u32[]{:S(2)}) collective-permute-start(bf16[2704,128]{1,0:T(8,128)(2,1)} %pack_influence.1.packed_ref), channel_id=1, source_target_pairs={{0,2},{1,5},{2,0},{3,7},{4,6},{5,1},{6,4},{7,3},{8,10},{9,13},{10,... | collective-permute-start | bytes 2076680 | tf_op jit(solution)/shard_map/ppermute | solution.py:534
  19.5 0.0 collective-permute-start.2
  19.6 2.7 %own_signs.1 = (s32[54,128]{1,0:T(8,128)}, s32[13,64,128]{2,1,0:T(8,128)}, f8e4m3fn[224,2048]{1,0:T(32,128)(4,1)}, f32[224,128]{1,0:T(8,128)}) custom-call(s32[3,48,48]{2,1,0:T(8,128)} %table_ref.1, s32[16,128]{1,0:T(8,128)} %bitcast.14), custom_call_target="tpu_custom_call" | custom-call | tf_op jit(solution)/shard_map/own_signs/pallas_call | solution.py:140
  22.3 11.2 %gram_rows.1 = (bf16[6912,224]{1,0:T(8,128)(2,1)}, bf16[1,12,192,224]{3,2,1,0:T(8,128)(2,1)}) custom-call(s32[54,128]{1,0:T(8,128)} %get-tuple-element.25.codes_ref, s32[13,64,128]{2,1,0:T(8,128)} %get-tuple-element.26.words, f8e4m3fn[224,2048]{1,0:T(32,128)(4,1)} %get-tuple-element.27.own_signs, f32[224,128]{1,0:T(8,128)} %get-tuple-element.28.own_sums, ...), custom_call_target="tpu_custom_call" | custom-call | flops 6341787648 | bytes 3096576 | tf_op jit(solution)/shard_map/gram_rows/pallas_call | solution.py:215
  33.5 0.3 collective-permute-done.1
  33.8 0.0 copy-start
  33.8 0.0 collective-permute-done
  33.8 0.3 collective-permute-start.4
  34.1 0.2 collective-permute-start.3
  34.3 1.5 %collective-permute-start.5 = (bf16[2704,128]{1,0:T(8,128)(2,1)}, bf16[2704,128]{1,0:T(8,128)(2,1)}, u32[]{:S(2)}, u32[]{:S(2)}) collective-permute-start(bf16[2704,128]{1,0:T(8,128)(2,1)} %collective-permute-done), channel_id=1, source_target_pairs={{0,4},{1,3},{2,6},{3,1},{4,0},{5,7},{6,2},{7,5},{8,12},{9,11},{10,... | collective-permute-start | bytes 2076680 | tf_op jit(solution)/shard_map/ppermute | solution.py:534
  35.8 0.0 collective-permute-done.2
  35.8 0.0 copy-done
  35.8 7.0 %bands.2 = (bf16[3,12,192,224]{3,2,1,0:T(8,128)(2,1)}, bf16[4,2,80,512]{3,2,1,0:T(8,128)(2,1)}, bf16[4,160,128]{2,1,0:T(8,128)(2,1)}) custom-call(bf16[6912,224]{1,0:T(8,128)(2,1)} %get-tuple-element.31.gram_any.refs_13_, bf16[1,2704,128]{2,1,0:T(8,128)(2,1)} %bitcast.4.refs_0_.refs_3_, bf16[1,2704,128]{2,1,0:T(8,128)(2,1)} %bitcast.5.refs_1_.refs_4_, ...), custom_call_target="tpu_custom_call" | custom-call | flops 792723456 | bytes 4128768 | tf_op jit(solution)/shard_map/bands/pallas_call | solution.py:349
  42.8 0.0 collective-permute-done.4
  42.9 0.0 collective-permute-done.3
  42.9 4.1 %bands.3.refs_12_ = bf16[2,12,192,224]{3,2,1,0:T(8,128)(2,1)} custom-call(bf16[6912,224]{1,0:T(8,128)(2,1)} %get-tuple-element.31.gram_any.refs_13_, bf16[1,2704,128]{2,1,0:T(8,128)(2,1)} %bitcast.8.refs_0_.refs_6_, bf16[1,2704,128]{2,1,0:T(8,128)(2,1)} %bitcast.9.refs_1_.refs_7_), custom_call_target="tpu_custom_call" | custom-call | flops 528482304 | bytes 2752512 | tf_op jit(solution)/shard_map/bands/pallas_call | solution.py:349
  47.0 0.0 collective-permute-done.5.refs_8_
  47.0 0.1 collective-permute-start.6
  47.1 2.3 %collective-permute-done.6.refs_9_ = bf16[2704,128]{1,0:T(8,128)(2,1)S(1)} collective-permute-done((bf16[2704,128]{1,0:T(8,128)(2,1)}, bf16[2704,128]{1,0:T(8,128)(2,1)S(1)}, u32[]{:S(2)}, u32[]{:S(2)}) %collective-permute-start.6) | collective-permute-done | bytes 692256 | tf_op jit(solution)/shard_map/ppermute | solution.py:530
  49.5 0.0 copy-start.1
  49.5 0.9 %copy-done.1 = bf16[2704,128]{1,0:T(8,128)(2,1)} copy-done((bf16[2704,128]{1,0:T(8,128)(2,1)}, bf16[2704,128]{1,0:T(8,128)(2,1)S(1)}, u32[]{:S(2)}) %copy-start.1) | copy-done | bytes 692248
  50.3 16.0 %decode.1 = bf16[216,4,2560]{2,1,0:T(4,128)(2,1)} custom-call(bf16[4,2,80,512]{3,2,1,0:T(8,128)(2,1)} %get-tuple-element.34.refs_0_, bf16[4,160,128]{2,1,0:T(8,128)(2,1)} %get-tuple-element.35.refs_1_, bf16[1,2704,128]{2,1,0:T(8,128)(2,1)} %bitcast.10, bf16[1,2704,128]{2,1,0:T(8,128)(2,1)} %bitcast.4.refs_0_.refs_3_, ...), custom_call_target="tpu_custom_call" | custom-call | flops 2642411520 | bytes 4423680 | tf_op jit(solution)/shard_map/decode/pallas_call | solution.py:505
Async XLA Ops:
  16.5 17.3 %collective-permute-start.1 = (bf16[2704,128]{1,0:T(8,128)(2,1)}, bf16[2704,128]{1,0:T(8,128)(2,1)S(1)}, u32[]{:S(2)}, u32[]{:S(2)}) collective-permute-start(bf16[2704,128]{1,0:T(8,128)(2,1)} %pack_influence.1.packed_ref), channel_id=1, source_target_pairs={{0,4},{1,3},{2,6},{3,1},{4,0},{5,7},{6,2},{7,5},{8,12},{9,11},{10,... | collective-permute-start | bytes 2076680 | tf_op jit(solution)/shard_map/ppermute | solution.py:534
  18.1 15.7 %collective-permute-start = (bf16[2704,128]{1,0:T(8,128)(2,1)}, bf16[2704,128]{1,0:T(8,128)(2,1)}, u32[]{:S(2)}, u32[]{:S(2)}) collective-permute-start(bf16[2704,128]{1,0:T(8,128)(2,1)} %pack_influence.1.packed_ref), channel_id=1, source_target_pairs={{0,2},{1,5},{2,0},{3,7},{4,6},{5,1},{6,4},{7,3},{8,10},{9,13},{10,... | collective-permute-start | bytes 2076680 | tf_op jit(solution)/shard_map/ppermute | solution.py:534
  19.5 16.3 %collective-permute-start.2 = (bf16[2704,128]{1,0:T(8,128)(2,1)}, bf16[2704,128]{1,0:T(8,128)(2,1)}, u32[]{:S(2)}, u32[]{:S(2)}) collective-permute-start(bf16[2704,128]{1,0:T(8,128)(2,1)} %pack_influence.1.packed_ref), channel_id=1, source_target_pairs={{0,1},{1,0},{2,3},{3,2},{4,5},{5,4},{6,7},{7,6},{8,9},{9,8},{10,11... | collective-permute-start | bytes 2076680 | tf_op jit(solution)/shard_map/ppermute | solution.py:530
  33.8 2.0 %copy-start = (bf16[2704,128]{1,0:T(8,128)(2,1)}, bf16[2704,128]{1,0:T(8,128)(2,1)S(1)}, u32[]{:S(2)}) copy-start(bf16[2704,128]{1,0:T(8,128)(2,1)S(1)} %collective-permute-done.1) | copy-start | bytes 2076676
  33.8 9.0 %collective-permute-start.4 = (bf16[2704,128]{1,0:T(8,128)(2,1)S(1)}, bf16[2704,128]{1,0:T(8,128)(2,1)}, u32[]{:S(2)}, u32[]{:S(2)}) collective-permute-start(bf16[2704,128]{1,0:T(8,128)(2,1)S(1)} %collective-permute-done.1), channel_id=1, source_target_pairs={{0,1},{1,0},{2,3},{3,2},{4,5},{5,4},{6,7},{7,6},{8,9},{9,8},{10,11... | collective-permute-start | bytes 2076680 | tf_op jit(solution)/shard_map/ppermute | solution.py:530
  34.1 8.7 %collective-permute-start.3 = (bf16[2704,128]{1,0:T(8,128)(2,1)}, bf16[2704,128]{1,0:T(8,128)(2,1)}, u32[]{:S(2)}, u32[]{:S(2)}) collective-permute-start(bf16[2704,128]{1,0:T(8,128)(2,1)} %collective-permute-done), channel_id=1, source_target_pairs={{0,1},{1,0},{2,3},{3,2},{4,5},{5,4},{6,7},{7,6},{8,9},{9,8},{10,11... | collective-permute-start | bytes 2076680 | tf_op jit(solution)/shard_map/ppermute | solution.py:530
  34.3 12.7 %collective-permute-start.5 = (bf16[2704,128]{1,0:T(8,128)(2,1)}, bf16[2704,128]{1,0:T(8,128)(2,1)}, u32[]{:S(2)}, u32[]{:S(2)}) collective-permute-start(bf16[2704,128]{1,0:T(8,128)(2,1)} %collective-permute-done), channel_id=1, source_target_pairs={{0,4},{1,3},{2,6},{3,1},{4,0},{5,7},{6,2},{7,5},{8,12},{9,11},{10,... | collective-permute-start | bytes 2076680 | tf_op jit(solution)/shard_map/ppermute | solution.py:534
  47.0 2.4 %collective-permute-start.6 = (bf16[2704,128]{1,0:T(8,128)(2,1)}, bf16[2704,128]{1,0:T(8,128)(2,1)S(1)}, u32[]{:S(2)}, u32[]{:S(2)}) collective-permute-start(bf16[2704,128]{1,0:T(8,128)(2,1)} %collective-permute-done.5.refs_8_), channel_id=1, source_target_pairs={{0,1},{1,0},{2,3},{3,2},{4,5},{5,4},{6,7},{7,6},{8,9},{9,8},{10,11... | collective-permute-start | bytes 2076680 | tf_op jit(solution)/shard_map/ppermute | solution.py:530
  49.5 0.9 %copy-start.1 = (bf16[2704,128]{1,0:T(8,128)(2,1)}, bf16[2704,128]{1,0:T(8,128)(2,1)S(1)}, u32[]{:S(2)}) copy-start(bf16[2704,128]{1,0:T(8,128)(2,1)S(1)} %collective-permute-done.6.refs_9_) | copy-start | bytes 2076676

commit v10 on v9

--- a/solution.py
+++ b/solution.py
@@ -12,11 +12,12 @@
 NAR = 48
 NA = 48
 BAND = 3
+REACH = 2
 BITS = 13
 NARROW = jnp.float8_e4m3fn
 LANES = 128
 WINDOW = 256
-VMEM_BYTES = 63 * 1024 * 1024
+VMEM_BYTES = 127 * 512 * 1024
 
 
 def parity(codes, rows):
@@ -199,7 +200,8 @@
             @pl.when(mirror == k)
             def _():
                 first_ref[0, l] = band_product(
-                    [packed_ref], k * row_shape[1] + l, row_shape, block, surface_rows, gram_ref
+                    packed_ref, k * row_shape[1] + l, row_shape, block, surface_rows,
+                    gram_ref.at[pl.ds(k * height, height)], 0,
                 )
 
     @pl.when(mirror == pl.num_programs(0) - 1)
@@ -257,36 +259,61 @@
     return jnp.where((distance >= 2) & (distance < 6), middle, distance)
 
 
-def band_product(parts, q, row_shape, block, surface_rows, gram_ref):
+def band_of(row, surface_rows):
+    return jnp.clip(row * NAR // surface_rows - 1, 0, NAR - BAND)
+
+
+def band_span(shard_rows, surface_rows):
+    bands_at = np.clip(np.arange(surface_rows) * NAR // surface_rows - 1, 0, NAR - BAND).reshape(-1, shard_rows)
+    return int((bands_at[:, -1] - bands_at[:, 0]).max()) + BAND
+
+
+def first_band(block, shard_rows, surface_rows):
+    return jnp.minimum(band_of(block * shard_rows, surface_rows), NAR - band_span(shard_rows, surface_rows))
+
+
+def band_product(source, q, row_shape, block, surface_rows, gram_view, first):
     mirrors, shard_rows, slots, samples = row_shape
     groups = mirrors * shard_rows // 2
-    own = gram_ref.shape[1]
+    own = gram_view.shape[1]
     narrow = slots - LANES
-    k, l = divmod(q, shard_rows)
-    band = jnp.clip((block * shard_rows + l) * NAR // surface_rows - 1, 0, NAR - BAND)
-    column = pl.multiple_of((k * NAR + band) * NA, 16)
+    band = band_of(block * shard_rows + q % shard_rows, surface_rows)
+    column = pl.multiple_of((band - first) * NA, 16)
     part, group = divmod(q, groups)
-    source, base = (parts[0], part * (groups + 1) * samples) if len(parts) == 1 else (parts[part], 0)
+    base = part * (groups + 1) * samples
     left = jnp.concatenate(
         [source[pl.ds(base + group * samples, samples), :], source[pl.ds(base + groups * samples, samples), :]],
         axis=1,
     )
-    right = [gram_ref[pl.ds(column, LANES), :]]
+    right = [gram_view[pl.ds(column, LANES), :]]
     if group:
         right.append(jnp.zeros((group * narrow, own), jnp.bfloat16))
-    right.append(gram_ref[pl.ds(column + LANES, narrow), :])
+    right.append(gram_view[pl.ds(column + LANES, narrow), :])
     right.append(jnp.zeros((LANES - (group + 1) * narrow, own), jnp.bfloat16))
     return jnp.dot(left, jnp.concatenate(right, axis=0), preferred_element_type=jnp.float32).astype(jnp.bfloat16)
 
 
-def fetch_gram(gram_any, gram_ref, semaphores, mirrors):
-    height = gram_ref.shape[0] // mirrors
+def fetch_gram(gram_any, gram_ref, semaphores, n, block, row_shape, surface_rows):
+    height = gram_ref.shape[2]
+    first = first_band(block, row_shape[1], surface_rows)
     return [
         pltpu.make_async_copy(
-            gram_any.at[pl.ds(k * height, height)], gram_ref.at[pl.ds(k * height, height)], semaphores.at[k]
+            gram_any.at[pl.ds(pl.multiple_of((k * NAR + first) * NA, 16), height)], gram_ref.at[n, k],
+            semaphores.at[n, k],
         )
-        for k in range(mirrors)
+        for k in range(row_shape[0])
     ]
+
+
+def block_products(source, n, row_shape, block, surface_rows, gram_ref, gram_copies, out_ref):
+    shard_rows = row_shape[1]
+    for q in range(row_shape[0] * shard_rows):
+        if q % shard_rows == 0:
+            gram_copies[q // shard_rows].wait()
+        out_ref[q] = band_product(
+            source, q, row_shape, block, surface_rows, gram_ref.at[n, q // shard_rows],
+            first_band(block, shard_rows, surface_rows),
+        )
 
 
 def bands_kernel(row_shape, surface_rows, first, counts, staged, gram_any, *refs):
@@ -300,18 +327,21 @@
         out_ref, *refs = refs
     gram_ref, blocks, gram_semaphores, block_semaphores = refs
     step = pl.program_id(0)
-    gram_copies = fetch_gram(gram_any, gram_ref, gram_semaphores, mirrors)
+    places = [row_block(first + n, staged) for n in range(len(sources))]
+    gram_copies = [
+        fetch_gram(gram_any, gram_ref, gram_semaphores, n, block, row_shape, surface_rows)
+        for n, block in enumerate(places)
+    ]
 
     def fetch(n):
         return pltpu.make_async_copy(sources[n], blocks.at[n], block_semaphores.at[n])
 
     @pl.when(step == 0)
     def _():
-        fetch(0).start()
-        for copy in gram_copies:
-            copy.start()
-        for n in range(1, len(sources)):
+        for n in range(len(sources)):
             fetch(n).start()
+            for copy in gram_copies[n]:
+                copy.start()
         if columns_ref is not None:
             build_differences(columns_ref, whole_ref, rest_ref, mirrors, samples)
 
@@ -319,11 +349,9 @@
         @pl.when(step == n)
         def _():
             fetch(n).wait()
-            block = row_block(first + n, staged)
-            for q in range(mirrors * shard_rows):
-                if n == 0 and q % shard_rows == 0:
-                    gram_copies[q // shard_rows].wait()
-                out_ref[0, q] = band_product([blocks.at[n]], q, row_shape, block, surface_rows, gram_ref)
+            block_products(
+                blocks.at[n], n, row_shape, places[n], surface_rows, gram_ref, gram_copies[n], out_ref.at[0]
+            )
 
 
 def bands(gram_rows, sources, first, staged, row_shape, surface_rows, columns=None, pupil=None):
@@ -353,9 +381,9 @@
         in_specs=in_specs,
         out_specs=out_specs,
         scratch_shapes=[
-            pltpu.VMEM((acts, own), jnp.bfloat16),
+            pltpu.VMEM((sum(counts), mirrors, band_span(shard_rows, surface_rows) * NA, own), jnp.bfloat16),
             pltpu.VMEM((sum(counts),) + sources[0].shape[1:], jnp.bfloat16),
-            pltpu.SemaphoreType.DMA((mirrors,)),
+            pltpu.SemaphoreType.DMA((sum(counts), mirrors)),
             pltpu.SemaphoreType.DMA((sum(counts),)),
         ],
         compiler_params=pltpu.CompilerParams(vmem_limit_bytes=VMEM_BYTES),
@@ -392,7 +420,7 @@
         rest_ref[d] = jnp.concatenate([upper, lower], axis=0).astype(jnp.bfloat16)
 
 
-def decode_kernel(row_shape, surface_rows, own, staged, norm, counts, late_parts, *refs):
+def decode_kernel(row_shape, surface_rows, own, staged, norm, counts, *refs):
     mirrors, shard_rows, slots, samples = row_shape
     whole_ref, rest_ref, *refs = refs
     lines_refs, refs = refs[:counts[0]], refs[counts[0]:]
@@ -406,10 +434,15 @@
     depth = whole_ref.shape[3]
     phases = out_ref.shape[2] // pupil
     blocks = surface_rows // shard_rows
-    late = len(late_parts)
+    late = counts[1]
     ready = blocks - late
     width = shard_rows // 2 + 1
     extra = lines.shape[1]
+
+    ready_blocks = [ref.at[n] for ref in ready_refs for n in range(ref.shape[0])]
+
+    def last_needed(at):
+        return min((2 * phases * (at + 1) - 1 + REACH) // shard_rows, blocks - 1)
 
     @pl.when(group == 0)
     def _():
@@ -422,41 +455,44 @@
         line_copies = started([
             pltpu.make_async_copy(end, packed_lines.at[n], line_semaphores.at[n]) for n, end in enumerate(ends)
         ])
-        late_copies = started([
-            pltpu.make_async_copy(late_refs[n], late_blocks[n], late_semaphores.at[n]) for n in range(counts[1])
-        ])
-        gram_copies = started(fetch_gram(gram_any, gram_ref, gram_semaphores, mirrors)) if late else []
-        ready_copies = started([
-            pltpu.make_async_copy(block, decoded.at[n], ready_semaphores.at[n])
-            for n, block in enumerate([ref.at[m] for ref in ready_refs for m in range(ref.shape[0])])
-        ])
+        late_copies, gram_copies = [], []
+        for n in range(late):
+            late_copies += started([pltpu.make_async_copy(late_refs[n], late_blocks[n], late_semaphores.at[n])])
+            gram_copies.append(started(fetch_gram(
+                gram_any, gram_ref, gram_semaphores, n, row_block(ready + n, staged), row_shape, surface_rows
+            )))
+        for block in range(blocks):
+            for place, source in enumerate(ready_blocks):
+                @pl.when(row_place(block, staged) == place)
+                def _():
+                    pltpu.make_async_copy(source, decoded.at[place], ready_semaphores.at[place]).start()
         for copy in line_copies + late_copies:
             copy.wait()
         held = [packed_lines[n] for n in range(len(ends))]
-        at = 0
-        for part in late_parts:
-            at += part
-            last = late_blocks[at - 1]
-            held.append(last[pl.ds(last.shape[0] - extra, extra), :])
+        held += [block[pl.ds(block.shape[0] - extra, extra), :] for block in late_blocks]
         for n, value in enumerate(held):
             lines[n] = value.astype(jnp.float32).astype(jnp.int32)
         to_scalars = pltpu.make_async_copy(lines, scalars, scalar_semaphore.at[0])
         to_scalars.start()
-        at = 0
-        for n, part in enumerate(late_parts):
-            parts, at = late_blocks[at:at + part], at + part
-            for q in range(mirrors * shard_rows):
-                if n == 0 and q % shard_rows == 0:
-                    gram_copies[q // shard_rows].wait()
-                decoded[ready + n, q] = band_product(
-                    parts, q, row_shape, row_block(ready + n, staged), surface_rows, gram_ref
-                )
+        for n in range(late):
+            block_products(
+                late_blocks[n], n, row_shape, row_block(ready + n, staged), surface_rows, gram_ref, gram_copies[n],
+                decoded.at[ready + n],
+            )
         to_scalars.wait()
-        for copy in ready_copies:
-            copy.wait()
+
+    for at in range(surface_rows // 2 // phases):
+        @pl.when(group == at)
+        def _():
+            for block in range(last_needed(at - 1) + 1 if at else 0, last_needed(at) + 1):
+                place = row_place(block, staged)
+
+                @pl.when(place < ready)
+                def _():
+                    pltpu.make_async_copy(ready_blocks[0], decoded.at[place], ready_semaphores.at[place]).wait()
 
     for d in range(directions):
-        held = d
+        held = d ^ position("dir", staged)
         products, factors = [], []
         for phase in range(phases):
             i = group * phases + phase
@@ -499,31 +535,30 @@
     lanes = phases * pupil
     flops = 2 * padded * mirrors * samples * pupil * directions * surface_rows // 2
     vmem, anywhere = pl.BlockSpec(memory_space=pltpu.VMEM), pl.BlockSpec(memory_space=pl.ANY)
-    parts = [part for block in late for part in block]
-    counts = (len(sources), len(parts), len(ready))
-    semaphores = [mirrors, blocks, blocks, max(len(parts), 1), 1]
+    counts = (len(sources), len(late), len(ready))
+    semaphores = [(max(len(late), 1), mirrors), (blocks,), (blocks,), (max(len(late), 1),), (1,)]
     return pl.pallas_call(
-        functools.partial(
-            decode_kernel, row_shape, surface_rows, own, staged, norm, counts, [len(block) for block in late]
-        ),
+        functools.partial(decode_kernel, row_shape, surface_rows, own, staged, norm, counts),
         grid=(width // lanes,),
         out_shape=jax.ShapeDtypeStruct((own, directions, width), jnp.bfloat16),
         in_specs=[vmem] * 2 + [anywhere] * (sum(counts) + 1),
         out_specs=pl.BlockSpec((own, directions, lanes), lambda s: (0, 0, s)),
         scratch_shapes=[
-            pltpu.VMEM((acts, padded), jnp.bfloat16),
+            pltpu.VMEM(
+                (max(len(late), 1), mirrors, band_span(shard_rows, surface_rows) * NA, padded), jnp.bfloat16
+            ),
             pltpu.VMEM((blocks, mirrors * shard_rows, samples, padded), jnp.bfloat16),
             pltpu.VMEM((lanes // LANES, own * directions, LANES), jnp.float32),
             pltpu.VMEM((blocks, extra, LANES), jnp.bfloat16),
             pltpu.VMEM((blocks, extra, LANES), jnp.int32),
             pltpu.SMEM((blocks, extra, LANES), jnp.int32),
-            *[pltpu.VMEM(part.shape, part.dtype) for part in parts],
-            *[pltpu.SemaphoreType.DMA((count,)) for count in semaphores],
+            *[pltpu.VMEM(block.shape, block.dtype) for block in late],
+            *[pltpu.SemaphoreType.DMA(count) for count in semaphores],
         ],
         compiler_params=pltpu.CompilerParams(vmem_limit_bytes=VMEM_BYTES),
         cost_estimate=pl.CostEstimate(flops=flops, bytes_accessed=2 * own * directions * width, transcendentals=0),
         name="decode",
-    )(*differences, *sources, *parts, *ready, gram_rows)
+    )(*differences, *sources, *late, *ready, gram_rows)
 
 
 def swap(block, axis, distance):
@@ -558,7 +593,7 @@
             differences, [every], [], [ready], gram_rows, own, row_shape, surface_rows, pupil, norm, staged
         )
 
-    lines = lax.all_to_all(jnp.broadcast_to(lines, (directions,) + lines.shape), "dir", 0, 0, tiled=True)
+    lines = jnp.stack([lines] + [swap(lines, "dir", e) for e in range(1, directions)])
     packed = pack(turned, [lines])
     packed, pokes = lax.optimization_barrier((packed, pokes))
     first, second = turn(packed, 2, 4), turn(packed, 4, 2)
@@ -569,11 +604,12 @@
     diagonal = turn(first, 4, 2)
     sources = [source[None] for source in (sibling, first, second)]
     near, *differences = bands(gram_rows, sources, 1, staged, row_shape, surface_rows, lines, pupil)
-    near, first_sibling, second_sibling = lax.optimization_barrier((near, first_sibling, second_sibling))
+    near, first_sibling, second_sibling, diagonal = lax.optimization_barrier(
+        (near, first_sibling, second_sibling, diagonal)
+    )
+    late = [diagonal, swap(diagonal, "row", 1)]
     others = [first_sibling[None], second_sibling[None]]
     far, = bands(gram_rows, others, 4, staged, row_shape, surface_rows)
-    far, diagonal = lax.optimization_barrier((far, diagonal))
-    late = [[diagonal], [swap(diagonal, "row", 1)]]
     return decode(
         differences, [packed[None], *sources, *others], late, [own_rows, near, far], gram_rows, own, row_shape,
         surface_rows, pupil, norm, staged,

time: 66.8 us -> 65.6 us (0.982)
  blocking collectives: 11.9 us -> 0 us
  starting transfers between devices: 5.11 us -> 10.2 us
  waiting for transfers between devices: 2.64 us -> 6.86 us
  Pallas kernels: 45.1 us -> 46.8 us
  local copies, waits for them, and re-layouts: 1.57 us -> 0 us
  other arithmetic: 0 us -> 1.3 us
    all_to_all x1 -> x0, blocking collectives: 11.9 us -> none  [shards(): lax.all_to_all(jnp.broadcast_to(lines, (directions,) + lines.shape), 'dir...]
    ppermute x4 -> x7, starting transfers between devices: 0.58 us -> 5.84 us  [swap(): lax.ppermute(block, axis, [(i, i ^ distance) for i in range(lax.axis_size...]
    ppermute x3, waiting for transfers between devices: 0.28 us -> 2.65 us  [turn(): lax.ppermute(block, 'row', [(i, i ^ (odd if i % 2 else even)) for i in ra...]
    ppermute x4 -> x7, waiting for transfers between devices: 2.36 us -> 4.21 us  [swap(): lax.ppermute(block, axis, [(i, i ^ distance) for i in range(lax.axis_size...]
    another operation x0 -> x1, other arithmetic: none -> 1.3 us  [shards(): jnp.stack([lines] + [swap(lines, 'dir', e) for e in range(1, directions)])]
    unnamed x4 -> x0, local copies, waits for them, and re-layouts: 0.87 us -> none
    pallas_call x2, Pallas kernels: 11.1 us -> 12 us  [bands(): pl.pallas_call(functools.partial(bands_kernel, row_shape, surface_rows, f...]
    pallas_call x1, Pallas kernels: 16 us -> 16.9 us  [decode(): pl.pallas_call(functools.partial(decode_kernel, row_shape, surface_rows,...]
  transfers between devices with their start and end apart: 7 -> 10, of which waited for: 2 -> 4; matrix products, arithmetic and copies ran while one was open for 0% -> 0% of each run, Pallas kernels for 38% -> 40%
where the time goes in v10:
time: 65.6 us; the launch traced here: 65.2 us
  Pallas kernels  46.8 us (71%)
  starting transfers between devices  10.2 us (16%)
  waiting for transfers between devices  6.86 us (10%)
  other arithmetic  1.3 us (2%)
    pallas_call x1, Pallas kernels, decode(): pl.pallas_call(functools.partial(decode_kernel, row_shape, surface_rows,...  16.9 us
    pallas_call x2, Pallas kernels, bands(): pl.pallas_call(functools.partial(bands_kernel, row_shape, surface_rows, f...  12 us
    pallas_call x1, Pallas kernels, gram(): pl.pallas_call(functools.partial(gram_kernel, row_shape, surface_rows), g...  11.2 us
    ppermute x7, starting transfers between devices, swap(): lax.ppermute(block, axis, [(i, i ^ distance) for i in range(lax.axis_size...  5.84 us
    ppermute x3, starting transfers between devices, turn(): lax.ppermute(block, 'row', [(i, i ^ (odd if i % 2 else even)) for i in ra...  4.32 us
    ppermute x7, waiting for transfers between devices, swap(): lax.ppermute(block, axis, [(i, i ^ distance) for i in range(lax.axis_size...  4.21 us
    pallas_call x1, Pallas kernels, own_side(): pl.pallas_call(signs_kernel, out_shape=[jax.ShapeDtypeStruct((table.size...  2.74 us
    ppermute x3, waiting for transfers between devices, turn(): lax.ppermute(block, 'row', [(i, i ^ (odd if i % 2 else even)) for i in ra...  2.65 us
  transfers between devices with their start and end apart: 10, of which 4 were waited for; matrix products, arithmetic and copies ran while one was open for 0% of the time, Pallas kernels for 40%

profile of v10, /device:TPU:0, one launch (start us, length us, event | category | flops | bytes accessed | tf_op | source)
XLA Modules:
  0.0 65.2 jit_solution(8320522401836098195)
XLA Ops:
  0.0 1.4 %small_lines.1 = s32[8,256]{1,0:T(8,128)} custom-call(s32[3,1,4]{2,1,0:T(1,128)} %bitcast.22, s32[3,1,160]{2,1,0:T(1,128)} %bitcast.21, s32[1,2,80]{2,1,0:T(2,128)} %valid_ref.1), custom_call_target="tpu_custom_call" | custom-call | tf_op jit(solution)/shard_map/small_lines/pallas_call | solution.py:39
  1.4 5.0 %collective-permute-start.2 = (s32[8,256]{1,0:T(8,128)}, s32[8,256]{1,0:T(8,128)S(1)}, u32[]{:S(2)}, u32[]{:S(2)}) collective-permute-start(s32[8,256]{1,0:T(8,128)} %small_lines.1), channel_id=1, source_target_pairs={{0,24},{8,16},{16,8},{24,0},{1,25},{9,17},{17,9},{25,1},{2,26},{10... | collective-permute-start | bytes 24584 | tf_op jit(solution)/shard_map/ppermute | solution.py:565
  6.4 0.0 collective-permute-start.1
  6.4 0.6 collective-permute-start
  7.0 1.3 %collective-permute-done.2 = s32[8,256]{1,0:T(8,128)S(1)} collective-permute-done((s32[8,256]{1,0:T(8,128)}, s32[8,256]{1,0:T(8,128)S(1)}, u32[]{:S(2)}, u32[]{:S(2)}) %collective-permute-start.2) | collective-permute-done | bytes 8224 | tf_op jit(solution)/shard_map/ppermute | solution.py:565
  8.3 2.9 %collective-permute-done.1 = s32[8,256]{1,0:T(8,128)S(1)} collective-permute-done((s32[8,256]{1,0:T(8,128)}, s32[8,256]{1,0:T(8,128)S(1)}, u32[]{:S(2)}, u32[]{:S(2)}) %collective-permute-start.1) | collective-permute-done | bytes 8224 | tf_op jit(solution)/shard_map/ppermute | solution.py:565
  11.2 0.0 collective-permute-done
  11.2 1.3 %pad_add_fusion.refs_0_.refs_3_ = s32[4,8,256]{2,1,0:T(8,128)} fusion(s32[1,8,256]{2,1,0:T(8,128)S(1)} %bitcast.18, s32[1,8,256]{2,1,0:T(8,128)S(1)} %bitcast.19, s32[1,8,256]{2,1,0:T(8,128)S(1)} %bitcast.20, s32[1,8,256]{2,1,0:T(8,128)} %bitcast.16), kind=kLoop, calls=%fused_computation | loop fusion | flops 24576 | bytes 65536 | tf_op jit(solution)/shard_map/stack | solution.py:596
  12.5 2.6 %pack_influence.1.packed_ref = bf16[2704,128]{1,0:T(8,128)(2,1)} custom-call(bf16[3,4,144,192]{3,2,1,0:T(8,128)(2,1)} %bitcast.15, s32[4,8,256]{2,1,0:T(8,128)} %pad_add_fusion.refs_0_.refs_3_), custom_call_target="tpu_custom_call" | custom-call | bytes 995328 | tf_op jit(solution)/shard_map/pack_influence/pallas_call | solution.py:80
  15.1 1.5 %collective-permute-start.4 = (bf16[2704,128]{1,0:T(8,128)(2,1)}, bf16[2704,128]{1,0:T(8,128)(2,1)}, u32[]{:S(2)}, u32[]{:S(2)}) collective-permute-start(bf16[2704,128]{1,0:T(8,128)(2,1)} %pack_influence.1.packed_ref), channel_id=1, source_target_pairs={{0,4},{1,3},{2,6},{3,1},{4,0},{5,7},{6,2},{7,5},{8,12},{9,11},{10,... | collective-permute-start | bytes 2076680 | tf_op jit(solution)/shard_map/ppermute | solution.py:569
  16.6 1.5 %collective-permute-start.3 = (bf16[2704,128]{1,0:T(8,128)(2,1)}, bf16[2704,128]{1,0:T(8,128)(2,1)}, u32[]{:S(2)}, u32[]{:S(2)}) collective-permute-start(bf16[2704,128]{1,0:T(8,128)(2,1)} %pack_influence.1.packed_ref), channel_id=1, source_target_pairs={{0,2},{1,5},{2,0},{3,7},{4,6},{5,1},{6,4},{7,3},{8,10},{9,13},{10,... | collective-permute-start | bytes 2076680 | tf_op jit(solution)/shard_map/ppermute | solution.py:569
  18.1 0.0 collective-permute-start.5
  18.1 2.7 %own_signs.1 = (s32[54,128]{1,0:T(8,128)}, s32[13,64,128]{2,1,0:T(8,128)}, f8e4m3fn[224,2048]{1,0:T(32,128)(4,1)}, f32[224,128]{1,0:T(8,128)}) custom-call(s32[3,48,48]{2,1,0:T(8,128)} %table_ref.1, s32[16,128]{1,0:T(8,128)} %bitcast.17), custom_call_target="tpu_custom_call" | custom-call | tf_op jit(solution)/shard_map/own_signs/pallas_call | solution.py:141
  20.8 11.2 %gram_rows.1 = (bf16[6912,224]{1,0:T(8,128)(2,1)}, bf16[1,12,192,224]{3,2,1,0:T(8,128)(2,1)}) custom-call(s32[54,128]{1,0:T(8,128)} %get-tuple-element.24.codes_ref, s32[13,64,128]{2,1,0:T(8,128)} %get-tuple-element.25.words, f8e4m3fn[224,2048]{1,0:T(32,128)(4,1)} %get-tuple-element.26.own_signs, f32[224,128]{1,0:T(8,128)} %get-tuple-element.27.own_sums, ...), custom_call_target="tpu_custom_call" | custom-call | flops 6341787648 | bytes 3096576 | tf_op jit(solution)/shard_map/gram_rows/pallas_call | solution.py:217
  32.1 0.4 collective-permute-done.4
  32.4 0.0 collective-permute-done.3
  32.5 0.2 collective-permute-start.7
  32.7 1.3 %collective-permute-start.8 = (bf16[2704,128]{1,0:T(8,128)(2,1)}, bf16[2704,128]{1,0:T(8,128)(2,1)}, u32[]{:S(2)}, u32[]{:S(2)}) collective-permute-start(bf16[2704,128]{1,0:T(8,128)(2,1)} %collective-permute-done.3), channel_id=1, source_target_pairs={{0,4},{1,3},{2,6},{3,1},{4,0},{5,7},{6,2},{7,5},{8,12},{9,11},{10,... | collective-permute-start | bytes 2076680 | tf_op jit(solution)/shard_map/ppermute | solution.py:569
  34.0 0.0 collective-permute-start.6
  34.0 0.0 collective-permute-done.5
  34.0 7.7 %bands.2 = (bf16[3,12,192,224]{3,2,1,0:T(8,128)(2,1)}, bf16[4,2,80,512]{3,2,1,0:T(8,128)(2,1)}, bf16[4,160,128]{2,1,0:T(8,128)(2,1)}) custom-call(bf16[6912,224]{1,0:T(8,128)(2,1)} %get-tuple-element.30.gram_any.refs_13_, bf16[1,2704,128]{2,1,0:T(8,128)(2,1)} %bitcast.8.refs_0_.refs_3_, bf16[1,2704,128]{2,1,0:T(8,128)(2,1)} %bitcast.9.refs_1_.refs_4_, ...), custom_call_target="tpu_custom_call" | custom-call | flops 792723456 | bytes 4128768 | tf_op jit(solution)/shard_map/bands/pallas_call | solution.py:377
  41.7 0.0 collective-permute-done.7
  41.7 2.3 %collective-permute-done.8.refs_8_ = bf16[2704,128]{1,0:T(8,128)(2,1)} collective-permute-done((bf16[2704,128]{1,0:T(8,128)(2,1)}, bf16[2704,128]{1,0:T(8,128)(2,1)}, u32[]{:S(2)}, u32[]{:S(2)}) %collective-permute-start.8) | collective-permute-done | bytes 692256 | tf_op jit(solution)/shard_map/ppermute | solution.py:569
  44.0 0.0 collective-permute-done.6
  44.0 0.0 collective-permute-start.9
  44.0 4.3 %bands.3.refs_12_ = bf16[2,12,192,224]{3,2,1,0:T(8,128)(2,1)} custom-call(bf16[6912,224]{1,0:T(8,128)(2,1)} %get-tuple-element.30.gram_any.refs_13_, bf16[1,2704,128]{2,1,0:T(8,128)(2,1)} %bitcast.12.refs_0_.refs_6_, bf16[1,2704,128]{2,1,0:T(8,128)(2,1)} %bitcast.13.refs_1_.refs_7_), custom_call_target="tpu_custom_call" | custom-call | flops 528482304 | bytes 2752512 | tf_op jit(solution)/shard_map/bands/pallas_call | solution.py:377
  48.3 0.0 collective-permute-done.9.refs_9_
  48.3 16.9 %decode.1 = bf16[216,4,2560]{2,1,0:T(4,128)(2,1)} custom-call(bf16[4,2,80,512]{3,2,1,0:T(8,128)(2,1)} %get-tuple-element.33.refs_0_, bf16[4,160,128]{2,1,0:T(8,128)(2,1)} %get-tuple-element.34.refs_1_, bf16[1,2704,128]{2,1,0:T(8,128)(2,1)} %bitcast.14, bf16[1,2704,128]{2,1,0:T(8,128)(2,1)} %bitcast.8.refs_0_.refs_3_, ...), custom_call_target="tpu_custom_call" | custom-call | flops 2642411520 | bytes 4423680 | tf_op jit(solution)/shard_map/decode/pallas_call | solution.py:540
Async XLA Ops:
  1.4 6.9 %collective-permute-start.2 = (s32[8,256]{1,0:T(8,128)}, s32[8,256]{1,0:T(8,128)S(1)}, u32[]{:S(2)}, u32[]{:S(2)}) collective-permute-start(s32[8,256]{1,0:T(8,128)} %small_lines.1), channel_id=1, source_target_pairs={{0,24},{8,16},{16,8},{24,0},{1,25},{9,17},{17,9},{25,1},{2,26},{10... | collective-permute-start | bytes 24584 | tf_op jit(solution)/shard_map/ppermute | solution.py:565
  6.4 4.8 %collective-permute-start.1 = (s32[8,256]{1,0:T(8,128)}, s32[8,256]{1,0:T(8,128)S(1)}, u32[]{:S(2)}, u32[]{:S(2)}) collective-permute-start(s32[8,256]{1,0:T(8,128)} %small_lines.1), channel_id=1, source_target_pairs={{0,16},{8,24},{16,0},{24,8},{1,17},{9,25},{17,1},{25,9},{2,18},{10... | collective-permute-start | bytes 24584 | tf_op jit(solution)/shard_map/ppermute | solution.py:565
  6.4 4.8 %collective-permute-start = (s32[8,256]{1,0:T(8,128)}, s32[8,256]{1,0:T(8,128)S(1)}, u32[]{:S(2)}, u32[]{:S(2)}) collective-permute-start(s32[8,256]{1,0:T(8,128)} %small_lines.1), channel_id=1, source_target_pairs={{0,8},{8,0},{16,24},{24,16},{1,9},{9,1},{17,25},{25,17},{2,10},{10... | collective-permute-start | bytes 24584 | tf_op jit(solution)/shard_map/ppermute | solution.py:565
  15.1 17.4 %collective-permute-start.4 = (bf16[2704,128]{1,0:T(8,128)(2,1)}, bf16[2704,128]{1,0:T(8,128)(2,1)}, u32[]{:S(2)}, u32[]{:S(2)}) collective-permute-start(bf16[2704,128]{1,0:T(8,128)(2,1)} %pack_influence.1.packed_ref), channel_id=1, source_target_pairs={{0,4},{1,3},{2,6},{3,1},{4,0},{5,7},{6,2},{7,5},{8,12},{9,11},{10,... | collective-permute-start | bytes 2076680 | tf_op jit(solution)/shard_map/ppermute | solution.py:569
  16.6 15.8 %collective-permute-start.3 = (bf16[2704,128]{1,0:T(8,128)(2,1)}, bf16[2704,128]{1,0:T(8,128)(2,1)}, u32[]{:S(2)}, u32[]{:S(2)}) collective-permute-start(bf16[2704,128]{1,0:T(8,128)(2,1)} %pack_influence.1.packed_ref), channel_id=1, source_target_pairs={{0,2},{1,5},{2,0},{3,7},{4,6},{5,1},{6,4},{7,3},{8,10},{9,13},{10,... | collective-permute-start | bytes 2076680 | tf_op jit(solution)/shard_map/ppermute | solution.py:569
  18.1 15.9 %collective-permute-start.5 = (bf16[2704,128]{1,0:T(8,128)(2,1)}, bf16[2704,128]{1,0:T(8,128)(2,1)}, u32[]{:S(2)}, u32[]{:S(2)}) collective-permute-start(bf16[2704,128]{1,0:T(8,128)(2,1)} %pack_influence.1.packed_ref), channel_id=1, source_target_pairs={{0,1},{1,0},{2,3},{3,2},{4,5},{5,4},{6,7},{7,6},{8,9},{9,8},{10,11... | collective-permute-start | bytes 2076680 | tf_op jit(solution)/shard_map/ppermute | solution.py:565
  32.5 9.2 %collective-permute-start.7 = (bf16[2704,128]{1,0:T(8,128)(2,1)}, bf16[2704,128]{1,0:T(8,128)(2,1)}, u32[]{:S(2)}, u32[]{:S(2)}) collective-permute-start(bf16[2704,128]{1,0:T(8,128)(2,1)} %collective-permute-done.4), channel_id=1, source_target_pairs={{0,1},{1,0},{2,3},{3,2},{4,5},{5,4},{6,7},{7,6},{8,9},{9,8},{10,11... | collective-permute-start | bytes 2076680 | tf_op jit(solution)/shard_map/ppermute | solution.py:565
  32.7 11.3 %collective-permute-start.8 = (bf16[2704,128]{1,0:T(8,128)(2,1)}, bf16[2704,128]{1,0:T(8,128)(2,1)}, u32[]{:S(2)}, u32[]{:S(2)}) collective-permute-start(bf16[2704,128]{1,0:T(8,128)(2,1)} %collective-permute-done.3), channel_id=1, source_target_pairs={{0,4},{1,3},{2,6},{3,1},{4,0},{5,7},{6,2},{7,5},{8,12},{9,11},{10,... | collective-permute-start | bytes 2076680 | tf_op jit(solution)/shard_map/ppermute | solution.py:569
  34.0 10.0 %collective-permute-start.6 = (bf16[2704,128]{1,0:T(8,128)(2,1)}, bf16[2704,128]{1,0:T(8,128)(2,1)}, u32[]{:S(2)}, u32[]{:S(2)}) collective-permute-start(bf16[2704,128]{1,0:T(8,128)(2,1)} %collective-permute-done.3), channel_id=1, source_target_pairs={{0,1},{1,0},{2,3},{3,2},{4,5},{5,4},{6,7},{7,6},{8,9},{9,8},{10,11... | collective-permute-start | bytes 2076680 | tf_op jit(solution)/shard_map/ppermute | solution.py:565
  44.0 4.3 %collective-permute-start.9 = (bf16[2704,128]{1,0:T(8,128)(2,1)}, bf16[2704,128]{1,0:T(8,128)(2,1)}, u32[]{:S(2)}, u32[]{:S(2)}) collective-permute-start(bf16[2704,128]{1,0:T(8,128)(2,1)} %collective-permute-done.8.refs_8_), channel_id=1, source_target_pairs={{0,1},{1,0},{2,3},{3,2},{4,5},{5,4},{6,7},{7,6},{8,9},{9,8},{10,11... | collective-permute-start | bytes 2076680 | tf_op jit(solution)/shard_map/ppermute | solution.py:565

commit v11 on v9

--- a/solution.py
+++ b/solution.py
@@ -16,7 +16,7 @@
 NARROW = jnp.float8_e4m3fn
 LANES = 128
 WINDOW = 256
-VMEM_BYTES = 63 * 1024 * 1024
+VMEM_BYTES = 127 * 512 * 1024
 
 
 def parity(codes, rows):
@@ -63,19 +63,26 @@
             tails.append(turned[:, LANES:])
         tails.append(jnp.zeros((samples, LANES - groups * (slots - LANES)), jnp.bfloat16))
         packed_ref[pl.ds(base + groups * samples, samples), :] = jnp.concatenate(tails, axis=1)
-    count = rows // 2 + 1
-    lines = [ref[n, mirrors:mirrors + count, :LANES] for ref in lines_refs for n in range(ref.shape[0])]
+    count = rows // 2
+    every = [ref.at[n] for ref in lines_refs for n in range(ref.shape[0])]
+    feet = [ref[mirrors + count:mirrors + count + 1, :mirrors * rows] for ref in every]
+    feet.append(jnp.zeros((1, LANES - mirrors * rows * len(every)), jnp.int32))
+    lines = [ref[mirrors:mirrors + count, :LANES] for ref in every] + [jnp.concatenate(feet, axis=1)]
     extra = packed_ref.shape[0] - 2 * (groups + 1) * samples
-    lines.append(jnp.zeros((extra - count * len(lines), LANES), jnp.int32))
+    lines.append(jnp.zeros((extra - count * len(every) - 1, LANES), jnp.int32))
     packed_ref[pl.ds(packed_ref.shape[0] - extra, extra), :] = (
         jnp.concatenate(lines, axis=0).astype(jnp.float32).astype(jnp.bfloat16)
     )
 
 
+def extra_rows(directions, rows):
+    return -(-(directions * (rows // 2) + 1) // 16) * 16
+
+
 def pack(block, lines):
     mirrors, rows, slots, samples = block.shape
     vmem = pl.BlockSpec(memory_space=pltpu.VMEM)
-    extra = -(-sum(line.shape[0] for line in lines) * (rows // 2 + 1) // 16) * 16
+    extra = extra_rows(sum(line.shape[0] for line in lines), rows)
     return pl.pallas_call(
         pack_kernel,
         out_shape=jax.ShapeDtypeStruct(((mirrors * rows + 2) * samples + extra, LANES), block.dtype),
@@ -91,7 +98,7 @@
     return jnp.transpose(jnp.broadcast_to(row, (LANES, LANES)), (1, 0))
 
 
-def signs_kernel(table_ref, pokes_ref, codes_ref, words, own_signs, own_sums):
+def own_side_of(table_ref, pokes_ref, codes_ref, words, own_signs, own_sums):
     planes = pokes_ref.shape[0]
     mirrors, rows, columns = table_ref.shape
     for line in range(codes_ref.shape[0]):
@@ -134,31 +141,20 @@
     own_sums[...] = jnp.broadcast_to(jnp.sum(total, axis=1, keepdims=True), own_sums.shape)
 
 
-def own_side(table, pokes, own):
-    own = -(-own // 32) * 32
-    vmem = pl.BlockSpec(memory_space=pltpu.VMEM)
-    return pl.pallas_call(
-        signs_kernel,
-        out_shape=[
-            jax.ShapeDtypeStruct((table.size // LANES, LANES), jnp.int32),
-            jax.ShapeDtypeStruct((BITS, LANES // 2, LANES), jnp.int32),
-            jax.ShapeDtypeStruct((own, pokes.size), NARROW),
-            jax.ShapeDtypeStruct((own, LANES), jnp.float32),
-        ],
-        in_specs=[vmem] * 2,
-        out_specs=[vmem] * 4,
-        compiler_params=pltpu.CompilerParams(vmem_limit_bytes=VMEM_BYTES),
-        name="own_signs",
-    )(table, pokes)
-
-
-def gram_kernel(row_shape, surface_rows, codes_ref, words, own_signs, own_sums, packed_ref, gram_out, first_ref, gram_ref, semaphores):
+def gram_kernel(
+    row_shape, surface_rows, table_ref, pokes_ref, packed_ref, gram_out, first_ref, gram_ref, codes_ref, words,
+    own_signs, own_sums, semaphores
+):
     mirror = pl.program_id(0)
     half = LANES // 2
     own, pokes = own_signs.shape
     planes = pokes // LANES
     lines = codes_ref.shape[0] // row_shape[0]
     height = gram_ref.shape[0] // row_shape[0]
+
+    @pl.when(mirror == 0)
+    def _():
+        own_side_of(table_ref, pokes_ref, codes_ref, words, own_signs, own_sums)
 
     def chunk(index, _):
         word = []
@@ -208,8 +204,9 @@
             send(k).wait()
 
 
-def gram(codes, words, own_signs, own_sums, packed, row_shape, surface_rows):
-    acts, (own, count) = codes.size, own_signs.shape
+def gram(table, pokes, packed, own, row_shape, surface_rows):
+    own = -(-own // 32) * 32
+    acts, count = table.size, pokes.size
     mirrors, shard_rows, slots, samples = row_shape
     vmem = pl.BlockSpec(memory_space=pltpu.VMEM)
     return pl.pallas_call(
@@ -219,18 +216,25 @@
             jax.ShapeDtypeStruct((acts, own), jnp.bfloat16),
             jax.ShapeDtypeStruct((1, mirrors * shard_rows, samples, own), jnp.bfloat16),
         ],
-        in_specs=[vmem] * 5,
+        in_specs=[vmem] * 3,
         out_specs=[
             pl.BlockSpec(memory_space=pl.ANY),
             pl.BlockSpec((1, shard_rows, samples, own), lambda s: (0, s, 0, 0)),
         ],
-        scratch_shapes=[pltpu.VMEM((acts, own), jnp.bfloat16), pltpu.SemaphoreType.DMA((mirrors,))],
+        scratch_shapes=[
+            pltpu.VMEM((acts, own), jnp.bfloat16),
+            pltpu.VMEM((acts // LANES, LANES), jnp.int32),
+            pltpu.VMEM((BITS, LANES // 2, LANES), jnp.int32),
+            pltpu.VMEM((own, count), NARROW),
+            pltpu.VMEM((own, LANES), jnp.float32),
+            pltpu.SemaphoreType.DMA((mirrors,)),
+        ],
         compiler_params=pltpu.CompilerParams(vmem_limit_bytes=VMEM_BYTES),
         cost_estimate=pl.CostEstimate(
             flops=2 * own * acts * count, bytes_accessed=2 * own * acts, transcendentals=0
         ),
         name="gram_rows",
-    )(codes, words, own_signs, own_sums, packed)
+    )(table, pokes, packed)
 
 
 def position(axis, staged):
@@ -398,7 +402,7 @@
     lines_refs, refs = refs[:counts[0]], refs[counts[0]:]
     late_refs, refs = refs[:counts[1]], refs[counts[1]:]
     ready_refs, refs = refs[:counts[2]], refs[counts[2]:]
-    (gram_any, out_ref, gram_ref, decoded, total, packed_lines, lines, scalars, *refs) = refs
+    (gram_any, out_ref, gram_ref, decoded, total, packed_lines, lines, foot_rows, scalars, *refs) = refs
     late_blocks, refs = refs[:counts[1]], refs[counts[1]:]
     gram_semaphores, ready_semaphores, line_semaphores, late_semaphores, scalar_semaphore = refs
     group = pl.program_id(0)
@@ -408,7 +412,8 @@
     blocks = surface_rows // shard_rows
     late = len(late_parts)
     ready = blocks - late
-    width = shard_rows // 2 + 1
+    count = shard_rows // 2
+    rows = mirrors * shard_rows
     extra = lines.shape[1]
 
     @pl.when(group == 0)
@@ -427,7 +432,7 @@
         ])
         gram_copies = started(fetch_gram(gram_any, gram_ref, gram_semaphores, mirrors)) if late else []
         ready_copies = started([
-            pltpu.make_async_copy(block, decoded.at[n], ready_semaphores.at[n])
+            pltpu.make_async_copy(block, decoded.at[pl.ds(n * rows, rows)], ready_semaphores.at[n])
             for n, block in enumerate([ref.at[m] for ref in ready_refs for m in range(ref.shape[0])])
         ])
         for copy in line_copies + late_copies:
@@ -440,7 +445,9 @@
             held.append(last[pl.ds(last.shape[0] - extra, extra), :])
         for n, value in enumerate(held):
             lines[n] = value.astype(jnp.float32).astype(jnp.int32)
-        to_scalars = pltpu.make_async_copy(lines, scalars, scalar_semaphore.at[0])
+        feet = jnp.concatenate([lines[n, directions * count:directions * count + 1] for n in range(blocks)], axis=0)
+        foot_rows[...] = row_place(feet // shard_rows, staged) * rows + feet % shard_rows
+        to_scalars = pltpu.make_async_copy(foot_rows, scalars, scalar_semaphore.at[0])
         to_scalars.start()
         at = 0
         for n, part in enumerate(late_parts):
@@ -448,7 +455,7 @@
             for q in range(mirrors * shard_rows):
                 if n == 0 and q % shard_rows == 0:
                     gram_copies[q // shard_rows].wait()
-                decoded[ready + n, q] = band_product(
+                decoded[(ready + n) * rows + q] = band_product(
                     parts, q, row_shape, row_block(ready + n, staged), surface_rows, gram_ref
                 )
         to_scalars.wait()
@@ -456,7 +463,7 @@
             copy.wait()
 
     for d in range(directions):
-        held = d
+        held = d ^ position("dir", staged)
         products, factors = [], []
         for phase in range(phases):
             i = group * phases + phase
@@ -465,17 +472,17 @@
             for k in range(mirrors):
                 picked = []
                 for y in range(2):
-                    row = scalars[block, held * width + width - 1, k * shard_rows + (2 * phase + y) % shard_rows]
-                    picked.append(decoded[row_place(row // shard_rows, staged), k * shard_rows + row % shard_rows])
+                    row = k * shard_rows + (2 * phase + y) % shard_rows
+                    picked.append(decoded[scalars[block, held * rows + row] + k * shard_rows])
                 sums.append(picked[0] + picked[1])
                 changes.append(picked[1] - picked[0])
-            right = [jnp.concatenate(rows, axis=0) for rows in (sums, changes)]
-            mixed = jnp.concatenate([rows[depth:] for rows in right], axis=0)
+            right = [jnp.concatenate(part, axis=0) for part in (sums, changes)]
+            mixed = jnp.concatenate([part[depth:] for part in right], axis=0)
             rest = jnp.dot(rest_ref[held], mixed, preferred_element_type=jnp.float32)
-            for kind, rows in enumerate(right):
-                whole = jnp.dot(whole_ref[held, kind], rows[:depth], preferred_element_type=jnp.float32)
+            for kind, part in enumerate(right):
+                whole = jnp.dot(whole_ref[held, kind], part[:depth], preferred_element_type=jnp.float32)
                 products.append(whole + rest[kind * pupil // 2:(kind + 1) * pupil // 2])
-            valid = lines[block, pl.ds(held * width + phase % (shard_rows // 2), 1), :][:, :pupil // 2]
+            valid = lines[block, pl.ds(held * count + phase % count, 1), :][:, :pupil // 2]
             factors += [valid.astype(jnp.float32) * norm] * 2
         product = jnp.concatenate(products, axis=0)
         factor = jnp.concatenate(factors, axis=1)
@@ -493,7 +500,7 @@
     acts, padded = gram_rows.shape
     directions = differences[0].shape[0]
     blocks = surface_rows // shard_rows
-    extra = -(-directions * (shard_rows // 2 + 1) // 16) * 16
+    extra = extra_rows(directions, shard_rows)
     phases = LANES // math.gcd(pupil, LANES)
     width = surface_rows // 2 * pupil
     lanes = phases * pupil
@@ -512,11 +519,12 @@
         out_specs=pl.BlockSpec((own, directions, lanes), lambda s: (0, 0, s)),
         scratch_shapes=[
             pltpu.VMEM((acts, padded), jnp.bfloat16),
-            pltpu.VMEM((blocks, mirrors * shard_rows, samples, padded), jnp.bfloat16),
+            pltpu.VMEM((blocks * mirrors * shard_rows, samples, padded), jnp.bfloat16),
             pltpu.VMEM((lanes // LANES, own * directions, LANES), jnp.float32),
             pltpu.VMEM((blocks, extra, LANES), jnp.bfloat16),
             pltpu.VMEM((blocks, extra, LANES), jnp.int32),
-            pltpu.SMEM((blocks, extra, LANES), jnp.int32),
+            pltpu.VMEM((blocks, LANES), jnp.int32),
+            pltpu.SMEM((blocks, LANES), jnp.int32),
             *[pltpu.VMEM(part.shape, part.dtype) for part in parts],
             *[pltpu.SemaphoreType.DMA((count,)) for count in semaphores],
         ],
@@ -552,31 +560,28 @@
         lines = lax.all_gather(lines, "dir")
         packed = pack(turned, [lines])
         every = lax.all_gather(packed, "row")
-        gram_rows, _ = gram(*own_side(actuator_codes, pokes, own), packed, row_shape, surface_rows)
+        gram_rows, _ = gram(actuator_codes, pokes, packed, own, row_shape, surface_rows)
         ready, *differences = bands(gram_rows, [every], 0, staged, row_shape, surface_rows, lines, pupil)
         return decode(
             differences, [every], [], [ready], gram_rows, own, row_shape, surface_rows, pupil, norm, staged
         )
 
-    lines = lax.all_to_all(jnp.broadcast_to(lines, (directions,) + lines.shape), "dir", 0, 0, tiled=True)
-    packed = pack(turned, [lines])
-    packed, pokes = lax.optimization_barrier((packed, pokes))
+    lines = [lines[None]] + [swap(lines, "dir", e)[None] for e in range(1, directions)]
+    packed = pack(turned, lines)
     first, second = turn(packed, 2, 4), turn(packed, 4, 2)
     sibling = swap(packed, "row", 1)
-    gram_rows, own_rows = gram(*own_side(actuator_codes, pokes, own), packed, row_shape, surface_rows)
+    gram_rows, own_rows = gram(actuator_codes, pokes, packed, own, row_shape, surface_rows)
     gram_rows, first, second = lax.optimization_barrier((gram_rows, first, second))
+    diagonal = turn(first, 4, 2)
     first_sibling, second_sibling = swap(first, "row", 1), swap(second, "row", 1)
-    diagonal = turn(first, 4, 2)
     sources = [source[None] for source in (sibling, first, second)]
+    lines = jnp.concatenate(lines, axis=0)
     near, *differences = bands(gram_rows, sources, 1, staged, row_shape, surface_rows, lines, pupil)
-    near, first_sibling, second_sibling = lax.optimization_barrier((near, first_sibling, second_sibling))
-    others = [first_sibling[None], second_sibling[None]]
-    far, = bands(gram_rows, others, 4, staged, row_shape, surface_rows)
-    far, diagonal = lax.optimization_barrier((far, diagonal))
-    late = [[diagonal], [swap(diagonal, "row", 1)]]
+    near, diagonal = lax.optimization_barrier((near, diagonal))
+    late = [[block] for block in (first_sibling, second_sibling, diagonal, swap(diagonal, "row", 1))]
     return decode(
-        differences, [packed[None], *sources, *others], late, [own_rows, near, far], gram_rows, own, row_shape,
-        surface_rows, pupil, norm, staged,
+        differences, [packed[None], *sources], late, [own_rows, near], gram_rows, own, row_shape, surface_rows, pupil,
+        norm, staged,
     )
 
 

time: 66.8 us -> 62.1 us (0.930)
  blocking collectives: 11.9 us -> 0 us
  waiting for transfers between devices: 2.64 us -> 10.6 us
  Pallas kernels: 45.1 us -> 39.3 us
  starting transfers between devices: 5.11 us -> 10.7 us
  local copies, waits for them, and re-layouts: 1.57 us -> 0.61 us
    all_to_all x1 -> x0, blocking collectives: 11.9 us -> none  [shards(): lax.all_to_all(jnp.broadcast_to(lines, (directions,) + lines.shape), 'dir...]
    ppermute x4 -> x7, starting transfers between devices: 0.58 us -> 6.13 us  [swap(): lax.ppermute(block, axis, [(i, i ^ distance) for i in range(lax.axis_size...]
    ppermute x4 -> x7, waiting for transfers between devices: 2.36 us -> 6.68 us  [swap(): lax.ppermute(block, axis, [(i, i ^ distance) for i in range(lax.axis_size...]
    pallas_call x2 -> x1, Pallas kernels: 11.1 us -> 6.91 us  [bands(): pl.pallas_call(functools.partial(bands_kernel, row_shape, surface_rows, f...]
    ppermute x3, waiting for transfers between devices: 0.28 us -> 3.96 us  [turn(): lax.ppermute(block, 'row', [(i, i ^ (odd if i % 2 else even)) for i in ra...]
    pallas_call x1 -> x0, Pallas kernels: 2.74 us -> none  [own_side(): pl.pallas_call(signs_kernel, out_shape=[jax.ShapeDtypeStruct((table.size...]
    pallas_call x1, Pallas kernels: 11.2 us -> 12.1 us  [gram(): pl.pallas_call(functools.partial(gram_kernel, row_shape, surface_rows), g...]
    broadcast_in_dim x1 -> x0, local copies, waits for them, and re-layouts: 0.7 us -> none  [shards(): jnp.broadcast_to(lines, (directions,) + lines.shape)]
  transfers between devices with their start and end apart: 7 -> 10, of which waited for: 2 -> 5; matrix products, arithmetic and copies ran while one was open for 0% -> 1% of each run, Pallas kernels for 38% -> 31%
where the time goes in v11:
time: 62.1 us; the launch traced here: 61.8 us
  Pallas kernels  39.3 us (63%)
  starting transfers between devices  10.7 us (17%)
  waiting for transfers between devices  10.6 us (17%)
    pallas_call x1, Pallas kernels, decode(): pl.pallas_call(functools.partial(decode_kernel, row_shape, surface_rows,...  16.2 us
    pallas_call x1, Pallas kernels, gram(): pl.pallas_call(functools.partial(gram_kernel, row_shape, surface_rows), g...  12.1 us
    pallas_call x1, Pallas kernels, bands(): pl.pallas_call(functools.partial(bands_kernel, row_shape, surface_rows, f...  6.91 us
    ppermute x7, waiting for transfers between devices, swap(): lax.ppermute(block, axis, [(i, i ^ distance) for i in range(lax.axis_size...  6.68 us
    ppermute x7, starting transfers between devices, swap(): lax.ppermute(block, axis, [(i, i ^ distance) for i in range(lax.axis_size...  6.13 us
    ppermute x3, starting transfers between devices, turn(): lax.ppermute(block, 'row', [(i, i ^ (odd if i % 2 else even)) for i in ra...  4.53 us
    ppermute x3, waiting for transfers between devices, turn(): lax.ppermute(block, 'row', [(i, i ^ (odd if i % 2 else even)) for i in ra...  3.96 us
    pallas_call x1, Pallas kernels, pack(): pl.pallas_call(pack_kernel, out_shape=jax.ShapeDtypeStruct(((mirrors * ro...  2.66 us
  transfers between devices with their start and end apart: 10, of which 5 were waited for; matrix products, arithmetic and copies ran while one was open for 1% of the time, Pallas kernels for 31%

profile of v11, /device:TPU:0, one launch (start us, length us, event | category | flops | bytes accessed | tf_op | source)
XLA Modules:
  0.0 61.8 jit_solution(12867023656270068339)
XLA Ops:
  0.0 1.4 %small_lines.1 = s32[8,256]{1,0:T(8,128)} custom-call(s32[3,1,4]{2,1,0:T(1,128)} %bitcast.23, s32[3,1,160]{2,1,0:T(1,128)} %bitcast.22, s32[1,2,80]{2,1,0:T(2,128)} %valid_ref.1), custom_call_target="tpu_custom_call" | custom-call | tf_op jit(solution)/shard_map/small_lines/pallas_call | solution.py:38
  1.4 5.0 %collective-permute-start.2 = (s32[8,256]{1,0:T(8,128)}, s32[8,256]{1,0:T(8,128)S(1)}, u32[]{:S(2)}, u32[]{:S(2)}) collective-permute-start(s32[8,256]{1,0:T(8,128)} %small_lines.1), channel_id=1, source_target_pairs={{0,24},{8,16},{16,8},{24,0},{1,25},{9,17},{17,9},{25,1},{2,26},{10... | collective-permute-start | bytes 24584 | tf_op jit(solution)/shard_map/ppermute | solution.py:538
  6.4 0.0 collective-permute-start.1
  6.4 0.6 collective-permute-start
  7.0 1.3 %collective-permute-done.2 = s32[8,256]{1,0:T(8,128)S(1)} collective-permute-done((s32[8,256]{1,0:T(8,128)}, s32[8,256]{1,0:T(8,128)S(1)}, u32[]{:S(2)}, u32[]{:S(2)}) %collective-permute-start.2) | collective-permute-done | bytes 8224 | tf_op jit(solution)/shard_map/ppermute | solution.py:538
  8.3 0.0 copy-start.1
  8.3 2.9 %collective-permute-done.1 = s32[8,256]{1,0:T(8,128)S(1)} collective-permute-done((s32[8,256]{1,0:T(8,128)}, s32[8,256]{1,0:T(8,128)S(1)}, u32[]{:S(2)}, u32[]{:S(2)}) %collective-permute-start.1) | collective-permute-done | bytes 8224 | tf_op jit(solution)/shard_map/ppermute | solution.py:538
  11.2 0.0 copy-start.3
  11.2 0.0 collective-permute-done
  11.2 0.0 copy-start.5
  11.2 0.0 copy-done.1
  11.2 0.6 copy-done.3
  11.8 0.0 copy-done.5
  11.8 2.7 %pack_influence.1.packed_ref = bf16[2704,128]{1,0:T(8,128)(2,1)} custom-call(bf16[3,4,144,192]{3,2,1,0:T(8,128)(2,1)} %bitcast.13, s32[1,8,256]{2,1,0:T(8,128)} %bitcast.14, s32[1,8,256]{2,1,0:T(8,128)} %bitcast.20, s32[1,8,256]{2,1,0:T(8,128)} %bitcast.18, s32[1,8,256]{2,1,0:T(8,128)} %bitcast.16), custom_call_target="tpu_custom_call" | custom-call | bytes 995328 | tf_op jit(solution)/shard_map/pack_influence/pallas_call | solution.py:86
  14.4 1.5 %collective-permute-start.4 = (bf16[2704,128]{1,0:T(8,128)(2,1)}, bf16[2704,128]{1,0:T(8,128)(2,1)}, u32[]{:S(2)}, u32[]{:S(2)}) collective-permute-start(bf16[2704,128]{1,0:T(8,128)(2,1)} %pack_influence.1.packed_ref), channel_id=1, source_target_pairs={{0,4},{1,3},{2,6},{3,1},{4,0},{5,7},{6,2},{7,5},{8,12},{9,11},{10,... | collective-permute-start | bytes 2076680 | tf_op jit(solution)/shard_map/ppermute | solution.py:542
  16.0 1.5 %collective-permute-start.3 = (bf16[2704,128]{1,0:T(8,128)(2,1)}, bf16[2704,128]{1,0:T(8,128)(2,1)}, u32[]{:S(2)}, u32[]{:S(2)}) collective-permute-start(bf16[2704,128]{1,0:T(8,128)(2,1)} %pack_influence.1.packed_ref), channel_id=1, source_target_pairs={{0,2},{1,5},{2,0},{3,7},{4,6},{5,1},{6,4},{7,3},{8,10},{9,13},{10,... | collective-permute-start | bytes 2076680 | tf_op jit(solution)/shard_map/ppermute | solution.py:542
  17.5 0.0 collective-permute-start.5
  17.5 0.0 copy-start
  17.5 0.0 copy-start.2
  17.5 0.0 copy-start.4
  17.5 0.0 copy-start.6
  17.5 12.1 %gram_rows.1 = (bf16[6912,224]{1,0:T(8,128)(2,1)}, bf16[1,12,192,224]{3,2,1,0:T(8,128)(2,1)}) custom-call(s32[3,48,48]{2,1,0:T(8,128)} %table_ref.1, s32[16,128]{1,0:T(8,128)} %bitcast.24, bf16[2704,128]{1,0:T(8,128)(2,1)} %pack_influence.1.packed_ref), custom_call_target="tpu_custom_call" | custom-call | flops 6341787648 | bytes 3096576 | tf_op jit(solution)/shard_map/gram_rows/pallas_call | solution.py:212
  29.6 2.2 %collective-permute-done.4 = bf16[2704,128]{1,0:T(8,128)(2,1)} collective-permute-done((bf16[2704,128]{1,0:T(8,128)(2,1)}, bf16[2704,128]{1,0:T(8,128)(2,1)}, u32[]{:S(2)}, u32[]{:S(2)}) %collective-permute-start.4) | collective-permute-done | bytes 692256 | tf_op jit(solution)/shard_map/ppermute | solution.py:542
  31.8 0.0 collective-permute-done.3
  31.8 1.5 %collective-permute-start.8 = (bf16[2704,128]{1,0:T(8,128)(2,1)}, bf16[2704,128]{1,0:T(8,128)(2,1)}, u32[]{:S(2)}, u32[]{:S(2)}) collective-permute-start(bf16[2704,128]{1,0:T(8,128)(2,1)} %collective-permute-done.3), channel_id=1, source_target_pairs={{0,4},{1,3},{2,6},{3,1},{4,0},{5,7},{6,2},{7,5},{8,12},{9,11},{10,... | collective-permute-start | bytes 2076680 | tf_op jit(solution)/shard_map/ppermute | solution.py:542
  33.3 0.0 copy-done
  33.3 0.0 copy-done.2
  33.3 0.0 copy-done.4
  33.3 0.0 copy-done.6
  33.3 0.6 %pad_add_fusion.refs_3_ = s32[4,8,256]{2,1,0:T(8,128)} fusion(s32[1,8,256]{2,1,0:T(8,128)S(1)} %bitcast.17, s32[1,8,256]{2,1,0:T(8,128)S(1)} %bitcast.19, s32[1,8,256]{2,1,0:T(8,128)S(1)} %bitcast.21, s32[1,8,256]{2,1,0:T(8,128)S(1)} %bitcast.15), kind=kLoop, calls=%fused_computation | loop fusion | flops 24576 | bytes 65536 | tf_op jit(solution)/shard_map/concatenate | solution.py:578
  34.0 0.0 collective-permute-start.6
  34.0 0.5 collective-permute-start.7
  34.5 0.0 collective-permute-done.5
  34.5 6.9 %bands.1 = (bf16[3,12,192,224]{3,2,1,0:T(8,128)(2,1)}, bf16[4,2,80,512]{3,2,1,0:T(8,128)(2,1)}, bf16[4,160,128]{2,1,0:T(8,128)(2,1)}) custom-call(bf16[6912,224]{1,0:T(8,128)(2,1)} %get-tuple-element.16.gram_any.refs_12_, bf16[1,2704,128]{2,1,0:T(8,128)(2,1)} %bitcast.8.refs_0_.refs_3_, bf16[1,2704,128]{2,1,0:T(8,128)(2,1)} %bitcast.9.refs_1_.refs_4_, ...), custom_call_target="tpu_custom_call" | custom-call | flops 792723456 | bytes 4128768 | tf_op jit(solution)/shard_map/bands/pallas_call | solution.py:353
  41.4 1.7 %collective-permute-done.8.refs_8_ = bf16[2704,128]{1,0:T(8,128)(2,1)} collective-permute-done((bf16[2704,128]{1,0:T(8,128)(2,1)}, bf16[2704,128]{1,0:T(8,128)(2,1)}, u32[]{:S(2)}, u32[]{:S(2)}) %collective-permute-start.8) | collective-permute-done | bytes 692256 | tf_op jit(solution)/shard_map/ppermute | solution.py:542
  43.1 0.0 collective-permute-start.9
  43.1 0.0 collective-permute-done.7.refs_7_
  43.1 0.0 collective-permute-done.6.refs_6_
  43.1 2.5 %collective-permute-done.9.refs_9_ = bf16[2704,128]{1,0:T(8,128)(2,1)} collective-permute-done((bf16[2704,128]{1,0:T(8,128)(2,1)}, bf16[2704,128]{1,0:T(8,128)(2,1)}, u32[]{:S(2)}, u32[]{:S(2)}) %collective-permute-start.9) | collective-permute-done | bytes 692256 | tf_op jit(solution)/shard_map/ppermute | solution.py:538
  45.6 16.2 %decode.1 = bf16[216,4,2560]{2,1,0:T(4,128)(2,1)} custom-call(bf16[4,2,80,512]{3,2,1,0:T(8,128)(2,1)} %get-tuple-element.19.refs_0_, bf16[4,160,128]{2,1,0:T(8,128)(2,1)} %get-tuple-element.20.refs_1_, bf16[1,2704,128]{2,1,0:T(8,128)(2,1)} %bitcast.12, bf16[1,2704,128]{2,1,0:T(8,128)(2,1)} %bitcast.8.refs_0_.refs_3_, ...), custom_call_target="tpu_custom_call" | custom-call | flops 2642411520 | bytes 4423680 | tf_op jit(solution)/shard_map/decode/pallas_call | solution.py:512
Async XLA Ops:
  1.4 6.9 %collective-permute-start.2 = (s32[8,256]{1,0:T(8,128)}, s32[8,256]{1,0:T(8,128)S(1)}, u32[]{:S(2)}, u32[]{:S(2)}) collective-permute-start(s32[8,256]{1,0:T(8,128)} %small_lines.1), channel_id=1, source_target_pairs={{0,24},{8,16},{16,8},{24,0},{1,25},{9,17},{17,9},{25,1},{2,26},{10... | collective-permute-start | bytes 24584 | tf_op jit(solution)/shard_map/ppermute | solution.py:538
  6.4 4.8 %collective-permute-start.1 = (s32[8,256]{1,0:T(8,128)}, s32[8,256]{1,0:T(8,128)S(1)}, u32[]{:S(2)}, u32[]{:S(2)}) collective-permute-start(s32[8,256]{1,0:T(8,128)} %small_lines.1), channel_id=1, source_target_pairs={{0,16},{8,24},{16,0},{24,8},{1,17},{9,25},{17,1},{25,9},{2,18},{10... | collective-permute-start | bytes 24584 | tf_op jit(solution)/shard_map/ppermute | solution.py:538
  6.4 4.8 %collective-permute-start = (s32[8,256]{1,0:T(8,128)}, s32[8,256]{1,0:T(8,128)S(1)}, u32[]{:S(2)}, u32[]{:S(2)}) collective-permute-start(s32[8,256]{1,0:T(8,128)} %small_lines.1), channel_id=1, source_target_pairs={{0,8},{8,0},{16,24},{24,16},{1,9},{9,1},{17,25},{25,17},{2,10},{10... | collective-permute-start | bytes 24584 | tf_op jit(solution)/shard_map/ppermute | solution.py:538
  8.3 2.9 %copy-start.1 = (s32[8,256]{1,0:T(8,128)}, s32[8,256]{1,0:T(8,128)S(1)}, u32[]{:S(2)}) copy-start(s32[8,256]{1,0:T(8,128)S(1)} %collective-permute-done.2) | copy-start | bytes 24580
  11.2 0.6 copy-start.3
  11.2 0.6 copy-start.5
  14.4 17.4 %collective-permute-start.4 = (bf16[2704,128]{1,0:T(8,128)(2,1)}, bf16[2704,128]{1,0:T(8,128)(2,1)}, u32[]{:S(2)}, u32[]{:S(2)}) collective-permute-start(bf16[2704,128]{1,0:T(8,128)(2,1)} %pack_influence.1.packed_ref), channel_id=1, source_target_pairs={{0,4},{1,3},{2,6},{3,1},{4,0},{5,7},{6,2},{7,5},{8,12},{9,11},{10,... | collective-permute-start | bytes 2076680 | tf_op jit(solution)/shard_map/ppermute | solution.py:542
  16.0 15.8 %collective-permute-start.3 = (bf16[2704,128]{1,0:T(8,128)(2,1)}, bf16[2704,128]{1,0:T(8,128)(2,1)}, u32[]{:S(2)}, u32[]{:S(2)}) collective-permute-start(bf16[2704,128]{1,0:T(8,128)(2,1)} %pack_influence.1.packed_ref), channel_id=1, source_target_pairs={{0,2},{1,5},{2,0},{3,7},{4,6},{5,1},{6,4},{7,3},{8,10},{9,13},{10,... | collective-permute-start | bytes 2076680 | tf_op jit(solution)/shard_map/ppermute | solution.py:542
  17.5 17.0 %collective-permute-start.5 = (bf16[2704,128]{1,0:T(8,128)(2,1)}, bf16[2704,128]{1,0:T(8,128)(2,1)}, u32[]{:S(2)}, u32[]{:S(2)}) collective-permute-start(bf16[2704,128]{1,0:T(8,128)(2,1)} %pack_influence.1.packed_ref), channel_id=1, source_target_pairs={{0,1},{1,0},{2,3},{3,2},{4,5},{5,4},{6,7},{7,6},{8,9},{9,8},{10,11... | collective-permute-start | bytes 2076680 | tf_op jit(solution)/shard_map/ppermute | solution.py:538
  17.5 15.9 %copy-start = (s32[8,256]{1,0:T(8,128)S(1)}, s32[8,256]{1,0:T(8,128)}, u32[]{:S(2)}) copy-start(s32[8,256]{1,0:T(8,128)} %small_lines.1) | copy-start | bytes 24580
  17.5 15.9 %copy-start.2 = (s32[8,256]{1,0:T(8,128)S(1)}, s32[8,256]{1,0:T(8,128)}, u32[]{:S(2)}) copy-start(s32[8,256]{1,0:T(8,128)} %copy-done.1) | copy-start | bytes 24580
  17.5 15.9 %copy-start.4 = (s32[8,256]{1,0:T(8,128)S(1)}, s32[8,256]{1,0:T(8,128)}, u32[]{:S(2)}) copy-start(s32[8,256]{1,0:T(8,128)} %copy-done.3) | copy-start | bytes 24580
  17.5 15.9 %copy-start.6 = (s32[8,256]{1,0:T(8,128)S(1)}, s32[8,256]{1,0:T(8,128)}, u32[]{:S(2)}) copy-start(s32[8,256]{1,0:T(8,128)} %copy-done.5) | copy-start | bytes 24580
  31.8 11.3 %collective-permute-start.8 = (bf16[2704,128]{1,0:T(8,128)(2,1)}, bf16[2704,128]{1,0:T(8,128)(2,1)}, u32[]{:S(2)}, u32[]{:S(2)}) collective-permute-start(bf16[2704,128]{1,0:T(8,128)(2,1)} %collective-permute-done.3), channel_id=1, source_target_pairs={{0,4},{1,3},{2,6},{3,1},{4,0},{5,7},{6,2},{7,5},{8,12},{9,11},{10,... | collective-permute-start | bytes 2076680 | tf_op jit(solution)/shard_map/ppermute | solution.py:542
  34.0 9.2 %collective-permute-start.6 = (bf16[2704,128]{1,0:T(8,128)(2,1)}, bf16[2704,128]{1,0:T(8,128)(2,1)}, u32[]{:S(2)}, u32[]{:S(2)}) collective-permute-start(bf16[2704,128]{1,0:T(8,128)(2,1)} %collective-permute-done.3), channel_id=1, source_target_pairs={{0,1},{1,0},{2,3},{3,2},{4,5},{5,4},{6,7},{7,6},{8,9},{9,8},{10,11... | collective-permute-start | bytes 2076680 | tf_op jit(solution)/shard_map/ppermute | solution.py:538
  34.0 9.1 %collective-permute-start.7 = (bf16[2704,128]{1,0:T(8,128)(2,1)}, bf16[2704,128]{1,0:T(8,128)(2,1)}, u32[]{:S(2)}, u32[]{:S(2)}) collective-permute-start(bf16[2704,128]{1,0:T(8,128)(2,1)} %collective-permute-done.4), channel_id=1, source_target_pairs={{0,1},{1,0},{2,3},{3,2},{4,5},{5,4},{6,7},{7,6},{8,9},{9,8},{10,11... | collective-permute-start | bytes 2076680 | tf_op jit(solution)/shard_map/ppermute | solution.py:538
  43.1 2.5 %collective-permute-start.9 = (bf16[2704,128]{1,0:T(8,128)(2,1)}, bf16[2704,128]{1,0:T(8,128)(2,1)}, u32[]{:S(2)}, u32[]{:S(2)}) collective-permute-start(bf16[2704,128]{1,0:T(8,128)(2,1)} %collective-permute-done.8.refs_8_), channel_id=1, source_target_pairs={{0,1},{1,0},{2,3},{3,2},{4,5},{5,4},{6,7},{7,6},{8,9},{9,8},{10,11... | collective-permute-start | bytes 2076680 | tf_op jit(solution)/shard_map/ppermute | solution.py:538

commit v12 on v11

--- a/solution.py
+++ b/solution.py
@@ -44,31 +44,39 @@
     )(jnp.swapaxes(foot_rows, 0, 1), jnp.swapaxes(foot_columns, 0, 1), valid)
 
 
+def narrow_places(q, slots, samples):
+    narrow = slots - LANES
+    whole = LANES // narrow
+    if q < whole:
+        return [(0, samples, 0, q * narrow)]
+    half = samples // 2
+    lane = (q - whole) * narrow
+    return [(0, half, samples, lane), (half, half, samples, LANES // 2 + lane)]
+
+
 def pack_kernel(block_ref, *refs):
     lines_refs, packed_ref = refs[:-1], refs[-1]
     mirrors, rows, slots, samples = block_ref.shape
-    groups = mirrors * rows // 2
     identity = (
         lax.broadcasted_iota(jnp.int32, (samples, samples), 0) == lax.broadcasted_iota(jnp.int32, (samples, samples), 1)
     ).astype(jnp.float32).astype(jnp.bfloat16)
-    for part in range(2):
-        base = part * (groups + 1) * samples
-        tails = []
-        for group in range(groups):
-            k, l = divmod(part * groups + group, rows)
-            turned = lax.dot_general(
-                identity, block_ref[k, l], (((1,), (1,)), ((), ())), preferred_element_type=jnp.float32
-            ).astype(jnp.bfloat16)
-            packed_ref[pl.ds(base + group * samples, samples), :] = turned[:, :LANES]
-            tails.append(turned[:, LANES:])
-        tails.append(jnp.zeros((samples, LANES - groups * (slots - LANES)), jnp.bfloat16))
-        packed_ref[pl.ds(base + groups * samples, samples), :] = jnp.concatenate(tails, axis=1)
+    wide = mirrors * rows * samples
+    tails = {}
+    for q in range(mirrors * rows):
+        turned = lax.dot_general(
+            identity, block_ref[q // rows, q % rows], (((1,), (1,)), ((), ())), preferred_element_type=jnp.float32
+        ).astype(jnp.bfloat16)
+        packed_ref[pl.ds(q * samples, samples), :] = turned[:, :LANES]
+        for start, length, row, lane in narrow_places(q, slots, samples):
+            tails.setdefault((row, length), {})[lane] = turned[start:start + length, LANES:]
+    for (row, length), pieces in tails.items():
+        packed_ref[pl.ds(wide + row, length), :] = jnp.concatenate([pieces[lane] for lane in sorted(pieces)], axis=1)
     count = rows // 2
     every = [ref.at[n] for ref in lines_refs for n in range(ref.shape[0])]
     feet = [ref[mirrors + count:mirrors + count + 1, :mirrors * rows] for ref in every]
     feet.append(jnp.zeros((1, LANES - mirrors * rows * len(every)), jnp.int32))
     lines = [ref[mirrors:mirrors + count, :LANES] for ref in every] + [jnp.concatenate(feet, axis=1)]
-    extra = packed_ref.shape[0] - 2 * (groups + 1) * samples
+    extra = packed_ref.shape[0] - mirrors * rows * samples * slots // LANES
     lines.append(jnp.zeros((extra - count * len(every) - 1, LANES), jnp.int32))
     packed_ref[pl.ds(packed_ref.shape[0] - extra, extra), :] = (
         jnp.concatenate(lines, axis=0).astype(jnp.float32).astype(jnp.bfloat16)
@@ -85,7 +93,7 @@
     extra = extra_rows(sum(line.shape[0] for line in lines), rows)
     return pl.pallas_call(
         pack_kernel,
-        out_shape=jax.ShapeDtypeStruct(((mirrors * rows + 2) * samples + extra, LANES), block.dtype),
+        out_shape=jax.ShapeDtypeStruct((mirrors * rows * samples * slots // LANES + extra, LANES), block.dtype),
         in_specs=[vmem] * (1 + len(lines)),
         out_specs=vmem,
         compiler_params=pltpu.CompilerParams(vmem_limit_bytes=VMEM_BYTES),
@@ -195,7 +203,7 @@
             @pl.when(mirror == k)
             def _():
                 first_ref[0, l] = band_product(
-                    [packed_ref], k * row_shape[1] + l, row_shape, block, surface_rows, gram_ref
+                    packed_ref, k * row_shape[1] + l, row_shape, block, surface_rows, gram_ref
                 )
 
     @pl.when(mirror == pl.num_programs(0) - 1)
@@ -261,26 +269,29 @@
     return jnp.where((distance >= 2) & (distance < 6), middle, distance)
 
 
-def band_product(parts, q, row_shape, block, surface_rows, gram_ref):
+def band_product(source, q, row_shape, block, surface_rows, gram_ref):
     mirrors, shard_rows, slots, samples = row_shape
-    groups = mirrors * shard_rows // 2
     own = gram_ref.shape[1]
     narrow = slots - LANES
     k, l = divmod(q, shard_rows)
     band = jnp.clip((block * shard_rows + l) * NAR // surface_rows - 1, 0, NAR - BAND)
     column = pl.multiple_of((k * NAR + band) * NA, 16)
-    part, group = divmod(q, groups)
-    source, base = (parts[0], part * (groups + 1) * samples) if len(parts) == 1 else (parts[part], 0)
-    left = jnp.concatenate(
-        [source[pl.ds(base + group * samples, samples), :], source[pl.ds(base + groups * samples, samples), :]],
-        axis=1,
-    )
-    right = [gram_ref[pl.ds(column, LANES), :]]
-    if group:
-        right.append(jnp.zeros((group * narrow, own), jnp.bfloat16))
-    right.append(gram_ref[pl.ds(column + LANES, narrow), :])
-    right.append(jnp.zeros((LANES - (group + 1) * narrow, own), jnp.bfloat16))
-    return jnp.dot(left, jnp.concatenate(right, axis=0), preferred_element_type=jnp.float32).astype(jnp.bfloat16)
+    wide = mirrors * shard_rows * samples
+    products = []
+    for start, length, row, lane in narrow_places(q, slots, samples):
+        left = jnp.concatenate(
+            [source[pl.ds(q * samples + start, length), :], source[pl.ds(wide + row, length), :]], axis=1
+        )
+        right = [gram_ref[pl.ds(column, LANES), :]]
+        if lane:
+            right.append(jnp.zeros((lane, own), jnp.bfloat16))
+        right.append(gram_ref[pl.ds(column + LANES, narrow), :])
+        if lane + narrow < LANES:
+            right.append(jnp.zeros((LANES - lane - narrow, own), jnp.bfloat16))
+        products.append(
+            jnp.dot(left, jnp.concatenate(right, axis=0), preferred_element_type=jnp.float32).astype(jnp.bfloat16)
+        )
+    return jnp.concatenate(products, axis=0)
 
 
 def fetch_gram(gram_any, gram_ref, semaphores, mirrors):
@@ -297,12 +308,7 @@
     mirrors, shard_rows, slots, samples = row_shape
     sources = [ref.at[n] for ref, count in zip(refs, counts) for n in range(count)]
     refs = refs[len(counts):]
-    columns_ref = None
-    if len(refs) == 8:
-        columns_ref, out_ref, whole_ref, rest_ref, *refs = refs
-    else:
-        out_ref, *refs = refs
-    gram_ref, blocks, gram_semaphores, block_semaphores = refs
+    *columns_refs, out_ref, whole_ref, rest_ref, gram_ref, blocks, gram_semaphores, block_semaphores = refs
     step = pl.program_id(0)
     gram_copies = fetch_gram(gram_any, gram_ref, gram_semaphores, mirrors)
 
@@ -316,8 +322,8 @@
             copy.start()
         for n in range(1, len(sources)):
             fetch(n).start()
-        if columns_ref is not None:
-            build_differences(columns_ref, whole_ref, rest_ref, mirrors, samples)
+        columns = [ref.at[n] for ref in columns_refs for n in range(ref.shape[0])]
+        build_differences(columns, whole_ref, rest_ref, mirrors, samples)
 
     for n in range(len(sources)):
         @pl.when(step == n)
@@ -327,10 +333,10 @@
             for q in range(mirrors * shard_rows):
                 if n == 0 and q % shard_rows == 0:
                     gram_copies[q // shard_rows].wait()
-                out_ref[0, q] = band_product([blocks.at[n]], q, row_shape, block, surface_rows, gram_ref)
-
-
-def bands(gram_rows, sources, first, staged, row_shape, surface_rows, columns=None, pupil=None):
+                out_ref[0, q] = band_product(blocks.at[n], q, row_shape, block, surface_rows, gram_ref)
+
+
+def bands(gram_rows, sources, first, staged, row_shape, surface_rows, columns, pupil):
     acts, own = gram_rows.shape
     mirrors, shard_rows, slots, samples = row_shape
     counts = [source.shape[0] for source in sources]
@@ -340,16 +346,16 @@
     out_shape = [jax.ShapeDtypeStruct((sum(counts), rows, samples, own), jnp.bfloat16)]
     out_specs = [pl.BlockSpec((1, rows, samples, own), lambda s: (s, 0, 0, 0))]
     arguments, in_specs = [gram_rows, *sources], [anywhere] * (1 + len(sources))
-    if columns is not None:
-        depth = mirrors * samples // WINDOW * WINDOW
-        rest = 2 * (mirrors * samples - depth)
-        out_shape += [
-            jax.ShapeDtypeStruct((columns.shape[0], 2, pupil // 2, depth), jnp.bfloat16),
-            jax.ShapeDtypeStruct((columns.shape[0], pupil, rest), jnp.bfloat16),
-        ]
-        out_specs += [vmem] * 2
-        arguments.append(columns)
-        in_specs.append(vmem)
+    directions = sum(lines.shape[0] for lines in columns)
+    depth = mirrors * samples // WINDOW * WINDOW
+    rest = 2 * (mirrors * samples - depth)
+    out_shape += [
+        jax.ShapeDtypeStruct((directions, 2, pupil // 2, depth), jnp.bfloat16),
+        jax.ShapeDtypeStruct((directions, pupil, rest), jnp.bfloat16),
+    ]
+    out_specs += [vmem] * 2
+    arguments += columns
+    in_specs += [vmem] * len(columns)
     return pl.pallas_call(
         functools.partial(bands_kernel, row_shape, surface_rows, first, counts, staged),
         grid=(sum(counts),),
@@ -370,19 +376,19 @@
     )(*arguments)
 
 
-def build_differences(columns_ref, whole_ref, rest_ref, mirrors, samples):
+def build_differences(columns, whole_ref, rest_ref, mirrors, samples):
     half = whole_ref.shape[2]
     pupil, depth = 2 * half, whole_ref.shape[3]
     remainder = mirrors * samples - depth
     slope = lax.broadcasted_iota(jnp.int32, (half, pupil), 0)
     lane = lax.broadcasted_iota(jnp.int32, (half, pupil), 1)
     at = lax.broadcasted_iota(jnp.int32, (half, mirrors * samples), 1)
-    for d in range(columns_ref.shape[0]):
+    for d, columns_ref in enumerate(columns):
         sides = []
         for side in range(2):
             hit = None
             for k in range(mirrors):
-                line = jnp.broadcast_to(columns_ref[d, k:k + 1, :pupil], (half, pupil))
+                line = jnp.broadcast_to(columns_ref[k:k + 1, :pupil], (half, pupil))
                 column = jnp.sum(jnp.where(lane == slope * 2 + side, line, 0), axis=1, keepdims=True)
                 here = (at == column + k * samples).astype(jnp.float32)
                 hit = here if hit is None else hit + here
@@ -451,12 +457,12 @@
         to_scalars.start()
         at = 0
         for n, part in enumerate(late_parts):
-            parts, at = late_blocks[at:at + part], at + part
+            source, at = late_blocks[at], at + part
             for q in range(mirrors * shard_rows):
                 if n == 0 and q % shard_rows == 0:
                     gram_copies[q // shard_rows].wait()
                 decoded[(ready + n) * rows + q] = band_product(
-                    parts, q, row_shape, row_block(ready + n, staged), surface_rows, gram_ref
+                    source, q, row_shape, row_block(ready + n, staged), surface_rows, gram_ref
                 )
         to_scalars.wait()
         for copy in ready_copies:
@@ -483,12 +489,13 @@
                 whole = jnp.dot(whole_ref[held, kind], part[:depth], preferred_element_type=jnp.float32)
                 products.append(whole + rest[kind * pupil // 2:(kind + 1) * pupil // 2])
             valid = lines[block, pl.ds(held * count + phase % count, 1), :][:, :pupil // 2]
-            factors += [valid.astype(jnp.float32) * norm] * 2
+            factors += [valid.astype(jnp.float32)] * 2
         product = jnp.concatenate(products, axis=0)
         factor = jnp.concatenate(factors, axis=1)
         for tile in range(out_ref.shape[2] // LANES):
             at = tile * LANES
-            value = jnp.transpose(product[at:at + LANES])[:own] * factor[:, at:at + LANES]
+            value = jnp.transpose((product[at:at + LANES] * norm).astype(jnp.bfloat16))
+            value = value.astype(jnp.float32)[:own] * factor[:, at:at + LANES]
             total[tile, pl.ds(d, own, stride=directions), :] = value
     for tile in range(out_ref.shape[2] // LANES):
         value = total[tile].reshape(own, directions, LANES)
@@ -561,7 +568,7 @@
         packed = pack(turned, [lines])
         every = lax.all_gather(packed, "row")
         gram_rows, _ = gram(actuator_codes, pokes, packed, own, row_shape, surface_rows)
-        ready, *differences = bands(gram_rows, [every], 0, staged, row_shape, surface_rows, lines, pupil)
+        ready, *differences = bands(gram_rows, [every], 0, staged, row_shape, surface_rows, [lines], pupil)
         return decode(
             differences, [every], [], [ready], gram_rows, own, row_shape, surface_rows, pupil, norm, staged
         )
@@ -575,7 +582,6 @@
     diagonal = turn(first, 4, 2)
     first_sibling, second_sibling = swap(first, "row", 1), swap(second, "row", 1)
     sources = [source[None] for source in (sibling, first, second)]
-    lines = jnp.concatenate(lines, axis=0)
     near, *differences = bands(gram_rows, sources, 1, staged, row_shape, surface_rows, lines, pupil)
     near, diagonal = lax.optimization_barrier((near, diagonal))
     late = [[block] for block in (first_sibling, second_sibling, diagonal, swap(diagonal, "row", 1))]

time: 62.1 us -> 60.9 us (0.981)
  transfers between devices with their start and end apart: 10 -> 10, of which waited for: 5 -> 5; matrix products, arithmetic and copies ran while one was open for 1% -> 0% of each run, Pallas kernels for 31% -> 31%
where the time goes in v12:
time: 60.9 us; the launch traced here: 60.6 us
  Pallas kernels  38.8 us (64%)
  starting transfers between devices  10.7 us (18%)
  waiting for transfers between devices  10.5 us (17%)
    pallas_call x1, Pallas kernels, decode(): pl.pallas_call(functools.partial(decode_kernel, row_shape, surface_rows,...  15.8 us
    pallas_call x1, Pallas kernels, gram(): pl.pallas_call(functools.partial(gram_kernel, row_shape, surface_rows), g...  12 us
    pallas_call x1, Pallas kernels, bands(): pl.pallas_call(functools.partial(bands_kernel, row_shape, surface_rows, f...  6.95 us
    ppermute x7, waiting for transfers between devices, swap(): lax.ppermute(block, axis, [(i, i ^ distance) for i in range(lax.axis_size...  6.65 us
    ppermute x7, starting transfers between devices, swap(): lax.ppermute(block, axis, [(i, i ^ distance) for i in range(lax.axis_size...  6.13 us
    ppermute x3, starting transfers between devices, turn(): lax.ppermute(block, 'row', [(i, i ^ (odd if i % 2 else even)) for i in ra...  4.53 us
    ppermute x3, waiting for transfers between devices, turn(): lax.ppermute(block, 'row', [(i, i ^ (odd if i % 2 else even)) for i in ra...  3.84 us
    pallas_call x1, Pallas kernels, pack(): pl.pallas_call(pack_kernel, out_shape=jax.ShapeDtypeStruct((mirrors * row...  2.64 us
  transfers between devices with their start and end apart: 10, of which 5 were waited for; matrix products, arithmetic and copies ran while one was open for 0% of the time, Pallas kernels for 31%

profile of v12, /device:TPU:0, one launch (start us, length us, event | category | flops | bytes accessed | tf_op | source)
XLA Modules:
  0.0 60.6 jit_solution(9972759939005489467)
XLA Ops:
  0.0 1.4 %small_lines.1 = s32[8,256]{1,0:T(8,128)} custom-call(s32[3,1,4]{2,1,0:T(1,128)} %bitcast.23, s32[3,1,160]{2,1,0:T(1,128)} %bitcast.22, s32[1,2,80]{2,1,0:T(2,128)} %valid_ref.1), custom_call_target="tpu_custom_call" | custom-call | tf_op jit(solution)/shard_map/small_lines/pallas_call | solution.py:38
  1.4 5.0 %collective-permute-start.2 = (s32[8,256]{1,0:T(8,128)}, s32[8,256]{1,0:T(8,128)S(1)}, u32[]{:S(2)}, u32[]{:S(2)}) collective-permute-start(s32[8,256]{1,0:T(8,128)} %small_lines.1), channel_id=1, source_target_pairs={{0,24},{8,16},{16,8},{24,0},{1,25},{9,17},{17,9},{25,1},{2,26},{10... | collective-permute-start | bytes 24584 | tf_op jit(solution)/shard_map/ppermute | solution.py:545
  6.4 0.0 collective-permute-start.1
  6.4 0.6 collective-permute-start
  7.0 1.3 %collective-permute-done.2 = s32[8,256]{1,0:T(8,128)S(1)} collective-permute-done((s32[8,256]{1,0:T(8,128)}, s32[8,256]{1,0:T(8,128)S(1)}, u32[]{:S(2)}, u32[]{:S(2)}) %collective-permute-start.2) | collective-permute-done | bytes 8224 | tf_op jit(solution)/shard_map/ppermute | solution.py:545
  8.3 0.0 copy-start
  8.3 2.9 %collective-permute-done.1 = s32[8,256]{1,0:T(8,128)S(1)} collective-permute-done((s32[8,256]{1,0:T(8,128)}, s32[8,256]{1,0:T(8,128)S(1)}, u32[]{:S(2)}, u32[]{:S(2)}) %collective-permute-start.1) | collective-permute-done | bytes 8224 | tf_op jit(solution)/shard_map/ppermute | solution.py:545
  11.2 0.0 copy-start.1
  11.2 0.0 collective-permute-done
  11.2 0.0 copy-start.2
  11.2 0.0 copy-done
  11.2 0.6 copy-done.1
  11.8 0.0 copy-done.2
  11.8 2.6 %pack_influence.1.packed_ref = bf16[2608,128]{1,0:T(8,128)(2,1)} custom-call(bf16[3,4,144,192]{3,2,1,0:T(8,128)(2,1)} %bitcast.13, s32[1,8,256]{2,1,0:T(8,128)} %bitcast.14, s32[1,8,256]{2,1,0:T(8,128)} %bitcast.20, s32[1,8,256]{2,1,0:T(8,128)} %bitcast.18, s32[1,8,256]{2,1,0:T(8,128)} %bitcast.16), custom_call_target="tpu_custom_call" | custom-call | bytes 995328 | tf_op jit(solution)/shard_map/pack_influence/pallas_call | solution.py:94
  14.4 1.5 %collective-permute-start.4 = (bf16[2608,128]{1,0:T(8,128)(2,1)}, bf16[2608,128]{1,0:T(8,128)(2,1)}, u32[]{:S(2)}, u32[]{:S(2)}) collective-permute-start(bf16[2608,128]{1,0:T(8,128)(2,1)} %pack_influence.1.packed_ref), channel_id=1, source_target_pairs={{0,4},{1,3},{2,6},{3,1},{4,0},{5,7},{6,2},{7,5},{8,12},{9,11},{10,... | collective-permute-start | bytes 2002952 | tf_op jit(solution)/shard_map/ppermute | solution.py:549
  16.0 1.5 %collective-permute-start.3 = (bf16[2608,128]{1,0:T(8,128)(2,1)}, bf16[2608,128]{1,0:T(8,128)(2,1)}, u32[]{:S(2)}, u32[]{:S(2)}) collective-permute-start(bf16[2608,128]{1,0:T(8,128)(2,1)} %pack_influence.1.packed_ref), channel_id=1, source_target_pairs={{0,2},{1,5},{2,0},{3,7},{4,6},{5,1},{6,4},{7,3},{8,10},{9,13},{10,... | collective-permute-start | bytes 2002952 | tf_op jit(solution)/shard_map/ppermute | solution.py:549
  17.4 0.0 collective-permute-start.5
  17.5 12.0 %gram_rows.1 = (bf16[6912,224]{1,0:T(8,128)(2,1)}, bf16[1,12,192,224]{3,2,1,0:T(8,128)(2,1)}) custom-call(s32[3,48,48]{2,1,0:T(8,128)} %table_ref.1, s32[16,128]{1,0:T(8,128)} %bitcast.24, bf16[2608,128]{1,0:T(8,128)(2,1)} %pack_influence.1.packed_ref), custom_call_target="tpu_custom_call" | custom-call | flops 6341787648 | bytes 3096576 | tf_op jit(solution)/shard_map/gram_rows/pallas_call | solution.py:220
  29.5 1.8 %collective-permute-done.4 = bf16[2608,128]{1,0:T(8,128)(2,1)} collective-permute-done((bf16[2608,128]{1,0:T(8,128)(2,1)}, bf16[2608,128]{1,0:T(8,128)(2,1)}, u32[]{:S(2)}, u32[]{:S(2)}) %collective-permute-start.4) | collective-permute-done | bytes 667680 | tf_op jit(solution)/shard_map/ppermute | solution.py:549
  31.3 0.0 collective-permute-done.3
  31.3 1.5 %collective-permute-start.8 = (bf16[2608,128]{1,0:T(8,128)(2,1)}, bf16[2608,128]{1,0:T(8,128)(2,1)}, u32[]{:S(2)}, u32[]{:S(2)}) collective-permute-start(bf16[2608,128]{1,0:T(8,128)(2,1)} %collective-permute-done.3), channel_id=1, source_target_pairs={{0,4},{1,3},{2,6},{3,1},{4,0},{5,7},{6,2},{7,5},{8,12},{9,11},{10,... | collective-permute-start | bytes 2002952 | tf_op jit(solution)/shard_map/ppermute | solution.py:549
  32.8 0.0 collective-permute-start.6
  32.8 0.5 collective-permute-start.7
  33.3 0.0 collective-permute-done.5
  33.3 6.9 %bands.1 = (bf16[3,12,192,224]{3,2,1,0:T(8,128)(2,1)}, bf16[4,2,80,512]{3,2,1,0:T(8,128)(2,1)}, bf16[4,160,128]{2,1,0:T(8,128)(2,1)}) custom-call(bf16[6912,224]{1,0:T(8,128)(2,1)} %get-tuple-element.16.gram_any.refs_12_, bf16[1,2608,128]{2,1,0:T(8,128)(2,1)} %bitcast.8.refs_0_.refs_3_, bf16[1,2608,128]{2,1,0:T(8,128)(2,1)} %bitcast.9.refs_1_.refs_4_, ...), custom_call_target="tpu_custom_call" | custom-call | flops 792723456 | bytes 4128768 | tf_op jit(solution)/shard_map/bands/pallas_call | solution.py:359
  40.3 2.1 %collective-permute-done.8.refs_8_ = bf16[2608,128]{1,0:T(8,128)(2,1)} collective-permute-done((bf16[2608,128]{1,0:T(8,128)(2,1)}, bf16[2608,128]{1,0:T(8,128)(2,1)}, u32[]{:S(2)}, u32[]{:S(2)}) %collective-permute-start.8) | collective-permute-done | bytes 667680 | tf_op jit(solution)/shard_map/ppermute | solution.py:549
  42.3 0.0 collective-permute-start.9
  42.3 0.0 collective-permute-done.7.refs_7_
  42.3 0.0 collective-permute-done.6.refs_6_
  42.3 2.4 %collective-permute-done.9.refs_9_ = bf16[2608,128]{1,0:T(8,128)(2,1)} collective-permute-done((bf16[2608,128]{1,0:T(8,128)(2,1)}, bf16[2608,128]{1,0:T(8,128)(2,1)}, u32[]{:S(2)}, u32[]{:S(2)}) %collective-permute-start.9) | collective-permute-done | bytes 667680 | tf_op jit(solution)/shard_map/ppermute | solution.py:545
  44.8 15.8 %decode.1 = bf16[216,4,2560]{2,1,0:T(4,128)(2,1)} custom-call(bf16[4,2,80,512]{3,2,1,0:T(8,128)(2,1)} %get-tuple-element.19.refs_0_, bf16[4,160,128]{2,1,0:T(8,128)(2,1)} %get-tuple-element.20.refs_1_, bf16[1,2608,128]{2,1,0:T(8,128)(2,1)} %bitcast.12, bf16[1,2608,128]{2,1,0:T(8,128)(2,1)} %bitcast.8.refs_0_.refs_3_, ...), custom_call_target="tpu_custom_call" | custom-call | flops 2642411520 | bytes 4423680 | tf_op jit(solution)/shard_map/decode/pallas_call | solution.py:519
Async XLA Ops:
  1.4 6.9 %collective-permute-start.2 = (s32[8,256]{1,0:T(8,128)}, s32[8,256]{1,0:T(8,128)S(1)}, u32[]{:S(2)}, u32[]{:S(2)}) collective-permute-start(s32[8,256]{1,0:T(8,128)} %small_lines.1), channel_id=1, source_target_pairs={{0,24},{8,16},{16,8},{24,0},{1,25},{9,17},{17,9},{25,1},{2,26},{10... | collective-permute-start | bytes 24584 | tf_op jit(solution)/shard_map/ppermute | solution.py:545
  6.4 4.8 %collective-permute-start.1 = (s32[8,256]{1,0:T(8,128)}, s32[8,256]{1,0:T(8,128)S(1)}, u32[]{:S(2)}, u32[]{:S(2)}) collective-permute-start(s32[8,256]{1,0:T(8,128)} %small_lines.1), channel_id=1, source_target_pairs={{0,16},{8,24},{16,0},{24,8},{1,17},{9,25},{17,1},{25,9},{2,18},{10... | collective-permute-start | bytes 24584 | tf_op jit(solution)/shard_map/ppermute | solution.py:545
  6.4 4.8 %collective-permute-start = (s32[8,256]{1,0:T(8,128)}, s32[8,256]{1,0:T(8,128)S(1)}, u32[]{:S(2)}, u32[]{:S(2)}) collective-permute-start(s32[8,256]{1,0:T(8,128)} %small_lines.1), channel_id=1, source_target_pairs={{0,8},{8,0},{16,24},{24,16},{1,9},{9,1},{17,25},{25,17},{2,10},{10... | collective-permute-start | bytes 24584 | tf_op jit(solution)/shard_map/ppermute | solution.py:545
  8.3 2.9 %copy-start = (s32[8,256]{1,0:T(8,128)}, s32[8,256]{1,0:T(8,128)S(1)}, u32[]{:S(2)}) copy-start(s32[8,256]{1,0:T(8,128)S(1)} %collective-permute-done.2) | copy-start | bytes 24580
  11.2 0.6 copy-start.1
  11.2 0.6 copy-start.2
  14.4 16.8 %collective-permute-start.4 = (bf16[2608,128]{1,0:T(8,128)(2,1)}, bf16[2608,128]{1,0:T(8,128)(2,1)}, u32[]{:S(2)}, u32[]{:S(2)}) collective-permute-start(bf16[2608,128]{1,0:T(8,128)(2,1)} %pack_influence.1.packed_ref), channel_id=1, source_target_pairs={{0,4},{1,3},{2,6},{3,1},{4,0},{5,7},{6,2},{7,5},{8,12},{9,11},{10,... | collective-permute-start | bytes 2002952 | tf_op jit(solution)/shard_map/ppermute | solution.py:549
  16.0 15.3 %collective-permute-start.3 = (bf16[2608,128]{1,0:T(8,128)(2,1)}, bf16[2608,128]{1,0:T(8,128)(2,1)}, u32[]{:S(2)}, u32[]{:S(2)}) collective-permute-start(bf16[2608,128]{1,0:T(8,128)(2,1)} %pack_influence.1.packed_ref), channel_id=1, source_target_pairs={{0,2},{1,5},{2,0},{3,7},{4,6},{5,1},{6,4},{7,3},{8,10},{9,13},{10,... | collective-permute-start | bytes 2002952 | tf_op jit(solution)/shard_map/ppermute | solution.py:549
  17.4 15.9 %collective-permute-start.5 = (bf16[2608,128]{1,0:T(8,128)(2,1)}, bf16[2608,128]{1,0:T(8,128)(2,1)}, u32[]{:S(2)}, u32[]{:S(2)}) collective-permute-start(bf16[2608,128]{1,0:T(8,128)(2,1)} %pack_influence.1.packed_ref), channel_id=1, source_target_pairs={{0,1},{1,0},{2,3},{3,2},{4,5},{5,4},{6,7},{7,6},{8,9},{9,8},{10,11... | collective-permute-start | bytes 2002952 | tf_op jit(solution)/shard_map/ppermute | solution.py:545
  31.3 11.0 %collective-permute-start.8 = (bf16[2608,128]{1,0:T(8,128)(2,1)}, bf16[2608,128]{1,0:T(8,128)(2,1)}, u32[]{:S(2)}, u32[]{:S(2)}) collective-permute-start(bf16[2608,128]{1,0:T(8,128)(2,1)} %collective-permute-done.3), channel_id=1, source_target_pairs={{0,4},{1,3},{2,6},{3,1},{4,0},{5,7},{6,2},{7,5},{8,12},{9,11},{10,... | collective-permute-start | bytes 2002952 | tf_op jit(solution)/shard_map/ppermute | solution.py:549
  32.8 9.5 %collective-permute-start.6 = (bf16[2608,128]{1,0:T(8,128)(2,1)}, bf16[2608,128]{1,0:T(8,128)(2,1)}, u32[]{:S(2)}, u32[]{:S(2)}) collective-permute-start(bf16[2608,128]{1,0:T(8,128)(2,1)} %collective-permute-done.3), channel_id=1, source_target_pairs={{0,1},{1,0},{2,3},{3,2},{4,5},{5,4},{6,7},{7,6},{8,9},{9,8},{10,11... | collective-permute-start | bytes 2002952 | tf_op jit(solution)/shard_map/ppermute | solution.py:545
  32.8 9.5 %collective-permute-start.7 = (bf16[2608,128]{1,0:T(8,128)(2,1)}, bf16[2608,128]{1,0:T(8,128)(2,1)}, u32[]{:S(2)}, u32[]{:S(2)}) collective-permute-start(bf16[2608,128]{1,0:T(8,128)(2,1)} %collective-permute-done.4), channel_id=1, source_target_pairs={{0,1},{1,0},{2,3},{3,2},{4,5},{5,4},{6,7},{7,6},{8,9},{9,8},{10,11... | collective-permute-start | bytes 2002952 | tf_op jit(solution)/shard_map/ppermute | solution.py:545
  42.3 2.5 %collective-permute-start.9 = (bf16[2608,128]{1,0:T(8,128)(2,1)}, bf16[2608,128]{1,0:T(8,128)(2,1)}, u32[]{:S(2)}, u32[]{:S(2)}) collective-permute-start(bf16[2608,128]{1,0:T(8,128)(2,1)} %collective-permute-done.8.refs_8_), channel_id=1, source_target_pairs={{0,1},{1,0},{2,3},{3,2},{4,5},{5,4},{6,7},{7,6},{8,9},{9,8},{10,11... | collective-permute-start | bytes 2002952 | tf_op jit(solution)/shard_map/ppermute | solution.py:545

commit v13 on v12

--- a/solution.py
+++ b/solution.py
@@ -12,6 +12,7 @@
 NAR = 48
 NA = 48
 BAND = 3
+REACH = 2
 BITS = 13
 NARROW = jnp.float8_e4m3fn
 LANES = 128
@@ -308,7 +309,11 @@
     mirrors, shard_rows, slots, samples = row_shape
     sources = [ref.at[n] for ref, count in zip(refs, counts) for n in range(count)]
     refs = refs[len(counts):]
-    *columns_refs, out_ref, whole_ref, rest_ref, gram_ref, blocks, gram_semaphores, block_semaphores = refs
+    *refs, gram_ref, blocks, gram_semaphores, block_semaphores = refs
+    if len(refs) > 1:
+        *columns_refs, out_ref, whole_ref, rest_ref = refs
+    else:
+        columns_refs, out_ref = [], refs[0]
     step = pl.program_id(0)
     gram_copies = fetch_gram(gram_any, gram_ref, gram_semaphores, mirrors)
 
@@ -323,7 +328,8 @@
         for n in range(1, len(sources)):
             fetch(n).start()
         columns = [ref.at[n] for ref in columns_refs for n in range(ref.shape[0])]
-        build_differences(columns, whole_ref, rest_ref, mirrors, samples)
+        if columns:
+            build_differences(columns, whole_ref, rest_ref, mirrors, samples)
 
     for n in range(len(sources)):
         @pl.when(step == n)
@@ -349,11 +355,12 @@
     directions = sum(lines.shape[0] for lines in columns)
     depth = mirrors * samples // WINDOW * WINDOW
     rest = 2 * (mirrors * samples - depth)
-    out_shape += [
-        jax.ShapeDtypeStruct((directions, 2, pupil // 2, depth), jnp.bfloat16),
-        jax.ShapeDtypeStruct((directions, pupil, rest), jnp.bfloat16),
-    ]
-    out_specs += [vmem] * 2
+    if columns:
+        out_shape += [
+            jax.ShapeDtypeStruct((directions, 2, pupil // 2, depth), jnp.bfloat16),
+            jax.ShapeDtypeStruct((directions, pupil, rest), jnp.bfloat16),
+        ]
+        out_specs += [vmem] * 2
     arguments += columns
     in_specs += [vmem] * len(columns)
     return pl.pallas_call(
@@ -380,19 +387,24 @@
     half = whole_ref.shape[2]
     pupil, depth = 2 * half, whole_ref.shape[3]
     remainder = mirrors * samples - depth
-    slope = lax.broadcasted_iota(jnp.int32, (half, pupil), 0)
-    lane = lax.broadcasted_iota(jnp.int32, (half, pupil), 1)
+    pick = lax.broadcasted_iota(jnp.int32, (pupil, pupil), 0)
+    lane = lax.broadcasted_iota(jnp.int32, (pupil, pupil), 1)
+    pick = (lane == pick % half * 2 + pick // half).astype(jnp.float32).astype(jnp.bfloat16)
+    lines = jnp.concatenate([ref[:, :pupil] for ref in columns], axis=0)
+    height = columns[0].shape[0]
+    turned = lax.dot_general(
+        pick, lines.astype(jnp.float32).astype(jnp.bfloat16), (((1,), (1,)), ((), ())),
+        preferred_element_type=jnp.float32,
+    ).astype(jnp.int32)
     at = lax.broadcasted_iota(jnp.int32, (half, mirrors * samples), 1)
-    for d, columns_ref in enumerate(columns):
+    for d in range(len(columns)):
         sides = []
         for side in range(2):
-            hit = None
+            wanted = None
             for k in range(mirrors):
-                line = jnp.broadcast_to(columns_ref[k:k + 1, :pupil], (half, pupil))
-                column = jnp.sum(jnp.where(lane == slope * 2 + side, line, 0), axis=1, keepdims=True)
-                here = (at == column + k * samples).astype(jnp.float32)
-                hit = here if hit is None else hit + here
-            sides.append(hit)
+                column = turned[side * half:(side + 1) * half, d * height + k:d * height + k + 1] + k * samples
+                wanted = column if wanted is None else jnp.where(at < k * samples, wanted, column)
+            sides.append((at == wanted).astype(jnp.float32))
         across, down = sides[1] - sides[0], sides[1] + sides[0]
         whole_ref[d, 0] = across[:, :depth].astype(jnp.bfloat16)
         whole_ref[d, 1] = down[:, :depth].astype(jnp.bfloat16)
@@ -422,6 +434,8 @@
     rows = mirrors * shard_rows
     extra = lines.shape[1]
 
+    ready_blocks = [ref.at[m] for ref in ready_refs for m in range(ref.shape[0])]
+
     @pl.when(group == 0)
     def _():
         def started(copies):
@@ -437,9 +451,9 @@
             pltpu.make_async_copy(late_refs[n], late_blocks[n], late_semaphores.at[n]) for n in range(counts[1])
         ])
         gram_copies = started(fetch_gram(gram_any, gram_ref, gram_semaphores, mirrors)) if late else []
-        ready_copies = started([
+        started([
             pltpu.make_async_copy(block, decoded.at[pl.ds(n * rows, rows)], ready_semaphores.at[n])
-            for n, block in enumerate([ref.at[m] for ref in ready_refs for m in range(ref.shape[0])])
+            for n, block in enumerate(ready_blocks)
         ])
         for copy in line_copies + late_copies:
             copy.wait()
@@ -465,8 +479,21 @@
                     source, q, row_shape, row_block(ready + n, staged), surface_rows, gram_ref
                 )
         to_scalars.wait()
-        for copy in ready_copies:
-            copy.wait()
+
+    def last_needed(at):
+        return min((2 * phases * (at + 1) - 1 + REACH) // shard_rows, blocks - 1)
+
+    for at in range(surface_rows // 2 // phases):
+        @pl.when(group == at)
+        def _():
+            for block in range(last_needed(at - 1) + 1 if at else 0, last_needed(at) + 1):
+                place = row_place(block, staged)
+
+                @pl.when(place < ready)
+                def _():
+                    pltpu.make_async_copy(
+                        ready_blocks[0], decoded.at[pl.ds(place * rows, rows)], ready_semaphores.at[place]
+                    ).wait()
 
     for d in range(directions):
         held = d ^ position("dir", staged)
@@ -583,11 +610,14 @@
     first_sibling, second_sibling = swap(first, "row", 1), swap(second, "row", 1)
     sources = [source[None] for source in (sibling, first, second)]
     near, *differences = bands(gram_rows, sources, 1, staged, row_shape, surface_rows, lines, pupil)
-    near, diagonal = lax.optimization_barrier((near, diagonal))
-    late = [[block] for block in (first_sibling, second_sibling, diagonal, swap(diagonal, "row", 1))]
+    near, first_sibling, second_sibling = lax.optimization_barrier((near, first_sibling, second_sibling))
+    others = [first_sibling[None], second_sibling[None]]
+    far, = bands(gram_rows, others, 4, staged, row_shape, surface_rows, [], pupil)
+    far, diagonal = lax.optimization_barrier((far, diagonal))
+    late = [[diagonal], [swap(diagonal, "row", 1)]]
     return decode(
-        differences, [packed[None], *sources], late, [own_rows, near], gram_rows, own, row_shape, surface_rows, pupil,
-        norm, staged,
+        differences, [packed[None], *sources, *others], late, [own_rows, near, far], gram_rows, own, row_shape,
+        surface_rows, pupil, norm, staged,
     )
 
 

time: 60.9 us -> 62.4 us (1.025)
  Pallas kernels: 38.8 us -> 42.3 us
  waiting for transfers between devices: 10.5 us -> 8.44 us
    pallas_call x1 -> x2, Pallas kernels: 6.95 us -> 10.5 us  [bands(): pl.pallas_call(functools.partial(bands_kernel, row_shape, surface_rows, f...]
    ppermute x3, waiting for transfers between devices: 3.84 us -> 1.79 us  [turn(): lax.ppermute(block, 'row', [(i, i ^ (odd if i % 2 else even)) for i in ra...]
  transfers between devices with their start and end apart: 10 -> 10, of which waited for: 5 -> 4; matrix products, arithmetic and copies ran while one was open for 0% -> 0% of each run, Pallas kernels for 31% -> 36%
where the time goes in v13:
time: 62.4 us; the launch traced here: 62.1 us
  Pallas kernels  42.3 us (68%)
  starting transfers between devices  10.7 us (17%)
  waiting for transfers between devices  8.44 us (14%)
    pallas_call x1, Pallas kernels, decode(): pl.pallas_call(functools.partial(decode_kernel, row_shape, surface_rows,...  15.7 us
    pallas_call x1, Pallas kernels, gram(): pl.pallas_call(functools.partial(gram_kernel, row_shape, surface_rows), g...  12 us
    pallas_call x2, Pallas kernels, bands(): pl.pallas_call(functools.partial(bands_kernel, row_shape, surface_rows, f...  10.5 us
    ppermute x7, waiting for transfers between devices, swap(): lax.ppermute(block, axis, [(i, i ^ distance) for i in range(lax.axis_size...  6.64 us
    ppermute x7, starting transfers between devices, swap(): lax.ppermute(block, axis, [(i, i ^ distance) for i in range(lax.axis_size...  6.2 us
    ppermute x3, starting transfers between devices, turn(): lax.ppermute(block, 'row', [(i, i ^ (odd if i % 2 else even)) for i in ra...  4.53 us
    pallas_call x1, Pallas kernels, pack(): pl.pallas_call(pack_kernel, out_shape=jax.ShapeDtypeStruct((mirrors * row...  2.64 us
    ppermute x3, waiting for transfers between devices, turn(): lax.ppermute(block, 'row', [(i, i ^ (odd if i % 2 else even)) for i in ra...  1.79 us
  transfers between devices with their start and end apart: 10, of which 4 were waited for; matrix products, arithmetic and copies ran while one was open for 0% of the time, Pallas kernels for 36%

profile of v13, /device:TPU:0, one launch (start us, length us, event | category | flops | bytes accessed | tf_op | source)
XLA Modules:
  0.0 62.1 jit_solution(15087827494483429403)
XLA Ops:
  0.0 1.4 %small_lines.1 = s32[8,256]{1,0:T(8,128)} custom-call(s32[3,1,4]{2,1,0:T(1,128)} %bitcast.25, s32[3,1,160]{2,1,0:T(1,128)} %bitcast.24, s32[1,2,80]{2,1,0:T(2,128)} %valid_ref.1), custom_call_target="tpu_custom_call" | custom-call | tf_op jit(solution)/shard_map/small_lines/pallas_call | solution.py:39
  1.4 5.0 %collective-permute-start.2 = (s32[8,256]{1,0:T(8,128)}, s32[8,256]{1,0:T(8,128)S(1)}, u32[]{:S(2)}, u32[]{:S(2)}) collective-permute-start(s32[8,256]{1,0:T(8,128)} %small_lines.1), channel_id=1, source_target_pairs={{0,24},{8,16},{16,8},{24,0},{1,25},{9,17},{17,9},{25,1},{2,26},{10... | collective-permute-start | bytes 24584 | tf_op jit(solution)/shard_map/ppermute | solution.py:572
  6.4 0.0 collective-permute-start.1
  6.4 0.6 collective-permute-start
  7.0 1.3 %collective-permute-done.2 = s32[8,256]{1,0:T(8,128)S(1)} collective-permute-done((s32[8,256]{1,0:T(8,128)}, s32[8,256]{1,0:T(8,128)S(1)}, u32[]{:S(2)}, u32[]{:S(2)}) %collective-permute-start.2) | collective-permute-done | bytes 8224 | tf_op jit(solution)/shard_map/ppermute | solution.py:572
  8.3 0.0 copy-start
  8.3 2.9 %collective-permute-done.1 = s32[8,256]{1,0:T(8,128)S(1)} collective-permute-done((s32[8,256]{1,0:T(8,128)}, s32[8,256]{1,0:T(8,128)S(1)}, u32[]{:S(2)}, u32[]{:S(2)}) %collective-permute-start.1) | collective-permute-done | bytes 8224 | tf_op jit(solution)/shard_map/ppermute | solution.py:572
  11.2 0.0 copy-start.1
  11.2 0.0 collective-permute-done
  11.2 0.0 copy-start.2
  11.2 0.0 copy-done
  11.2 0.6 copy-done.1
  11.8 0.0 copy-done.2
  11.8 2.6 %pack_influence.1.packed_ref = bf16[2608,128]{1,0:T(8,128)(2,1)} custom-call(bf16[3,4,144,192]{3,2,1,0:T(8,128)(2,1)} %bitcast.15, s32[1,8,256]{2,1,0:T(8,128)} %bitcast.16, s32[1,8,256]{2,1,0:T(8,128)} %bitcast.22, s32[1,8,256]{2,1,0:T(8,128)} %bitcast.20, s32[1,8,256]{2,1,0:T(8,128)} %bitcast.18), custom_call_target="tpu_custom_call" | custom-call | bytes 995328 | tf_op jit(solution)/shard_map/pack_influence/pallas_call | solution.py:95
  14.4 1.5 %collective-permute-start.4 = (bf16[2608,128]{1,0:T(8,128)(2,1)}, bf16[2608,128]{1,0:T(8,128)(2,1)}, u32[]{:S(2)}, u32[]{:S(2)}) collective-permute-start(bf16[2608,128]{1,0:T(8,128)(2,1)} %pack_influence.1.packed_ref), channel_id=1, source_target_pairs={{0,4},{1,3},{2,6},{3,1},{4,0},{5,7},{6,2},{7,5},{8,12},{9,11},{10,... | collective-permute-start | bytes 2002952 | tf_op jit(solution)/shard_map/ppermute | solution.py:576
  16.0 1.5 %collective-permute-start.3 = (bf16[2608,128]{1,0:T(8,128)(2,1)}, bf16[2608,128]{1,0:T(8,128)(2,1)}, u32[]{:S(2)}, u32[]{:S(2)}) collective-permute-start(bf16[2608,128]{1,0:T(8,128)(2,1)} %pack_influence.1.packed_ref), channel_id=1, source_target_pairs={{0,2},{1,5},{2,0},{3,7},{4,6},{5,1},{6,4},{7,3},{8,10},{9,13},{10,... | collective-permute-start | bytes 2002952 | tf_op jit(solution)/shard_map/ppermute | solution.py:576
  17.4 0.0 collective-permute-start.5
  17.5 12.0 %gram_rows.1 = (bf16[6912,224]{1,0:T(8,128)(2,1)}, bf16[1,12,192,224]{3,2,1,0:T(8,128)(2,1)}) custom-call(s32[3,48,48]{2,1,0:T(8,128)} %table_ref.1, s32[16,128]{1,0:T(8,128)} %bitcast.26, bf16[2608,128]{1,0:T(8,128)(2,1)} %pack_influence.1.packed_ref), custom_call_target="tpu_custom_call" | custom-call | flops 6341787648 | bytes 3096576 | tf_op jit(solution)/shard_map/gram_rows/pallas_call | solution.py:221
  29.5 1.8 %collective-permute-done.4 = bf16[2608,128]{1,0:T(8,128)(2,1)} collective-permute-done((bf16[2608,128]{1,0:T(8,128)(2,1)}, bf16[2608,128]{1,0:T(8,128)(2,1)}, u32[]{:S(2)}, u32[]{:S(2)}) %collective-permute-start.4) | collective-permute-done | bytes 667680 | tf_op jit(solution)/shard_map/ppermute | solution.py:576
  31.3 0.0 collective-permute-done.3
  31.3 0.0 collective-permute-start.7
  31.3 0.5 collective-permute-start.6
  31.8 1.5 %collective-permute-start.8 = (bf16[2608,128]{1,0:T(8,128)(2,1)}, bf16[2608,128]{1,0:T(8,128)(2,1)}, u32[]{:S(2)}, u32[]{:S(2)}) collective-permute-start(bf16[2608,128]{1,0:T(8,128)(2,1)} %collective-permute-done.3), channel_id=1, source_target_pairs={{0,4},{1,3},{2,6},{3,1},{4,0},{5,7},{6,2},{7,5},{8,12},{9,11},{10,... | collective-permute-start | bytes 2002952 | tf_op jit(solution)/shard_map/ppermute | solution.py:576
  33.3 0.0 collective-permute-done.5
  33.3 6.5 %bands.2 = (bf16[3,12,192,224]{3,2,1,0:T(8,128)(2,1)}, bf16[4,2,80,512]{3,2,1,0:T(8,128)(2,1)}, bf16[4,160,128]{2,1,0:T(8,128)(2,1)}) custom-call(bf16[6912,224]{1,0:T(8,128)(2,1)} %get-tuple-element.19.gram_any.refs_13_, bf16[1,2608,128]{2,1,0:T(8,128)(2,1)} %bitcast.8.refs_0_.refs_3_, bf16[1,2608,128]{2,1,0:T(8,128)(2,1)} %bitcast.9.refs_1_.refs_4_, ...), custom_call_target="tpu_custom_call" | custom-call | flops 792723456 | bytes 4128768 | tf_op jit(solution)/shard_map/bands/pallas_call | solution.py:366
  39.8 0.0 collective-permute-done.7
  39.8 0.0 collective-permute-done.6
  39.8 4.1 %bands.3.refs_12_ = bf16[2,12,192,224]{3,2,1,0:T(8,128)(2,1)} custom-call(bf16[6912,224]{1,0:T(8,128)(2,1)} %get-tuple-element.19.gram_any.refs_13_, bf16[1,2608,128]{2,1,0:T(8,128)(2,1)} %bitcast.12.refs_0_.refs_6_, bf16[1,2608,128]{2,1,0:T(8,128)(2,1)} %bitcast.13.refs_1_.refs_7_), custom_call_target="tpu_custom_call" | custom-call | flops 528482304 | bytes 2752512 | tf_op jit(solution)/shard_map/bands/pallas_call | solution.py:366
  43.9 0.0 collective-permute-done.8.refs_8_
  43.9 0.1 collective-permute-start.9
  44.0 2.4 %collective-permute-done.9.refs_9_ = bf16[2608,128]{1,0:T(8,128)(2,1)} collective-permute-done((bf16[2608,128]{1,0:T(8,128)(2,1)}, bf16[2608,128]{1,0:T(8,128)(2,1)}, u32[]{:S(2)}, u32[]{:S(2)}) %collective-permute-start.9) | collective-permute-done | bytes 667680 | tf_op jit(solution)/shard_map/ppermute | solution.py:572
  46.4 15.7 %decode.1 = bf16[216,4,2560]{2,1,0:T(4,128)(2,1)} custom-call(bf16[4,2,80,512]{3,2,1,0:T(8,128)(2,1)} %get-tuple-element.22.refs_0_, bf16[4,160,128]{2,1,0:T(8,128)(2,1)} %get-tuple-element.23.refs_1_, bf16[1,2608,128]{2,1,0:T(8,128)(2,1)} %bitcast.14, bf16[1,2608,128]{2,1,0:T(8,128)(2,1)} %bitcast.8.refs_0_.refs_3_, ...), custom_call_target="tpu_custom_call" | custom-call | flops 2642411520 | bytes 4423680 | tf_op jit(solution)/shard_map/decode/pallas_call | solution.py:546
Async XLA Ops:
  1.4 6.9 %collective-permute-start.2 = (s32[8,256]{1,0:T(8,128)}, s32[8,256]{1,0:T(8,128)S(1)}, u32[]{:S(2)}, u32[]{:S(2)}) collective-permute-start(s32[8,256]{1,0:T(8,128)} %small_lines.1), channel_id=1, source_target_pairs={{0,24},{8,16},{16,8},{24,0},{1,25},{9,17},{17,9},{25,1},{2,26},{10... | collective-permute-start | bytes 24584 | tf_op jit(solution)/shard_map/ppermute | solution.py:572
  6.4 4.8 %collective-permute-start.1 = (s32[8,256]{1,0:T(8,128)}, s32[8,256]{1,0:T(8,128)S(1)}, u32[]{:S(2)}, u32[]{:S(2)}) collective-permute-start(s32[8,256]{1,0:T(8,128)} %small_lines.1), channel_id=1, source_target_pairs={{0,16},{8,24},{16,0},{24,8},{1,17},{9,25},{17,1},{25,9},{2,18},{10... | collective-permute-start | bytes 24584 | tf_op jit(solution)/shard_map/ppermute | solution.py:572
  6.4 4.8 %collective-permute-start = (s32[8,256]{1,0:T(8,128)}, s32[8,256]{1,0:T(8,128)S(1)}, u32[]{:S(2)}, u32[]{:S(2)}) collective-permute-start(s32[8,256]{1,0:T(8,128)} %small_lines.1), channel_id=1, source_target_pairs={{0,8},{8,0},{16,24},{24,16},{1,9},{9,1},{17,25},{25,17},{2,10},{10... | collective-permute-start | bytes 24584 | tf_op jit(solution)/shard_map/ppermute | solution.py:572
  8.3 2.9 %copy-start = (s32[8,256]{1,0:T(8,128)}, s32[8,256]{1,0:T(8,128)S(1)}, u32[]{:S(2)}) copy-start(s32[8,256]{1,0:T(8,128)S(1)} %collective-permute-done.2) | copy-start | bytes 24580
  11.2 0.6 copy-start.1
  11.2 0.6 copy-start.2
  14.4 16.8 %collective-permute-start.4 = (bf16[2608,128]{1,0:T(8,128)(2,1)}, bf16[2608,128]{1,0:T(8,128)(2,1)}, u32[]{:S(2)}, u32[]{:S(2)}) collective-permute-start(bf16[2608,128]{1,0:T(8,128)(2,1)} %pack_influence.1.packed_ref), channel_id=1, source_target_pairs={{0,4},{1,3},{2,6},{3,1},{4,0},{5,7},{6,2},{7,5},{8,12},{9,11},{10,... | collective-permute-start | bytes 2002952 | tf_op jit(solution)/shard_map/ppermute | solution.py:576
  16.0 15.3 %collective-permute-start.3 = (bf16[2608,128]{1,0:T(8,128)(2,1)}, bf16[2608,128]{1,0:T(8,128)(2,1)}, u32[]{:S(2)}, u32[]{:S(2)}) collective-permute-start(bf16[2608,128]{1,0:T(8,128)(2,1)} %pack_influence.1.packed_ref), channel_id=1, source_target_pairs={{0,2},{1,5},{2,0},{3,7},{4,6},{5,1},{6,4},{7,3},{8,10},{9,13},{10,... | collective-permute-start | bytes 2002952 | tf_op jit(solution)/shard_map/ppermute | solution.py:576
  17.4 15.9 %collective-permute-start.5 = (bf16[2608,128]{1,0:T(8,128)(2,1)}, bf16[2608,128]{1,0:T(8,128)(2,1)}, u32[]{:S(2)}, u32[]{:S(2)}) collective-permute-start(bf16[2608,128]{1,0:T(8,128)(2,1)} %pack_influence.1.packed_ref), channel_id=1, source_target_pairs={{0,1},{1,0},{2,3},{3,2},{4,5},{5,4},{6,7},{7,6},{8,9},{9,8},{10,11... | collective-permute-start | bytes 2002952 | tf_op jit(solution)/shard_map/ppermute | solution.py:572
  31.3 8.5 %collective-permute-start.7 = (bf16[2608,128]{1,0:T(8,128)(2,1)}, bf16[2608,128]{1,0:T(8,128)(2,1)}, u32[]{:S(2)}, u32[]{:S(2)}) collective-permute-start(bf16[2608,128]{1,0:T(8,128)(2,1)} %collective-permute-done.4), channel_id=1, source_target_pairs={{0,1},{1,0},{2,3},{3,2},{4,5},{5,4},{6,7},{7,6},{8,9},{9,8},{10,11... | collective-permute-start | bytes 2002952 | tf_op jit(solution)/shard_map/ppermute | solution.py:572
  31.3 8.5 %collective-permute-start.6 = (bf16[2608,128]{1,0:T(8,128)(2,1)}, bf16[2608,128]{1,0:T(8,128)(2,1)}, u32[]{:S(2)}, u32[]{:S(2)}) collective-permute-start(bf16[2608,128]{1,0:T(8,128)(2,1)} %collective-permute-done.3), channel_id=1, source_target_pairs={{0,1},{1,0},{2,3},{3,2},{4,5},{5,4},{6,7},{7,6},{8,9},{9,8},{10,11... | collective-permute-start | bytes 2002952 | tf_op jit(solution)/shard_map/ppermute | solution.py:572
  31.8 12.1 %collective-permute-start.8 = (bf16[2608,128]{1,0:T(8,128)(2,1)}, bf16[2608,128]{1,0:T(8,128)(2,1)}, u32[]{:S(2)}, u32[]{:S(2)}) collective-permute-start(bf16[2608,128]{1,0:T(8,128)(2,1)} %collective-permute-done.3), channel_id=1, source_target_pairs={{0,4},{1,3},{2,6},{3,1},{4,0},{5,7},{6,2},{7,5},{8,12},{9,11},{10,... | collective-permute-start | bytes 2002952 | tf_op jit(solution)/shard_map/ppermute | solution.py:576
  43.9 2.5 %collective-permute-start.9 = (bf16[2608,128]{1,0:T(8,128)(2,1)}, bf16[2608,128]{1,0:T(8,128)(2,1)}, u32[]{:S(2)}, u32[]{:S(2)}) collective-permute-start(bf16[2608,128]{1,0:T(8,128)(2,1)} %collective-permute-done.8.refs_8_), channel_id=1, source_target_pairs={{0,1},{1,0},{2,3},{3,2},{4,5},{5,4},{6,7},{7,6},{8,9},{9,8},{10,11... | collective-permute-start | bytes 2002952 | tf_op jit(solution)/shard_map/ppermute | solution.py:572

commit v14 on v13

--- a/solution.py
+++ b/solution.py
@@ -525,8 +525,8 @@
             value = value.astype(jnp.float32)[:own] * factor[:, at:at + LANES]
             total[tile, pl.ds(d, own, stride=directions), :] = value
     for tile in range(out_ref.shape[2] // LANES):
-        value = total[tile].reshape(own, directions, LANES)
-        out_ref[:, :, tile * LANES:(tile + 1) * LANES] = value.astype(out_ref.dtype)
+        value = total[tile].astype(out_ref.dtype).reshape(own, directions, LANES)
+        out_ref[:, :, tile * LANES:(tile + 1) * LANES] = value
 
 
 def decode(differences, sources, late, ready, gram_rows, own, row_shape, surface_rows, pupil, norm, staged):
@@ -610,14 +610,11 @@
     first_sibling, second_sibling = swap(first, "row", 1), swap(second, "row", 1)
     sources = [source[None] for source in (sibling, first, second)]
     near, *differences = bands(gram_rows, sources, 1, staged, row_shape, surface_rows, lines, pupil)
-    near, first_sibling, second_sibling = lax.optimization_barrier((near, first_sibling, second_sibling))
-    others = [first_sibling[None], second_sibling[None]]
-    far, = bands(gram_rows, others, 4, staged, row_shape, surface_rows, [], pupil)
-    far, diagonal = lax.optimization_barrier((far, diagonal))
-    late = [[diagonal], [swap(diagonal, "row", 1)]]
+    near, diagonal = lax.optimization_barrier((near, diagonal))
+    late = [[block] for block in (first_sibling, second_sibling, diagonal, swap(diagonal, "row", 1))]
     return decode(
-        differences, [packed[None], *sources, *others], late, [own_rows, near, far], gram_rows, own, row_shape,
-        surface_rows, pupil, norm, staged,
+        differences, [packed[None], *sources], late, [own_rows, near], gram_rows, own, row_shape, surface_rows, pupil,
+        norm, staged,
     )
 
 

time: 62.4 us -> 61.3 us (0.982)
  Pallas kernels: 42.3 us -> 38.7 us
  waiting for transfers between devices: 8.44 us -> 11 us
    pallas_call x2 -> x1, Pallas kernels: 10.5 us -> 6.47 us  [bands(): pl.pallas_call(functools.partial(bands_kernel, row_shape, surface_rows, f...]
    ppermute x3, waiting for transfers between devices: 1.79 us -> 4.32 us  [turn(): lax.ppermute(block, 'row', [(i, i ^ (odd if i % 2 else even)) for i in ra...]
  transfers between devices with their start and end apart: 10 -> 10, of which waited for: 4 -> 5; matrix products, arithmetic and copies ran while one was open for 0% -> 0% of each run, Pallas kernels for 36% -> 30%
where the time goes in v14:
time: 61.3 us; the launch traced here: 61 us
  Pallas kernels  38.7 us (63%)
  waiting for transfers between devices  11 us (18%)
  starting transfers between devices  10.7 us (17%)
    pallas_call x1, Pallas kernels, decode(): pl.pallas_call(functools.partial(decode_kernel, row_shape, surface_rows,...  16.2 us
    pallas_call x1, Pallas kernels, gram(): pl.pallas_call(functools.partial(gram_kernel, row_shape, surface_rows), g...  12 us
    ppermute x7, waiting for transfers between devices, swap(): lax.ppermute(block, axis, [(i, i ^ distance) for i in range(lax.axis_size...  6.65 us
    pallas_call x1, Pallas kernels, bands(): pl.pallas_call(functools.partial(bands_kernel, row_shape, surface_rows, f...  6.47 us
    ppermute x7, starting transfers between devices, swap(): lax.ppermute(block, axis, [(i, i ^ distance) for i in range(lax.axis_size...  6.13 us
    ppermute x3, starting transfers between devices, turn(): lax.ppermute(block, 'row', [(i, i ^ (odd if i % 2 else even)) for i in ra...  4.53 us
    ppermute x3, waiting for transfers between devices, turn(): lax.ppermute(block, 'row', [(i, i ^ (odd if i % 2 else even)) for i in ra...  4.32 us
    pallas_call x1, Pallas kernels, pack(): pl.pallas_call(pack_kernel, out_shape=jax.ShapeDtypeStruct((mirrors * row...  2.64 us
  transfers between devices with their start and end apart: 10, of which 5 were waited for; matrix products, arithmetic and copies ran while one was open for 0% of the time, Pallas kernels for 30%

profile of v14, /device:TPU:0, one launch (start us, length us, event | category | flops | bytes accessed | tf_op | source)
XLA Modules:
  0.0 61.0 jit_solution(787061228284824269)
XLA Ops:
  0.0 1.4 %small_lines.1 = s32[8,256]{1,0:T(8,128)} custom-call(s32[3,1,4]{2,1,0:T(1,128)} %bitcast.23, s32[3,1,160]{2,1,0:T(1,128)} %bitcast.22, s32[1,2,80]{2,1,0:T(2,128)} %valid_ref.1), custom_call_target="tpu_custom_call" | custom-call | tf_op jit(solution)/shard_map/small_lines/pallas_call | solution.py:39
  1.4 5.0 %collective-permute-start.2 = (s32[8,256]{1,0:T(8,128)}, s32[8,256]{1,0:T(8,128)S(1)}, u32[]{:S(2)}, u32[]{:S(2)}) collective-permute-start(s32[8,256]{1,0:T(8,128)} %small_lines.1), channel_id=1, source_target_pairs={{0,24},{8,16},{16,8},{24,0},{1,25},{9,17},{17,9},{25,1},{2,26},{10... | collective-permute-start | bytes 24584 | tf_op jit(solution)/shard_map/ppermute | solution.py:572
  6.4 0.0 collective-permute-start.1
  6.4 0.6 collective-permute-start
  7.0 1.3 %collective-permute-done.2 = s32[8,256]{1,0:T(8,128)S(1)} collective-permute-done((s32[8,256]{1,0:T(8,128)}, s32[8,256]{1,0:T(8,128)S(1)}, u32[]{:S(2)}, u32[]{:S(2)}) %collective-permute-start.2) | collective-permute-done | bytes 8224 | tf_op jit(solution)/shard_map/ppermute | solution.py:572
  8.3 0.0 copy-start
  8.3 2.9 %collective-permute-done.1 = s32[8,256]{1,0:T(8,128)S(1)} collective-permute-done((s32[8,256]{1,0:T(8,128)}, s32[8,256]{1,0:T(8,128)S(1)}, u32[]{:S(2)}, u32[]{:S(2)}) %collective-permute-start.1) | collective-permute-done | bytes 8224 | tf_op jit(solution)/shard_map/ppermute | solution.py:572
  11.2 0.0 copy-start.1
  11.2 0.0 collective-permute-done
  11.2 0.0 copy-start.2
  11.2 0.0 copy-done
  11.2 0.6 copy-done.1
  11.8 0.0 copy-done.2
  11.8 2.6 %pack_influence.1.packed_ref = bf16[2608,128]{1,0:T(8,128)(2,1)} custom-call(bf16[3,4,144,192]{3,2,1,0:T(8,128)(2,1)} %bitcast.13, s32[1,8,256]{2,1,0:T(8,128)} %bitcast.14, s32[1,8,256]{2,1,0:T(8,128)} %bitcast.20, s32[1,8,256]{2,1,0:T(8,128)} %bitcast.18, s32[1,8,256]{2,1,0:T(8,128)} %bitcast.16), custom_call_target="tpu_custom_call" | custom-call | bytes 995328 | tf_op jit(solution)/shard_map/pack_influence/pallas_call | solution.py:95
  14.4 1.5 %collective-permute-start.4 = (bf16[2608,128]{1,0:T(8,128)(2,1)}, bf16[2608,128]{1,0:T(8,128)(2,1)}, u32[]{:S(2)}, u32[]{:S(2)}) collective-permute-start(bf16[2608,128]{1,0:T(8,128)(2,1)} %pack_influence.1.packed_ref), channel_id=1, source_target_pairs={{0,4},{1,3},{2,6},{3,1},{4,0},{5,7},{6,2},{7,5},{8,12},{9,11},{10,... | collective-permute-start | bytes 2002952 | tf_op jit(solution)/shard_map/ppermute | solution.py:576
  16.0 1.5 %collective-permute-start.3 = (bf16[2608,128]{1,0:T(8,128)(2,1)}, bf16[2608,128]{1,0:T(8,128)(2,1)}, u32[]{:S(2)}, u32[]{:S(2)}) collective-permute-start(bf16[2608,128]{1,0:T(8,128)(2,1)} %pack_influence.1.packed_ref), channel_id=1, source_target_pairs={{0,2},{1,5},{2,0},{3,7},{4,6},{5,1},{6,4},{7,3},{8,10},{9,13},{10,... | collective-permute-start | bytes 2002952 | tf_op jit(solution)/shard_map/ppermute | solution.py:576
  17.4 0.0 collective-permute-start.5
  17.5 12.0 %gram_rows.1 = (bf16[6912,224]{1,0:T(8,128)(2,1)}, bf16[1,12,192,224]{3,2,1,0:T(8,128)(2,1)}) custom-call(s32[3,48,48]{2,1,0:T(8,128)} %table_ref.1, s32[16,128]{1,0:T(8,128)} %bitcast.24, bf16[2608,128]{1,0:T(8,128)(2,1)} %pack_influence.1.packed_ref), custom_call_target="tpu_custom_call" | custom-call | flops 6341787648 | bytes 3096576 | tf_op jit(solution)/shard_map/gram_rows/pallas_call | solution.py:221
  29.5 1.8 %collective-permute-done.4 = bf16[2608,128]{1,0:T(8,128)(2,1)} collective-permute-done((bf16[2608,128]{1,0:T(8,128)(2,1)}, bf16[2608,128]{1,0:T(8,128)(2,1)}, u32[]{:S(2)}, u32[]{:S(2)}) %collective-permute-start.4) | collective-permute-done | bytes 667680 | tf_op jit(solution)/shard_map/ppermute | solution.py:576
  31.3 0.0 collective-permute-done.3
  31.3 1.5 %collective-permute-start.8 = (bf16[2608,128]{1,0:T(8,128)(2,1)}, bf16[2608,128]{1,0:T(8,128)(2,1)}, u32[]{:S(2)}, u32[]{:S(2)}) collective-permute-start(bf16[2608,128]{1,0:T(8,128)(2,1)} %collective-permute-done.3), channel_id=1, source_target_pairs={{0,4},{1,3},{2,6},{3,1},{4,0},{5,7},{6,2},{7,5},{8,12},{9,11},{10,... | collective-permute-start | bytes 2002952 | tf_op jit(solution)/shard_map/ppermute | solution.py:576
  32.8 0.0 collective-permute-start.6
  32.8 0.5 collective-permute-start.7
  33.3 0.0 collective-permute-done.5
  33.3 6.5 %bands.1 = (bf16[3,12,192,224]{3,2,1,0:T(8,128)(2,1)}, bf16[4,2,80,512]{3,2,1,0:T(8,128)(2,1)}, bf16[4,160,128]{2,1,0:T(8,128)(2,1)}) custom-call(bf16[6912,224]{1,0:T(8,128)(2,1)} %get-tuple-element.16.gram_any.refs_12_, bf16[1,2608,128]{2,1,0:T(8,128)(2,1)} %bitcast.8.refs_0_.refs_3_, bf16[1,2608,128]{2,1,0:T(8,128)(2,1)} %bitcast.9.refs_1_.refs_4_, ...), custom_call_target="tpu_custom_call" | custom-call | flops 792723456 | bytes 4128768 | tf_op jit(solution)/shard_map/bands/pallas_call | solution.py:366
  39.8 2.5 %collective-permute-done.8.refs_8_ = bf16[2608,128]{1,0:T(8,128)(2,1)} collective-permute-done((bf16[2608,128]{1,0:T(8,128)(2,1)}, bf16[2608,128]{1,0:T(8,128)(2,1)}, u32[]{:S(2)}, u32[]{:S(2)}) %collective-permute-start.8) | collective-permute-done | bytes 667680 | tf_op jit(solution)/shard_map/ppermute | solution.py:576
  42.3 0.0 collective-permute-start.9
  42.3 0.0 collective-permute-done.7.refs_7_
  42.3 0.0 collective-permute-done.6.refs_6_
  42.3 2.4 %collective-permute-done.9.refs_9_ = bf16[2608,128]{1,0:T(8,128)(2,1)} collective-permute-done((bf16[2608,128]{1,0:T(8,128)(2,1)}, bf16[2608,128]{1,0:T(8,128)(2,1)}, u32[]{:S(2)}, u32[]{:S(2)}) %collective-permute-start.9) | collective-permute-done | bytes 667680 | tf_op jit(solution)/shard_map/ppermute | solution.py:572
  44.8 16.2 %decode.1 = bf16[216,4,2560]{2,1,0:T(4,128)(2,1)} custom-call(bf16[4,2,80,512]{3,2,1,0:T(8,128)(2,1)} %get-tuple-element.19.refs_0_, bf16[4,160,128]{2,1,0:T(8,128)(2,1)} %get-tuple-element.20.refs_1_, bf16[1,2608,128]{2,1,0:T(8,128)(2,1)} %bitcast.12, bf16[1,2608,128]{2,1,0:T(8,128)(2,1)} %bitcast.8.refs_0_.refs_3_, ...), custom_call_target="tpu_custom_call" | custom-call | flops 2642411520 | bytes 4423680 | tf_op jit(solution)/shard_map/decode/pallas_call | solution.py:546
Async XLA Ops:
  1.4 6.9 %collective-permute-start.2 = (s32[8,256]{1,0:T(8,128)}, s32[8,256]{1,0:T(8,128)S(1)}, u32[]{:S(2)}, u32[]{:S(2)}) collective-permute-start(s32[8,256]{1,0:T(8,128)} %small_lines.1), channel_id=1, source_target_pairs={{0,24},{8,16},{16,8},{24,0},{1,25},{9,17},{17,9},{25,1},{2,26},{10... | collective-permute-start | bytes 24584 | tf_op jit(solution)/shard_map/ppermute | solution.py:572
  6.4 4.8 %collective-permute-start.1 = (s32[8,256]{1,0:T(8,128)}, s32[8,256]{1,0:T(8,128)S(1)}, u32[]{:S(2)}, u32[]{:S(2)}) collective-permute-start(s32[8,256]{1,0:T(8,128)} %small_lines.1), channel_id=1, source_target_pairs={{0,16},{8,24},{16,0},{24,8},{1,17},{9,25},{17,1},{25,9},{2,18},{10... | collective-permute-start | bytes 24584 | tf_op jit(solution)/shard_map/ppermute | solution.py:572
  6.4 4.8 %collective-permute-start = (s32[8,256]{1,0:T(8,128)}, s32[8,256]{1,0:T(8,128)S(1)}, u32[]{:S(2)}, u32[]{:S(2)}) collective-permute-start(s32[8,256]{1,0:T(8,128)} %small_lines.1), channel_id=1, source_target_pairs={{0,8},{8,0},{16,24},{24,16},{1,9},{9,1},{17,25},{25,17},{2,10},{10... | collective-permute-start | bytes 24584 | tf_op jit(solution)/shard_map/ppermute | solution.py:572
  8.3 2.9 %copy-start = (s32[8,256]{1,0:T(8,128)}, s32[8,256]{1,0:T(8,128)S(1)}, u32[]{:S(2)}) copy-start(s32[8,256]{1,0:T(8,128)S(1)} %collective-permute-done.2) | copy-start | bytes 24580
  11.2 0.6 copy-start.1
  11.2 0.6 copy-start.2
  14.4 16.8 %collective-permute-start.4 = (bf16[2608,128]{1,0:T(8,128)(2,1)}, bf16[2608,128]{1,0:T(8,128)(2,1)}, u32[]{:S(2)}, u32[]{:S(2)}) collective-permute-start(bf16[2608,128]{1,0:T(8,128)(2,1)} %pack_influence.1.packed_ref), channel_id=1, source_target_pairs={{0,4},{1,3},{2,6},{3,1},{4,0},{5,7},{6,2},{7,5},{8,12},{9,11},{10,... | collective-permute-start | bytes 2002952 | tf_op jit(solution)/shard_map/ppermute | solution.py:576
  16.0 15.3 %collective-permute-start.3 = (bf16[2608,128]{1,0:T(8,128)(2,1)}, bf16[2608,128]{1,0:T(8,128)(2,1)}, u32[]{:S(2)}, u32[]{:S(2)}) collective-permute-start(bf16[2608,128]{1,0:T(8,128)(2,1)} %pack_influence.1.packed_ref), channel_id=1, source_target_pairs={{0,2},{1,5},{2,0},{3,7},{4,6},{5,1},{6,4},{7,3},{8,10},{9,13},{10,... | collective-permute-start | bytes 2002952 | tf_op jit(solution)/shard_map/ppermute | solution.py:576
  17.4 15.9 %collective-permute-start.5 = (bf16[2608,128]{1,0:T(8,128)(2,1)}, bf16[2608,128]{1,0:T(8,128)(2,1)}, u32[]{:S(2)}, u32[]{:S(2)}) collective-permute-start(bf16[2608,128]{1,0:T(8,128)(2,1)} %pack_influence.1.packed_ref), channel_id=1, source_target_pairs={{0,1},{1,0},{2,3},{3,2},{4,5},{5,4},{6,7},{7,6},{8,9},{9,8},{10,11... | collective-permute-start | bytes 2002952 | tf_op jit(solution)/shard_map/ppermute | solution.py:572
  31.3 11.0 %collective-permute-start.8 = (bf16[2608,128]{1,0:T(8,128)(2,1)}, bf16[2608,128]{1,0:T(8,128)(2,1)}, u32[]{:S(2)}, u32[]{:S(2)}) collective-permute-start(bf16[2608,128]{1,0:T(8,128)(2,1)} %collective-permute-done.3), channel_id=1, source_target_pairs={{0,4},{1,3},{2,6},{3,1},{4,0},{5,7},{6,2},{7,5},{8,12},{9,11},{10,... | collective-permute-start | bytes 2002952 | tf_op jit(solution)/shard_map/ppermute | solution.py:576
  32.8 9.5 %collective-permute-start.6 = (bf16[2608,128]{1,0:T(8,128)(2,1)}, bf16[2608,128]{1,0:T(8,128)(2,1)}, u32[]{:S(2)}, u32[]{:S(2)}) collective-permute-start(bf16[2608,128]{1,0:T(8,128)(2,1)} %collective-permute-done.3), channel_id=1, source_target_pairs={{0,1},{1,0},{2,3},{3,2},{4,5},{5,4},{6,7},{7,6},{8,9},{9,8},{10,11... | collective-permute-start | bytes 2002952 | tf_op jit(solution)/shard_map/ppermute | solution.py:572
  32.8 9.5 %collective-permute-start.7 = (bf16[2608,128]{1,0:T(8,128)(2,1)}, bf16[2608,128]{1,0:T(8,128)(2,1)}, u32[]{:S(2)}, u32[]{:S(2)}) collective-permute-start(bf16[2608,128]{1,0:T(8,128)(2,1)} %collective-permute-done.4), channel_id=1, source_target_pairs={{0,1},{1,0},{2,3},{3,2},{4,5},{5,4},{6,7},{7,6},{8,9},{9,8},{10,11... | collective-permute-start | bytes 2002952 | tf_op jit(solution)/shard_map/ppermute | solution.py:572
  42.3 2.5 %collective-permute-start.9 = (bf16[2608,128]{1,0:T(8,128)(2,1)}, bf16[2608,128]{1,0:T(8,128)(2,1)}, u32[]{:S(2)}, u32[]{:S(2)}) collective-permute-start(bf16[2608,128]{1,0:T(8,128)(2,1)} %collective-permute-done.8.refs_8_), channel_id=1, source_target_pairs={{0,1},{1,0},{2,3},{3,2},{4,5},{5,4},{6,7},{7,6},{8,9},{9,8},{10,11... | collective-permute-start | bytes 2002952 | tf_op jit(solution)/shard_map/ppermute | solution.py:572

commit v15 on v13

--- a/solution.py
+++ b/solution.py
@@ -24,27 +24,6 @@
     return lax.population_count(codes & rows) & 1
 
 
-def lines_kernel(rows_ref, columns_ref, valid_ref, lines_ref):
-    mirrors, rows = rows_ref.shape[0], rows_ref.shape[2]
-    lines_ref[...] = jnp.zeros(lines_ref.shape, lines_ref.dtype)
-    lines_ref[mirrors:mirrors + valid_ref.shape[1], :valid_ref.shape[2]] = valid_ref[0]
-    for k in range(mirrors):
-        lines_ref[k:k + 1, :columns_ref.shape[2]] = columns_ref[k]
-        lines_ref[mirrors + valid_ref.shape[1]:mirrors + valid_ref.shape[1] + 1, k * rows:(k + 1) * rows] = rows_ref[k]
-
-
-def small_lines(foot_rows, foot_columns, valid):
-    vmem = pl.BlockSpec(memory_space=pltpu.VMEM)
-    count = foot_rows.shape[1] + valid.shape[1] + 1
-    return pl.pallas_call(
-        lines_kernel,
-        out_shape=jax.ShapeDtypeStruct((-(-count // 8) * 8, WINDOW), jnp.int32),
-        in_specs=[vmem] * 3,
-        out_specs=vmem,
-        name="small_lines",
-    )(jnp.swapaxes(foot_rows, 0, 1), jnp.swapaxes(foot_columns, 0, 1), valid)
-
-
 def narrow_places(q, slots, samples):
     narrow = slots - LANES
     whole = LANES // narrow
@@ -55,9 +34,14 @@
     return [(0, half, samples, lane), (half, half, samples, LANES // 2 + lane)]
 
 
-def pack_kernel(block_ref, *refs):
-    lines_refs, packed_ref = refs[:-1], refs[-1]
+def pack_kernel(block_ref, rows_ref, columns_ref, valid_ref, packed_ref, lines_ref):
     mirrors, rows, slots, samples = block_ref.shape
+    foot_line = mirrors + valid_ref.shape[1]
+    lines_ref[...] = jnp.zeros(lines_ref.shape, lines_ref.dtype)
+    lines_ref[mirrors:foot_line, :valid_ref.shape[2]] = valid_ref[0]
+    for k in range(mirrors):
+        lines_ref[k:k + 1, :columns_ref.shape[2]] = columns_ref[k]
+        lines_ref[foot_line:foot_line + 1, k * rows:(k + 1) * rows] = rows_ref[k]
     identity = (
         lax.broadcasted_iota(jnp.int32, (samples, samples), 0) == lax.broadcasted_iota(jnp.int32, (samples, samples), 1)
     ).astype(jnp.float32).astype(jnp.bfloat16)
@@ -72,35 +56,24 @@
             tails.setdefault((row, length), {})[lane] = turned[start:start + length, LANES:]
     for (row, length), pieces in tails.items():
         packed_ref[pl.ds(wide + row, length), :] = jnp.concatenate([pieces[lane] for lane in sorted(pieces)], axis=1)
-    count = rows // 2
-    every = [ref.at[n] for ref in lines_refs for n in range(ref.shape[0])]
-    feet = [ref[mirrors + count:mirrors + count + 1, :mirrors * rows] for ref in every]
-    feet.append(jnp.zeros((1, LANES - mirrors * rows * len(every)), jnp.int32))
-    lines = [ref[mirrors:mirrors + count, :LANES] for ref in every] + [jnp.concatenate(feet, axis=1)]
-    extra = packed_ref.shape[0] - mirrors * rows * samples * slots // LANES
-    lines.append(jnp.zeros((extra - count * len(every) - 1, LANES), jnp.int32))
-    packed_ref[pl.ds(packed_ref.shape[0] - extra, extra), :] = (
-        jnp.concatenate(lines, axis=0).astype(jnp.float32).astype(jnp.bfloat16)
-    )
-
-
-def extra_rows(directions, rows):
-    return -(-(directions * (rows // 2) + 1) // 16) * 16
-
-
-def pack(block, lines):
+
+
+def pack(block, foot_rows, foot_columns, valid):
     mirrors, rows, slots, samples = block.shape
     vmem = pl.BlockSpec(memory_space=pltpu.VMEM)
-    extra = extra_rows(sum(line.shape[0] for line in lines), rows)
+    height = mirrors + valid.shape[1] + 1
     return pl.pallas_call(
         pack_kernel,
-        out_shape=jax.ShapeDtypeStruct((mirrors * rows * samples * slots // LANES + extra, LANES), block.dtype),
-        in_specs=[vmem] * (1 + len(lines)),
-        out_specs=vmem,
+        out_shape=[
+            jax.ShapeDtypeStruct((mirrors * rows * samples * slots // LANES, LANES), block.dtype),
+            jax.ShapeDtypeStruct((-(-height // 8) * 8, WINDOW), jnp.int32),
+        ],
+        in_specs=[vmem] * 4,
+        out_specs=[vmem] * 2,
         compiler_params=pltpu.CompilerParams(vmem_limit_bytes=VMEM_BYTES),
         cost_estimate=pl.CostEstimate(flops=0, bytes_accessed=3 * block.size, transcendentals=0),
         name="pack_influence",
-    )(block, *lines)
+    )(block, jnp.swapaxes(foot_rows, 0, 1), jnp.swapaxes(foot_columns, 0, 1), valid)
 
 
 def column_of(row):
@@ -414,27 +387,24 @@
         rest_ref[d] = jnp.concatenate([upper, lower], axis=0).astype(jnp.bfloat16)
 
 
-def decode_kernel(row_shape, surface_rows, own, staged, norm, counts, late_parts, *refs):
+def decode_kernel(row_shape, surface_rows, own, staged, norm, counts, late, places, *refs):
     mirrors, shard_rows, slots, samples = row_shape
     whole_ref, rest_ref, *refs = refs
     lines_refs, refs = refs[:counts[0]], refs[counts[0]:]
     late_refs, refs = refs[:counts[1]], refs[counts[1]:]
     ready_refs, refs = refs[:counts[2]], refs[counts[2]:]
-    (gram_any, out_ref, gram_ref, decoded, total, packed_lines, lines, foot_rows, scalars, *refs) = refs
+    (gram_any, out_ref, gram_ref, decoded, total, lines, foot_rows, scalars, *refs) = refs
     late_blocks, refs = refs[:counts[1]], refs[counts[1]:]
-    gram_semaphores, ready_semaphores, line_semaphores, late_semaphores, scalar_semaphore = refs
+    gram_semaphores, ready_semaphores, late_semaphores, scalar_semaphore = refs
     group = pl.program_id(0)
     directions, pupil = whole_ref.shape[0], 2 * whole_ref.shape[2]
     depth = whole_ref.shape[3]
     phases = out_ref.shape[2] // pupil
     blocks = surface_rows // shard_rows
-    late = len(late_parts)
     ready = blocks - late
     count = shard_rows // 2
     rows = mirrors * shard_rows
-    extra = lines.shape[1]
-
-    ready_blocks = [ref.at[m] for ref in ready_refs for m in range(ref.shape[0])]
+    foot_line = mirrors + count
 
     @pl.when(group == 0)
     def _():
@@ -443,35 +413,30 @@
                 copy.start()
             return copies
 
-        ends = [ref.at[n, pl.ds(ref.shape[1] - extra, extra)] for ref in lines_refs for n in range(ref.shape[0])]
-        line_copies = started([
-            pltpu.make_async_copy(end, packed_lines.at[n], line_semaphores.at[n]) for n, end in enumerate(ends)
-        ])
         late_copies = started([
             pltpu.make_async_copy(late_refs[n], late_blocks[n], late_semaphores.at[n]) for n in range(counts[1])
         ])
         gram_copies = started(fetch_gram(gram_any, gram_ref, gram_semaphores, mirrors)) if late else []
-        started([
+        ready_copies = started([
             pltpu.make_async_copy(block, decoded.at[pl.ds(n * rows, rows)], ready_semaphores.at[n])
-            for n, block in enumerate(ready_blocks)
+            for n, block in enumerate([ref.at[m] for ref in ready_refs for m in range(ref.shape[0])])
         ])
-        for copy in line_copies + late_copies:
-            copy.wait()
-        held = [packed_lines[n] for n in range(len(ends))]
-        at = 0
-        for part in late_parts:
-            at += part
-            last = late_blocks[at - 1]
-            held.append(last[pl.ds(last.shape[0] - extra, extra), :])
-        for n, value in enumerate(held):
-            lines[n] = value.astype(jnp.float32).astype(jnp.int32)
-        feet = jnp.concatenate([lines[n, directions * count:directions * count + 1] for n in range(blocks)], axis=0)
+        held = [ref.at[n] for ref in lines_refs for n in range(ref.shape[0])]
+        feet = [None] * blocks
+        for place, ref in zip(places, held):
+            for d in range(directions):
+                lines[place, d * count:(d + 1) * count] = ref[d, mirrors:foot_line, :LANES]
+            pieces = [ref[d, foot_line:foot_line + 1, :rows] for d in range(directions)]
+            pieces.append(jnp.zeros((1, LANES - rows * directions), jnp.int32))
+            feet[place] = jnp.concatenate(pieces, axis=1)
+        feet = jnp.concatenate(feet, axis=0)
         foot_rows[...] = row_place(feet // shard_rows, staged) * rows + feet % shard_rows
         to_scalars = pltpu.make_async_copy(foot_rows, scalars, scalar_semaphore.at[0])
         to_scalars.start()
-        at = 0
-        for n, part in enumerate(late_parts):
-            source, at = late_blocks[at], at + part
+        for copy in late_copies:
+            copy.wait()
+        for n in range(late):
+            source = late_blocks[n]
             for q in range(mirrors * shard_rows):
                 if n == 0 and q % shard_rows == 0:
                     gram_copies[q // shard_rows].wait()
@@ -479,21 +444,8 @@
                     source, q, row_shape, row_block(ready + n, staged), surface_rows, gram_ref
                 )
         to_scalars.wait()
-
-    def last_needed(at):
-        return min((2 * phases * (at + 1) - 1 + REACH) // shard_rows, blocks - 1)
-
-    for at in range(surface_rows // 2 // phases):
-        @pl.when(group == at)
-        def _():
-            for block in range(last_needed(at - 1) + 1 if at else 0, last_needed(at) + 1):
-                place = row_place(block, staged)
-
-                @pl.when(place < ready)
-                def _():
-                    pltpu.make_async_copy(
-                        ready_blocks[0], decoded.at[pl.ds(place * rows, rows)], ready_semaphores.at[place]
-                    ).wait()
+        for copy in ready_copies:
+            copy.wait()
 
     for d in range(directions):
         held = d ^ position("dir", staged)
@@ -529,43 +481,41 @@
         out_ref[:, :, tile * LANES:(tile + 1) * LANES] = value.astype(out_ref.dtype)
 
 
-def decode(differences, sources, late, ready, gram_rows, own, row_shape, surface_rows, pupil, norm, staged):
+def decode(differences, lines, places, late, ready, gram_rows, own, row_shape, surface_rows, pupil, norm, staged):
     mirrors, shard_rows, slots, samples = row_shape
     acts, padded = gram_rows.shape
     directions = differences[0].shape[0]
     blocks = surface_rows // shard_rows
-    extra = extra_rows(directions, shard_rows)
     phases = LANES // math.gcd(pupil, LANES)
     width = surface_rows // 2 * pupil
     lanes = phases * pupil
     flops = 2 * padded * mirrors * samples * pupil * directions * surface_rows // 2
     vmem, anywhere = pl.BlockSpec(memory_space=pltpu.VMEM), pl.BlockSpec(memory_space=pl.ANY)
-    parts = [part for block in late for part in block]
-    counts = (len(sources), len(parts), len(ready))
-    semaphores = [mirrors, blocks, blocks, max(len(parts), 1), 1]
+    counts = (len(lines), len(late), len(ready))
+    semaphores = [mirrors, blocks, max(len(late), 1), 1]
+    held = -(-directions * (shard_rows // 2) // 8) * 8
     return pl.pallas_call(
         functools.partial(
-            decode_kernel, row_shape, surface_rows, own, staged, norm, counts, [len(block) for block in late]
+            decode_kernel, row_shape, surface_rows, own, staged, norm, counts, len(late), places
         ),
         grid=(width // lanes,),
         out_shape=jax.ShapeDtypeStruct((own, directions, width), jnp.bfloat16),
-        in_specs=[vmem] * 2 + [anywhere] * (sum(counts) + 1),
+        in_specs=[vmem] * (2 + len(lines)) + [anywhere] * (len(late) + len(ready) + 1),
         out_specs=pl.BlockSpec((own, directions, lanes), lambda s: (0, 0, s)),
         scratch_shapes=[
             pltpu.VMEM((acts, padded), jnp.bfloat16),
             pltpu.VMEM((blocks * mirrors * shard_rows, samples, padded), jnp.bfloat16),
             pltpu.VMEM((lanes // LANES, own * directions, LANES), jnp.float32),
-            pltpu.VMEM((blocks, extra, LANES), jnp.bfloat16),
-            pltpu.VMEM((blocks, extra, LANES), jnp.int32),
+            pltpu.VMEM((blocks, held, LANES), jnp.int32),
             pltpu.VMEM((blocks, LANES), jnp.int32),
             pltpu.SMEM((blocks, LANES), jnp.int32),
-            *[pltpu.VMEM(part.shape, part.dtype) for part in parts],
+            *[pltpu.VMEM(block.shape, block.dtype) for block in late],
             *[pltpu.SemaphoreType.DMA((count,)) for count in semaphores],
         ],
         compiler_params=pltpu.CompilerParams(vmem_limit_bytes=VMEM_BYTES),
         cost_estimate=pl.CostEstimate(flops=flops, bytes_accessed=2 * own * directions * width, transcendentals=0),
         name="decode",
-    )(*differences, *sources, *parts, *ready, gram_rows)
+    )(*differences, *lines, *late, *ready, gram_rows)
 
 
 def swap(block, axis, distance):
@@ -589,34 +539,36 @@
     staged = devices == 8 and directions & (directions - 1) == 0
     turned = jnp.swapaxes(influence, 2, 3)
     pokes = poke_rows.reshape(-1, LANES)
-    lines = small_lines(foot_rows, foot_columns, subaperture_valid)
+    packed, lines = pack(turned, foot_rows, foot_columns, subaperture_valid)
     if not staged:
-        lines = lax.all_gather(lines, "dir")
-        packed = pack(turned, [lines])
         every = lax.all_gather(packed, "row")
+        lines = lax.all_gather(lax.all_gather(lines, "dir"), "row")
         gram_rows, _ = gram(actuator_codes, pokes, packed, own, row_shape, surface_rows)
-        ready, *differences = bands(gram_rows, [every], 0, staged, row_shape, surface_rows, [lines], pupil)
+        ready, *differences = bands(gram_rows, [every], 0, staged, row_shape, surface_rows, [lines[0]], pupil)
         return decode(
-            differences, [every], [], [ready], gram_rows, own, row_shape, surface_rows, pupil, norm, staged
+            differences, [lines], list(range(devices)), [], [ready], gram_rows, own, row_shape, surface_rows, pupil,
+            norm, staged,
         )
 
     lines = [lines[None]] + [swap(lines, "dir", e)[None] for e in range(1, directions)]
-    packed = pack(turned, lines)
     first, second = turn(packed, 2, 4), turn(packed, 4, 2)
     sibling = swap(packed, "row", 1)
+    held = jnp.concatenate(lines, axis=0)[None]
     gram_rows, own_rows = gram(actuator_codes, pokes, packed, own, row_shape, surface_rows)
-    gram_rows, first, second = lax.optimization_barrier((gram_rows, first, second))
+    gram_rows, first, second, held = lax.optimization_barrier((gram_rows, first, second, held))
     diagonal = turn(first, 4, 2)
-    first_sibling, second_sibling = swap(first, "row", 1), swap(second, "row", 1)
+    first_sibling = swap(first, "row", 1)
+    mine = [held, turn(held, 2, 4), turn(held, 4, 2), swap(held, "row", 6)]
     sources = [source[None] for source in (sibling, first, second)]
     near, *differences = bands(gram_rows, sources, 1, staged, row_shape, surface_rows, lines, pupil)
-    near, first_sibling, second_sibling = lax.optimization_barrier((near, first_sibling, second_sibling))
-    others = [first_sibling[None], second_sibling[None]]
-    far, = bands(gram_rows, others, 4, staged, row_shape, surface_rows, [], pupil)
-    far, diagonal = lax.optimization_barrier((far, diagonal))
-    late = [[diagonal], [swap(diagonal, "row", 1)]]
+    near, second = lax.optimization_barrier((near, second))
+    second_sibling = swap(second, "row", 1)
+    mine = jnp.concatenate(mine, axis=0)
+    near, diagonal, mine = lax.optimization_barrier((near, diagonal, mine))
+    theirs = swap(mine, "row", 1)
+    late = [first_sibling, second_sibling, diagonal, swap(diagonal, "row", 1)]
     return decode(
-        differences, [packed[None], *sources, *others], late, [own_rows, near, far], gram_rows, own, row_shape,
+        differences, [mine, theirs], [0, 2, 3, 6, 1, 4, 5, 7], late, [own_rows, near], gram_rows, own, row_shape,
         surface_rows, pupil, norm, staged,
     )
 

time: 62.4 us -> 57.8 us (0.926)
  Pallas kernels: 42.3 us -> 37.3 us
  starting transfers between devices: 10.7 us -> 15.2 us
  waiting for transfers between devices: 8.44 us -> 4.9 us
    ppermute x7 -> x9, waiting for transfers between devices: 6.64 us -> 2.61 us  [swap(): lax.ppermute(block, axis, [(i, i ^ distance) for i in range(lax.axis_size...]
    pallas_call x2 -> x1, Pallas kernels: 10.5 us -> 6.53 us  [bands(): pl.pallas_call(functools.partial(bands_kernel, row_shape, surface_rows, f...]
    ppermute x3 -> x5, starting transfers between devices: 4.53 us -> 6.92 us  [turn(): lax.ppermute(block, 'row', [(i, i ^ (odd if i % 2 else even)) for i in ra...]
    ppermute x7 -> x9, starting transfers between devices: 6.2 us -> 8.29 us  [swap(): lax.ppermute(block, axis, [(i, i ^ distance) for i in range(lax.axis_size...]
    pallas_call x2 -> x1, Pallas kernels: 4.02 us -> 2.57 us  [pack(): pl.pallas_call(pack_kernel, out_shape=[jax.ShapeDtypeStruct((mirrors * ro...]
    ppermute x3 -> x5, waiting for transfers between devices: 1.79 us -> 2.29 us  [turn(): lax.ppermute(block, 'row', [(i, i ^ (odd if i % 2 else even)) for i in ra...]
  transfers between devices with their start and end apart: 10 -> 14, of which waited for: 4 -> 4; matrix products, arithmetic and copies ran while one was open for 0% -> 0% of each run, Pallas kernels for 36% -> 32%
where the time goes in v15:
time: 57.8 us; the launch traced here: 57.6 us
  Pallas kernels  37.3 us (65%)
  starting transfers between devices  15.2 us (26%)
  waiting for transfers between devices  4.9 us (8%)
    pallas_call x1, Pallas kernels, decode(): pl.pallas_call(functools.partial(decode_kernel, row_shape, surface_rows,...  16.2 us
    pallas_call x1, Pallas kernels, gram(): pl.pallas_call(functools.partial(gram_kernel, row_shape, surface_rows), g...  12 us
    ppermute x9, starting transfers between devices, swap(): lax.ppermute(block, axis, [(i, i ^ distance) for i in range(lax.axis_size...  8.29 us
    ppermute x5, starting transfers between devices, turn(): lax.ppermute(block, 'row', [(i, i ^ (odd if i % 2 else even)) for i in ra...  6.92 us
    pallas_call x1, Pallas kernels, bands(): pl.pallas_call(functools.partial(bands_kernel, row_shape, surface_rows, f...  6.53 us
    ppermute x9, waiting for transfers between devices, swap(): lax.ppermute(block, axis, [(i, i ^ distance) for i in range(lax.axis_size...  2.61 us
    pallas_call x1, Pallas kernels, pack(): pl.pallas_call(pack_kernel, out_shape=[jax.ShapeDtypeStruct((mirrors * ro...  2.57 us
    ppermute x5, waiting for transfers between devices, turn(): lax.ppermute(block, 'row', [(i, i ^ (odd if i % 2 else even)) for i in ra...  2.29 us
  transfers between devices with their start and end apart: 14, of which 4 were waited for; matrix products, arithmetic and copies ran while one was open for 0% of the time, Pallas kernels for 32%

profile of v15, /device:TPU:0, one launch (start us, length us, event | category | flops | bytes accessed | tf_op | source)
XLA Modules:
  0.0 57.6 jit_solution(6403997471795801270)
XLA Ops:
  0.0 2.6 %pack_influence.1 = (bf16[2592,128]{1,0:T(8,128)(2,1)}, s32[8,256]{1,0:T(8,128)}) custom-call(bf16[3,4,144,192]{3,2,1,0:T(8,128)(2,1)} %bitcast.13, s32[3,1,4]{2,1,0:T(1,128)} %bitcast.23, s32[3,1,160]{2,1,0:T(1,128)} %bitcast.22, s32[1,2,80]{2,1,0:T(2,128)} %valid_ref.1), custom_call_target="tpu_custom_call" | custom-call | bytes 995328 | tf_op jit(solution)/shard_map/pack_influence/pallas_call | solution.py:65
  2.6 5.1 %collective-permute-start.4 = (s32[8,256]{1,0:T(8,128)}, s32[8,256]{1,0:T(8,128)S(1)}, u32[]{:S(2)}, u32[]{:S(2)}) collective-permute-start(s32[8,256]{1,0:T(8,128)} %get-tuple-element.23), channel_id=1, source_target_pairs={{0,24},{8,16},{16,8},{24,0},{1,25},{9,17},{17,9},{25,1},{2,26},{10... | collective-permute-start | bytes 24584 | tf_op jit(solution)/shard_map/ppermute | solution.py:522
  7.6 0.0 collective-permute-start.3
  7.6 0.6 collective-permute-start.2
  8.2 0.0 collective-permute-start.5
  8.2 1.7 %collective-permute-start.1 = (bf16[2592,128]{1,0:T(8,128)(2,1)}, bf16[2592,128]{1,0:T(8,128)(2,1)}, u32[]{:S(2)}, u32[]{:S(2)}) collective-permute-start(bf16[2592,128]{1,0:T(8,128)(2,1)} %get-tuple-element.21.packed_ref), channel_id=1, source_target_pairs={{0,4},{1,3},{2,6},{3,1},{4,0},{5,7},{6,2},{7,5},{8,12},{9,11},{10,... | collective-permute-start | bytes 1990664 | tf_op jit(solution)/shard_map/ppermute | solution.py:526
  9.9 0.0 collective-permute-done.4
  9.9 0.0 copy-start.3
  9.9 1.5 %collective-permute-start = (bf16[2592,128]{1,0:T(8,128)(2,1)}, bf16[2592,128]{1,0:T(8,128)(2,1)}, u32[]{:S(2)}, u32[]{:S(2)}) collective-permute-start(bf16[2592,128]{1,0:T(8,128)(2,1)} %get-tuple-element.21.packed_ref), channel_id=1, source_target_pairs={{0,2},{1,5},{2,0},{3,7},{4,6},{5,1},{6,4},{7,3},{8,10},{9,13},{10,... | collective-permute-start | bytes 1990664 | tf_op jit(solution)/shard_map/ppermute | solution.py:526
  11.4 0.0 copy-start.2
  11.4 12.0 %gram_rows.1 = (bf16[6912,224]{1,0:T(8,128)(2,1)}, bf16[1,12,192,224]{3,2,1,0:T(8,128)(2,1)}) custom-call(s32[3,48,48]{2,1,0:T(8,128)} %table_ref.1, s32[16,128]{1,0:T(8,128)} %bitcast.24, bf16[2592,128]{1,0:T(8,128)(2,1)} %get-tuple-element.21.packed_ref), custom_call_target="tpu_custom_call" | custom-call | flops 6341787648 | bytes 3096576 | tf_op jit(solution)/shard_map/gram_rows/pallas_call | solution.py:194
  23.5 0.0 collective-permute-done.3
  23.5 0.0 copy-start.4
  23.5 0.0 collective-permute-done.2
  23.5 0.0 copy-start.5
  23.5 0.0 copy-done.3
  23.5 0.0 copy-done.2
  23.6 1.8 %collective-permute-done.1 = bf16[2592,128]{1,0:T(8,128)(2,1)} collective-permute-done((bf16[2592,128]{1,0:T(8,128)(2,1)}, bf16[2592,128]{1,0:T(8,128)(2,1)}, u32[]{:S(2)}, u32[]{:S(2)}) %collective-permute-start.1) | collective-permute-done | bytes 663584 | tf_op jit(solution)/shard_map/ppermute | solution.py:526
  25.3 0.5 collective-permute-done
  25.8 1.7 %collective-permute-start.6 = (bf16[2592,128]{1,0:T(8,128)(2,1)}, bf16[2592,128]{1,0:T(8,128)(2,1)}, u32[]{:S(2)}, u32[]{:S(2)}) collective-permute-start(bf16[2592,128]{1,0:T(8,128)(2,1)} %collective-permute-done), channel_id=1, source_target_pairs={{0,4},{1,3},{2,6},{3,1},{4,0},{5,7},{6,2},{7,5},{8,12},{9,11},{10,... | collective-permute-start | bytes 1990664 | tf_op jit(solution)/shard_map/ppermute | solution.py:526
  27.6 1.5 %collective-permute-start.9 = (s32[1,4,8,256]{3,2,1,0:T(8,128)S(1)}, s32[1,4,8,256]{3,2,1,0:T(8,128)S(1)}, u32[]{:S(2)}, u32[]{:S(2)}) collective-permute-start(s32[1,4,8,256]{3,2,1,0:T(8,128)S(1)} %add_bitcast_fusion), channel_id=1, source_target_pairs={{0,6},{1,7},{2,4},{3,5},{4,2},{5,3},{6,0},{7,1},{8,14},{9,15},{10,... | collective-permute-start | bytes 98312 | tf_op jit(solution)/shard_map/ppermute | solution.py:522
  29.1 1.7 %collective-permute-start.8 = (s32[1,4,8,256]{3,2,1,0:T(8,128)S(1)}, s32[1,4,8,256]{3,2,1,0:T(8,128)S(1)}, u32[]{:S(2)}, u32[]{:S(2)}) collective-permute-start(s32[1,4,8,256]{3,2,1,0:T(8,128)S(1)} %add_bitcast_fusion), channel_id=1, source_target_pairs={{0,4},{1,3},{2,6},{3,1},{4,0},{5,7},{6,2},{7,5},{8,12},{9,11},{10,... | collective-permute-start | bytes 98312 | tf_op jit(solution)/shard_map/ppermute | solution.py:526
  30.8 0.3 collective-permute-start.7
  31.1 0.0 collective-permute-done.5
  31.1 0.0 collective-permute-start.11
  31.1 0.0 copy-done.4
  31.1 0.0 copy-done.5
  31.1 6.5 %bands.1 = (bf16[3,12,192,224]{3,2,1,0:T(8,128)(2,1)}, bf16[4,2,80,512]{3,2,1,0:T(8,128)(2,1)}, bf16[4,160,128]{2,1,0:T(8,128)(2,1)}) custom-call(bf16[6912,224]{1,0:T(8,128)(2,1)} %get-tuple-element.24.gram_any.refs_10_, bf16[1,2592,128]{2,1,0:T(8,128)(2,1)} %bitcast.9.refs_0_, bf16[1,2592,128]{2,1,0:T(8,128)(2,1)} %bitcast.10.refs_1_, ...), custom_call_target="tpu_custom_call" | custom-call | flops 792723456 | bytes 4128768 | tf_op jit(solution)/shard_map/bands/pallas_call | solution.py:339
  37.6 0.0 collective-permute-done.9
  37.6 0.6 collective-permute-start.12
  38.2 0.0 collective-permute-done.8
  38.2 0.0 collective-permute-done.7
  38.2 0.0 copy-start
  38.2 0.0 collective-permute-done.6.refs_6_
  38.2 0.1 collective-permute-start.13
  38.3 0.5 collective-permute-start.10
  38.8 0.0 collective-permute-done.11.refs_4_
  38.8 1.5 %collective-permute-done.12.refs_5_ = bf16[2592,128]{1,0:T(8,128)(2,1)} collective-permute-done((bf16[2592,128]{1,0:T(8,128)(2,1)}, bf16[2592,128]{1,0:T(8,128)(2,1)}, u32[]{:S(2)}, u32[]{:S(2)}) %collective-permute-start.12) | collective-permute-done | bytes 663584 | tf_op jit(solution)/shard_map/ppermute | solution.py:522
  40.3 0.0 collective-permute-done.10.refs_3_
  40.3 0.0 copy-start.1
  40.3 1.1 %collective-permute-done.13.refs_7_ = bf16[2592,128]{1,0:T(8,128)(2,1)} collective-permute-done((bf16[2592,128]{1,0:T(8,128)(2,1)}, bf16[2592,128]{1,0:T(8,128)(2,1)}, u32[]{:S(2)}, u32[]{:S(2)}) %collective-permute-start.13) | collective-permute-done | bytes 663584 | tf_op jit(solution)/shard_map/ppermute | solution.py:522
  41.4 0.0 copy-done
  41.4 0.0 copy-done.1
  41.4 16.2 %decode.1 = bf16[216,4,2560]{2,1,0:T(4,128)(2,1)} custom-call(bf16[4,2,80,512]{3,2,1,0:T(8,128)(2,1)} %get-tuple-element.27.refs_0_, bf16[4,160,128]{2,1,0:T(8,128)(2,1)} %get-tuple-element.28.refs_1_, s32[4,4,8,256]{3,2,1,0:T(8,128)} %copy-done, s32[4,4,8,256]{3,2,1,0:T(8,128)} %copy-done.1, bf16[2592,128]{1,0:T(8,128)(2,1)} %collective-permute-done.11.refs_4_, ...), custom_call_target="tpu_custom_call" | custom-call | flops 2642411520 | bytes 4423680 | tf_op jit(solution)/shard_map/decode/pallas_call | solution.py:497
  (2 shorter events, 0.0 us)
Async XLA Ops:
  2.6 7.4 %collective-permute-start.4 = (s32[8,256]{1,0:T(8,128)}, s32[8,256]{1,0:T(8,128)S(1)}, u32[]{:S(2)}, u32[]{:S(2)}) collective-permute-start(s32[8,256]{1,0:T(8,128)} %get-tuple-element.23), channel_id=1, source_target_pairs={{0,24},{8,16},{16,8},{24,0},{1,25},{9,17},{17,9},{25,1},{2,26},{10... | collective-permute-start | bytes 24584 | tf_op jit(solution)/shard_map/ppermute | solution.py:522
  7.6 15.9 %collective-permute-start.3 = (s32[8,256]{1,0:T(8,128)}, s32[8,256]{1,0:T(8,128)S(1)}, u32[]{:S(2)}, u32[]{:S(2)}) collective-permute-start(s32[8,256]{1,0:T(8,128)} %get-tuple-element.23), channel_id=1, source_target_pairs={{0,16},{8,24},{16,0},{24,8},{1,17},{9,25},{17,1},{25,9},{2,18},{10... | collective-permute-start | bytes 24584 | tf_op jit(solution)/shard_map/ppermute | solution.py:522
  7.6 15.9 %collective-permute-start.2 = (s32[8,256]{1,0:T(8,128)}, s32[8,256]{1,0:T(8,128)S(1)}, u32[]{:S(2)}, u32[]{:S(2)}) collective-permute-start(s32[8,256]{1,0:T(8,128)} %get-tuple-element.23), channel_id=1, source_target_pairs={{0,8},{8,0},{16,24},{24,16},{1,9},{9,1},{17,25},{25,17},{2,10},{10... | collective-permute-start | bytes 24584 | tf_op jit(solution)/shard_map/ppermute | solution.py:522
  8.2 22.9 %collective-permute-start.5 = (bf16[2592,128]{1,0:T(8,128)(2,1)}, bf16[2592,128]{1,0:T(8,128)(2,1)}, u32[]{:S(2)}, u32[]{:S(2)}) collective-permute-start(bf16[2592,128]{1,0:T(8,128)(2,1)} %get-tuple-element.21.packed_ref), channel_id=1, source_target_pairs={{0,1},{1,0},{2,3},{3,2},{4,5},{5,4},{6,7},{7,6},{8,9},{9,8},{10,11... | collective-permute-start | bytes 1990664 | tf_op jit(solution)/shard_map/ppermute | solution.py:522
  8.2 17.1 %collective-permute-start.1 = (bf16[2592,128]{1,0:T(8,128)(2,1)}, bf16[2592,128]{1,0:T(8,128)(2,1)}, u32[]{:S(2)}, u32[]{:S(2)}) collective-permute-start(bf16[2592,128]{1,0:T(8,128)(2,1)} %get-tuple-element.21.packed_ref), channel_id=1, source_target_pairs={{0,4},{1,3},{2,6},{3,1},{4,0},{5,7},{6,2},{7,5},{8,12},{9,11},{10,... | collective-permute-start | bytes 1990664 | tf_op jit(solution)/shard_map/ppermute | solution.py:526
  9.9 13.6 %copy-start.3 = (s32[8,256]{1,0:T(8,128)}, s32[8,256]{1,0:T(8,128)S(1)}, u32[]{:S(2)}) copy-start(s32[8,256]{1,0:T(8,128)S(1)} %collective-permute-done.4) | copy-start | bytes 24580
  9.9 15.9 %collective-permute-start = (bf16[2592,128]{1,0:T(8,128)(2,1)}, bf16[2592,128]{1,0:T(8,128)(2,1)}, u32[]{:S(2)}, u32[]{:S(2)}) collective-permute-start(bf16[2592,128]{1,0:T(8,128)(2,1)} %get-tuple-element.21.packed_ref), channel_id=1, source_target_pairs={{0,2},{1,5},{2,0},{3,7},{4,6},{5,1},{6,4},{7,3},{8,10},{9,13},{10,... | collective-permute-start | bytes 1990664 | tf_op jit(solution)/shard_map/ppermute | solution.py:526
  11.4 12.1 %copy-start.2 = (s32[8,256]{1,0:T(8,128)S(1)}, s32[8,256]{1,0:T(8,128)}, u32[]{:S(2)}) copy-start(s32[8,256]{1,0:T(8,128)} %get-tuple-element.23) | copy-start | bytes 24580
  23.5 7.6 %copy-start.4 = (s32[8,256]{1,0:T(8,128)}, s32[8,256]{1,0:T(8,128)S(1)}, u32[]{:S(2)}) copy-start(s32[8,256]{1,0:T(8,128)S(1)} %collective-permute-done.3) | copy-start | bytes 24580
  23.5 7.6 %copy-start.5 = (s32[8,256]{1,0:T(8,128)}, s32[8,256]{1,0:T(8,128)S(1)}, u32[]{:S(2)}) copy-start(s32[8,256]{1,0:T(8,128)S(1)} %collective-permute-done.2) | copy-start | bytes 24580
  25.8 12.4 %collective-permute-start.6 = (bf16[2592,128]{1,0:T(8,128)(2,1)}, bf16[2592,128]{1,0:T(8,128)(2,1)}, u32[]{:S(2)}, u32[]{:S(2)}) collective-permute-start(bf16[2592,128]{1,0:T(8,128)(2,1)} %collective-permute-done), channel_id=1, source_target_pairs={{0,4},{1,3},{2,6},{3,1},{4,0},{5,7},{6,2},{7,5},{8,12},{9,11},{10,... | collective-permute-start | bytes 1990664 | tf_op jit(solution)/shard_map/ppermute | solution.py:526
  27.6 10.1 %collective-permute-start.9 = (s32[1,4,8,256]{3,2,1,0:T(8,128)S(1)}, s32[1,4,8,256]{3,2,1,0:T(8,128)S(1)}, u32[]{:S(2)}, u32[]{:S(2)}) collective-permute-start(s32[1,4,8,256]{3,2,1,0:T(8,128)S(1)} %add_bitcast_fusion), channel_id=1, source_target_pairs={{0,6},{1,7},{2,4},{3,5},{4,2},{5,3},{6,0},{7,1},{8,14},{9,15},{10,... | collective-permute-start | bytes 98312 | tf_op jit(solution)/shard_map/ppermute | solution.py:522
  29.1 9.1 %collective-permute-start.8 = (s32[1,4,8,256]{3,2,1,0:T(8,128)S(1)}, s32[1,4,8,256]{3,2,1,0:T(8,128)S(1)}, u32[]{:S(2)}, u32[]{:S(2)}) collective-permute-start(s32[1,4,8,256]{3,2,1,0:T(8,128)S(1)} %add_bitcast_fusion), channel_id=1, source_target_pairs={{0,4},{1,3},{2,6},{3,1},{4,0},{5,7},{6,2},{7,5},{8,12},{9,11},{10,... | collective-permute-start | bytes 98312 | tf_op jit(solution)/shard_map/ppermute | solution.py:526
  30.8 7.4 %collective-permute-start.7 = (s32[1,4,8,256]{3,2,1,0:T(8,128)S(1)}, s32[1,4,8,256]{3,2,1,0:T(8,128)S(1)}, u32[]{:S(2)}, u32[]{:S(2)}) collective-permute-start(s32[1,4,8,256]{3,2,1,0:T(8,128)S(1)} %add_bitcast_fusion), channel_id=1, source_target_pairs={{0,2},{1,5},{2,0},{3,7},{4,6},{5,1},{6,4},{7,3},{8,10},{9,13},{10,... | collective-permute-start | bytes 98312 | tf_op jit(solution)/shard_map/ppermute | solution.py:526
  31.1 7.7 %collective-permute-start.11 = (bf16[2592,128]{1,0:T(8,128)(2,1)}, bf16[2592,128]{1,0:T(8,128)(2,1)}, u32[]{:S(2)}, u32[]{:S(2)}) collective-permute-start(bf16[2592,128]{1,0:T(8,128)(2,1)} %collective-permute-done), channel_id=1, source_target_pairs={{0,1},{1,0},{2,3},{3,2},{4,5},{5,4},{6,7},{7,6},{8,9},{9,8},{10,11... | collective-permute-start | bytes 1990664 | tf_op jit(solution)/shard_map/ppermute | solution.py:522
  37.6 2.6 %collective-permute-start.12 = (bf16[2592,128]{1,0:T(8,128)(2,1)}, bf16[2592,128]{1,0:T(8,128)(2,1)}, u32[]{:S(2)}, u32[]{:S(2)}) collective-permute-start(bf16[2592,128]{1,0:T(8,128)(2,1)} %collective-permute-done.1), channel_id=1, source_target_pairs={{0,1},{1,0},{2,3},{3,2},{4,5},{5,4},{6,7},{7,6},{8,9},{9,8},{10,11... | collective-permute-start | bytes 1990664 | tf_op jit(solution)/shard_map/ppermute | solution.py:522
  38.2 3.2 %copy-start = (s32[4,4,8,256]{3,2,1,0:T(8,128)}, s32[4,4,8,256]{3,2,1,0:T(8,128)S(1)}, u32[]{:S(2)}) copy-start(s32[4,4,8,256]{3,2,1,0:T(8,128)S(1)} %pad_add_fusion.refs_2_) | copy-start | bytes 393220
  38.2 3.2 %collective-permute-start.13 = (bf16[2592,128]{1,0:T(8,128)(2,1)}, bf16[2592,128]{1,0:T(8,128)(2,1)}, u32[]{:S(2)}, u32[]{:S(2)}) collective-permute-start(bf16[2592,128]{1,0:T(8,128)(2,1)} %collective-permute-done.6.refs_6_), channel_id=1, source_target_pairs={{0,1},{1,0},{2,3},{3,2},{4,5},{5,4},{6,7},{7,6},{8,9},{9,8},{10,11... | collective-permute-start | bytes 1990664 | tf_op jit(solution)/shard_map/ppermute | solution.py:522
  38.3 2.0 %collective-permute-start.10 = (s32[4,4,8,256]{3,2,1,0:T(8,128)S(1)}, s32[4,4,8,256]{3,2,1,0:T(8,128)S(1)}, u32[]{:S(2)}, u32[]{:S(2)}) collective-permute-start(s32[4,4,8,256]{3,2,1,0:T(8,128)S(1)} %pad_add_fusion.refs_2_), channel_id=1, source_target_pairs={{0,1},{1,0},{2,3},{3,2},{4,5},{5,4},{6,7},{7,6},{8,9},{9,8},{10,11... | collective-permute-start | bytes 393224 | tf_op jit(solution)/shard_map/ppermute | solution.py:522
  40.3 1.1 %copy-start.1 = (s32[4,4,8,256]{3,2,1,0:T(8,128)}, s32[4,4,8,256]{3,2,1,0:T(8,128)S(1)}, u32[]{:S(2)}) copy-start(s32[4,4,8,256]{3,2,1,0:T(8,128)S(1)} %collective-permute-done.10.refs_3_) | copy-start | bytes 393220

commit v16 on v15

--- a/solution.py
+++ b/solution.py
@@ -536,7 +536,7 @@
     pupil = foot_columns.shape[2]
     norm = 0.5 * poke_rows.shape[0] ** (-0.5)
     own = actuator_codes.size // (directions * devices)
-    staged = devices == 8 and directions & (directions - 1) == 0
+    staged = devices == 8 and directions > 1 and directions & (directions - 1) == 0
     turned = jnp.swapaxes(influence, 2, 3)
     pokes = poke_rows.reshape(-1, LANES)
     packed, lines = pack(turned, foot_rows, foot_columns, subaperture_valid)
@@ -550,9 +550,13 @@
             norm, staged,
         )
 
-    lines = [lines[None]] + [swap(lines, "dir", e)[None] for e in range(1, directions)]
     first, second = turn(packed, 2, 4), turn(packed, 4, 2)
     sibling = swap(packed, "row", 1)
+    lines, distance = [jnp.stack([lines, swap(lines, "dir", 1)])], 2
+    lines[0], pokes = lax.optimization_barrier((lines[0], pokes))
+    while distance < directions:
+        lines.append(swap(jnp.concatenate(lines, axis=0), "dir", distance))
+        distance *= 2
     held = jnp.concatenate(lines, axis=0)[None]
     gram_rows, own_rows = gram(actuator_codes, pokes, packed, own, row_shape, surface_rows)
     gram_rows, first, second, held = lax.optimization_barrier((gram_rows, first, second, held))

time: 57.8 us -> 55.9 us (0.967)
  waiting for transfers between devices: 4.9 us -> 3.01 us
  starting transfers between devices: 15.2 us -> 14.1 us
  other arithmetic: 0.01 us -> 0.71 us
    ppermute x5, waiting for transfers between devices: 2.29 us -> 0.92 us  [turn(): lax.ppermute(block, 'row', [(i, i ^ (odd if i % 2 else even)) for i in ra...]
    ppermute x5, starting transfers between devices: 6.92 us -> 5.77 us  [turn(): lax.ppermute(block, 'row', [(i, i ^ (odd if i % 2 else even)) for i in ra...]
    another operation x0 -> x1, other arithmetic: none -> 0.7 us  [shards(): lines, distance = ([jnp.stack([lines, swap(lines, 'dir', 1)])], 2)]
    ppermute x9 -> x8, waiting for transfers between devices: 2.61 us -> 2.1 us  [swap(): lax.ppermute(block, axis, [(i, i ^ distance) for i in range(lax.axis_size...]
    ppermute x9 -> x8, starting transfers between devices: 8.29 us -> 8.3 us  [swap(): lax.ppermute(block, axis, [(i, i ^ distance) for i in range(lax.axis_size...]
  transfers between devices with their start and end apart: 14 -> 13, of which waited for: 4 -> 4; matrix products, arithmetic and copies ran while one was open for 0% -> 1% of each run, Pallas kernels for 32% -> 33%
where the time goes in v16:
time: 55.9 us; the launch traced here: 55.6 us
  Pallas kernels  37.3 us (67%)
  starting transfers between devices  14.1 us (25%)
  waiting for transfers between devices  3.01 us (5%)
  other arithmetic  0.71 us (1%)
    pallas_call x1, Pallas kernels, decode(): pl.pallas_call(functools.partial(decode_kernel, row_shape, surface_rows,...  16.2 us
    pallas_call x1, Pallas kernels, gram(): pl.pallas_call(functools.partial(gram_kernel, row_shape, surface_rows), g...  12 us
    ppermute x8, starting transfers between devices, swap(): lax.ppermute(block, axis, [(i, i ^ distance) for i in range(lax.axis_size...  8.3 us
    pallas_call x1, Pallas kernels, bands(): pl.pallas_call(functools.partial(bands_kernel, row_shape, surface_rows, f...  6.54 us
    ppermute x5, starting transfers between devices, turn(): lax.ppermute(block, 'row', [(i, i ^ (odd if i % 2 else even)) for i in ra...  5.77 us
    pallas_call x1, Pallas kernels, pack(): pl.pallas_call(pack_kernel, out_shape=[jax.ShapeDtypeStruct((mirrors * ro...  2.57 us
    ppermute x8, waiting for transfers between devices, swap(): lax.ppermute(block, axis, [(i, i ^ distance) for i in range(lax.axis_size...  2.1 us
  transfers between devices with their start and end apart: 13, of which 4 were waited for; matrix products, arithmetic and copies ran while one was open for 1% of the time, Pallas kernels for 33%

profile of v16, /device:TPU:0, one launch (start us, length us, event | category | flops | bytes accessed | tf_op | source)
XLA Modules:
  0.0 55.6 jit_solution(8977366986307220469)
XLA Ops:
  0.0 2.6 %pack_influence.1 = (bf16[2592,128]{1,0:T(8,128)(2,1)}, s32[8,256]{1,0:T(8,128)}) custom-call(bf16[3,4,144,192]{3,2,1,0:T(8,128)(2,1)} %bitcast.11, s32[3,1,4]{2,1,0:T(1,128)} %bitcast.15, s32[3,1,160]{2,1,0:T(1,128)} %bitcast.14, s32[1,2,80]{2,1,0:T(2,128)} %valid_ref.1), custom_call_target="tpu_custom_call" | custom-call | bytes 995328 | tf_op jit(solution)/shard_map/pack_influence/pallas_call | solution.py:65
  2.6 3.0 %collective-permute-start = (s32[8,256]{1,0:T(8,128)}, s32[8,256]{1,0:T(8,128)S(1)}, u32[]{:S(2)}, u32[]{:S(2)}) collective-permute-start(s32[8,256]{1,0:T(8,128)} %get-tuple-element.23), channel_id=1, source_target_pairs={{0,8},{8,0},{16,24},{24,16},{1,9},{9,1},{17,25},{25,17},{2,10},{10... | collective-permute-start | bytes 24584 | tf_op jit(solution)/shard_map/ppermute | solution.py:522
  5.6 0.0 collective-permute-start.4
  5.6 1.5 %collective-permute-start.2 = (bf16[2592,128]{1,0:T(8,128)(2,1)}, bf16[2592,128]{1,0:T(8,128)(2,1)}, u32[]{:S(2)}, u32[]{:S(2)}) collective-permute-start(bf16[2592,128]{1,0:T(8,128)(2,1)} %get-tuple-element.25.packed_ref), channel_id=1, source_target_pairs={{0,4},{1,3},{2,6},{3,1},{4,0},{5,7},{6,2},{7,5},{8,12},{9,11},{10,... | collective-permute-start | bytes 1990664 | tf_op jit(solution)/shard_map/ppermute | solution.py:526
  7.1 1.5 %collective-permute-start.1 = (bf16[2592,128]{1,0:T(8,128)(2,1)}, bf16[2592,128]{1,0:T(8,128)(2,1)}, u32[]{:S(2)}, u32[]{:S(2)}) collective-permute-start(bf16[2592,128]{1,0:T(8,128)(2,1)} %get-tuple-element.25.packed_ref), channel_id=1, source_target_pairs={{0,2},{1,5},{2,0},{3,7},{4,6},{5,1},{6,4},{7,3},{8,10},{9,13},{10,... | collective-permute-start | bytes 1990664 | tf_op jit(solution)/shard_map/ppermute | solution.py:526
  8.6 0.0 collective-permute-done
  8.6 0.7 %pad_add_fusion.1.refs_3_ = s32[2,8,256]{2,1,0:T(8,128)S(1)} fusion(s32[1,8,256]{2,1,0:T(8,128)S(1)} %bitcast.13, s32[1,8,256]{2,1,0:T(8,128)} %bitcast.12), kind=kLoop, calls=%fused_computation.2 | loop fusion | flops 4096 | bytes 32768 | tf_op jit(solution)/shard_map/stack | solution.py:555
  9.3 0.0 copy-start.1
  9.3 2.6 %collective-permute-start.3 = (s32[2,8,256]{2,1,0:T(8,128)S(1)}, s32[2,8,256]{2,1,0:T(8,128)S(1)}, u32[]{:S(2)}, u32[]{:S(2)}) collective-permute-start(s32[2,8,256]{2,1,0:T(8,128)S(1)} %pad_add_fusion.1.refs_3_), channel_id=1, source_target_pairs={{0,16},{8,24},{16,0},{24,8},{1,17},{9,25},{17,1},{25,9},{2,18},{10... | collective-permute-start | bytes 49160 | tf_op jit(solution)/shard_map/ppermute | solution.py:522
  11.9 12.0 %gram_rows.1 = (bf16[6912,224]{1,0:T(8,128)(2,1)}, bf16[1,12,192,224]{3,2,1,0:T(8,128)(2,1)}) custom-call(s32[3,48,48]{2,1,0:T(8,128)} %table_ref.1, s32[16,128]{1,0:T(8,128)} %bitcast.16, bf16[2592,128]{1,0:T(8,128)(2,1)} %get-tuple-element.25.packed_ref), custom_call_target="tpu_custom_call" | custom-call | flops 6341787648 | bytes 3096576 | tf_op jit(solution)/shard_map/gram_rows/pallas_call | solution.py:194
  24.0 0.0 collective-permute-done.3.refs_4_
  24.0 0.0 copy-done.1
  24.0 0.0 copy-start.3
  24.0 0.0 collective-permute-done.2
  24.0 0.0 collective-permute-done.1
  24.0 0.9 %collective-permute-start.5 = (bf16[2592,128]{1,0:T(8,128)(2,1)}, bf16[2592,128]{1,0:T(8,128)(2,1)}, u32[]{:S(2)}, u32[]{:S(2)}) collective-permute-start(bf16[2592,128]{1,0:T(8,128)(2,1)} %collective-permute-done.1), channel_id=1, source_target_pairs={{0,4},{1,3},{2,6},{3,1},{4,0},{5,7},{6,2},{7,5},{8,12},{9,11},{10,... | collective-permute-start | bytes 1990664 | tf_op jit(solution)/shard_map/ppermute | solution.py:526
  24.9 1.6 %collective-permute-start.8 = (s32[1,4,8,256]{3,2,1,0:T(8,128)S(1)}, s32[1,4,8,256]{3,2,1,0:T(8,128)S(1)}, u32[]{:S(2)}, u32[]{:S(2)}) collective-permute-start(s32[1,4,8,256]{3,2,1,0:T(8,128)S(1)} %add_bitcast_fusion), channel_id=1, source_target_pairs={{0,6},{1,7},{2,4},{3,5},{4,2},{5,3},{6,0},{7,1},{8,14},{9,15},{10,... | collective-permute-start | bytes 98312 | tf_op jit(solution)/shard_map/ppermute | solution.py:522
  26.5 1.5 %collective-permute-start.7 = (s32[1,4,8,256]{3,2,1,0:T(8,128)S(1)}, s32[1,4,8,256]{3,2,1,0:T(8,128)S(1)}, u32[]{:S(2)}, u32[]{:S(2)}) collective-permute-start(s32[1,4,8,256]{3,2,1,0:T(8,128)S(1)} %add_bitcast_fusion), channel_id=1, source_target_pairs={{0,4},{1,3},{2,6},{3,1},{4,0},{5,7},{6,2},{7,5},{8,12},{9,11},{10,... | collective-permute-start | bytes 98312 | tf_op jit(solution)/shard_map/ppermute | solution.py:526
  28.0 0.4 collective-permute-start.6
  28.4 0.0 collective-permute-done.4
  28.4 0.0 collective-permute-start.10
  28.4 0.0 copy-done.3
  28.4 6.5 %bands.1 = (bf16[3,12,192,224]{3,2,1,0:T(8,128)(2,1)}, bf16[4,2,80,512]{3,2,1,0:T(8,128)(2,1)}, bf16[4,160,128]{2,1,0:T(8,128)(2,1)}) custom-call(bf16[6912,224]{1,0:T(8,128)(2,1)} %get-tuple-element.28.gram_any.refs_10_, bf16[1,2592,128]{2,1,0:T(8,128)(2,1)} %bitcast.7.refs_0_, bf16[1,2592,128]{2,1,0:T(8,128)(2,1)} %bitcast.8.refs_1_, ...), custom_call_target="tpu_custom_call" | custom-call | flops 792723456 | bytes 4128768 | tf_op jit(solution)/shard_map/bands/pallas_call | solution.py:339
  34.9 0.0 collective-permute-done.8
  34.9 0.5 collective-permute-start.11
  35.5 0.9 %collective-permute-done.7 = s32[1,4,8,256]{3,2,1,0:T(8,128)S(1)} collective-permute-done((s32[1,4,8,256]{3,2,1,0:T(8,128)S(1)}, s32[1,4,8,256]{3,2,1,0:T(8,128)S(1)}, u32[]{:S(2)}, u32[]{:S(2)}) %collective-permute-start.7) | collective-permute-done | bytes 32800 | tf_op jit(solution)/shard_map/ppermute | solution.py:526
  36.4 0.0 collective-permute-done.6
  36.4 0.0 copy-start
  36.4 0.0 collective-permute-done.5.refs_6_
  36.4 0.1 collective-permute-start.12
  36.5 0.5 collective-permute-start.9
  37.0 0.0 collective-permute-done.10.refs_4_
  37.0 0.6 collective-permute-done.11.refs_5_
  37.5 1.2 %collective-permute-done.9.refs_3_ = s32[4,4,8,256]{3,2,1,0:T(8,128)S(1)} collective-permute-done((s32[4,4,8,256]{3,2,1,0:T(8,128)S(1)}, s32[4,4,8,256]{3,2,1,0:T(8,128)S(1)}, u32[]{:S(2)}, u32[]{:S(2)}) %collective-permute-start.9) | collective-permute-done | bytes 131104 | tf_op jit(solution)/shard_map/ppermute | solution.py:522
  38.8 0.0 copy-start.2
  38.8 0.3 collective-permute-done.12.refs_7_
  39.1 0.0 copy-done
  39.1 0.3 copy-done.2
  39.4 16.2 %decode.1 = bf16[216,4,2560]{2,1,0:T(4,128)(2,1)} custom-call(bf16[4,2,80,512]{3,2,1,0:T(8,128)(2,1)} %get-tuple-element.31.refs_0_, bf16[4,160,128]{2,1,0:T(8,128)(2,1)} %get-tuple-element.32.refs_1_, s32[4,4,8,256]{3,2,1,0:T(8,128)} %copy-done, s32[4,4,8,256]{3,2,1,0:T(8,128)} %copy-done.2, bf16[2592,128]{1,0:T(8,128)(2,1)} %collective-permute-done.10.refs_4_, ...), custom_call_target="tpu_custom_call" | custom-call | flops 2642411520 | bytes 4423680 | tf_op jit(solution)/shard_map/decode/pallas_call | solution.py:497
  (2 shorter events, 0.0 us)
Async XLA Ops:
  2.6 6.0 %collective-permute-start = (s32[8,256]{1,0:T(8,128)}, s32[8,256]{1,0:T(8,128)S(1)}, u32[]{:S(2)}, u32[]{:S(2)}) collective-permute-start(s32[8,256]{1,0:T(8,128)} %get-tuple-element.23), channel_id=1, source_target_pairs={{0,8},{8,0},{16,24},{24,16},{1,9},{9,1},{17,25},{25,17},{2,10},{10... | collective-permute-start | bytes 24584 | tf_op jit(solution)/shard_map/ppermute | solution.py:522
  5.6 22.8 %collective-permute-start.4 = (bf16[2592,128]{1,0:T(8,128)(2,1)}, bf16[2592,128]{1,0:T(8,128)(2,1)}, u32[]{:S(2)}, u32[]{:S(2)}) collective-permute-start(bf16[2592,128]{1,0:T(8,128)(2,1)} %get-tuple-element.25.packed_ref), channel_id=1, source_target_pairs={{0,1},{1,0},{2,3},{3,2},{4,5},{5,4},{6,7},{7,6},{8,9},{9,8},{10,11... | collective-permute-start | bytes 1990664 | tf_op jit(solution)/shard_map/ppermute | solution.py:522
  5.6 18.4 %collective-permute-start.2 = (bf16[2592,128]{1,0:T(8,128)(2,1)}, bf16[2592,128]{1,0:T(8,128)(2,1)}, u32[]{:S(2)}, u32[]{:S(2)}) collective-permute-start(bf16[2592,128]{1,0:T(8,128)(2,1)} %get-tuple-element.25.packed_ref), channel_id=1, source_target_pairs={{0,4},{1,3},{2,6},{3,1},{4,0},{5,7},{6,2},{7,5},{8,12},{9,11},{10,... | collective-permute-start | bytes 1990664 | tf_op jit(solution)/shard_map/ppermute | solution.py:526
  7.1 16.9 %collective-permute-start.1 = (bf16[2592,128]{1,0:T(8,128)(2,1)}, bf16[2592,128]{1,0:T(8,128)(2,1)}, u32[]{:S(2)}, u32[]{:S(2)}) collective-permute-start(bf16[2592,128]{1,0:T(8,128)(2,1)} %get-tuple-element.25.packed_ref), channel_id=1, source_target_pairs={{0,2},{1,5},{2,0},{3,7},{4,6},{5,1},{6,4},{7,3},{8,10},{9,13},{10,... | collective-permute-start | bytes 1990664 | tf_op jit(solution)/shard_map/ppermute | solution.py:526
  9.3 14.6 %copy-start.1 = (s32[2,8,256]{2,1,0:T(8,128)}, s32[2,8,256]{2,1,0:T(8,128)S(1)}, u32[]{:S(2)}) copy-start(s32[2,8,256]{2,1,0:T(8,128)S(1)} %pad_add_fusion.1.refs_3_) | copy-start | bytes 49156
  9.3 14.6 %collective-permute-start.3 = (s32[2,8,256]{2,1,0:T(8,128)S(1)}, s32[2,8,256]{2,1,0:T(8,128)S(1)}, u32[]{:S(2)}, u32[]{:S(2)}) collective-permute-start(s32[2,8,256]{2,1,0:T(8,128)S(1)} %pad_add_fusion.1.refs_3_), channel_id=1, source_target_pairs={{0,16},{8,24},{16,0},{24,8},{1,17},{9,25},{17,1},{25,9},{2,18},{10... | collective-permute-start | bytes 49160 | tf_op jit(solution)/shard_map/ppermute | solution.py:522
  24.0 4.4 %copy-start.3 = (s32[2,8,256]{2,1,0:T(8,128)}, s32[2,8,256]{2,1,0:T(8,128)S(1)}, u32[]{:S(2)}) copy-start(s32[2,8,256]{2,1,0:T(8,128)S(1)} %collective-permute-done.3.refs_4_) | copy-start | bytes 49156
  24.0 12.4 %collective-permute-start.5 = (bf16[2592,128]{1,0:T(8,128)(2,1)}, bf16[2592,128]{1,0:T(8,128)(2,1)}, u32[]{:S(2)}, u32[]{:S(2)}) collective-permute-start(bf16[2592,128]{1,0:T(8,128)(2,1)} %collective-permute-done.1), channel_id=1, source_target_pairs={{0,4},{1,3},{2,6},{3,1},{4,0},{5,7},{6,2},{7,5},{8,12},{9,11},{10,... | collective-permute-start | bytes 1990664 | tf_op jit(solution)/shard_map/ppermute | solution.py:526
  24.9 10.1 %collective-permute-start.8 = (s32[1,4,8,256]{3,2,1,0:T(8,128)S(1)}, s32[1,4,8,256]{3,2,1,0:T(8,128)S(1)}, u32[]{:S(2)}, u32[]{:S(2)}) collective-permute-start(s32[1,4,8,256]{3,2,1,0:T(8,128)S(1)} %add_bitcast_fusion), channel_id=1, source_target_pairs={{0,6},{1,7},{2,4},{3,5},{4,2},{5,3},{6,0},{7,1},{8,14},{9,15},{10,... | collective-permute-start | bytes 98312 | tf_op jit(solution)/shard_map/ppermute | solution.py:522
  26.5 9.9 %collective-permute-start.7 = (s32[1,4,8,256]{3,2,1,0:T(8,128)S(1)}, s32[1,4,8,256]{3,2,1,0:T(8,128)S(1)}, u32[]{:S(2)}, u32[]{:S(2)}) collective-permute-start(s32[1,4,8,256]{3,2,1,0:T(8,128)S(1)} %add_bitcast_fusion), channel_id=1, source_target_pairs={{0,4},{1,3},{2,6},{3,1},{4,0},{5,7},{6,2},{7,5},{8,12},{9,11},{10,... | collective-permute-start | bytes 98312 | tf_op jit(solution)/shard_map/ppermute | solution.py:526
  28.0 8.4 %collective-permute-start.6 = (s32[1,4,8,256]{3,2,1,0:T(8,128)S(1)}, s32[1,4,8,256]{3,2,1,0:T(8,128)S(1)}, u32[]{:S(2)}, u32[]{:S(2)}) collective-permute-start(s32[1,4,8,256]{3,2,1,0:T(8,128)S(1)} %add_bitcast_fusion), channel_id=1, source_target_pairs={{0,2},{1,5},{2,0},{3,7},{4,6},{5,1},{6,4},{7,3},{8,10},{9,13},{10,... | collective-permute-start | bytes 98312 | tf_op jit(solution)/shard_map/ppermute | solution.py:526
  28.4 8.6 %collective-permute-start.10 = (bf16[2592,128]{1,0:T(8,128)(2,1)}, bf16[2592,128]{1,0:T(8,128)(2,1)}, u32[]{:S(2)}, u32[]{:S(2)}) collective-permute-start(bf16[2592,128]{1,0:T(8,128)(2,1)} %collective-permute-done.1), channel_id=1, source_target_pairs={{0,1},{1,0},{2,3},{3,2},{4,5},{5,4},{6,7},{7,6},{8,9},{9,8},{10,11... | collective-permute-start | bytes 1990664 | tf_op jit(solution)/shard_map/ppermute | solution.py:522
  34.9 2.6 %collective-permute-start.11 = (bf16[2592,128]{1,0:T(8,128)(2,1)}, bf16[2592,128]{1,0:T(8,128)(2,1)}, u32[]{:S(2)}, u32[]{:S(2)}) collective-permute-start(bf16[2592,128]{1,0:T(8,128)(2,1)} %collective-permute-done.2), channel_id=1, source_target_pairs={{0,1},{1,0},{2,3},{3,2},{4,5},{5,4},{6,7},{7,6},{8,9},{9,8},{10,11... | collective-permute-start | bytes 1990664 | tf_op jit(solution)/shard_map/ppermute | solution.py:522
  36.4 2.7 %copy-start = (s32[4,4,8,256]{3,2,1,0:T(8,128)}, s32[4,4,8,256]{3,2,1,0:T(8,128)S(1)}, u32[]{:S(2)}) copy-start(s32[4,4,8,256]{3,2,1,0:T(8,128)S(1)} %pad_add_fusion.refs_2_) | copy-start | bytes 393220
  36.4 2.7 %collective-permute-start.12 = (bf16[2592,128]{1,0:T(8,128)(2,1)}, bf16[2592,128]{1,0:T(8,128)(2,1)}, u32[]{:S(2)}, u32[]{:S(2)}) collective-permute-start(bf16[2592,128]{1,0:T(8,128)(2,1)} %collective-permute-done.5.refs_6_), channel_id=1, source_target_pairs={{0,1},{1,0},{2,3},{3,2},{4,5},{5,4},{6,7},{7,6},{8,9},{9,8},{10,11... | collective-permute-start | bytes 1990664 | tf_op jit(solution)/shard_map/ppermute | solution.py:522
  36.5 2.3 %collective-permute-start.9 = (s32[4,4,8,256]{3,2,1,0:T(8,128)S(1)}, s32[4,4,8,256]{3,2,1,0:T(8,128)S(1)}, u32[]{:S(2)}, u32[]{:S(2)}) collective-permute-start(s32[4,4,8,256]{3,2,1,0:T(8,128)S(1)} %pad_add_fusion.refs_2_), channel_id=1, source_target_pairs={{0,1},{1,0},{2,3},{3,2},{4,5},{5,4},{6,7},{7,6},{8,9},{9,8},{10,11... | collective-permute-start | bytes 393224 | tf_op jit(solution)/shard_map/ppermute | solution.py:522
  38.8 0.7 %copy-start.2 = (s32[4,4,8,256]{3,2,1,0:T(8,128)}, s32[4,4,8,256]{3,2,1,0:T(8,128)S(1)}, u32[]{:S(2)}) copy-start(s32[4,4,8,256]{3,2,1,0:T(8,128)S(1)} %collective-permute-done.9.refs_3_) | copy-start | bytes 393220

commit v17 on v16

--- a/solution.py
+++ b/solution.py
@@ -283,10 +283,7 @@
     sources = [ref.at[n] for ref, count in zip(refs, counts) for n in range(count)]
     refs = refs[len(counts):]
     *refs, gram_ref, blocks, gram_semaphores, block_semaphores = refs
-    if len(refs) > 1:
-        *columns_refs, out_ref, whole_ref, rest_ref = refs
-    else:
-        columns_refs, out_ref = [], refs[0]
+    out_ref, = refs
     step = pl.program_id(0)
     gram_copies = fetch_gram(gram_any, gram_ref, gram_semaphores, mirrors)
 
@@ -300,9 +297,6 @@
             copy.start()
         for n in range(1, len(sources)):
             fetch(n).start()
-        columns = [ref.at[n] for ref in columns_refs for n in range(ref.shape[0])]
-        if columns:
-            build_differences(columns, whole_ref, rest_ref, mirrors, samples)
 
     for n in range(len(sources)):
         @pl.when(step == n)
@@ -315,7 +309,7 @@
                 out_ref[0, q] = band_product(blocks.at[n], q, row_shape, block, surface_rows, gram_ref)
 
 
-def bands(gram_rows, sources, first, staged, row_shape, surface_rows, columns, pupil):
+def bands(gram_rows, sources, first, staged, row_shape, surface_rows):
     acts, own = gram_rows.shape
     mirrors, shard_rows, slots, samples = row_shape
     counts = [source.shape[0] for source in sources]
@@ -325,17 +319,6 @@
     out_shape = [jax.ShapeDtypeStruct((sum(counts), rows, samples, own), jnp.bfloat16)]
     out_specs = [pl.BlockSpec((1, rows, samples, own), lambda s: (s, 0, 0, 0))]
     arguments, in_specs = [gram_rows, *sources], [anywhere] * (1 + len(sources))
-    directions = sum(lines.shape[0] for lines in columns)
-    depth = mirrors * samples // WINDOW * WINDOW
-    rest = 2 * (mirrors * samples - depth)
-    if columns:
-        out_shape += [
-            jax.ShapeDtypeStruct((directions, 2, pupil // 2, depth), jnp.bfloat16),
-            jax.ShapeDtypeStruct((directions, pupil, rest), jnp.bfloat16),
-        ]
-        out_specs += [vmem] * 2
-    arguments += columns
-    in_specs += [vmem] * len(columns)
     return pl.pallas_call(
         functools.partial(bands_kernel, row_shape, surface_rows, first, counts, staged),
         grid=(sum(counts),),
@@ -389,11 +372,11 @@
 
 def decode_kernel(row_shape, surface_rows, own, staged, norm, counts, late, places, *refs):
     mirrors, shard_rows, slots, samples = row_shape
-    whole_ref, rest_ref, *refs = refs
+    columns_refs, refs = refs[:counts[3]], refs[counts[3]:]
     lines_refs, refs = refs[:counts[0]], refs[counts[0]:]
     late_refs, refs = refs[:counts[1]], refs[counts[1]:]
     ready_refs, refs = refs[:counts[2]], refs[counts[2]:]
-    (gram_any, out_ref, gram_ref, decoded, total, lines, foot_rows, scalars, *refs) = refs
+    (gram_any, out_ref, gram_ref, decoded, whole_ref, rest_ref, total, lines, foot_rows, scalars, *refs) = refs
     late_blocks, refs = refs[:counts[1]], refs[counts[1]:]
     gram_semaphores, ready_semaphores, late_semaphores, scalar_semaphore = refs
     group = pl.program_id(0)
@@ -433,6 +416,8 @@
         foot_rows[...] = row_place(feet // shard_rows, staged) * rows + feet % shard_rows
         to_scalars = pltpu.make_async_copy(foot_rows, scalars, scalar_semaphore.at[0])
         to_scalars.start()
+        columns = [ref.at[n] for ref in columns_refs for n in range(ref.shape[0])]
+        build_differences(columns, whole_ref, rest_ref, mirrors, samples)
         for copy in late_copies:
             copy.wait()
         for n in range(late):
@@ -481,17 +466,18 @@
         out_ref[:, :, tile * LANES:(tile + 1) * LANES] = value.astype(out_ref.dtype)
 
 
-def decode(differences, lines, places, late, ready, gram_rows, own, row_shape, surface_rows, pupil, norm, staged):
+def decode(columns, lines, places, late, ready, gram_rows, own, row_shape, surface_rows, pupil, norm, staged):
     mirrors, shard_rows, slots, samples = row_shape
     acts, padded = gram_rows.shape
-    directions = differences[0].shape[0]
+    directions = sum(line.shape[0] for line in columns)
+    depth = mirrors * samples // WINDOW * WINDOW
     blocks = surface_rows // shard_rows
     phases = LANES // math.gcd(pupil, LANES)
     width = surface_rows // 2 * pupil
     lanes = phases * pupil
     flops = 2 * padded * mirrors * samples * pupil * directions * surface_rows // 2
     vmem, anywhere = pl.BlockSpec(memory_space=pltpu.VMEM), pl.BlockSpec(memory_space=pl.ANY)
-    counts = (len(lines), len(late), len(ready))
+    counts = (len(lines), len(late), len(ready), len(columns))
     semaphores = [mirrors, blocks, max(len(late), 1), 1]
     held = -(-directions * (shard_rows // 2) // 8) * 8
     return pl.pallas_call(
@@ -500,11 +486,13 @@
         ),
         grid=(width // lanes,),
         out_shape=jax.ShapeDtypeStruct((own, directions, width), jnp.bfloat16),
-        in_specs=[vmem] * (2 + len(lines)) + [anywhere] * (len(late) + len(ready) + 1),
+        in_specs=[vmem] * (len(columns) + len(lines)) + [anywhere] * (len(late) + len(ready) + 1),
         out_specs=pl.BlockSpec((own, directions, lanes), lambda s: (0, 0, s)),
         scratch_shapes=[
             pltpu.VMEM((acts, padded), jnp.bfloat16),
             pltpu.VMEM((blocks * mirrors * shard_rows, samples, padded), jnp.bfloat16),
+            pltpu.VMEM((directions, 2, pupil // 2, depth), jnp.bfloat16),
+            pltpu.VMEM((directions, pupil, 2 * (mirrors * samples - depth)), jnp.bfloat16),
             pltpu.VMEM((lanes // LANES, own * directions, LANES), jnp.float32),
             pltpu.VMEM((blocks, held, LANES), jnp.int32),
             pltpu.VMEM((blocks, LANES), jnp.int32),
@@ -515,7 +503,7 @@
         compiler_params=pltpu.CompilerParams(vmem_limit_bytes=VMEM_BYTES),
         cost_estimate=pl.CostEstimate(flops=flops, bytes_accessed=2 * own * directions * width, transcendentals=0),
         name="decode",
-    )(*differences, *lines, *late, *ready, gram_rows)
+    )(*columns, *lines, *late, *ready, gram_rows)
 
 
 def swap(block, axis, distance):
@@ -544,9 +532,9 @@
         every = lax.all_gather(packed, "row")
         lines = lax.all_gather(lax.all_gather(lines, "dir"), "row")
         gram_rows, _ = gram(actuator_codes, pokes, packed, own, row_shape, surface_rows)
-        ready, *differences = bands(gram_rows, [every], 0, staged, row_shape, surface_rows, [lines[0]], pupil)
+        ready, = bands(gram_rows, [every], 0, staged, row_shape, surface_rows)
         return decode(
-            differences, [lines], list(range(devices)), [], [ready], gram_rows, own, row_shape, surface_rows, pupil,
+            [lines[0]], [lines], list(range(devices)), [], [ready], gram_rows, own, row_shape, surface_rows, pupil,
             norm, staged,
         )
 
@@ -557,14 +545,14 @@
     while distance < directions:
         lines.append(swap(jnp.concatenate(lines, axis=0), "dir", distance))
         distance *= 2
-    held = jnp.concatenate(lines, axis=0)[None]
+    held = jnp.concatenate(lines, axis=0)[None, :, :, :LANES]
     gram_rows, own_rows = gram(actuator_codes, pokes, packed, own, row_shape, surface_rows)
     gram_rows, first, second, held = lax.optimization_barrier((gram_rows, first, second, held))
     diagonal = turn(first, 4, 2)
     first_sibling = swap(first, "row", 1)
     mine = [held, turn(held, 2, 4), turn(held, 4, 2), swap(held, "row", 6)]
     sources = [source[None] for source in (sibling, first, second)]
-    near, *differences = bands(gram_rows, sources, 1, staged, row_shape, surface_rows, lines, pupil)
+    near, = bands(gram_rows, sources, 1, staged, row_shape, surface_rows)
     near, second = lax.optimization_barrier((near, second))
     second_sibling = swap(second, "row", 1)
     mine = jnp.concatenate(mine, axis=0)
@@ -572,7 +560,7 @@
     theirs = swap(mine, "row", 1)
     late = [first_sibling, second_sibling, diagonal, swap(diagonal, "row", 1)]
     return decode(
-        differences, [mine, theirs], [0, 2, 3, 6, 1, 4, 5, 7], late, [own_rows, near], gram_rows, own, row_shape,
+        lines, [mine, theirs], [0, 2, 3, 6, 1, 4, 5, 7], late, [own_rows, near], gram_rows, own, row_shape,
         surface_rows, pupil, norm, staged,
     )
 

time: 55.9 us -> 53.9 us (0.964)
  Pallas kernels: 37.3 us -> 35 us
  starting transfers between devices: 14.1 us -> 14.7 us
    pallas_call x1, Pallas kernels: 6.54 us -> 5.29 us  [bands(): pl.pallas_call(functools.partial(bands_kernel, row_shape, surface_rows, f...]
    pallas_call x1, Pallas kernels: 16.2 us -> 15.1 us  [decode(): pl.pallas_call(functools.partial(decode_kernel, row_shape, surface_rows,...]
    ppermute x8, starting transfers between devices: 8.3 us -> 8.9 us  [swap(): lax.ppermute(block, axis, [(i, i ^ distance) for i in range(lax.axis_size...]
  transfers between devices with their start and end apart: 13 -> 13, of which waited for: 4 -> 4; matrix products, arithmetic and copies ran while one was open for 1% -> 1% of each run, Pallas kernels for 33% -> 32%
where the time goes in v17:
time: 53.9 us; the launch traced here: 53.7 us
  Pallas kernels  35 us (65%)
  starting transfers between devices  14.7 us (27%)
  waiting for transfers between devices  2.89 us (5%)
  other arithmetic  0.71 us (1%)
    pallas_call x1, Pallas kernels, decode(): pl.pallas_call(functools.partial(decode_kernel, row_shape, surface_rows,...  15.1 us
    pallas_call x1, Pallas kernels, gram(): pl.pallas_call(functools.partial(gram_kernel, row_shape, surface_rows), g...  12.1 us
    ppermute x8, starting transfers between devices, swap(): lax.ppermute(block, axis, [(i, i ^ distance) for i in range(lax.axis_size...  8.9 us
    ppermute x5, starting transfers between devices, turn(): lax.ppermute(block, 'row', [(i, i ^ (odd if i % 2 else even)) for i in ra...  5.78 us
    pallas_call x1, Pallas kernels, bands(): pl.pallas_call(functools.partial(bands_kernel, row_shape, surface_rows, f...  5.29 us
    pallas_call x1, Pallas kernels, pack(): pl.pallas_call(pack_kernel, out_shape=[jax.ShapeDtypeStruct((mirrors * ro...  2.57 us
    ppermute x8, waiting for transfers between devices, swap(): lax.ppermute(block, axis, [(i, i ^ distance) for i in range(lax.axis_size...  2.04 us
  transfers between devices with their start and end apart: 13, of which 4 were waited for; matrix products, arithmetic and copies ran while one was open for 1% of the time, Pallas kernels for 32%

profile of v17, /device:TPU:0, one launch (start us, length us, event | category | flops | bytes accessed | tf_op | source)
XLA Modules:
  0.0 53.7 jit_solution(11764299916526187233)
XLA Ops:
  0.0 2.6 %pack_influence.1 = (bf16[2592,128]{1,0:T(8,128)(2,1)}, s32[8,256]{1,0:T(8,128)}) custom-call(bf16[3,4,144,192]{3,2,1,0:T(8,128)(2,1)} %bitcast.11, s32[3,1,4]{2,1,0:T(1,128)} %bitcast.15, s32[3,1,160]{2,1,0:T(1,128)} %bitcast.14, s32[1,2,80]{2,1,0:T(2,128)} %valid_ref.1), custom_call_target="tpu_custom_call" | custom-call | bytes 995328 | tf_op jit(solution)/shard_map/pack_influence/pallas_call | solution.py:65
  2.6 3.0 %collective-permute-start = (s32[8,256]{1,0:T(8,128)}, s32[8,256]{1,0:T(8,128)S(1)}, u32[]{:S(2)}, u32[]{:S(2)}) collective-permute-start(s32[8,256]{1,0:T(8,128)} %get-tuple-element.20), channel_id=1, source_target_pairs={{0,8},{8,0},{16,24},{24,16},{1,9},{9,1},{17,25},{25,17},{2,10},{10... | collective-permute-start | bytes 24584 | tf_op jit(solution)/shard_map/ppermute | solution.py:510
  5.6 0.0 collective-permute-start.4
  5.6 1.5 %collective-permute-start.3 = (bf16[2592,128]{1,0:T(8,128)(2,1)}, bf16[2592,128]{1,0:T(8,128)(2,1)}, u32[]{:S(2)}, u32[]{:S(2)}) collective-permute-start(bf16[2592,128]{1,0:T(8,128)(2,1)} %get-tuple-element.23.packed_ref), channel_id=1, source_target_pairs={{0,4},{1,3},{2,6},{3,1},{4,0},{5,7},{6,2},{7,5},{8,12},{9,11},{10,... | collective-permute-start | bytes 1990664 | tf_op jit(solution)/shard_map/ppermute | solution.py:514
  7.1 1.5 %collective-permute-start.2 = (bf16[2592,128]{1,0:T(8,128)(2,1)}, bf16[2592,128]{1,0:T(8,128)(2,1)}, u32[]{:S(2)}, u32[]{:S(2)}) collective-permute-start(bf16[2592,128]{1,0:T(8,128)(2,1)} %get-tuple-element.23.packed_ref), channel_id=1, source_target_pairs={{0,2},{1,5},{2,0},{3,7},{4,6},{5,1},{6,4},{7,3},{8,10},{9,13},{10,... | collective-permute-start | bytes 1990664 | tf_op jit(solution)/shard_map/ppermute | solution.py:514
  8.6 0.0 collective-permute-done
  8.6 0.7 %pad_add_fusion.2.refs_0_ = s32[2,8,256]{2,1,0:T(8,128)S(1)} fusion(s32[1,8,256]{2,1,0:T(8,128)S(1)} %bitcast.13, s32[1,8,256]{2,1,0:T(8,128)} %bitcast.12), kind=kLoop, calls=%fused_computation.3 | loop fusion | flops 4096 | bytes 32768 | tf_op jit(solution)/shard_map/stack | solution.py:543
  9.3 0.0 copy-start.1
  9.3 2.6 %collective-permute-start.1 = (s32[2,8,256]{2,1,0:T(8,128)S(1)}, s32[2,8,256]{2,1,0:T(8,128)S(1)}, u32[]{:S(2)}, u32[]{:S(2)}) collective-permute-start(s32[2,8,256]{2,1,0:T(8,128)S(1)} %pad_add_fusion.2.refs_0_), channel_id=1, source_target_pairs={{0,16},{8,24},{16,0},{24,8},{1,17},{9,25},{17,1},{25,9},{2,18},{10... | collective-permute-start | bytes 49160 | tf_op jit(solution)/shard_map/ppermute | solution.py:510
  11.9 12.1 %gram_rows.1 = (bf16[6912,224]{1,0:T(8,128)(2,1)}, bf16[1,12,192,224]{3,2,1,0:T(8,128)(2,1)}) custom-call(s32[3,48,48]{2,1,0:T(8,128)} %table_ref.1, s32[16,128]{1,0:T(8,128)} %bitcast.16, bf16[2592,128]{1,0:T(8,128)(2,1)} %get-tuple-element.23.packed_ref), custom_call_target="tpu_custom_call" | custom-call | flops 6341787648 | bytes 3096576 | tf_op jit(solution)/shard_map/gram_rows/pallas_call | solution.py:194
  24.0 0.0 collective-permute-done.1.refs_1_
  24.0 0.0 copy-done.1
  24.0 0.0 copy-start.3
  24.0 0.0 collective-permute-done.3
  24.0 0.0 collective-permute-done.2
  24.0 0.9 %collective-permute-start.5 = (bf16[2592,128]{1,0:T(8,128)(2,1)}, bf16[2592,128]{1,0:T(8,128)(2,1)}, u32[]{:S(2)}, u32[]{:S(2)}) collective-permute-start(bf16[2592,128]{1,0:T(8,128)(2,1)} %collective-permute-done.2), channel_id=1, source_target_pairs={{0,4},{1,3},{2,6},{3,1},{4,0},{5,7},{6,2},{7,5},{8,12},{9,11},{10,... | collective-permute-start | bytes 1990664 | tf_op jit(solution)/shard_map/ppermute | solution.py:514
  24.9 1.6 %collective-permute-start.8 = (s32[1,4,8,128]{3,2,1,0:T(8,128)S(1)}, s32[1,4,8,128]{3,2,1,0:T(8,128)S(1)}, u32[]{:S(2)}, u32[]{:S(2)}) collective-permute-start(s32[1,4,8,128]{3,2,1,0:T(8,128)S(1)} %fusion), channel_id=1, source_target_pairs={{0,6},{1,7},{2,4},{3,5},{4,2},{5,3},{6,0},{7,1},{8,14},{9,15},{10,... | collective-permute-start | bytes 49160 | tf_op jit(solution)/shard_map/ppermute | solution.py:510
  26.5 1.5 %collective-permute-start.7 = (s32[1,4,8,128]{3,2,1,0:T(8,128)S(1)}, s32[1,4,8,128]{3,2,1,0:T(8,128)S(1)}, u32[]{:S(2)}, u32[]{:S(2)}) collective-permute-start(s32[1,4,8,128]{3,2,1,0:T(8,128)S(1)} %fusion), channel_id=1, source_target_pairs={{0,4},{1,3},{2,6},{3,1},{4,0},{5,7},{6,2},{7,5},{8,12},{9,11},{10,... | collective-permute-start | bytes 49160 | tf_op jit(solution)/shard_map/ppermute | solution.py:514
  28.0 0.4 collective-permute-start.6
  28.4 0.0 collective-permute-done.4
  28.4 0.0 collective-permute-start.10
  28.4 5.3 %bands.1.refs_9_ = bf16[3,12,192,224]{3,2,1,0:T(8,128)(2,1)} custom-call(bf16[6912,224]{1,0:T(8,128)(2,1)} %get-tuple-element.25.gram_any.refs_10_, bf16[1,2592,128]{2,1,0:T(8,128)(2,1)} %bitcast.7.refs_0_, bf16[1,2592,128]{2,1,0:T(8,128)(2,1)} %bitcast.8.refs_1_, bf16[1,2592,128]{2,1,0:T(8,128)(2,1)} %bitcast.9.refs_2_), custom_call_target="tpu_custom_call" | custom-call | flops 792723456 | bytes 4128768 | tf_op jit(solution)/shard_map/bands/pallas_call | solution.py:322
  33.7 0.0 copy-done.3
  33.7 0.0 collective-permute-done.8
  33.7 1.1 %collective-permute-start.11 = (bf16[2592,128]{1,0:T(8,128)(2,1)}, bf16[2592,128]{1,0:T(8,128)(2,1)}, u32[]{:S(2)}, u32[]{:S(2)}) collective-permute-start(bf16[2592,128]{1,0:T(8,128)(2,1)} %collective-permute-done.3), channel_id=1, source_target_pairs={{0,1},{1,0},{2,3},{3,2},{4,5},{5,4},{6,7},{7,6},{8,9},{9,8},{10,11... | collective-permute-start | bytes 1990664 | tf_op jit(solution)/shard_map/ppermute | solution.py:510
  34.8 0.8 %collective-permute-done.7 = s32[1,4,8,128]{3,2,1,0:T(8,128)S(1)} collective-permute-done((s32[1,4,8,128]{3,2,1,0:T(8,128)S(1)}, s32[1,4,8,128]{3,2,1,0:T(8,128)S(1)}, u32[]{:S(2)}, u32[]{:S(2)}) %collective-permute-start.7) | collective-permute-done | bytes 16416 | tf_op jit(solution)/shard_map/ppermute | solution.py:514
  35.7 0.0 collective-permute-done.6
  35.7 0.0 copy-start
  35.7 0.0 collective-permute-done.5.refs_6_
  35.7 0.1 collective-permute-start.12
  35.8 0.5 collective-permute-start.9
  36.3 0.0 collective-permute-done.10.refs_4_
  36.3 0.6 %collective-permute-done.11.refs_5_ = bf16[2592,128]{1,0:T(8,128)(2,1)} collective-permute-done((bf16[2592,128]{1,0:T(8,128)(2,1)}, bf16[2592,128]{1,0:T(8,128)(2,1)}, u32[]{:S(2)}, u32[]{:S(2)}) %collective-permute-start.11) | collective-permute-done | bytes 663584 | tf_op jit(solution)/shard_map/ppermute | solution.py:510
  36.9 1.0 %collective-permute-done.9.refs_3_ = s32[4,4,8,128]{3,2,1,0:T(8,128)S(1)} collective-permute-done((s32[4,4,8,128]{3,2,1,0:T(8,128)S(1)}, s32[4,4,8,128]{3,2,1,0:T(8,128)S(1)}, u32[]{:S(2)}, u32[]{:S(2)}) %collective-permute-start.9) | collective-permute-done | bytes 65568 | tf_op jit(solution)/shard_map/ppermute | solution.py:510
  37.9 0.0 copy-start.2
  37.9 0.4 collective-permute-done.12.refs_7_
  38.3 0.0 copy-done
  38.3 0.2 copy-done.2
  38.5 15.1 %decode.1 = bf16[216,4,2560]{2,1,0:T(4,128)(2,1)} custom-call(s32[2,8,256]{2,1,0:T(8,128)} %copy-done.1, s32[2,8,256]{2,1,0:T(8,128)} %copy-done.3, s32[4,4,8,128]{3,2,1,0:T(8,128)} %copy-done, s32[4,4,8,128]{3,2,1,0:T(8,128)} %copy-done.2, bf16[2592,128]{1,0:T(8,128)(2,1)} %collective-permute-done.10.refs_4_, ...), custom_call_target="tpu_custom_call" | custom-call | flops 2642411520 | bytes 4423680 | tf_op jit(solution)/shard_map/decode/pallas_call | solution.py:483
  (2 shorter events, 0.0 us)
Async XLA Ops:
  2.6 6.0 %collective-permute-start = (s32[8,256]{1,0:T(8,128)}, s32[8,256]{1,0:T(8,128)S(1)}, u32[]{:S(2)}, u32[]{:S(2)}) collective-permute-start(s32[8,256]{1,0:T(8,128)} %get-tuple-element.20), channel_id=1, source_target_pairs={{0,8},{8,0},{16,24},{24,16},{1,9},{9,1},{17,25},{25,17},{2,10},{10... | collective-permute-start | bytes 24584 | tf_op jit(solution)/shard_map/ppermute | solution.py:510
  5.6 22.8 %collective-permute-start.4 = (bf16[2592,128]{1,0:T(8,128)(2,1)}, bf16[2592,128]{1,0:T(8,128)(2,1)}, u32[]{:S(2)}, u32[]{:S(2)}) collective-permute-start(bf16[2592,128]{1,0:T(8,128)(2,1)} %get-tuple-element.23.packed_ref), channel_id=1, source_target_pairs={{0,1},{1,0},{2,3},{3,2},{4,5},{5,4},{6,7},{7,6},{8,9},{9,8},{10,11... | collective-permute-start | bytes 1990664 | tf_op jit(solution)/shard_map/ppermute | solution.py:510
  5.6 18.4 %collective-permute-start.3 = (bf16[2592,128]{1,0:T(8,128)(2,1)}, bf16[2592,128]{1,0:T(8,128)(2,1)}, u32[]{:S(2)}, u32[]{:S(2)}) collective-permute-start(bf16[2592,128]{1,0:T(8,128)(2,1)} %get-tuple-element.23.packed_ref), channel_id=1, source_target_pairs={{0,4},{1,3},{2,6},{3,1},{4,0},{5,7},{6,2},{7,5},{8,12},{9,11},{10,... | collective-permute-start | bytes 1990664 | tf_op jit(solution)/shard_map/ppermute | solution.py:514
  7.1 16.9 %collective-permute-start.2 = (bf16[2592,128]{1,0:T(8,128)(2,1)}, bf16[2592,128]{1,0:T(8,128)(2,1)}, u32[]{:S(2)}, u32[]{:S(2)}) collective-permute-start(bf16[2592,128]{1,0:T(8,128)(2,1)} %get-tuple-element.23.packed_ref), channel_id=1, source_target_pairs={{0,2},{1,5},{2,0},{3,7},{4,6},{5,1},{6,4},{7,3},{8,10},{9,13},{10,... | collective-permute-start | bytes 1990664 | tf_op jit(solution)/shard_map/ppermute | solution.py:514
  9.3 14.7 %copy-start.1 = (s32[2,8,256]{2,1,0:T(8,128)}, s32[2,8,256]{2,1,0:T(8,128)S(1)}, u32[]{:S(2)}) copy-start(s32[2,8,256]{2,1,0:T(8,128)S(1)} %pad_add_fusion.2.refs_0_) | copy-start | bytes 49156
  9.3 14.7 %collective-permute-start.1 = (s32[2,8,256]{2,1,0:T(8,128)S(1)}, s32[2,8,256]{2,1,0:T(8,128)S(1)}, u32[]{:S(2)}, u32[]{:S(2)}) collective-permute-start(s32[2,8,256]{2,1,0:T(8,128)S(1)} %pad_add_fusion.2.refs_0_), channel_id=1, source_target_pairs={{0,16},{8,24},{16,0},{24,8},{1,17},{9,25},{17,1},{25,9},{2,18},{10... | collective-permute-start | bytes 49160 | tf_op jit(solution)/shard_map/ppermute | solution.py:510
  24.0 9.7 %copy-start.3 = (s32[2,8,256]{2,1,0:T(8,128)}, s32[2,8,256]{2,1,0:T(8,128)S(1)}, u32[]{:S(2)}) copy-start(s32[2,8,256]{2,1,0:T(8,128)S(1)} %collective-permute-done.1.refs_1_) | copy-start | bytes 49156
  24.0 11.7 %collective-permute-start.5 = (bf16[2592,128]{1,0:T(8,128)(2,1)}, bf16[2592,128]{1,0:T(8,128)(2,1)}, u32[]{:S(2)}, u32[]{:S(2)}) collective-permute-start(bf16[2592,128]{1,0:T(8,128)(2,1)} %collective-permute-done.2), channel_id=1, source_target_pairs={{0,4},{1,3},{2,6},{3,1},{4,0},{5,7},{6,2},{7,5},{8,12},{9,11},{10,... | collective-permute-start | bytes 1990664 | tf_op jit(solution)/shard_map/ppermute | solution.py:514
  24.9 8.8 %collective-permute-start.8 = (s32[1,4,8,128]{3,2,1,0:T(8,128)S(1)}, s32[1,4,8,128]{3,2,1,0:T(8,128)S(1)}, u32[]{:S(2)}, u32[]{:S(2)}) collective-permute-start(s32[1,4,8,128]{3,2,1,0:T(8,128)S(1)} %fusion), channel_id=1, source_target_pairs={{0,6},{1,7},{2,4},{3,5},{4,2},{5,3},{6,0},{7,1},{8,14},{9,15},{10,... | collective-permute-start | bytes 49160 | tf_op jit(solution)/shard_map/ppermute | solution.py:510
  26.5 9.2 %collective-permute-start.7 = (s32[1,4,8,128]{3,2,1,0:T(8,128)S(1)}, s32[1,4,8,128]{3,2,1,0:T(8,128)S(1)}, u32[]{:S(2)}, u32[]{:S(2)}) collective-permute-start(s32[1,4,8,128]{3,2,1,0:T(8,128)S(1)} %fusion), channel_id=1, source_target_pairs={{0,4},{1,3},{2,6},{3,1},{4,0},{5,7},{6,2},{7,5},{8,12},{9,11},{10,... | collective-permute-start | bytes 49160 | tf_op jit(solution)/shard_map/ppermute | solution.py:514
  28.0 7.7 %collective-permute-start.6 = (s32[1,4,8,128]{3,2,1,0:T(8,128)S(1)}, s32[1,4,8,128]{3,2,1,0:T(8,128)S(1)}, u32[]{:S(2)}, u32[]{:S(2)}) collective-permute-start(s32[1,4,8,128]{3,2,1,0:T(8,128)S(1)} %fusion), channel_id=1, source_target_pairs={{0,2},{1,5},{2,0},{3,7},{4,6},{5,1},{6,4},{7,3},{8,10},{9,13},{10,... | collective-permute-start | bytes 49160 | tf_op jit(solution)/shard_map/ppermute | solution.py:514
  28.4 7.9 %collective-permute-start.10 = (bf16[2592,128]{1,0:T(8,128)(2,1)}, bf16[2592,128]{1,0:T(8,128)(2,1)}, u32[]{:S(2)}, u32[]{:S(2)}) collective-permute-start(bf16[2592,128]{1,0:T(8,128)(2,1)} %collective-permute-done.2), channel_id=1, source_target_pairs={{0,1},{1,0},{2,3},{3,2},{4,5},{5,4},{6,7},{7,6},{8,9},{9,8},{10,11... | collective-permute-start | bytes 1990664 | tf_op jit(solution)/shard_map/ppermute | solution.py:510
  33.7 3.2 %collective-permute-start.11 = (bf16[2592,128]{1,0:T(8,128)(2,1)}, bf16[2592,128]{1,0:T(8,128)(2,1)}, u32[]{:S(2)}, u32[]{:S(2)}) collective-permute-start(bf16[2592,128]{1,0:T(8,128)(2,1)} %collective-permute-done.3), channel_id=1, source_target_pairs={{0,1},{1,0},{2,3},{3,2},{4,5},{5,4},{6,7},{7,6},{8,9},{9,8},{10,11... | collective-permute-start | bytes 1990664 | tf_op jit(solution)/shard_map/ppermute | solution.py:510
  35.7 2.6 %copy-start = (s32[4,4,8,128]{3,2,1,0:T(8,128)}, s32[4,4,8,128]{3,2,1,0:T(8,128)S(1)}, u32[]{:S(2)}) copy-start(s32[4,4,8,128]{3,2,1,0:T(8,128)S(1)} %pad_add_fusion.refs_2_) | copy-start | bytes 196612
  35.7 2.6 %collective-permute-start.12 = (bf16[2592,128]{1,0:T(8,128)(2,1)}, bf16[2592,128]{1,0:T(8,128)(2,1)}, u32[]{:S(2)}, u32[]{:S(2)}) collective-permute-start(bf16[2592,128]{1,0:T(8,128)(2,1)} %collective-permute-done.5.refs_6_), channel_id=1, source_target_pairs={{0,1},{1,0},{2,3},{3,2},{4,5},{5,4},{6,7},{7,6},{8,9},{9,8},{10,11... | collective-permute-start | bytes 1990664 | tf_op jit(solution)/shard_map/ppermute | solution.py:510
  35.8 2.1 %collective-permute-start.9 = (s32[4,4,8,128]{3,2,1,0:T(8,128)S(1)}, s32[4,4,8,128]{3,2,1,0:T(8,128)S(1)}, u32[]{:S(2)}, u32[]{:S(2)}) collective-permute-start(s32[4,4,8,128]{3,2,1,0:T(8,128)S(1)} %pad_add_fusion.refs_2_), channel_id=1, source_target_pairs={{0,1},{1,0},{2,3},{3,2},{4,5},{5,4},{6,7},{7,6},{8,9},{9,8},{10,11... | collective-permute-start | bytes 196616 | tf_op jit(solution)/shard_map/ppermute | solution.py:510
  37.9 0.6 %copy-start.2 = (s32[4,4,8,128]{3,2,1,0:T(8,128)}, s32[4,4,8,128]{3,2,1,0:T(8,128)S(1)}, u32[]{:S(2)}) copy-start(s32[4,4,8,128]{3,2,1,0:T(8,128)S(1)} %collective-permute-done.9.refs_3_) | copy-start | bytes 196612

commit v18 on v17

--- a/solution.py
+++ b/solution.py
@@ -539,9 +539,9 @@
         )
 
     first, second = turn(packed, 2, 4), turn(packed, 4, 2)
-    sibling = swap(packed, "row", 1)
     lines, distance = [jnp.stack([lines, swap(lines, "dir", 1)])], 2
-    lines[0], pokes = lax.optimization_barrier((lines[0], pokes))
+    lines[0], pokes, again = lax.optimization_barrier((lines[0], pokes, packed))
+    sibling = swap(again, "row", 1)
     while distance < directions:
         lines.append(swap(jnp.concatenate(lines, axis=0), "dir", distance))
         distance *= 2
@@ -549,13 +549,14 @@
     gram_rows, own_rows = gram(actuator_codes, pokes, packed, own, row_shape, surface_rows)
     gram_rows, first, second, held = lax.optimization_barrier((gram_rows, first, second, held))
     diagonal = turn(first, 4, 2)
-    first_sibling = swap(first, "row", 1)
-    mine = [held, turn(held, 2, 4), turn(held, 4, 2), swap(held, "row", 6)]
+    first_sibling, second_sibling = swap(first, "row", 1), swap(second, "row", 1)
+    mine = jnp.concatenate([held, turn(held, 2, 4)], axis=0)
     sources = [source[None] for source in (sibling, first, second)]
     near, = bands(gram_rows, sources, 1, staged, row_shape, surface_rows)
-    near, second = lax.optimization_barrier((near, second))
-    second_sibling = swap(second, "row", 1)
-    mine = jnp.concatenate(mine, axis=0)
+    near, mine, first_sibling, second_sibling = lax.optimization_barrier(
+        (near, mine, first_sibling, second_sibling)
+    )
+    mine = jnp.concatenate([mine, turn(mine, 4, 2)], axis=0)
     near, diagonal, mine = lax.optimization_barrier((near, diagonal, mine))
     theirs = swap(mine, "row", 1)
     late = [first_sibling, second_sibling, diagonal, swap(diagonal, "row", 1)]

time: 53.9 us -> 54.5 us (1.011)
  waiting for transfers between devices: 2.89 us -> 5.46 us
  starting transfers between devices: 14.7 us -> 12.7 us
    ppermute x5, waiting for transfers between devices: 0.85 us -> 3.42 us  [turn(): lax.ppermute(block, 'row', [(i, i ^ (odd if i % 2 else even)) for i in ra...]
    ppermute x8 -> x7, starting transfers between devices: 8.9 us -> 6.83 us  [swap(): lax.ppermute(block, axis, [(i, i ^ distance) for i in range(lax.axis_size...]
    ppermute x8 -> x7, waiting for transfers between devices: 2.04 us -> 2.05 us  [swap(): lax.ppermute(block, axis, [(i, i ^ distance) for i in range(lax.axis_size...]
  transfers between devices with their start and end apart: 13 -> 12, of which waited for: 4 -> 3; matrix products, arithmetic and copies ran while one was open for 1% -> 1% of each run, Pallas kernels for 32% -> 32%
where the time goes in v18:
time: 54.5 us; the launch traced here: 54.3 us
  Pallas kernels  35 us (64%)
  starting transfers between devices  12.7 us (23%)
  waiting for transfers between devices  5.46 us (10%)
  other arithmetic  0.71 us (1%)
    pallas_call x1, Pallas kernels, decode(): pl.pallas_call(functools.partial(decode_kernel, row_shape, surface_rows,...  15.1 us
    pallas_call x1, Pallas kernels, gram(): pl.pallas_call(functools.partial(gram_kernel, row_shape, surface_rows), g...  12.1 us
    ppermute x7, starting transfers between devices, swap(): lax.ppermute(block, axis, [(i, i ^ distance) for i in range(lax.axis_size...  6.83 us
    ppermute x5, starting transfers between devices, turn(): lax.ppermute(block, 'row', [(i, i ^ (odd if i % 2 else even)) for i in ra...  5.87 us
    pallas_call x1, Pallas kernels, bands(): pl.pallas_call(functools.partial(bands_kernel, row_shape, surface_rows, f...  5.29 us
    ppermute x5, waiting for transfers between devices, turn(): lax.ppermute(block, 'row', [(i, i ^ (odd if i % 2 else even)) for i in ra...  3.42 us
    pallas_call x1, Pallas kernels, pack(): pl.pallas_call(pack_kernel, out_shape=[jax.ShapeDtypeStruct((mirrors * ro...  2.57 us
    ppermute x7, waiting for transfers between devices, swap(): lax.ppermute(block, axis, [(i, i ^ distance) for i in range(lax.axis_size...  2.05 us
  transfers between devices with their start and end apart: 12, of which 3 were waited for; matrix products, arithmetic and copies ran while one was open for 1% of the time, Pallas kernels for 32%

profile of v18, /device:TPU:0, one launch (start us, length us, event | category | flops | bytes accessed | tf_op | source)
XLA Modules:
  0.0 54.3 jit_solution(2104234759295566339)
XLA Ops:
  0.0 2.6 %pack_influence.1 = (bf16[2592,128]{1,0:T(8,128)(2,1)}, s32[8,256]{1,0:T(8,128)}) custom-call(bf16[3,4,144,192]{3,2,1,0:T(8,128)(2,1)} %bitcast.11, s32[3,1,4]{2,1,0:T(1,128)} %bitcast.15, s32[3,1,160]{2,1,0:T(1,128)} %bitcast.14, s32[1,2,80]{2,1,0:T(2,128)} %valid_ref.1), custom_call_target="tpu_custom_call" | custom-call | bytes 995328 | tf_op jit(solution)/shard_map/pack_influence/pallas_call | solution.py:65
  2.6 3.0 %collective-permute-start = (s32[8,256]{1,0:T(8,128)}, s32[8,256]{1,0:T(8,128)S(1)}, u32[]{:S(2)}, u32[]{:S(2)}) collective-permute-start(s32[8,256]{1,0:T(8,128)} %get-tuple-element.23), channel_id=1, source_target_pairs={{0,8},{8,0},{16,24},{24,16},{1,9},{9,1},{17,25},{25,17},{2,10},{10... | collective-permute-start | bytes 24584 | tf_op jit(solution)/shard_map/ppermute | solution.py:510
  5.6 1.5 %collective-permute-start.3 = (bf16[2592,128]{1,0:T(8,128)(2,1)}, bf16[2592,128]{1,0:T(8,128)(2,1)}, u32[]{:S(2)}, u32[]{:S(2)}) collective-permute-start(bf16[2592,128]{1,0:T(8,128)(2,1)} %get-tuple-element.29.packed_ref), channel_id=1, source_target_pairs={{0,4},{1,3},{2,6},{3,1},{4,0},{5,7},{6,2},{7,5},{8,12},{9,11},{10,... | collective-permute-start | bytes 1990664 | tf_op jit(solution)/shard_map/ppermute | solution.py:514
  7.1 1.5 %collective-permute-start.2 = (bf16[2592,128]{1,0:T(8,128)(2,1)}, bf16[2592,128]{1,0:T(8,128)(2,1)}, u32[]{:S(2)}, u32[]{:S(2)}) collective-permute-start(bf16[2592,128]{1,0:T(8,128)(2,1)} %get-tuple-element.29.packed_ref), channel_id=1, source_target_pairs={{0,2},{1,5},{2,0},{3,7},{4,6},{5,1},{6,4},{7,3},{8,10},{9,13},{10,... | collective-permute-start | bytes 1990664 | tf_op jit(solution)/shard_map/ppermute | solution.py:514
  8.6 0.0 collective-permute-done
  8.6 0.7 %pad_add_fusion.3.refs_0_ = s32[2,8,256]{2,1,0:T(8,128)S(1)} fusion(s32[1,8,256]{2,1,0:T(8,128)S(1)} %bitcast.13, s32[1,8,256]{2,1,0:T(8,128)} %bitcast.12), kind=kLoop, calls=%fused_computation.4 | loop fusion | flops 4096 | bytes 32768 | tf_op jit(solution)/shard_map/stack | solution.py:542
  9.3 0.0 copy-start.1
  9.3 2.6 %collective-permute-start.1 = (s32[2,8,256]{2,1,0:T(8,128)S(1)}, s32[2,8,256]{2,1,0:T(8,128)S(1)}, u32[]{:S(2)}, u32[]{:S(2)}) collective-permute-start(s32[2,8,256]{2,1,0:T(8,128)S(1)} %pad_add_fusion.3.refs_0_), channel_id=1, source_target_pairs={{0,16},{8,24},{16,0},{24,8},{1,17},{9,25},{17,1},{25,9},{2,18},{10... | collective-permute-start | bytes 49160 | tf_op jit(solution)/shard_map/ppermute | solution.py:510
  11.9 0.0 collective-permute-start.4
  11.9 12.1 %gram_rows.1 = (bf16[6912,224]{1,0:T(8,128)(2,1)}, bf16[1,12,192,224]{3,2,1,0:T(8,128)(2,1)}) custom-call(s32[3,48,48]{2,1,0:T(8,128)} %table_ref.1, s32[16,128]{1,0:T(8,128)} %bitcast.16, bf16[2592,128]{1,0:T(8,128)(2,1)} %get-tuple-element.29.packed_ref), custom_call_target="tpu_custom_call" | custom-call | flops 6341787648 | bytes 3096576 | tf_op jit(solution)/shard_map/gram_rows/pallas_call | solution.py:194
  24.0 0.0 collective-permute-done.1.refs_1_
  24.0 0.0 copy-done.1
  24.0 0.0 copy-start.3
  24.0 0.0 collective-permute-done.3
  24.0 0.0 collective-permute-done.2
  24.0 0.6 %collective-permute-start.7 = (bf16[2592,128]{1,0:T(8,128)(2,1)}, bf16[2592,128]{1,0:T(8,128)(2,1)}, u32[]{:S(2)}, u32[]{:S(2)}) collective-permute-start(bf16[2592,128]{1,0:T(8,128)(2,1)} %collective-permute-done.3), channel_id=1, source_target_pairs={{0,1},{1,0},{2,3},{3,2},{4,5},{5,4},{6,7},{7,6},{8,9},{9,8},{10,11... | collective-permute-start | bytes 1990664 | tf_op jit(solution)/shard_map/ppermute | solution.py:510
  24.6 0.1 collective-permute-start.6
  24.7 0.8 %collective-permute-start.8 = (bf16[2592,128]{1,0:T(8,128)(2,1)}, bf16[2592,128]{1,0:T(8,128)(2,1)}, u32[]{:S(2)}, u32[]{:S(2)}) collective-permute-start(bf16[2592,128]{1,0:T(8,128)(2,1)} %collective-permute-done.2), channel_id=1, source_target_pairs={{0,4},{1,3},{2,6},{3,1},{4,0},{5,7},{6,2},{7,5},{8,12},{9,11},{10,... | collective-permute-start | bytes 1990664 | tf_op jit(solution)/shard_map/ppermute | solution.py:514
  25.5 1.4 %collective-permute-start.5 = (s32[1,4,8,128]{3,2,1,0:T(8,128)S(1)}, s32[1,4,8,128]{3,2,1,0:T(8,128)S(1)}, u32[]{:S(2)}, u32[]{:S(2)}) collective-permute-start(s32[1,4,8,128]{3,2,1,0:T(8,128)S(1)} %fusion), channel_id=1, source_target_pairs={{0,2},{1,5},{2,0},{3,7},{4,6},{5,1},{6,4},{7,3},{8,10},{9,13},{10,... | collective-permute-start | bytes 49160 | tf_op jit(solution)/shard_map/ppermute | solution.py:514
  27.0 0.0 collective-permute-done.4
  27.0 5.3 %bands.1.refs_9_ = bf16[3,12,192,224]{3,2,1,0:T(8,128)(2,1)} custom-call(bf16[6912,224]{1,0:T(8,128)(2,1)} %get-tuple-element.28.gram_any.refs_10_, bf16[1,2592,128]{2,1,0:T(8,128)(2,1)} %bitcast.7.refs_0_, bf16[1,2592,128]{2,1,0:T(8,128)(2,1)} %bitcast.8.refs_1_, bf16[1,2592,128]{2,1,0:T(8,128)(2,1)} %bitcast.9.refs_2_), custom_call_target="tpu_custom_call" | custom-call | flops 792723456 | bytes 4128768 | tf_op jit(solution)/shard_map/bands/pallas_call | solution.py:322
  32.3 0.0 copy-done.3
  32.3 0.0 collective-permute-done.5
  32.3 0.0 collective-permute-done.7.refs_5_
  32.3 0.0 collective-permute-done.6.refs_4_
  32.3 0.6 %collective-permute-start.9 = (s32[2,4,8,128]{3,2,1,0:T(8,128)S(1)}, s32[2,4,8,128]{3,2,1,0:T(8,128)S(1)}, u32[]{:S(2)}, u32[]{:S(2)}) collective-permute-start(s32[2,4,8,128]{3,2,1,0:T(8,128)S(1)} %pad_add_fusion.1), channel_id=1, source_target_pairs={{0,4},{1,3},{2,6},{3,1},{4,0},{5,7},{6,2},{7,5},{8,12},{9,11},{10,... | collective-permute-start | bytes 98312 | tf_op jit(solution)/shard_map/ppermute | solution.py:514
  32.9 3.4 %collective-permute-done.9 = s32[2,4,8,128]{3,2,1,0:T(8,128)S(1)} collective-permute-done((s32[2,4,8,128]{3,2,1,0:T(8,128)S(1)}, s32[2,4,8,128]{3,2,1,0:T(8,128)S(1)}, u32[]{:S(2)}, u32[]{:S(2)}) %collective-permute-start.9) | collective-permute-done | bytes 32800 | tf_op jit(solution)/shard_map/ppermute | solution.py:514
  36.3 0.0 copy-start
  36.3 0.0 collective-permute-done.8.refs_6_
  36.3 0.1 collective-permute-start.11
  36.4 0.5 collective-permute-start.10
  36.9 1.6 %collective-permute-done.10.refs_3_ = s32[4,4,8,128]{3,2,1,0:T(8,128)S(1)} collective-permute-done((s32[4,4,8,128]{3,2,1,0:T(8,128)S(1)}, s32[4,4,8,128]{3,2,1,0:T(8,128)S(1)}, u32[]{:S(2)}, u32[]{:S(2)}) %collective-permute-start.10) | collective-permute-done | bytes 65568 | tf_op jit(solution)/shard_map/ppermute | solution.py:510
  38.5 0.0 copy-start.2
  38.5 0.4 collective-permute-done.11.refs_7_
  38.9 0.0 copy-done
  38.9 0.2 copy-done.2
  39.1 15.1 %decode.1 = bf16[216,4,2560]{2,1,0:T(4,128)(2,1)} custom-call(s32[2,8,256]{2,1,0:T(8,128)} %copy-done.1, s32[2,8,256]{2,1,0:T(8,128)} %copy-done.3, s32[4,4,8,128]{3,2,1,0:T(8,128)} %copy-done, s32[4,4,8,128]{3,2,1,0:T(8,128)} %copy-done.2, bf16[2592,128]{1,0:T(8,128)(2,1)} %collective-permute-done.6.refs_4_, ...), custom_call_target="tpu_custom_call" | custom-call | flops 2642411520 | bytes 4423680 | tf_op jit(solution)/shard_map/decode/pallas_call | solution.py:483
  (3 shorter events, 0.0 us)
Async XLA Ops:
  2.6 6.0 %collective-permute-start = (s32[8,256]{1,0:T(8,128)}, s32[8,256]{1,0:T(8,128)S(1)}, u32[]{:S(2)}, u32[]{:S(2)}) collective-permute-start(s32[8,256]{1,0:T(8,128)} %get-tuple-element.23), channel_id=1, source_target_pairs={{0,8},{8,0},{16,24},{24,16},{1,9},{9,1},{17,25},{25,17},{2,10},{10... | collective-permute-start | bytes 24584 | tf_op jit(solution)/shard_map/ppermute | solution.py:510
  5.6 18.4 %collective-permute-start.3 = (bf16[2592,128]{1,0:T(8,128)(2,1)}, bf16[2592,128]{1,0:T(8,128)(2,1)}, u32[]{:S(2)}, u32[]{:S(2)}) collective-permute-start(bf16[2592,128]{1,0:T(8,128)(2,1)} %get-tuple-element.29.packed_ref), channel_id=1, source_target_pairs={{0,4},{1,3},{2,6},{3,1},{4,0},{5,7},{6,2},{7,5},{8,12},{9,11},{10,... | collective-permute-start | bytes 1990664 | tf_op jit(solution)/shard_map/ppermute | solution.py:514
  7.1 16.9 %collective-permute-start.2 = (bf16[2592,128]{1,0:T(8,128)(2,1)}, bf16[2592,128]{1,0:T(8,128)(2,1)}, u32[]{:S(2)}, u32[]{:S(2)}) collective-permute-start(bf16[2592,128]{1,0:T(8,128)(2,1)} %get-tuple-element.29.packed_ref), channel_id=1, source_target_pairs={{0,2},{1,5},{2,0},{3,7},{4,6},{5,1},{6,4},{7,3},{8,10},{9,13},{10,... | collective-permute-start | bytes 1990664 | tf_op jit(solution)/shard_map/ppermute | solution.py:514
  9.3 14.7 %copy-start.1 = (s32[2,8,256]{2,1,0:T(8,128)}, s32[2,8,256]{2,1,0:T(8,128)S(1)}, u32[]{:S(2)}) copy-start(s32[2,8,256]{2,1,0:T(8,128)S(1)} %pad_add_fusion.3.refs_0_) | copy-start | bytes 49156
  9.3 14.7 %collective-permute-start.1 = (s32[2,8,256]{2,1,0:T(8,128)S(1)}, s32[2,8,256]{2,1,0:T(8,128)S(1)}, u32[]{:S(2)}, u32[]{:S(2)}) collective-permute-start(s32[2,8,256]{2,1,0:T(8,128)S(1)} %pad_add_fusion.3.refs_0_), channel_id=1, source_target_pairs={{0,16},{8,24},{16,0},{24,8},{1,17},{9,25},{17,1},{25,9},{2,18},{10... | collective-permute-start | bytes 49160 | tf_op jit(solution)/shard_map/ppermute | solution.py:510
  11.9 15.1 %collective-permute-start.4 = (bf16[2592,128]{1,0:T(8,128)(2,1)}, bf16[2592,128]{1,0:T(8,128)(2,1)}, u32[]{:S(2)}, u32[]{:S(2)}) collective-permute-start(bf16[2592,128]{1,0:T(8,128)(2,1)} %get-tuple-element.29.packed_ref), channel_id=1, source_target_pairs={{0,1},{1,0},{2,3},{3,2},{4,5},{5,4},{6,7},{7,6},{8,9},{9,8},{10,11... | collective-permute-start | bytes 1990664 | tf_op jit(solution)/shard_map/ppermute | solution.py:510
  24.0 8.3 %copy-start.3 = (s32[2,8,256]{2,1,0:T(8,128)}, s32[2,8,256]{2,1,0:T(8,128)S(1)}, u32[]{:S(2)}) copy-start(s32[2,8,256]{2,1,0:T(8,128)S(1)} %collective-permute-done.1.refs_1_) | copy-start | bytes 49156
  24.0 8.3 %collective-permute-start.7 = (bf16[2592,128]{1,0:T(8,128)(2,1)}, bf16[2592,128]{1,0:T(8,128)(2,1)}, u32[]{:S(2)}, u32[]{:S(2)}) collective-permute-start(bf16[2592,128]{1,0:T(8,128)(2,1)} %collective-permute-done.3), channel_id=1, source_target_pairs={{0,1},{1,0},{2,3},{3,2},{4,5},{5,4},{6,7},{7,6},{8,9},{9,8},{10,11... | collective-permute-start | bytes 1990664 | tf_op jit(solution)/shard_map/ppermute | solution.py:510
  24.6 7.7 %collective-permute-start.6 = (bf16[2592,128]{1,0:T(8,128)(2,1)}, bf16[2592,128]{1,0:T(8,128)(2,1)}, u32[]{:S(2)}, u32[]{:S(2)}) collective-permute-start(bf16[2592,128]{1,0:T(8,128)(2,1)} %collective-permute-done.2), channel_id=1, source_target_pairs={{0,1},{1,0},{2,3},{3,2},{4,5},{5,4},{6,7},{7,6},{8,9},{9,8},{10,11... | collective-permute-start | bytes 1990664 | tf_op jit(solution)/shard_map/ppermute | solution.py:510
  24.7 11.6 %collective-permute-start.8 = (bf16[2592,128]{1,0:T(8,128)(2,1)}, bf16[2592,128]{1,0:T(8,128)(2,1)}, u32[]{:S(2)}, u32[]{:S(2)}) collective-permute-start(bf16[2592,128]{1,0:T(8,128)(2,1)} %collective-permute-done.2), channel_id=1, source_target_pairs={{0,4},{1,3},{2,6},{3,1},{4,0},{5,7},{6,2},{7,5},{8,12},{9,11},{10,... | collective-permute-start | bytes 1990664 | tf_op jit(solution)/shard_map/ppermute | solution.py:514
  25.5 6.7 %collective-permute-start.5 = (s32[1,4,8,128]{3,2,1,0:T(8,128)S(1)}, s32[1,4,8,128]{3,2,1,0:T(8,128)S(1)}, u32[]{:S(2)}, u32[]{:S(2)}) collective-permute-start(s32[1,4,8,128]{3,2,1,0:T(8,128)S(1)} %fusion), channel_id=1, source_target_pairs={{0,2},{1,5},{2,0},{3,7},{4,6},{5,1},{6,4},{7,3},{8,10},{9,13},{10,... | collective-permute-start | bytes 49160 | tf_op jit(solution)/shard_map/ppermute | solution.py:514
  32.3 4.0 %collective-permute-start.9 = (s32[2,4,8,128]{3,2,1,0:T(8,128)S(1)}, s32[2,4,8,128]{3,2,1,0:T(8,128)S(1)}, u32[]{:S(2)}, u32[]{:S(2)}) collective-permute-start(s32[2,4,8,128]{3,2,1,0:T(8,128)S(1)} %pad_add_fusion.1), channel_id=1, source_target_pairs={{0,4},{1,3},{2,6},{3,1},{4,0},{5,7},{6,2},{7,5},{8,12},{9,11},{10,... | collective-permute-start | bytes 98312 | tf_op jit(solution)/shard_map/ppermute | solution.py:514
  36.3 2.6 %copy-start = (s32[4,4,8,128]{3,2,1,0:T(8,128)}, s32[4,4,8,128]{3,2,1,0:T(8,128)S(1)}, u32[]{:S(2)}) copy-start(s32[4,4,8,128]{3,2,1,0:T(8,128)S(1)} %pad_add_fusion.refs_2_) | copy-start | bytes 196612
  36.3 2.6 %collective-permute-start.11 = (bf16[2592,128]{1,0:T(8,128)(2,1)}, bf16[2592,128]{1,0:T(8,128)(2,1)}, u32[]{:S(2)}, u32[]{:S(2)}) collective-permute-start(bf16[2592,128]{1,0:T(8,128)(2,1)} %collective-permute-done.8.refs_6_), channel_id=1, source_target_pairs={{0,1},{1,0},{2,3},{3,2},{4,5},{5,4},{6,7},{7,6},{8,9},{9,8},{10,11... | collective-permute-start | bytes 1990664 | tf_op jit(solution)/shard_map/ppermute | solution.py:510
  36.4 2.1 %collective-permute-start.10 = (s32[4,4,8,128]{3,2,1,0:T(8,128)S(1)}, s32[4,4,8,128]{3,2,1,0:T(8,128)S(1)}, u32[]{:S(2)}, u32[]{:S(2)}) collective-permute-start(s32[4,4,8,128]{3,2,1,0:T(8,128)S(1)} %pad_add_fusion.refs_2_), channel_id=1, source_target_pairs={{0,1},{1,0},{2,3},{3,2},{4,5},{5,4},{6,7},{7,6},{8,9},{9,8},{10,11... | collective-permute-start | bytes 196616 | tf_op jit(solution)/shard_map/ppermute | solution.py:510
  38.5 0.6 %copy-start.2 = (s32[4,4,8,128]{3,2,1,0:T(8,128)}, s32[4,4,8,128]{3,2,1,0:T(8,128)S(1)}, u32[]{:S(2)}) copy-start(s32[4,4,8,128]{3,2,1,0:T(8,128)S(1)} %collective-permute-done.10.refs_3_) | copy-start | bytes 196612

commit v19 on v18

--- a/solution.py
+++ b/solution.py
@@ -539,9 +539,9 @@
         )
 
     first, second = turn(packed, 2, 4), turn(packed, 4, 2)
+    sibling = swap(packed, "row", 1)
     lines, distance = [jnp.stack([lines, swap(lines, "dir", 1)])], 2
-    lines[0], pokes, again = lax.optimization_barrier((lines[0], pokes, packed))
-    sibling = swap(again, "row", 1)
+    lines[0], pokes = lax.optimization_barrier((lines[0], pokes))
     while distance < directions:
         lines.append(swap(jnp.concatenate(lines, axis=0), "dir", distance))
         distance *= 2

time: 54.5 us -> 54.6 us (level)
  no operation moved by 1% of the time
where the time goes in v19:
time: 54.6 us; the launch traced here: 54.3 us
  Pallas kernels  35 us (64%)
  starting transfers between devices  12.8 us (23%)
  waiting for transfers between devices  5.47 us (10%)
  other arithmetic  0.71 us (1%)
    pallas_call x1, Pallas kernels, decode(): pl.pallas_call(functools.partial(decode_kernel, row_shape, surface_rows,...  15.1 us
    pallas_call x1, Pallas kernels, gram(): pl.pallas_call(functools.partial(gram_kernel, row_shape, surface_rows), g...  12 us
    ppermute x7, starting transfers between devices, swap(): lax.ppermute(block, axis, [(i, i ^ distance) for i in range(lax.axis_size...  6.75 us
    ppermute x5, starting transfers between devices, turn(): lax.ppermute(block, 'row', [(i, i ^ (odd if i % 2 else even)) for i in ra...  6.02 us
    pallas_call x1, Pallas kernels, bands(): pl.pallas_call(functools.partial(bands_kernel, row_shape, surface_rows, f...  5.29 us
    ppermute x5, waiting for transfers between devices, turn(): lax.ppermute(block, 'row', [(i, i ^ (odd if i % 2 else even)) for i in ra...  3.42 us
    pallas_call x1, Pallas kernels, pack(): pl.pallas_call(pack_kernel, out_shape=[jax.ShapeDtypeStruct((mirrors * ro...  2.57 us
    ppermute x7, waiting for transfers between devices, swap(): lax.ppermute(block, axis, [(i, i ^ distance) for i in range(lax.axis_size...  2.05 us
  transfers between devices with their start and end apart: 12, of which 3 were waited for; matrix products, arithmetic and copies ran while one was open for 1% of the time, Pallas kernels for 32%

profile of v19, /device:TPU:0, one launch (start us, length us, event | category | flops | bytes accessed | tf_op | source)
XLA Modules:
  0.0 54.3 jit_solution(15039591641623059712)
XLA Ops:
  0.0 2.6 %pack_influence.1 = (bf16[2592,128]{1,0:T(8,128)(2,1)}, s32[8,256]{1,0:T(8,128)}) custom-call(bf16[3,4,144,192]{3,2,1,0:T(8,128)(2,1)} %bitcast.11, s32[3,1,4]{2,1,0:T(1,128)} %bitcast.15, s32[3,1,160]{2,1,0:T(1,128)} %bitcast.14, s32[1,2,80]{2,1,0:T(2,128)} %valid_ref.1), custom_call_target="tpu_custom_call" | custom-call | bytes 995328 | tf_op jit(solution)/shard_map/pack_influence/pallas_call | solution.py:65
  2.6 3.0 %collective-permute-start = (s32[8,256]{1,0:T(8,128)}, s32[8,256]{1,0:T(8,128)S(1)}, u32[]{:S(2)}, u32[]{:S(2)}) collective-permute-start(s32[8,256]{1,0:T(8,128)} %get-tuple-element.22), channel_id=1, source_target_pairs={{0,8},{8,0},{16,24},{24,16},{1,9},{9,1},{17,25},{25,17},{2,10},{10... | collective-permute-start | bytes 24584 | tf_op jit(solution)/shard_map/ppermute | solution.py:510
  5.6 0.0 collective-permute-start.4
  5.6 1.5 %collective-permute-start.3 = (bf16[2592,128]{1,0:T(8,128)(2,1)}, bf16[2592,128]{1,0:T(8,128)(2,1)}, u32[]{:S(2)}, u32[]{:S(2)}) collective-permute-start(bf16[2592,128]{1,0:T(8,128)(2,1)} %get-tuple-element.25.packed_ref), channel_id=1, source_target_pairs={{0,4},{1,3},{2,6},{3,1},{4,0},{5,7},{6,2},{7,5},{8,12},{9,11},{10,... | collective-permute-start | bytes 1990664 | tf_op jit(solution)/shard_map/ppermute | solution.py:514
  7.1 1.5 %collective-permute-start.2 = (bf16[2592,128]{1,0:T(8,128)(2,1)}, bf16[2592,128]{1,0:T(8,128)(2,1)}, u32[]{:S(2)}, u32[]{:S(2)}) collective-permute-start(bf16[2592,128]{1,0:T(8,128)(2,1)} %get-tuple-element.25.packed_ref), channel_id=1, source_target_pairs={{0,2},{1,5},{2,0},{3,7},{4,6},{5,1},{6,4},{7,3},{8,10},{9,13},{10,... | collective-permute-start | bytes 1990664 | tf_op jit(solution)/shard_map/ppermute | solution.py:514
  8.6 0.0 collective-permute-done
  8.6 0.7 %pad_add_fusion.3.refs_0_ = s32[2,8,256]{2,1,0:T(8,128)S(1)} fusion(s32[1,8,256]{2,1,0:T(8,128)S(1)} %bitcast.13, s32[1,8,256]{2,1,0:T(8,128)} %bitcast.12), kind=kLoop, calls=%fused_computation.4 | loop fusion | flops 4096 | bytes 32768 | tf_op jit(solution)/shard_map/stack | solution.py:543
  9.3 0.0 copy-start.1
  9.3 2.6 %collective-permute-start.1 = (s32[2,8,256]{2,1,0:T(8,128)S(1)}, s32[2,8,256]{2,1,0:T(8,128)S(1)}, u32[]{:S(2)}, u32[]{:S(2)}) collective-permute-start(s32[2,8,256]{2,1,0:T(8,128)S(1)} %pad_add_fusion.3.refs_0_), channel_id=1, source_target_pairs={{0,16},{8,24},{16,0},{24,8},{1,17},{9,25},{17,1},{25,9},{2,18},{10... | collective-permute-start | bytes 49160 | tf_op jit(solution)/shard_map/ppermute | solution.py:510
  11.9 12.0 %gram_rows.1 = (bf16[6912,224]{1,0:T(8,128)(2,1)}, bf16[1,12,192,224]{3,2,1,0:T(8,128)(2,1)}) custom-call(s32[3,48,48]{2,1,0:T(8,128)} %table_ref.1, s32[16,128]{1,0:T(8,128)} %bitcast.16, bf16[2592,128]{1,0:T(8,128)(2,1)} %get-tuple-element.25.packed_ref), custom_call_target="tpu_custom_call" | custom-call | flops 6341787648 | bytes 3096576 | tf_op jit(solution)/shard_map/gram_rows/pallas_call | solution.py:194
  23.9 0.0 collective-permute-done.1.refs_1_
  23.9 0.0 copy-done.1
  24.0 0.0 copy-start.3
  24.0 0.0 collective-permute-done.3
  24.0 0.0 collective-permute-done.2
  24.0 0.1 collective-permute-start.7
  24.1 0.5 collective-permute-start.6
  24.6 0.8 %collective-permute-start.8 = (bf16[2592,128]{1,0:T(8,128)(2,1)}, bf16[2592,128]{1,0:T(8,128)(2,1)}, u32[]{:S(2)}, u32[]{:S(2)}) collective-permute-start(bf16[2592,128]{1,0:T(8,128)(2,1)} %collective-permute-done.2), channel_id=1, source_target_pairs={{0,4},{1,3},{2,6},{3,1},{4,0},{5,7},{6,2},{7,5},{8,12},{9,11},{10,... | collective-permute-start | bytes 1990664 | tf_op jit(solution)/shard_map/ppermute | solution.py:514
  25.4 1.7 %collective-permute-start.5 = (s32[1,4,8,128]{3,2,1,0:T(8,128)S(1)}, s32[1,4,8,128]{3,2,1,0:T(8,128)S(1)}, u32[]{:S(2)}, u32[]{:S(2)}) collective-permute-start(s32[1,4,8,128]{3,2,1,0:T(8,128)S(1)} %fusion), channel_id=1, source_target_pairs={{0,2},{1,5},{2,0},{3,7},{4,6},{5,1},{6,4},{7,3},{8,10},{9,13},{10,... | collective-permute-start | bytes 49160 | tf_op jit(solution)/shard_map/ppermute | solution.py:514
  27.0 0.0 collective-permute-done.4
  27.0 5.3 %bands.1.refs_9_ = bf16[3,12,192,224]{3,2,1,0:T(8,128)(2,1)} custom-call(bf16[6912,224]{1,0:T(8,128)(2,1)} %get-tuple-element.27.gram_any.refs_10_, bf16[1,2592,128]{2,1,0:T(8,128)(2,1)} %bitcast.7.refs_0_, bf16[1,2592,128]{2,1,0:T(8,128)(2,1)} %bitcast.8.refs_1_, bf16[1,2592,128]{2,1,0:T(8,128)(2,1)} %bitcast.9.refs_2_), custom_call_target="tpu_custom_call" | custom-call | flops 792723456 | bytes 4128768 | tf_op jit(solution)/shard_map/bands/pallas_call | solution.py:322
  32.3 0.0 copy-done.3
  32.3 0.0 collective-permute-done.5
  32.4 0.0 collective-permute-done.7.refs_5_
  32.4 0.0 collective-permute-done.6.refs_4_
  32.4 0.6 %collective-permute-start.9 = (s32[2,4,8,128]{3,2,1,0:T(8,128)S(1)}, s32[2,4,8,128]{3,2,1,0:T(8,128)S(1)}, u32[]{:S(2)}, u32[]{:S(2)}) collective-permute-start(s32[2,4,8,128]{3,2,1,0:T(8,128)S(1)} %pad_add_fusion.1), channel_id=1, source_target_pairs={{0,4},{1,3},{2,6},{3,1},{4,0},{5,7},{6,2},{7,5},{8,12},{9,11},{10,... | collective-permute-start | bytes 98312 | tf_op jit(solution)/shard_map/ppermute | solution.py:514
  32.9 3.4 %collective-permute-done.9 = s32[2,4,8,128]{3,2,1,0:T(8,128)S(1)} collective-permute-done((s32[2,4,8,128]{3,2,1,0:T(8,128)S(1)}, s32[2,4,8,128]{3,2,1,0:T(8,128)S(1)}, u32[]{:S(2)}, u32[]{:S(2)}) %collective-permute-start.9) | collective-permute-done | bytes 32800 | tf_op jit(solution)/shard_map/ppermute | solution.py:514
  36.4 0.0 copy-start
  36.4 0.0 collective-permute-done.8.refs_6_
  36.4 0.1 collective-permute-start.11
  36.5 0.5 collective-permute-start.10
  37.0 1.6 %collective-permute-done.10.refs_3_ = s32[4,4,8,128]{3,2,1,0:T(8,128)S(1)} collective-permute-done((s32[4,4,8,128]{3,2,1,0:T(8,128)S(1)}, s32[4,4,8,128]{3,2,1,0:T(8,128)S(1)}, u32[]{:S(2)}, u32[]{:S(2)}) %collective-permute-start.10) | collective-permute-done | bytes 65568 | tf_op jit(solution)/shard_map/ppermute | solution.py:510
  38.6 0.0 copy-start.2
  38.6 0.4 collective-permute-done.11.refs_7_
  39.0 0.0 copy-done
  39.0 0.2 copy-done.2
  39.2 15.1 %decode.1 = bf16[216,4,2560]{2,1,0:T(4,128)(2,1)} custom-call(s32[2,8,256]{2,1,0:T(8,128)} %copy-done.1, s32[2,8,256]{2,1,0:T(8,128)} %copy-done.3, s32[4,4,8,128]{3,2,1,0:T(8,128)} %copy-done, s32[4,4,8,128]{3,2,1,0:T(8,128)} %copy-done.2, bf16[2592,128]{1,0:T(8,128)(2,1)} %collective-permute-done.6.refs_4_, ...), custom_call_target="tpu_custom_call" | custom-call | flops 2642411520 | bytes 4423680 | tf_op jit(solution)/shard_map/decode/pallas_call | solution.py:483
  (3 shorter events, 0.0 us)
Async XLA Ops:
  2.6 6.0 %collective-permute-start = (s32[8,256]{1,0:T(8,128)}, s32[8,256]{1,0:T(8,128)S(1)}, u32[]{:S(2)}, u32[]{:S(2)}) collective-permute-start(s32[8,256]{1,0:T(8,128)} %get-tuple-element.22), channel_id=1, source_target_pairs={{0,8},{8,0},{16,24},{24,16},{1,9},{9,1},{17,25},{25,17},{2,10},{10... | collective-permute-start | bytes 24584 | tf_op jit(solution)/shard_map/ppermute | solution.py:510
  5.6 21.4 %collective-permute-start.4 = (bf16[2592,128]{1,0:T(8,128)(2,1)}, bf16[2592,128]{1,0:T(8,128)(2,1)}, u32[]{:S(2)}, u32[]{:S(2)}) collective-permute-start(bf16[2592,128]{1,0:T(8,128)(2,1)} %get-tuple-element.25.packed_ref), channel_id=1, source_target_pairs={{0,1},{1,0},{2,3},{3,2},{4,5},{5,4},{6,7},{7,6},{8,9},{9,8},{10,11... | collective-permute-start | bytes 1990664 | tf_op jit(solution)/shard_map/ppermute | solution.py:510
  5.6 18.4 %collective-permute-start.3 = (bf16[2592,128]{1,0:T(8,128)(2,1)}, bf16[2592,128]{1,0:T(8,128)(2,1)}, u32[]{:S(2)}, u32[]{:S(2)}) collective-permute-start(bf16[2592,128]{1,0:T(8,128)(2,1)} %get-tuple-element.25.packed_ref), channel_id=1, source_target_pairs={{0,4},{1,3},{2,6},{3,1},{4,0},{5,7},{6,2},{7,5},{8,12},{9,11},{10,... | collective-permute-start | bytes 1990664 | tf_op jit(solution)/shard_map/ppermute | solution.py:514
  7.1 16.9 %collective-permute-start.2 = (bf16[2592,128]{1,0:T(8,128)(2,1)}, bf16[2592,128]{1,0:T(8,128)(2,1)}, u32[]{:S(2)}, u32[]{:S(2)}) collective-permute-start(bf16[2592,128]{1,0:T(8,128)(2,1)} %get-tuple-element.25.packed_ref), channel_id=1, source_target_pairs={{0,2},{1,5},{2,0},{3,7},{4,6},{5,1},{6,4},{7,3},{8,10},{9,13},{10,... | collective-permute-start | bytes 1990664 | tf_op jit(solution)/shard_map/ppermute | solution.py:514
  9.3 14.6 %copy-start.1 = (s32[2,8,256]{2,1,0:T(8,128)}, s32[2,8,256]{2,1,0:T(8,128)S(1)}, u32[]{:S(2)}) copy-start(s32[2,8,256]{2,1,0:T(8,128)S(1)} %pad_add_fusion.3.refs_0_) | copy-start | bytes 49156
  9.3 14.6 %collective-permute-start.1 = (s32[2,8,256]{2,1,0:T(8,128)S(1)}, s32[2,8,256]{2,1,0:T(8,128)S(1)}, u32[]{:S(2)}, u32[]{:S(2)}) collective-permute-start(s32[2,8,256]{2,1,0:T(8,128)S(1)} %pad_add_fusion.3.refs_0_), channel_id=1, source_target_pairs={{0,16},{8,24},{16,0},{24,8},{1,17},{9,25},{17,1},{25,9},{2,18},{10... | collective-permute-start | bytes 49160 | tf_op jit(solution)/shard_map/ppermute | solution.py:510
  24.0 8.4 %copy-start.3 = (s32[2,8,256]{2,1,0:T(8,128)}, s32[2,8,256]{2,1,0:T(8,128)S(1)}, u32[]{:S(2)}) copy-start(s32[2,8,256]{2,1,0:T(8,128)S(1)} %collective-permute-done.1.refs_1_) | copy-start | bytes 49156
  24.0 8.4 %collective-permute-start.7 = (bf16[2592,128]{1,0:T(8,128)(2,1)}, bf16[2592,128]{1,0:T(8,128)(2,1)}, u32[]{:S(2)}, u32[]{:S(2)}) collective-permute-start(bf16[2592,128]{1,0:T(8,128)(2,1)} %collective-permute-done.3), channel_id=1, source_target_pairs={{0,1},{1,0},{2,3},{3,2},{4,5},{5,4},{6,7},{7,6},{8,9},{9,8},{10,11... | collective-permute-start | bytes 1990664 | tf_op jit(solution)/shard_map/ppermute | solution.py:510
  24.1 8.3 %collective-permute-start.6 = (bf16[2592,128]{1,0:T(8,128)(2,1)}, bf16[2592,128]{1,0:T(8,128)(2,1)}, u32[]{:S(2)}, u32[]{:S(2)}) collective-permute-start(bf16[2592,128]{1,0:T(8,128)(2,1)} %collective-permute-done.2), channel_id=1, source_target_pairs={{0,1},{1,0},{2,3},{3,2},{4,5},{5,4},{6,7},{7,6},{8,9},{9,8},{10,11... | collective-permute-start | bytes 1990664 | tf_op jit(solution)/shard_map/ppermute | solution.py:510
  24.6 11.8 %collective-permute-start.8 = (bf16[2592,128]{1,0:T(8,128)(2,1)}, bf16[2592,128]{1,0:T(8,128)(2,1)}, u32[]{:S(2)}, u32[]{:S(2)}) collective-permute-start(bf16[2592,128]{1,0:T(8,128)(2,1)} %collective-permute-done.2), channel_id=1, source_target_pairs={{0,4},{1,3},{2,6},{3,1},{4,0},{5,7},{6,2},{7,5},{8,12},{9,11},{10,... | collective-permute-start | bytes 1990664 | tf_op jit(solution)/shard_map/ppermute | solution.py:514
  25.4 7.0 %collective-permute-start.5 = (s32[1,4,8,128]{3,2,1,0:T(8,128)S(1)}, s32[1,4,8,128]{3,2,1,0:T(8,128)S(1)}, u32[]{:S(2)}, u32[]{:S(2)}) collective-permute-start(s32[1,4,8,128]{3,2,1,0:T(8,128)S(1)} %fusion), channel_id=1, source_target_pairs={{0,2},{1,5},{2,0},{3,7},{4,6},{5,1},{6,4},{7,3},{8,10},{9,13},{10,... | collective-permute-start | bytes 49160 | tf_op jit(solution)/shard_map/ppermute | solution.py:514
  32.4 4.0 %collective-permute-start.9 = (s32[2,4,8,128]{3,2,1,0:T(8,128)S(1)}, s32[2,4,8,128]{3,2,1,0:T(8,128)S(1)}, u32[]{:S(2)}, u32[]{:S(2)}) collective-permute-start(s32[2,4,8,128]{3,2,1,0:T(8,128)S(1)} %pad_add_fusion.1), channel_id=1, source_target_pairs={{0,4},{1,3},{2,6},{3,1},{4,0},{5,7},{6,2},{7,5},{8,12},{9,11},{10,... | collective-permute-start | bytes 98312 | tf_op jit(solution)/shard_map/ppermute | solution.py:514
  36.4 2.6 %copy-start = (s32[4,4,8,128]{3,2,1,0:T(8,128)}, s32[4,4,8,128]{3,2,1,0:T(8,128)S(1)}, u32[]{:S(2)}) copy-start(s32[4,4,8,128]{3,2,1,0:T(8,128)S(1)} %pad_add_fusion.refs_2_) | copy-start | bytes 196612
  36.4 2.6 %collective-permute-start.11 = (bf16[2592,128]{1,0:T(8,128)(2,1)}, bf16[2592,128]{1,0:T(8,128)(2,1)}, u32[]{:S(2)}, u32[]{:S(2)}) collective-permute-start(bf16[2592,128]{1,0:T(8,128)(2,1)} %collective-permute-done.8.refs_6_), channel_id=1, source_target_pairs={{0,1},{1,0},{2,3},{3,2},{4,5},{5,4},{6,7},{7,6},{8,9},{9,8},{10,11... | collective-permute-start | bytes 1990664 | tf_op jit(solution)/shard_map/ppermute | solution.py:510
  36.5 2.1 %collective-permute-start.10 = (s32[4,4,8,128]{3,2,1,0:T(8,128)S(1)}, s32[4,4,8,128]{3,2,1,0:T(8,128)S(1)}, u32[]{:S(2)}, u32[]{:S(2)}) collective-permute-start(s32[4,4,8,128]{3,2,1,0:T(8,128)S(1)} %pad_add_fusion.refs_2_), channel_id=1, source_target_pairs={{0,1},{1,0},{2,3},{3,2},{4,5},{5,4},{6,7},{7,6},{8,9},{9,8},{10,11... | collective-permute-start | bytes 196616 | tf_op jit(solution)/shard_map/ppermute | solution.py:510
  38.6 0.6 %copy-start.2 = (s32[4,4,8,128]{3,2,1,0:T(8,128)}, s32[4,4,8,128]{3,2,1,0:T(8,128)S(1)}, u32[]{:S(2)}) copy-start(s32[4,4,8,128]{3,2,1,0:T(8,128)S(1)} %collective-permute-done.10.refs_3_) | copy-start | bytes 196612

commit v20 on v17

--- a/solution.py
+++ b/solution.py
@@ -549,12 +549,11 @@
     gram_rows, own_rows = gram(actuator_codes, pokes, packed, own, row_shape, surface_rows)
     gram_rows, first, second, held = lax.optimization_barrier((gram_rows, first, second, held))
     diagonal = turn(first, 4, 2)
-    first_sibling = swap(first, "row", 1)
     mine = [held, turn(held, 2, 4), turn(held, 4, 2), swap(held, "row", 6)]
     sources = [source[None] for source in (sibling, first, second)]
     near, = bands(gram_rows, sources, 1, staged, row_shape, surface_rows)
-    near, second = lax.optimization_barrier((near, second))
-    second_sibling = swap(second, "row", 1)
+    near, first, second = lax.optimization_barrier((near, first, second))
+    first_sibling, second_sibling = swap(first, "row", 1), swap(second, "row", 1)
     mine = jnp.concatenate(mine, axis=0)
     near, diagonal, mine = lax.optimization_barrier((near, diagonal, mine))
     theirs = swap(mine, "row", 1)

time: 53.9 us -> 53.9 us (level)
  no operation moved by 1% of the time
where the time goes in v20:
time: 53.9 us; the launch traced here: 53.7 us
  Pallas kernels  35 us (65%)
  starting transfers between devices  14.7 us (27%)
  waiting for transfers between devices  2.89 us (5%)
  other arithmetic  0.71 us (1%)
    pallas_call x1, Pallas kernels, decode(): pl.pallas_call(functools.partial(decode_kernel, row_shape, surface_rows,...  15.1 us
    pallas_call x1, Pallas kernels, gram(): pl.pallas_call(functools.partial(gram_kernel, row_shape, surface_rows), g...  12.1 us
    ppermute x8, starting transfers between devices, swap(): lax.ppermute(block, axis, [(i, i ^ distance) for i in range(lax.axis_size...  8.89 us
    ppermute x5, starting transfers between devices, turn(): lax.ppermute(block, 'row', [(i, i ^ (odd if i % 2 else even)) for i in ra...  5.78 us
    pallas_call x1, Pallas kernels, bands(): pl.pallas_call(functools.partial(bands_kernel, row_shape, surface_rows, f...  5.29 us
    pallas_call x1, Pallas kernels, pack(): pl.pallas_call(pack_kernel, out_shape=[jax.ShapeDtypeStruct((mirrors * ro...  2.57 us
    ppermute x8, waiting for transfers between devices, swap(): lax.ppermute(block, axis, [(i, i ^ distance) for i in range(lax.axis_size...  2.04 us
  transfers between devices with their start and end apart: 13, of which 4 were waited for; matrix products, arithmetic and copies ran while one was open for 1% of the time, Pallas kernels for 32%

profile of v20, /device:TPU:0, one launch (start us, length us, event | category | flops | bytes accessed | tf_op | source)
XLA Modules:
  0.0 53.7 jit_solution(1476334988446419781)
XLA Ops:
  0.0 2.6 %pack_influence.1 = (bf16[2592,128]{1,0:T(8,128)(2,1)}, s32[8,256]{1,0:T(8,128)}) custom-call(bf16[3,4,144,192]{3,2,1,0:T(8,128)(2,1)} %bitcast.11, s32[3,1,4]{2,1,0:T(1,128)} %bitcast.15, s32[3,1,160]{2,1,0:T(1,128)} %bitcast.14, s32[1,2,80]{2,1,0:T(2,128)} %valid_ref.1), custom_call_target="tpu_custom_call" | custom-call | bytes 995328 | tf_op jit(solution)/shard_map/pack_influence/pallas_call | solution.py:65
  2.6 3.0 %collective-permute-start = (s32[8,256]{1,0:T(8,128)}, s32[8,256]{1,0:T(8,128)S(1)}, u32[]{:S(2)}, u32[]{:S(2)}) collective-permute-start(s32[8,256]{1,0:T(8,128)} %get-tuple-element.21), channel_id=1, source_target_pairs={{0,8},{8,0},{16,24},{24,16},{1,9},{9,1},{17,25},{25,17},{2,10},{10... | collective-permute-start | bytes 24584 | tf_op jit(solution)/shard_map/ppermute | solution.py:510
  5.6 0.0 collective-permute-start.4
  5.6 1.5 %collective-permute-start.3 = (bf16[2592,128]{1,0:T(8,128)(2,1)}, bf16[2592,128]{1,0:T(8,128)(2,1)}, u32[]{:S(2)}, u32[]{:S(2)}) collective-permute-start(bf16[2592,128]{1,0:T(8,128)(2,1)} %get-tuple-element.24.packed_ref), channel_id=1, source_target_pairs={{0,4},{1,3},{2,6},{3,1},{4,0},{5,7},{6,2},{7,5},{8,12},{9,11},{10,... | collective-permute-start | bytes 1990664 | tf_op jit(solution)/shard_map/ppermute | solution.py:514
  7.1 1.5 %collective-permute-start.2 = (bf16[2592,128]{1,0:T(8,128)(2,1)}, bf16[2592,128]{1,0:T(8,128)(2,1)}, u32[]{:S(2)}, u32[]{:S(2)}) collective-permute-start(bf16[2592,128]{1,0:T(8,128)(2,1)} %get-tuple-element.24.packed_ref), channel_id=1, source_target_pairs={{0,2},{1,5},{2,0},{3,7},{4,6},{5,1},{6,4},{7,3},{8,10},{9,13},{10,... | collective-permute-start | bytes 1990664 | tf_op jit(solution)/shard_map/ppermute | solution.py:514
  8.6 0.0 collective-permute-done
  8.6 0.7 %pad_add_fusion.2.refs_0_ = s32[2,8,256]{2,1,0:T(8,128)S(1)} fusion(s32[1,8,256]{2,1,0:T(8,128)S(1)} %bitcast.13, s32[1,8,256]{2,1,0:T(8,128)} %bitcast.12), kind=kLoop, calls=%fused_computation.3 | loop fusion | flops 4096 | bytes 32768 | tf_op jit(solution)/shard_map/stack | solution.py:543
  9.3 0.0 copy-start.1
  9.3 2.6 %collective-permute-start.1 = (s32[2,8,256]{2,1,0:T(8,128)S(1)}, s32[2,8,256]{2,1,0:T(8,128)S(1)}, u32[]{:S(2)}, u32[]{:S(2)}) collective-permute-start(s32[2,8,256]{2,1,0:T(8,128)S(1)} %pad_add_fusion.2.refs_0_), channel_id=1, source_target_pairs={{0,16},{8,24},{16,0},{24,8},{1,17},{9,25},{17,1},{25,9},{2,18},{10... | collective-permute-start | bytes 49160 | tf_op jit(solution)/shard_map/ppermute | solution.py:510
  11.9 12.1 %gram_rows.1 = (bf16[6912,224]{1,0:T(8,128)(2,1)}, bf16[1,12,192,224]{3,2,1,0:T(8,128)(2,1)}) custom-call(s32[3,48,48]{2,1,0:T(8,128)} %table_ref.1, s32[16,128]{1,0:T(8,128)} %bitcast.16, bf16[2592,128]{1,0:T(8,128)(2,1)} %get-tuple-element.24.packed_ref), custom_call_target="tpu_custom_call" | custom-call | flops 6341787648 | bytes 3096576 | tf_op jit(solution)/shard_map/gram_rows/pallas_call | solution.py:194
  24.0 0.0 collective-permute-done.1.refs_1_
  24.0 0.0 copy-done.1
  24.0 0.0 copy-start.3
  24.0 0.0 collective-permute-done.3
  24.0 0.0 collective-permute-done.2
  24.0 0.9 %collective-permute-start.5 = (bf16[2592,128]{1,0:T(8,128)(2,1)}, bf16[2592,128]{1,0:T(8,128)(2,1)}, u32[]{:S(2)}, u32[]{:S(2)}) collective-permute-start(bf16[2592,128]{1,0:T(8,128)(2,1)} %collective-permute-done.2), channel_id=1, source_target_pairs={{0,4},{1,3},{2,6},{3,1},{4,0},{5,7},{6,2},{7,5},{8,12},{9,11},{10,... | collective-permute-start | bytes 1990664 | tf_op jit(solution)/shard_map/ppermute | solution.py:514
  24.9 1.6 %collective-permute-start.8 = (s32[1,4,8,128]{3,2,1,0:T(8,128)S(1)}, s32[1,4,8,128]{3,2,1,0:T(8,128)S(1)}, u32[]{:S(2)}, u32[]{:S(2)}) collective-permute-start(s32[1,4,8,128]{3,2,1,0:T(8,128)S(1)} %fusion), channel_id=1, source_target_pairs={{0,6},{1,7},{2,4},{3,5},{4,2},{5,3},{6,0},{7,1},{8,14},{9,15},{10,... | collective-permute-start | bytes 49160 | tf_op jit(solution)/shard_map/ppermute | solution.py:510
  26.5 1.5 %collective-permute-start.7 = (s32[1,4,8,128]{3,2,1,0:T(8,128)S(1)}, s32[1,4,8,128]{3,2,1,0:T(8,128)S(1)}, u32[]{:S(2)}, u32[]{:S(2)}) collective-permute-start(s32[1,4,8,128]{3,2,1,0:T(8,128)S(1)} %fusion), channel_id=1, source_target_pairs={{0,4},{1,3},{2,6},{3,1},{4,0},{5,7},{6,2},{7,5},{8,12},{9,11},{10,... | collective-permute-start | bytes 49160 | tf_op jit(solution)/shard_map/ppermute | solution.py:514
  28.0 0.4 collective-permute-start.6
  28.4 0.0 collective-permute-done.4
  28.4 5.3 %bands.1.refs_9_ = bf16[3,12,192,224]{3,2,1,0:T(8,128)(2,1)} custom-call(bf16[6912,224]{1,0:T(8,128)(2,1)} %get-tuple-element.26.gram_any.refs_10_, bf16[1,2592,128]{2,1,0:T(8,128)(2,1)} %bitcast.7.refs_0_, bf16[1,2592,128]{2,1,0:T(8,128)(2,1)} %bitcast.8.refs_1_, bf16[1,2592,128]{2,1,0:T(8,128)(2,1)} %bitcast.9.refs_2_), custom_call_target="tpu_custom_call" | custom-call | flops 792723456 | bytes 4128768 | tf_op jit(solution)/shard_map/bands/pallas_call | solution.py:322
  33.7 0.0 copy-done.3
  33.7 0.1 collective-permute-start.10
  33.8 0.0 collective-permute-done.8
  33.8 1.1 %collective-permute-start.11 = (bf16[2592,128]{1,0:T(8,128)(2,1)}, bf16[2592,128]{1,0:T(8,128)(2,1)}, u32[]{:S(2)}, u32[]{:S(2)}) collective-permute-start(bf16[2592,128]{1,0:T(8,128)(2,1)} %collective-permute-done.3), channel_id=1, source_target_pairs={{0,1},{1,0},{2,3},{3,2},{4,5},{5,4},{6,7},{7,6},{8,9},{9,8},{10,11... | collective-permute-start | bytes 1990664 | tf_op jit(solution)/shard_map/ppermute | solution.py:510
  34.8 0.8 %collective-permute-done.7 = s32[1,4,8,128]{3,2,1,0:T(8,128)S(1)} collective-permute-done((s32[1,4,8,128]{3,2,1,0:T(8,128)S(1)}, s32[1,4,8,128]{3,2,1,0:T(8,128)S(1)}, u32[]{:S(2)}, u32[]{:S(2)}) %collective-permute-start.7) | collective-permute-done | bytes 16416 | tf_op jit(solution)/shard_map/ppermute | solution.py:514
  35.7 0.0 collective-permute-done.6
  35.7 0.0 copy-start
  35.7 0.0 collective-permute-done.5.refs_6_
  35.7 0.1 collective-permute-start.12
  35.8 0.5 collective-permute-start.9
  36.3 0.0 collective-permute-done.10.refs_4_
  36.3 0.9 %collective-permute-done.11.refs_5_ = bf16[2592,128]{1,0:T(8,128)(2,1)} collective-permute-done((bf16[2592,128]{1,0:T(8,128)(2,1)}, bf16[2592,128]{1,0:T(8,128)(2,1)}, u32[]{:S(2)}, u32[]{:S(2)}) %collective-permute-start.11) | collective-permute-done | bytes 663584 | tf_op jit(solution)/shard_map/ppermute | solution.py:510
  37.2 0.8 %collective-permute-done.9.refs_3_ = s32[4,4,8,128]{3,2,1,0:T(8,128)S(1)} collective-permute-done((s32[4,4,8,128]{3,2,1,0:T(8,128)S(1)}, s32[4,4,8,128]{3,2,1,0:T(8,128)S(1)}, u32[]{:S(2)}, u32[]{:S(2)}) %collective-permute-start.9) | collective-permute-done | bytes 65568 | tf_op jit(solution)/shard_map/ppermute | solution.py:510
  37.9 0.0 copy-start.2
  37.9 0.4 collective-permute-done.12.refs_7_
  38.3 0.0 copy-done
  38.3 0.2 copy-done.2
  38.5 15.1 %decode.1 = bf16[216,4,2560]{2,1,0:T(4,128)(2,1)} custom-call(s32[2,8,256]{2,1,0:T(8,128)} %copy-done.1, s32[2,8,256]{2,1,0:T(8,128)} %copy-done.3, s32[4,4,8,128]{3,2,1,0:T(8,128)} %copy-done, s32[4,4,8,128]{3,2,1,0:T(8,128)} %copy-done.2, bf16[2592,128]{1,0:T(8,128)(2,1)} %collective-permute-done.10.refs_4_, ...), custom_call_target="tpu_custom_call" | custom-call | flops 2642411520 | bytes 4423680 | tf_op jit(solution)/shard_map/decode/pallas_call | solution.py:483
  (2 shorter events, 0.0 us)
Async XLA Ops:
  2.6 6.0 %collective-permute-start = (s32[8,256]{1,0:T(8,128)}, s32[8,256]{1,0:T(8,128)S(1)}, u32[]{:S(2)}, u32[]{:S(2)}) collective-permute-start(s32[8,256]{1,0:T(8,128)} %get-tuple-element.21), channel_id=1, source_target_pairs={{0,8},{8,0},{16,24},{24,16},{1,9},{9,1},{17,25},{25,17},{2,10},{10... | collective-permute-start | bytes 24584 | tf_op jit(solution)/shard_map/ppermute | solution.py:510
  5.6 22.8 %collective-permute-start.4 = (bf16[2592,128]{1,0:T(8,128)(2,1)}, bf16[2592,128]{1,0:T(8,128)(2,1)}, u32[]{:S(2)}, u32[]{:S(2)}) collective-permute-start(bf16[2592,128]{1,0:T(8,128)(2,1)} %get-tuple-element.24.packed_ref), channel_id=1, source_target_pairs={{0,1},{1,0},{2,3},{3,2},{4,5},{5,4},{6,7},{7,6},{8,9},{9,8},{10,11... | collective-permute-start | bytes 1990664 | tf_op jit(solution)/shard_map/ppermute | solution.py:510
  5.6 18.4 %collective-permute-start.3 = (bf16[2592,128]{1,0:T(8,128)(2,1)}, bf16[2592,128]{1,0:T(8,128)(2,1)}, u32[]{:S(2)}, u32[]{:S(2)}) collective-permute-start(bf16[2592,128]{1,0:T(8,128)(2,1)} %get-tuple-element.24.packed_ref), channel_id=1, source_target_pairs={{0,4},{1,3},{2,6},{3,1},{4,0},{5,7},{6,2},{7,5},{8,12},{9,11},{10,... | collective-permute-start | bytes 1990664 | tf_op jit(solution)/shard_map/ppermute | solution.py:514
  7.1 16.9 %collective-permute-start.2 = (bf16[2592,128]{1,0:T(8,128)(2,1)}, bf16[2592,128]{1,0:T(8,128)(2,1)}, u32[]{:S(2)}, u32[]{:S(2)}) collective-permute-start(bf16[2592,128]{1,0:T(8,128)(2,1)} %get-tuple-element.24.packed_ref), channel_id=1, source_target_pairs={{0,2},{1,5},{2,0},{3,7},{4,6},{5,1},{6,4},{7,3},{8,10},{9,13},{10,... | collective-permute-start | bytes 1990664 | tf_op jit(solution)/shard_map/ppermute | solution.py:514
  9.3 14.7 %copy-start.1 = (s32[2,8,256]{2,1,0:T(8,128)}, s32[2,8,256]{2,1,0:T(8,128)S(1)}, u32[]{:S(2)}) copy-start(s32[2,8,256]{2,1,0:T(8,128)S(1)} %pad_add_fusion.2.refs_0_) | copy-start | bytes 49156
  9.3 14.7 %collective-permute-start.1 = (s32[2,8,256]{2,1,0:T(8,128)S(1)}, s32[2,8,256]{2,1,0:T(8,128)S(1)}, u32[]{:S(2)}, u32[]{:S(2)}) collective-permute-start(s32[2,8,256]{2,1,0:T(8,128)S(1)} %pad_add_fusion.2.refs_0_), channel_id=1, source_target_pairs={{0,16},{8,24},{16,0},{24,8},{1,17},{9,25},{17,1},{25,9},{2,18},{10... | collective-permute-start | bytes 49160 | tf_op jit(solution)/shard_map/ppermute | solution.py:510
  24.0 9.7 %copy-start.3 = (s32[2,8,256]{2,1,0:T(8,128)}, s32[2,8,256]{2,1,0:T(8,128)S(1)}, u32[]{:S(2)}) copy-start(s32[2,8,256]{2,1,0:T(8,128)S(1)} %collective-permute-done.1.refs_1_) | copy-start | bytes 49156
  24.0 11.7 %collective-permute-start.5 = (bf16[2592,128]{1,0:T(8,128)(2,1)}, bf16[2592,128]{1,0:T(8,128)(2,1)}, u32[]{:S(2)}, u32[]{:S(2)}) collective-permute-start(bf16[2592,128]{1,0:T(8,128)(2,1)} %collective-permute-done.2), channel_id=1, source_target_pairs={{0,4},{1,3},{2,6},{3,1},{4,0},{5,7},{6,2},{7,5},{8,12},{9,11},{10,... | collective-permute-start | bytes 1990664 | tf_op jit(solution)/shard_map/ppermute | solution.py:514
  24.9 8.9 %collective-permute-start.8 = (s32[1,4,8,128]{3,2,1,0:T(8,128)S(1)}, s32[1,4,8,128]{3,2,1,0:T(8,128)S(1)}, u32[]{:S(2)}, u32[]{:S(2)}) collective-permute-start(s32[1,4,8,128]{3,2,1,0:T(8,128)S(1)} %fusion), channel_id=1, source_target_pairs={{0,6},{1,7},{2,4},{3,5},{4,2},{5,3},{6,0},{7,1},{8,14},{9,15},{10,... | collective-permute-start | bytes 49160 | tf_op jit(solution)/shard_map/ppermute | solution.py:510
  26.5 9.2 %collective-permute-start.7 = (s32[1,4,8,128]{3,2,1,0:T(8,128)S(1)}, s32[1,4,8,128]{3,2,1,0:T(8,128)S(1)}, u32[]{:S(2)}, u32[]{:S(2)}) collective-permute-start(s32[1,4,8,128]{3,2,1,0:T(8,128)S(1)} %fusion), channel_id=1, source_target_pairs={{0,4},{1,3},{2,6},{3,1},{4,0},{5,7},{6,2},{7,5},{8,12},{9,11},{10,... | collective-permute-start | bytes 49160 | tf_op jit(solution)/shard_map/ppermute | solution.py:514
  28.0 7.7 %collective-permute-start.6 = (s32[1,4,8,128]{3,2,1,0:T(8,128)S(1)}, s32[1,4,8,128]{3,2,1,0:T(8,128)S(1)}, u32[]{:S(2)}, u32[]{:S(2)}) collective-permute-start(s32[1,4,8,128]{3,2,1,0:T(8,128)S(1)} %fusion), channel_id=1, source_target_pairs={{0,2},{1,5},{2,0},{3,7},{4,6},{5,1},{6,4},{7,3},{8,10},{9,13},{10,... | collective-permute-start | bytes 49160 | tf_op jit(solution)/shard_map/ppermute | solution.py:514
  33.7 2.6 %collective-permute-start.10 = (bf16[2592,128]{1,0:T(8,128)(2,1)}, bf16[2592,128]{1,0:T(8,128)(2,1)}, u32[]{:S(2)}, u32[]{:S(2)}) collective-permute-start(bf16[2592,128]{1,0:T(8,128)(2,1)} %collective-permute-done.2), channel_id=1, source_target_pairs={{0,1},{1,0},{2,3},{3,2},{4,5},{5,4},{6,7},{7,6},{8,9},{9,8},{10,11... | collective-permute-start | bytes 1990664 | tf_op jit(solution)/shard_map/ppermute | solution.py:510
  33.8 3.4 %collective-permute-start.11 = (bf16[2592,128]{1,0:T(8,128)(2,1)}, bf16[2592,128]{1,0:T(8,128)(2,1)}, u32[]{:S(2)}, u32[]{:S(2)}) collective-permute-start(bf16[2592,128]{1,0:T(8,128)(2,1)} %collective-permute-done.3), channel_id=1, source_target_pairs={{0,1},{1,0},{2,3},{3,2},{4,5},{5,4},{6,7},{7,6},{8,9},{9,8},{10,11... | collective-permute-start | bytes 1990664 | tf_op jit(solution)/shard_map/ppermute | solution.py:510
  35.7 2.6 %copy-start = (s32[4,4,8,128]{3,2,1,0:T(8,128)}, s32[4,4,8,128]{3,2,1,0:T(8,128)S(1)}, u32[]{:S(2)}) copy-start(s32[4,4,8,128]{3,2,1,0:T(8,128)S(1)} %pad_add_fusion.refs_2_) | copy-start | bytes 196612
  35.7 2.6 %collective-permute-start.12 = (bf16[2592,128]{1,0:T(8,128)(2,1)}, bf16[2592,128]{1,0:T(8,128)(2,1)}, u32[]{:S(2)}, u32[]{:S(2)}) collective-permute-start(bf16[2592,128]{1,0:T(8,128)(2,1)} %collective-permute-done.5.refs_6_), channel_id=1, source_target_pairs={{0,1},{1,0},{2,3},{3,2},{4,5},{5,4},{6,7},{7,6},{8,9},{9,8},{10,11... | collective-permute-start | bytes 1990664 | tf_op jit(solution)/shard_map/ppermute | solution.py:510
  35.8 2.1 %collective-permute-start.9 = (s32[4,4,8,128]{3,2,1,0:T(8,128)S(1)}, s32[4,4,8,128]{3,2,1,0:T(8,128)S(1)}, u32[]{:S(2)}, u32[]{:S(2)}) collective-permute-start(s32[4,4,8,128]{3,2,1,0:T(8,128)S(1)} %pad_add_fusion.refs_2_), channel_id=1, source_target_pairs={{0,1},{1,0},{2,3},{3,2},{4,5},{5,4},{6,7},{7,6},{8,9},{9,8},{10,11... | collective-permute-start | bytes 196616 | tf_op jit(solution)/shard_map/ppermute | solution.py:510
  37.9 0.6 %copy-start.2 = (s32[4,4,8,128]{3,2,1,0:T(8,128)}, s32[4,4,8,128]{3,2,1,0:T(8,128)S(1)}, u32[]{:S(2)}) copy-start(s32[4,4,8,128]{3,2,1,0:T(8,128)S(1)} %collective-permute-done.9.refs_3_) | copy-start | bytes 196612

commit v21 on v17

--- a/solution.py
+++ b/solution.py
@@ -378,7 +378,9 @@
     ready_refs, refs = refs[:counts[2]], refs[counts[2]:]
     (gram_any, out_ref, gram_ref, decoded, whole_ref, rest_ref, total, lines, foot_rows, scalars, *refs) = refs
     late_blocks, refs = refs[:counts[1]], refs[counts[1]:]
-    gram_semaphores, ready_semaphores, late_semaphores, scalar_semaphore = refs
+    held_columns, refs = refs[:counts[3]], refs[counts[3]:]
+    held_lines, refs = refs[:counts[0]], refs[counts[0]:]
+    gram_semaphores, ready_semaphores, late_semaphores, scalar_semaphore, line_semaphores = refs
     group = pl.program_id(0)
     directions, pupil = whole_ref.shape[0], 2 * whole_ref.shape[2]
     depth = whole_ref.shape[3]
@@ -396,6 +398,10 @@
                 copy.start()
             return copies
 
+        line_copies = started([
+            pltpu.make_async_copy(source, target, line_semaphores.at[n])
+            for n, (source, target) in enumerate(zip([*columns_refs, *lines_refs], [*held_columns, *held_lines]))
+        ])
         late_copies = started([
             pltpu.make_async_copy(late_refs[n], late_blocks[n], late_semaphores.at[n]) for n in range(counts[1])
         ])
@@ -404,7 +410,9 @@
             pltpu.make_async_copy(block, decoded.at[pl.ds(n * rows, rows)], ready_semaphores.at[n])
             for n, block in enumerate([ref.at[m] for ref in ready_refs for m in range(ref.shape[0])])
         ])
-        held = [ref.at[n] for ref in lines_refs for n in range(ref.shape[0])]
+        for copy in line_copies:
+            copy.wait()
+        held = [ref.at[n] for ref in held_lines for n in range(ref.shape[0])]
         feet = [None] * blocks
         for place, ref in zip(places, held):
             for d in range(directions):
@@ -416,7 +424,7 @@
         foot_rows[...] = row_place(feet // shard_rows, staged) * rows + feet % shard_rows
         to_scalars = pltpu.make_async_copy(foot_rows, scalars, scalar_semaphore.at[0])
         to_scalars.start()
-        columns = [ref.at[n] for ref in columns_refs for n in range(ref.shape[0])]
+        columns = [ref.at[n] for ref in held_columns for n in range(ref.shape[0])]
         build_differences(columns, whole_ref, rest_ref, mirrors, samples)
         for copy in late_copies:
             copy.wait()
@@ -478,7 +486,7 @@
     flops = 2 * padded * mirrors * samples * pupil * directions * surface_rows // 2
     vmem, anywhere = pl.BlockSpec(memory_space=pltpu.VMEM), pl.BlockSpec(memory_space=pl.ANY)
     counts = (len(lines), len(late), len(ready), len(columns))
-    semaphores = [mirrors, blocks, max(len(late), 1), 1]
+    semaphores = [mirrors, blocks, max(len(late), 1), 1, len(columns) + len(lines)]
     held = -(-directions * (shard_rows // 2) // 8) * 8
     return pl.pallas_call(
         functools.partial(
@@ -486,7 +494,7 @@
         ),
         grid=(width // lanes,),
         out_shape=jax.ShapeDtypeStruct((own, directions, width), jnp.bfloat16),
-        in_specs=[vmem] * (len(columns) + len(lines)) + [anywhere] * (len(late) + len(ready) + 1),
+        in_specs=[anywhere] * (len(columns) + len(lines) + len(late) + len(ready) + 1),
         out_specs=pl.BlockSpec((own, directions, lanes), lambda s: (0, 0, s)),
         scratch_shapes=[
             pltpu.VMEM((acts, padded), jnp.bfloat16),
@@ -497,7 +505,7 @@
             pltpu.VMEM((blocks, held, LANES), jnp.int32),
             pltpu.VMEM((blocks, LANES), jnp.int32),
             pltpu.SMEM((blocks, LANES), jnp.int32),
-            *[pltpu.VMEM(block.shape, block.dtype) for block in late],
+            *[pltpu.VMEM(block.shape, block.dtype) for block in [*late, *columns, *lines]],
             *[pltpu.SemaphoreType.DMA((count,)) for count in semaphores],
         ],
         compiler_params=pltpu.CompilerParams(vmem_limit_bytes=VMEM_BYTES),

time: 53.9 us -> 53.8 us (level)
  no operation moved by 1% of the time
where the time goes in v21:
time: 53.8 us; the launch traced here: 53.5 us
  Pallas kernels  34.9 us (65%)
  starting transfers between devices  14.7 us (27%)
  waiting for transfers between devices  2.89 us (5%)
  other arithmetic  0.71 us (1%)
    pallas_call x1, Pallas kernels, decode(): pl.pallas_call(functools.partial(decode_kernel, row_shape, surface_rows,...  14.9 us
    pallas_call x1, Pallas kernels, gram(): pl.pallas_call(functools.partial(gram_kernel, row_shape, surface_rows), g...  12.1 us
    ppermute x8, starting transfers between devices, swap(): lax.ppermute(block, axis, [(i, i ^ distance) for i in range(lax.axis_size...  8.9 us
    ppermute x5, starting transfers between devices, turn(): lax.ppermute(block, 'row', [(i, i ^ (odd if i % 2 else even)) for i in ra...  5.78 us
    pallas_call x1, Pallas kernels, bands(): pl.pallas_call(functools.partial(bands_kernel, row_shape, surface_rows, f...  5.29 us
    pallas_call x1, Pallas kernels, pack(): pl.pallas_call(pack_kernel, out_shape=[jax.ShapeDtypeStruct((mirrors * ro...  2.57 us
    ppermute x8, waiting for transfers between devices, swap(): lax.ppermute(block, axis, [(i, i ^ distance) for i in range(lax.axis_size...  2.04 us
  transfers between devices with their start and end apart: 13, of which 4 were waited for; matrix products, arithmetic and copies ran while one was open for 1% of the time, Pallas kernels for 32%

profile of v21, /device:TPU:0, one launch (start us, length us, event | category | flops | bytes accessed | tf_op | source)
XLA Modules:
  0.0 53.5 jit_solution(14782507063468541542)
XLA Ops:
  0.0 2.6 %pack_influence.1 = (bf16[2592,128]{1,0:T(8,128)(2,1)}, s32[8,256]{1,0:T(8,128)}) custom-call(bf16[3,4,144,192]{3,2,1,0:T(8,128)(2,1)} %bitcast.11, s32[3,1,4]{2,1,0:T(1,128)} %bitcast.15, s32[3,1,160]{2,1,0:T(1,128)} %bitcast.14, s32[1,2,80]{2,1,0:T(2,128)} %valid_ref.1), custom_call_target="tpu_custom_call" | custom-call | bytes 995328 | tf_op jit(solution)/shard_map/pack_influence/pallas_call | solution.py:65
  2.6 3.0 %collective-permute-start = (s32[8,256]{1,0:T(8,128)}, s32[8,256]{1,0:T(8,128)S(1)}, u32[]{:S(2)}, u32[]{:S(2)}) collective-permute-start(s32[8,256]{1,0:T(8,128)} %get-tuple-element.20), channel_id=1, source_target_pairs={{0,8},{8,0},{16,24},{24,16},{1,9},{9,1},{17,25},{25,17},{2,10},{10... | collective-permute-start | bytes 24584 | tf_op jit(solution)/shard_map/ppermute | solution.py:518
  5.6 0.0 collective-permute-start.4
  5.6 1.5 %collective-permute-start.3 = (bf16[2592,128]{1,0:T(8,128)(2,1)}, bf16[2592,128]{1,0:T(8,128)(2,1)}, u32[]{:S(2)}, u32[]{:S(2)}) collective-permute-start(bf16[2592,128]{1,0:T(8,128)(2,1)} %get-tuple-element.23.packed_ref), channel_id=1, source_target_pairs={{0,4},{1,3},{2,6},{3,1},{4,0},{5,7},{6,2},{7,5},{8,12},{9,11},{10,... | collective-permute-start | bytes 1990664 | tf_op jit(solution)/shard_map/ppermute | solution.py:522
  7.1 1.5 %collective-permute-start.2 = (bf16[2592,128]{1,0:T(8,128)(2,1)}, bf16[2592,128]{1,0:T(8,128)(2,1)}, u32[]{:S(2)}, u32[]{:S(2)}) collective-permute-start(bf16[2592,128]{1,0:T(8,128)(2,1)} %get-tuple-element.23.packed_ref), channel_id=1, source_target_pairs={{0,2},{1,5},{2,0},{3,7},{4,6},{5,1},{6,4},{7,3},{8,10},{9,13},{10,... | collective-permute-start | bytes 1990664 | tf_op jit(solution)/shard_map/ppermute | solution.py:522
  8.6 0.0 collective-permute-done
  8.6 0.7 %pad_add_fusion.2.refs_0_ = s32[2,8,256]{2,1,0:T(8,128)S(1)} fusion(s32[1,8,256]{2,1,0:T(8,128)S(1)} %bitcast.13, s32[1,8,256]{2,1,0:T(8,128)} %bitcast.12), kind=kLoop, calls=%fused_computation.3 | loop fusion | flops 4096 | bytes 32768 | tf_op jit(solution)/shard_map/stack | solution.py:551
  9.3 0.0 copy-start.1
  9.3 2.6 %collective-permute-start.1 = (s32[2,8,256]{2,1,0:T(8,128)S(1)}, s32[2,8,256]{2,1,0:T(8,128)S(1)}, u32[]{:S(2)}, u32[]{:S(2)}) collective-permute-start(s32[2,8,256]{2,1,0:T(8,128)S(1)} %pad_add_fusion.2.refs_0_), channel_id=1, source_target_pairs={{0,16},{8,24},{16,0},{24,8},{1,17},{9,25},{17,1},{25,9},{2,18},{10... | collective-permute-start | bytes 49160 | tf_op jit(solution)/shard_map/ppermute | solution.py:518
  11.9 12.1 %gram_rows.1 = (bf16[6912,224]{1,0:T(8,128)(2,1)}, bf16[1,12,192,224]{3,2,1,0:T(8,128)(2,1)}) custom-call(s32[3,48,48]{2,1,0:T(8,128)} %table_ref.1, s32[16,128]{1,0:T(8,128)} %bitcast.16, bf16[2592,128]{1,0:T(8,128)(2,1)} %get-tuple-element.23.packed_ref), custom_call_target="tpu_custom_call" | custom-call | flops 6341787648 | bytes 3096576 | tf_op jit(solution)/shard_map/gram_rows/pallas_call | solution.py:194
  24.0 0.0 collective-permute-done.1.refs_1_
  24.0 0.0 copy-done.1
  24.0 0.0 copy-start.3
  24.0 0.0 collective-permute-done.3
  24.0 0.0 collective-permute-done.2
  24.0 0.9 %collective-permute-start.5 = (bf16[2592,128]{1,0:T(8,128)(2,1)}, bf16[2592,128]{1,0:T(8,128)(2,1)}, u32[]{:S(2)}, u32[]{:S(2)}) collective-permute-start(bf16[2592,128]{1,0:T(8,128)(2,1)} %collective-permute-done.2), channel_id=1, source_target_pairs={{0,4},{1,3},{2,6},{3,1},{4,0},{5,7},{6,2},{7,5},{8,12},{9,11},{10,... | collective-permute-start | bytes 1990664 | tf_op jit(solution)/shard_map/ppermute | solution.py:522
  24.9 1.6 %collective-permute-start.8 = (s32[1,4,8,128]{3,2,1,0:T(8,128)S(1)}, s32[1,4,8,128]{3,2,1,0:T(8,128)S(1)}, u32[]{:S(2)}, u32[]{:S(2)}) collective-permute-start(s32[1,4,8,128]{3,2,1,0:T(8,128)S(1)} %fusion), channel_id=1, source_target_pairs={{0,6},{1,7},{2,4},{3,5},{4,2},{5,3},{6,0},{7,1},{8,14},{9,15},{10,... | collective-permute-start | bytes 49160 | tf_op jit(solution)/shard_map/ppermute | solution.py:518
  26.5 1.5 %collective-permute-start.7 = (s32[1,4,8,128]{3,2,1,0:T(8,128)S(1)}, s32[1,4,8,128]{3,2,1,0:T(8,128)S(1)}, u32[]{:S(2)}, u32[]{:S(2)}) collective-permute-start(s32[1,4,8,128]{3,2,1,0:T(8,128)S(1)} %fusion), channel_id=1, source_target_pairs={{0,4},{1,3},{2,6},{3,1},{4,0},{5,7},{6,2},{7,5},{8,12},{9,11},{10,... | collective-permute-start | bytes 49160 | tf_op jit(solution)/shard_map/ppermute | solution.py:522
  28.0 0.4 collective-permute-start.6
  28.4 0.0 collective-permute-done.4
  28.4 0.0 collective-permute-start.10
  28.4 5.3 %bands.1.refs_9_ = bf16[3,12,192,224]{3,2,1,0:T(8,128)(2,1)} custom-call(bf16[6912,224]{1,0:T(8,128)(2,1)} %get-tuple-element.25.gram_any.refs_10_, bf16[1,2592,128]{2,1,0:T(8,128)(2,1)} %bitcast.7.refs_0_, bf16[1,2592,128]{2,1,0:T(8,128)(2,1)} %bitcast.8.refs_1_, bf16[1,2592,128]{2,1,0:T(8,128)(2,1)} %bitcast.9.refs_2_), custom_call_target="tpu_custom_call" | custom-call | flops 792723456 | bytes 4128768 | tf_op jit(solution)/shard_map/bands/pallas_call | solution.py:322
  33.7 0.0 copy-done.3
  33.7 0.0 collective-permute-done.8
  33.7 1.1 %collective-permute-start.11 = (bf16[2592,128]{1,0:T(8,128)(2,1)}, bf16[2592,128]{1,0:T(8,128)(2,1)}, u32[]{:S(2)}, u32[]{:S(2)}) collective-permute-start(bf16[2592,128]{1,0:T(8,128)(2,1)} %collective-permute-done.3), channel_id=1, source_target_pairs={{0,1},{1,0},{2,3},{3,2},{4,5},{5,4},{6,7},{7,6},{8,9},{9,8},{10,11... | collective-permute-start | bytes 1990664 | tf_op jit(solution)/shard_map/ppermute | solution.py:518
  34.8 0.8 %collective-permute-done.7 = s32[1,4,8,128]{3,2,1,0:T(8,128)S(1)} collective-permute-done((s32[1,4,8,128]{3,2,1,0:T(8,128)S(1)}, s32[1,4,8,128]{3,2,1,0:T(8,128)S(1)}, u32[]{:S(2)}, u32[]{:S(2)}) %collective-permute-start.7) | collective-permute-done | bytes 16416 | tf_op jit(solution)/shard_map/ppermute | solution.py:522
  35.7 0.0 collective-permute-done.6
  35.7 0.0 copy-start
  35.7 0.0 collective-permute-done.5.refs_6_
  35.7 0.1 collective-permute-start.12
  35.8 0.5 collective-permute-start.9
  36.3 0.0 collective-permute-done.10.refs_4_
  36.3 0.6 %collective-permute-done.11.refs_5_ = bf16[2592,128]{1,0:T(8,128)(2,1)} collective-permute-done((bf16[2592,128]{1,0:T(8,128)(2,1)}, bf16[2592,128]{1,0:T(8,128)(2,1)}, u32[]{:S(2)}, u32[]{:S(2)}) %collective-permute-start.11) | collective-permute-done | bytes 663584 | tf_op jit(solution)/shard_map/ppermute | solution.py:518
  36.9 1.0 %collective-permute-done.9.refs_3_ = s32[4,4,8,128]{3,2,1,0:T(8,128)S(1)} collective-permute-done((s32[4,4,8,128]{3,2,1,0:T(8,128)S(1)}, s32[4,4,8,128]{3,2,1,0:T(8,128)S(1)}, u32[]{:S(2)}, u32[]{:S(2)}) %collective-permute-start.9) | collective-permute-done | bytes 65568 | tf_op jit(solution)/shard_map/ppermute | solution.py:518
  37.9 0.0 copy-start.2
  37.9 0.4 collective-permute-done.12.refs_7_
  38.3 0.0 copy-done
  38.3 0.2 copy-done.2
  38.5 14.9 %decode.1 = bf16[216,4,2560]{2,1,0:T(4,128)(2,1)} custom-call(s32[2,8,256]{2,1,0:T(8,128)} %copy-done.1, s32[2,8,256]{2,1,0:T(8,128)} %copy-done.3, s32[4,4,8,128]{3,2,1,0:T(8,128)} %copy-done, s32[4,4,8,128]{3,2,1,0:T(8,128)} %copy-done.2, bf16[2592,128]{1,0:T(8,128)(2,1)} %collective-permute-done.10.refs_4_, ...), custom_call_target="tpu_custom_call" | custom-call | flops 2642411520 | bytes 4423680 | tf_op jit(solution)/shard_map/decode/pallas_call | solution.py:491
  (2 shorter events, 0.0 us)
Async XLA Ops:
  2.6 6.0 %collective-permute-start = (s32[8,256]{1,0:T(8,128)}, s32[8,256]{1,0:T(8,128)S(1)}, u32[]{:S(2)}, u32[]{:S(2)}) collective-permute-start(s32[8,256]{1,0:T(8,128)} %get-tuple-element.20), channel_id=1, source_target_pairs={{0,8},{8,0},{16,24},{24,16},{1,9},{9,1},{17,25},{25,17},{2,10},{10... | collective-permute-start | bytes 24584 | tf_op jit(solution)/shard_map/ppermute | solution.py:518
  5.6 22.8 %collective-permute-start.4 = (bf16[2592,128]{1,0:T(8,128)(2,1)}, bf16[2592,128]{1,0:T(8,128)(2,1)}, u32[]{:S(2)}, u32[]{:S(2)}) collective-permute-start(bf16[2592,128]{1,0:T(8,128)(2,1)} %get-tuple-element.23.packed_ref), channel_id=1, source_target_pairs={{0,1},{1,0},{2,3},{3,2},{4,5},{5,4},{6,7},{7,6},{8,9},{9,8},{10,11... | collective-permute-start | bytes 1990664 | tf_op jit(solution)/shard_map/ppermute | solution.py:518
  5.6 18.4 %collective-permute-start.3 = (bf16[2592,128]{1,0:T(8,128)(2,1)}, bf16[2592,128]{1,0:T(8,128)(2,1)}, u32[]{:S(2)}, u32[]{:S(2)}) collective-permute-start(bf16[2592,128]{1,0:T(8,128)(2,1)} %get-tuple-element.23.packed_ref), channel_id=1, source_target_pairs={{0,4},{1,3},{2,6},{3,1},{4,0},{5,7},{6,2},{7,5},{8,12},{9,11},{10,... | collective-permute-start | bytes 1990664 | tf_op jit(solution)/shard_map/ppermute | solution.py:522
  7.1 16.9 %collective-permute-start.2 = (bf16[2592,128]{1,0:T(8,128)(2,1)}, bf16[2592,128]{1,0:T(8,128)(2,1)}, u32[]{:S(2)}, u32[]{:S(2)}) collective-permute-start(bf16[2592,128]{1,0:T(8,128)(2,1)} %get-tuple-element.23.packed_ref), channel_id=1, source_target_pairs={{0,2},{1,5},{2,0},{3,7},{4,6},{5,1},{6,4},{7,3},{8,10},{9,13},{10,... | collective-permute-start | bytes 1990664 | tf_op jit(solution)/shard_map/ppermute | solution.py:522
  9.3 14.7 %copy-start.1 = (s32[2,8,256]{2,1,0:T(8,128)}, s32[2,8,256]{2,1,0:T(8,128)S(1)}, u32[]{:S(2)}) copy-start(s32[2,8,256]{2,1,0:T(8,128)S(1)} %pad_add_fusion.2.refs_0_) | copy-start | bytes 49156
  9.3 14.7 %collective-permute-start.1 = (s32[2,8,256]{2,1,0:T(8,128)S(1)}, s32[2,8,256]{2,1,0:T(8,128)S(1)}, u32[]{:S(2)}, u32[]{:S(2)}) collective-permute-start(s32[2,8,256]{2,1,0:T(8,128)S(1)} %pad_add_fusion.2.refs_0_), channel_id=1, source_target_pairs={{0,16},{8,24},{16,0},{24,8},{1,17},{9,25},{17,1},{25,9},{2,18},{10... | collective-permute-start | bytes 49160 | tf_op jit(solution)/shard_map/ppermute | solution.py:518
  24.0 9.7 %copy-start.3 = (s32[2,8,256]{2,1,0:T(8,128)}, s32[2,8,256]{2,1,0:T(8,128)S(1)}, u32[]{:S(2)}) copy-start(s32[2,8,256]{2,1,0:T(8,128)S(1)} %collective-permute-done.1.refs_1_) | copy-start | bytes 49156
  24.0 11.7 %collective-permute-start.5 = (bf16[2592,128]{1,0:T(8,128)(2,1)}, bf16[2592,128]{1,0:T(8,128)(2,1)}, u32[]{:S(2)}, u32[]{:S(2)}) collective-permute-start(bf16[2592,128]{1,0:T(8,128)(2,1)} %collective-permute-done.2), channel_id=1, source_target_pairs={{0,4},{1,3},{2,6},{3,1},{4,0},{5,7},{6,2},{7,5},{8,12},{9,11},{10,... | collective-permute-start | bytes 1990664 | tf_op jit(solution)/shard_map/ppermute | solution.py:522
  24.9 8.8 %collective-permute-start.8 = (s32[1,4,8,128]{3,2,1,0:T(8,128)S(1)}, s32[1,4,8,128]{3,2,1,0:T(8,128)S(1)}, u32[]{:S(2)}, u32[]{:S(2)}) collective-permute-start(s32[1,4,8,128]{3,2,1,0:T(8,128)S(1)} %fusion), channel_id=1, source_target_pairs={{0,6},{1,7},{2,4},{3,5},{4,2},{5,3},{6,0},{7,1},{8,14},{9,15},{10,... | collective-permute-start | bytes 49160 | tf_op jit(solution)/shard_map/ppermute | solution.py:518
  26.5 9.2 %collective-permute-start.7 = (s32[1,4,8,128]{3,2,1,0:T(8,128)S(1)}, s32[1,4,8,128]{3,2,1,0:T(8,128)S(1)}, u32[]{:S(2)}, u32[]{:S(2)}) collective-permute-start(s32[1,4,8,128]{3,2,1,0:T(8,128)S(1)} %fusion), channel_id=1, source_target_pairs={{0,4},{1,3},{2,6},{3,1},{4,0},{5,7},{6,2},{7,5},{8,12},{9,11},{10,... | collective-permute-start | bytes 49160 | tf_op jit(solution)/shard_map/ppermute | solution.py:522
  28.0 7.7 %collective-permute-start.6 = (s32[1,4,8,128]{3,2,1,0:T(8,128)S(1)}, s32[1,4,8,128]{3,2,1,0:T(8,128)S(1)}, u32[]{:S(2)}, u32[]{:S(2)}) collective-permute-start(s32[1,4,8,128]{3,2,1,0:T(8,128)S(1)} %fusion), channel_id=1, source_target_pairs={{0,2},{1,5},{2,0},{3,7},{4,6},{5,1},{6,4},{7,3},{8,10},{9,13},{10,... | collective-permute-start | bytes 49160 | tf_op jit(solution)/shard_map/ppermute | solution.py:522
  28.4 7.9 %collective-permute-start.10 = (bf16[2592,128]{1,0:T(8,128)(2,1)}, bf16[2592,128]{1,0:T(8,128)(2,1)}, u32[]{:S(2)}, u32[]{:S(2)}) collective-permute-start(bf16[2592,128]{1,0:T(8,128)(2,1)} %collective-permute-done.2), channel_id=1, source_target_pairs={{0,1},{1,0},{2,3},{3,2},{4,5},{5,4},{6,7},{7,6},{8,9},{9,8},{10,11... | collective-permute-start | bytes 1990664 | tf_op jit(solution)/shard_map/ppermute | solution.py:518
  33.7 3.2 %collective-permute-start.11 = (bf16[2592,128]{1,0:T(8,128)(2,1)}, bf16[2592,128]{1,0:T(8,128)(2,1)}, u32[]{:S(2)}, u32[]{:S(2)}) collective-permute-start(bf16[2592,128]{1,0:T(8,128)(2,1)} %collective-permute-done.3), channel_id=1, source_target_pairs={{0,1},{1,0},{2,3},{3,2},{4,5},{5,4},{6,7},{7,6},{8,9},{9,8},{10,11... | collective-permute-start | bytes 1990664 | tf_op jit(solution)/shard_map/ppermute | solution.py:518
  35.7 2.6 %copy-start = (s32[4,4,8,128]{3,2,1,0:T(8,128)}, s32[4,4,8,128]{3,2,1,0:T(8,128)S(1)}, u32[]{:S(2)}) copy-start(s32[4,4,8,128]{3,2,1,0:T(8,128)S(1)} %pad_add_fusion.refs_2_) | copy-start | bytes 196612
  35.7 2.6 %collective-permute-start.12 = (bf16[2592,128]{1,0:T(8,128)(2,1)}, bf16[2592,128]{1,0:T(8,128)(2,1)}, u32[]{:S(2)}, u32[]{:S(2)}) collective-permute-start(bf16[2592,128]{1,0:T(8,128)(2,1)} %collective-permute-done.5.refs_6_), channel_id=1, source_target_pairs={{0,1},{1,0},{2,3},{3,2},{4,5},{5,4},{6,7},{7,6},{8,9},{9,8},{10,11... | collective-permute-start | bytes 1990664 | tf_op jit(solution)/shard_map/ppermute | solution.py:518
  35.8 2.1 %collective-permute-start.9 = (s32[4,4,8,128]{3,2,1,0:T(8,128)S(1)}, s32[4,4,8,128]{3,2,1,0:T(8,128)S(1)}, u32[]{:S(2)}, u32[]{:S(2)}) collective-permute-start(s32[4,4,8,128]{3,2,1,0:T(8,128)S(1)} %pad_add_fusion.refs_2_), channel_id=1, source_target_pairs={{0,1},{1,0},{2,3},{3,2},{4,5},{5,4},{6,7},{7,6},{8,9},{9,8},{10,11... | collective-permute-start | bytes 196616 | tf_op jit(solution)/shard_map/ppermute | solution.py:518
  37.9 0.6 %copy-start.2 = (s32[4,4,8,128]{3,2,1,0:T(8,128)}, s32[4,4,8,128]{3,2,1,0:T(8,128)S(1)}, u32[]{:S(2)}) copy-start(s32[4,4,8,128]{3,2,1,0:T(8,128)S(1)} %collective-permute-done.9.refs_3_) | copy-start | bytes 196612

commit v22 on v21

--- a/solution.py
+++ b/solution.py
@@ -228,7 +228,7 @@
         return place
     row = lax.axis_index("row")
     core = row & 1
-    return row ^ [0, 1, 2 << core, 4 >> core, (4 >> core) | 1, (2 << core) | 1, 6, 7][place]
+    return row ^ [0, 2 << core, 4 >> core, 1, (4 >> core) | 1, (2 << core) | 1, 6, 7][place]
 
 
 def row_place(block, staged):
@@ -237,10 +237,10 @@
     row = lax.axis_index("row")
     core = row & 1
     distance = block ^ row
-    near = jnp.where(distance == 2 << core, 2, 3)
+    near = jnp.where(distance == 2 << core, 1, 2)
     far = jnp.where(distance == (4 >> core) | 1, 4, 5)
     middle = jnp.where(distance & 1 == 0, near, far)
-    return jnp.where((distance >= 2) & (distance < 6), middle, distance)
+    return jnp.where((distance >= 2) & (distance < 6), middle, jnp.where(distance == 1, 3, distance))
 
 
 def band_product(source, q, row_shape, block, surface_rows, gram_ref):
@@ -555,20 +555,22 @@
         distance *= 2
     held = jnp.concatenate(lines, axis=0)[None, :, :, :LANES]
     gram_rows, own_rows = gram(actuator_codes, pokes, packed, own, row_shape, surface_rows)
-    gram_rows, first, second, held = lax.optimization_barrier((gram_rows, first, second, held))
+    gram_rows, first, second, held, sibling = lax.optimization_barrier(
+        (gram_rows, first, second, held, sibling)
+    )
     diagonal = turn(first, 4, 2)
     first_sibling = swap(first, "row", 1)
     mine = [held, turn(held, 2, 4), turn(held, 4, 2), swap(held, "row", 6)]
-    sources = [source[None] for source in (sibling, first, second)]
+    sources = [source[None] for source in (first, second)]
     near, = bands(gram_rows, sources, 1, staged, row_shape, surface_rows)
     near, second = lax.optimization_barrier((near, second))
     second_sibling = swap(second, "row", 1)
     mine = jnp.concatenate(mine, axis=0)
     near, diagonal, mine = lax.optimization_barrier((near, diagonal, mine))
     theirs = swap(mine, "row", 1)
-    late = [first_sibling, second_sibling, diagonal, swap(diagonal, "row", 1)]
+    late = [sibling, first_sibling, second_sibling, diagonal, swap(diagonal, "row", 1)]
     return decode(
-        lines, [mine, theirs], [0, 2, 3, 6, 1, 4, 5, 7], late, [own_rows, near], gram_rows, own, row_shape,
+        lines, [mine, theirs], [0, 1, 2, 6, 3, 4, 5, 7], late, [own_rows, near], gram_rows, own, row_shape,
         surface_rows, pupil, norm, staged,
     )
 

time: 53.8 us -> 53.6 us (level)
  Pallas kernels: 34.9 us -> 33.5 us
  starting transfers between devices: 14.7 us -> 16 us
    ppermute x8, starting transfers between devices: 8.9 us -> 10.2 us  [swap(): lax.ppermute(block, axis, [(i, i ^ distance) for i in range(lax.axis_size...]
    pallas_call x1, Pallas kernels: 5.29 us -> 4.07 us  [bands(): pl.pallas_call(functools.partial(bands_kernel, row_shape, surface_rows, f...]
  transfers between devices with their start and end apart: 13 -> 13, of which waited for: 4 -> 4; matrix products, arithmetic and copies ran while one was open for 1% -> 1% of each run, Pallas kernels for 32% -> 30%
where the time goes in v22:
time: 53.6 us; the launch traced here: 53.3 us
  Pallas kernels  33.5 us (62%)
  starting transfers between devices  16 us (30%)
  waiting for transfers between devices  2.83 us (5%)
  other arithmetic  0.71 us (1%)
    pallas_call x1, Pallas kernels, decode(): pl.pallas_call(functools.partial(decode_kernel, row_shape, surface_rows,...  14.9 us
    pallas_call x1, Pallas kernels, gram(): pl.pallas_call(functools.partial(gram_kernel, row_shape, surface_rows), g...  12 us
    ppermute x8, starting transfers between devices, swap(): lax.ppermute(block, axis, [(i, i ^ distance) for i in range(lax.axis_size...  10.2 us
    ppermute x5, starting transfers between devices, turn(): lax.ppermute(block, 'row', [(i, i ^ (odd if i % 2 else even)) for i in ra...  5.72 us
    pallas_call x1, Pallas kernels, bands(): pl.pallas_call(functools.partial(bands_kernel, row_shape, surface_rows, f...  4.07 us
    pallas_call x1, Pallas kernels, pack(): pl.pallas_call(pack_kernel, out_shape=[jax.ShapeDtypeStruct((mirrors * ro...  2.57 us
    ppermute x8, waiting for transfers between devices, swap(): lax.ppermute(block, axis, [(i, i ^ distance) for i in range(lax.axis_size...  2.04 us
  transfers between devices with their start and end apart: 13, of which 4 were waited for; matrix products, arithmetic and copies ran while one was open for 1% of the time, Pallas kernels for 30%

profile of v22, /device:TPU:0, one launch (start us, length us, event | category | flops | bytes accessed | tf_op | source)
XLA Modules:
  0.0 53.3 jit_solution(14727612661157956706)
XLA Ops:
  0.0 2.6 %pack_influence.1 = (bf16[2592,128]{1,0:T(8,128)(2,1)}, s32[8,256]{1,0:T(8,128)}) custom-call(bf16[3,4,144,192]{3,2,1,0:T(8,128)(2,1)} %bitcast.10, s32[3,1,4]{2,1,0:T(1,128)} %bitcast.14, s32[3,1,160]{2,1,0:T(1,128)} %bitcast.13, s32[1,2,80]{2,1,0:T(2,128)} %valid_ref.1), custom_call_target="tpu_custom_call" | custom-call | bytes 995328 | tf_op jit(solution)/shard_map/pack_influence/pallas_call | solution.py:65
  2.6 3.0 %collective-permute-start = (s32[8,256]{1,0:T(8,128)}, s32[8,256]{1,0:T(8,128)S(1)}, u32[]{:S(2)}, u32[]{:S(2)}) collective-permute-start(s32[8,256]{1,0:T(8,128)} %get-tuple-element.21), channel_id=1, source_target_pairs={{0,8},{8,0},{16,24},{24,16},{1,9},{9,1},{17,25},{25,17},{2,10},{10... | collective-permute-start | bytes 24584 | tf_op jit(solution)/shard_map/ppermute | solution.py:518
  5.6 0.0 collective-permute-start.4
  5.6 1.5 %collective-permute-start.3 = (bf16[2592,128]{1,0:T(8,128)(2,1)}, bf16[2592,128]{1,0:T(8,128)(2,1)}, u32[]{:S(2)}, u32[]{:S(2)}) collective-permute-start(bf16[2592,128]{1,0:T(8,128)(2,1)} %get-tuple-element.24.packed_ref), channel_id=1, source_target_pairs={{0,4},{1,3},{2,6},{3,1},{4,0},{5,7},{6,2},{7,5},{8,12},{9,11},{10,... | collective-permute-start | bytes 1990664 | tf_op jit(solution)/shard_map/ppermute | solution.py:522
  7.1 1.5 %collective-permute-start.2 = (bf16[2592,128]{1,0:T(8,128)(2,1)}, bf16[2592,128]{1,0:T(8,128)(2,1)}, u32[]{:S(2)}, u32[]{:S(2)}) collective-permute-start(bf16[2592,128]{1,0:T(8,128)(2,1)} %get-tuple-element.24.packed_ref), channel_id=1, source_target_pairs={{0,2},{1,5},{2,0},{3,7},{4,6},{5,1},{6,4},{7,3},{8,10},{9,13},{10,... | collective-permute-start | bytes 1990664 | tf_op jit(solution)/shard_map/ppermute | solution.py:522
  8.6 0.0 collective-permute-done
  8.6 0.7 %pad_add_fusion.2.refs_0_ = s32[2,8,256]{2,1,0:T(8,128)S(1)} fusion(s32[1,8,256]{2,1,0:T(8,128)S(1)} %bitcast.12, s32[1,8,256]{2,1,0:T(8,128)} %bitcast.11), kind=kLoop, calls=%fused_computation.3 | loop fusion | flops 4096 | bytes 32768 | tf_op jit(solution)/shard_map/stack | solution.py:551
  9.3 0.0 copy-start.1
  9.3 2.6 %collective-permute-start.1 = (s32[2,8,256]{2,1,0:T(8,128)S(1)}, s32[2,8,256]{2,1,0:T(8,128)S(1)}, u32[]{:S(2)}, u32[]{:S(2)}) collective-permute-start(s32[2,8,256]{2,1,0:T(8,128)S(1)} %pad_add_fusion.2.refs_0_), channel_id=1, source_target_pairs={{0,16},{8,24},{16,0},{24,8},{1,17},{9,25},{17,1},{25,9},{2,18},{10... | collective-permute-start | bytes 49160 | tf_op jit(solution)/shard_map/ppermute | solution.py:518
  11.9 12.0 %gram_rows.1 = (bf16[6912,224]{1,0:T(8,128)(2,1)}, bf16[1,12,192,224]{3,2,1,0:T(8,128)(2,1)}) custom-call(s32[3,48,48]{2,1,0:T(8,128)} %table_ref.1, s32[16,128]{1,0:T(8,128)} %bitcast.15, bf16[2592,128]{1,0:T(8,128)(2,1)} %get-tuple-element.24.packed_ref), custom_call_target="tpu_custom_call" | custom-call | flops 6341787648 | bytes 3096576 | tf_op jit(solution)/shard_map/gram_rows/pallas_call | solution.py:194
  23.9 0.0 collective-permute-done.1.refs_1_
  23.9 0.0 copy-done.1
  23.9 0.0 copy-start.3
  23.9 0.0 collective-permute-done.4.refs_4_
  24.0 0.0 collective-permute-done.3
  24.0 0.0 collective-permute-done.2
  24.0 0.9 %collective-permute-start.5 = (bf16[2592,128]{1,0:T(8,128)(2,1)}, bf16[2592,128]{1,0:T(8,128)(2,1)}, u32[]{:S(2)}, u32[]{:S(2)}) collective-permute-start(bf16[2592,128]{1,0:T(8,128)(2,1)} %collective-permute-done.2), channel_id=1, source_target_pairs={{0,4},{1,3},{2,6},{3,1},{4,0},{5,7},{6,2},{7,5},{8,12},{9,11},{10,... | collective-permute-start | bytes 1990664 | tf_op jit(solution)/shard_map/ppermute | solution.py:522
  24.8 1.6 %collective-permute-start.8 = (s32[1,4,8,128]{3,2,1,0:T(8,128)S(1)}, s32[1,4,8,128]{3,2,1,0:T(8,128)S(1)}, u32[]{:S(2)}, u32[]{:S(2)}) collective-permute-start(s32[1,4,8,128]{3,2,1,0:T(8,128)S(1)} %fusion), channel_id=1, source_target_pairs={{0,6},{1,7},{2,4},{3,5},{4,2},{5,3},{6,0},{7,1},{8,14},{9,15},{10,... | collective-permute-start | bytes 49160 | tf_op jit(solution)/shard_map/ppermute | solution.py:518
  26.5 1.5 %collective-permute-start.7 = (s32[1,4,8,128]{3,2,1,0:T(8,128)S(1)}, s32[1,4,8,128]{3,2,1,0:T(8,128)S(1)}, u32[]{:S(2)}, u32[]{:S(2)}) collective-permute-start(s32[1,4,8,128]{3,2,1,0:T(8,128)S(1)} %fusion), channel_id=1, source_target_pairs={{0,4},{1,3},{2,6},{3,1},{4,0},{5,7},{6,2},{7,5},{8,12},{9,11},{10,... | collective-permute-start | bytes 49160 | tf_op jit(solution)/shard_map/ppermute | solution.py:522
  28.0 0.3 collective-permute-start.6
  28.3 0.0 collective-permute-start.10
  28.3 4.1 %bands.1.refs_10_ = bf16[2,12,192,224]{3,2,1,0:T(8,128)(2,1)} custom-call(bf16[6912,224]{1,0:T(8,128)(2,1)} %get-tuple-element.26.gram_any.refs_11_, bf16[1,2592,128]{2,1,0:T(8,128)(2,1)} %bitcast.7.refs_0_, bf16[1,2592,128]{2,1,0:T(8,128)(2,1)} %bitcast.8.refs_1_), custom_call_target="tpu_custom_call" | custom-call | flops 528482304 | bytes 2752512 | tf_op jit(solution)/shard_map/bands/pallas_call | solution.py:322
  32.4 0.0 copy-done.3
  32.4 0.0 collective-permute-done.8
  32.4 2.4 %collective-permute-start.11 = (bf16[2592,128]{1,0:T(8,128)(2,1)}, bf16[2592,128]{1,0:T(8,128)(2,1)}, u32[]{:S(2)}, u32[]{:S(2)}) collective-permute-start(bf16[2592,128]{1,0:T(8,128)(2,1)} %collective-permute-done.3), channel_id=1, source_target_pairs={{0,1},{1,0},{2,3},{3,2},{4,5},{5,4},{6,7},{7,6},{8,9},{9,8},{10,11... | collective-permute-start | bytes 1990664 | tf_op jit(solution)/shard_map/ppermute | solution.py:518
  34.8 0.8 %collective-permute-done.7 = s32[1,4,8,128]{3,2,1,0:T(8,128)S(1)} collective-permute-done((s32[1,4,8,128]{3,2,1,0:T(8,128)S(1)}, s32[1,4,8,128]{3,2,1,0:T(8,128)S(1)}, u32[]{:S(2)}, u32[]{:S(2)}) %collective-permute-start.7) | collective-permute-done | bytes 16416 | tf_op jit(solution)/shard_map/ppermute | solution.py:522
  35.6 0.0 collective-permute-done.6
  35.6 0.0 copy-start
  35.6 0.0 collective-permute-done.5.refs_7_
  35.7 0.1 collective-permute-start.12
  35.7 0.5 collective-permute-start.9
  36.2 0.0 collective-permute-done.10.refs_5_
  36.2 0.7 %collective-permute-done.11.refs_6_ = bf16[2592,128]{1,0:T(8,128)(2,1)} collective-permute-done((bf16[2592,128]{1,0:T(8,128)(2,1)}, bf16[2592,128]{1,0:T(8,128)(2,1)}, u32[]{:S(2)}, u32[]{:S(2)}) %collective-permute-start.11) | collective-permute-done | bytes 663584 | tf_op jit(solution)/shard_map/ppermute | solution.py:518
  36.9 0.9 %collective-permute-done.9.refs_3_ = s32[4,4,8,128]{3,2,1,0:T(8,128)S(1)} collective-permute-done((s32[4,4,8,128]{3,2,1,0:T(8,128)S(1)}, s32[4,4,8,128]{3,2,1,0:T(8,128)S(1)}, u32[]{:S(2)}, u32[]{:S(2)}) %collective-permute-start.9) | collective-permute-done | bytes 65568 | tf_op jit(solution)/shard_map/ppermute | solution.py:518
  37.9 0.0 copy-start.2
  37.9 0.4 collective-permute-done.12.refs_8_
  38.3 0.0 copy-done
  38.3 0.2 copy-done.2
  38.5 14.9 %decode.1 = bf16[216,4,2560]{2,1,0:T(4,128)(2,1)} custom-call(s32[2,8,256]{2,1,0:T(8,128)} %copy-done.1, s32[2,8,256]{2,1,0:T(8,128)} %copy-done.3, s32[4,4,8,128]{3,2,1,0:T(8,128)} %copy-done, s32[4,4,8,128]{3,2,1,0:T(8,128)} %copy-done.2, bf16[2592,128]{1,0:T(8,128)(2,1)} %collective-permute-done.4.refs_4_, ...), custom_call_target="tpu_custom_call" | custom-call | flops 2642411520 | bytes 4423680 | tf_op jit(solution)/shard_map/decode/pallas_call | solution.py:491
  (2 shorter events, 0.0 us)
Async XLA Ops:
  2.6 6.0 %collective-permute-start = (s32[8,256]{1,0:T(8,128)}, s32[8,256]{1,0:T(8,128)S(1)}, u32[]{:S(2)}, u32[]{:S(2)}) collective-permute-start(s32[8,256]{1,0:T(8,128)} %get-tuple-element.21), channel_id=1, source_target_pairs={{0,8},{8,0},{16,24},{24,16},{1,9},{9,1},{17,25},{25,17},{2,10},{10... | collective-permute-start | bytes 24584 | tf_op jit(solution)/shard_map/ppermute | solution.py:518
  5.6 18.3 %collective-permute-start.4 = (bf16[2592,128]{1,0:T(8,128)(2,1)}, bf16[2592,128]{1,0:T(8,128)(2,1)}, u32[]{:S(2)}, u32[]{:S(2)}) collective-permute-start(bf16[2592,128]{1,0:T(8,128)(2,1)} %get-tuple-element.24.packed_ref), channel_id=1, source_target_pairs={{0,1},{1,0},{2,3},{3,2},{4,5},{5,4},{6,7},{7,6},{8,9},{9,8},{10,11... | collective-permute-start | bytes 1990664 | tf_op jit(solution)/shard_map/ppermute | solution.py:518
  5.6 18.4 %collective-permute-start.3 = (bf16[2592,128]{1,0:T(8,128)(2,1)}, bf16[2592,128]{1,0:T(8,128)(2,1)}, u32[]{:S(2)}, u32[]{:S(2)}) collective-permute-start(bf16[2592,128]{1,0:T(8,128)(2,1)} %get-tuple-element.24.packed_ref), channel_id=1, source_target_pairs={{0,4},{1,3},{2,6},{3,1},{4,0},{5,7},{6,2},{7,5},{8,12},{9,11},{10,... | collective-permute-start | bytes 1990664 | tf_op jit(solution)/shard_map/ppermute | solution.py:522
  7.1 16.8 %collective-permute-start.2 = (bf16[2592,128]{1,0:T(8,128)(2,1)}, bf16[2592,128]{1,0:T(8,128)(2,1)}, u32[]{:S(2)}, u32[]{:S(2)}) collective-permute-start(bf16[2592,128]{1,0:T(8,128)(2,1)} %get-tuple-element.24.packed_ref), channel_id=1, source_target_pairs={{0,2},{1,5},{2,0},{3,7},{4,6},{5,1},{6,4},{7,3},{8,10},{9,13},{10,... | collective-permute-start | bytes 1990664 | tf_op jit(solution)/shard_map/ppermute | solution.py:522
  9.3 14.6 %copy-start.1 = (s32[2,8,256]{2,1,0:T(8,128)}, s32[2,8,256]{2,1,0:T(8,128)S(1)}, u32[]{:S(2)}) copy-start(s32[2,8,256]{2,1,0:T(8,128)S(1)} %pad_add_fusion.2.refs_0_) | copy-start | bytes 49156
  9.3 14.6 %collective-permute-start.1 = (s32[2,8,256]{2,1,0:T(8,128)S(1)}, s32[2,8,256]{2,1,0:T(8,128)S(1)}, u32[]{:S(2)}, u32[]{:S(2)}) collective-permute-start(s32[2,8,256]{2,1,0:T(8,128)S(1)} %pad_add_fusion.2.refs_0_), channel_id=1, source_target_pairs={{0,16},{8,24},{16,0},{24,8},{1,17},{9,25},{17,1},{25,9},{2,18},{10... | collective-permute-start | bytes 49160 | tf_op jit(solution)/shard_map/ppermute | solution.py:518
  23.9 8.5 %copy-start.3 = (s32[2,8,256]{2,1,0:T(8,128)}, s32[2,8,256]{2,1,0:T(8,128)S(1)}, u32[]{:S(2)}) copy-start(s32[2,8,256]{2,1,0:T(8,128)S(1)} %collective-permute-done.1.refs_1_) | copy-start | bytes 49156
  24.0 11.7 %collective-permute-start.5 = (bf16[2592,128]{1,0:T(8,128)(2,1)}, bf16[2592,128]{1,0:T(8,128)(2,1)}, u32[]{:S(2)}, u32[]{:S(2)}) collective-permute-start(bf16[2592,128]{1,0:T(8,128)(2,1)} %collective-permute-done.2), channel_id=1, source_target_pairs={{0,4},{1,3},{2,6},{3,1},{4,0},{5,7},{6,2},{7,5},{8,12},{9,11},{10,... | collective-permute-start | bytes 1990664 | tf_op jit(solution)/shard_map/ppermute | solution.py:522
  24.8 7.6 %collective-permute-start.8 = (s32[1,4,8,128]{3,2,1,0:T(8,128)S(1)}, s32[1,4,8,128]{3,2,1,0:T(8,128)S(1)}, u32[]{:S(2)}, u32[]{:S(2)}) collective-permute-start(s32[1,4,8,128]{3,2,1,0:T(8,128)S(1)} %fusion), channel_id=1, source_target_pairs={{0,6},{1,7},{2,4},{3,5},{4,2},{5,3},{6,0},{7,1},{8,14},{9,15},{10,... | collective-permute-start | bytes 49160 | tf_op jit(solution)/shard_map/ppermute | solution.py:518
  26.5 9.2 %collective-permute-start.7 = (s32[1,4,8,128]{3,2,1,0:T(8,128)S(1)}, s32[1,4,8,128]{3,2,1,0:T(8,128)S(1)}, u32[]{:S(2)}, u32[]{:S(2)}) collective-permute-start(s32[1,4,8,128]{3,2,1,0:T(8,128)S(1)} %fusion), channel_id=1, source_target_pairs={{0,4},{1,3},{2,6},{3,1},{4,0},{5,7},{6,2},{7,5},{8,12},{9,11},{10,... | collective-permute-start | bytes 49160 | tf_op jit(solution)/shard_map/ppermute | solution.py:522
  28.0 7.7 %collective-permute-start.6 = (s32[1,4,8,128]{3,2,1,0:T(8,128)S(1)}, s32[1,4,8,128]{3,2,1,0:T(8,128)S(1)}, u32[]{:S(2)}, u32[]{:S(2)}) collective-permute-start(s32[1,4,8,128]{3,2,1,0:T(8,128)S(1)} %fusion), channel_id=1, source_target_pairs={{0,2},{1,5},{2,0},{3,7},{4,6},{5,1},{6,4},{7,3},{8,10},{9,13},{10,... | collective-permute-start | bytes 49160 | tf_op jit(solution)/shard_map/ppermute | solution.py:522
  28.3 7.9 %collective-permute-start.10 = (bf16[2592,128]{1,0:T(8,128)(2,1)}, bf16[2592,128]{1,0:T(8,128)(2,1)}, u32[]{:S(2)}, u32[]{:S(2)}) collective-permute-start(bf16[2592,128]{1,0:T(8,128)(2,1)} %collective-permute-done.2), channel_id=1, source_target_pairs={{0,1},{1,0},{2,3},{3,2},{4,5},{5,4},{6,7},{7,6},{8,9},{9,8},{10,11... | collective-permute-start | bytes 1990664 | tf_op jit(solution)/shard_map/ppermute | solution.py:518
  32.4 4.5 %collective-permute-start.11 = (bf16[2592,128]{1,0:T(8,128)(2,1)}, bf16[2592,128]{1,0:T(8,128)(2,1)}, u32[]{:S(2)}, u32[]{:S(2)}) collective-permute-start(bf16[2592,128]{1,0:T(8,128)(2,1)} %collective-permute-done.3), channel_id=1, source_target_pairs={{0,1},{1,0},{2,3},{3,2},{4,5},{5,4},{6,7},{7,6},{8,9},{9,8},{10,11... | collective-permute-start | bytes 1990664 | tf_op jit(solution)/shard_map/ppermute | solution.py:518
  35.6 2.6 %copy-start = (s32[4,4,8,128]{3,2,1,0:T(8,128)}, s32[4,4,8,128]{3,2,1,0:T(8,128)S(1)}, u32[]{:S(2)}) copy-start(s32[4,4,8,128]{3,2,1,0:T(8,128)S(1)} %pad_add_fusion.refs_2_) | copy-start | bytes 196612
  35.7 2.6 %collective-permute-start.12 = (bf16[2592,128]{1,0:T(8,128)(2,1)}, bf16[2592,128]{1,0:T(8,128)(2,1)}, u32[]{:S(2)}, u32[]{:S(2)}) collective-permute-start(bf16[2592,128]{1,0:T(8,128)(2,1)} %collective-permute-done.5.refs_7_), channel_id=1, source_target_pairs={{0,1},{1,0},{2,3},{3,2},{4,5},{5,4},{6,7},{7,6},{8,9},{9,8},{10,11... | collective-permute-start | bytes 1990664 | tf_op jit(solution)/shard_map/ppermute | solution.py:518
  35.7 2.1 %collective-permute-start.9 = (s32[4,4,8,128]{3,2,1,0:T(8,128)S(1)}, s32[4,4,8,128]{3,2,1,0:T(8,128)S(1)}, u32[]{:S(2)}, u32[]{:S(2)}) collective-permute-start(s32[4,4,8,128]{3,2,1,0:T(8,128)S(1)} %pad_add_fusion.refs_2_), channel_id=1, source_target_pairs={{0,1},{1,0},{2,3},{3,2},{4,5},{5,4},{6,7},{7,6},{8,9},{9,8},{10,11... | collective-permute-start | bytes 196616 | tf_op jit(solution)/shard_map/ppermute | solution.py:518
  37.9 0.6 %copy-start.2 = (s32[4,4,8,128]{3,2,1,0:T(8,128)}, s32[4,4,8,128]{3,2,1,0:T(8,128)S(1)}, u32[]{:S(2)}) copy-start(s32[4,4,8,128]{3,2,1,0:T(8,128)S(1)} %collective-permute-done.9.refs_3_) | copy-start | bytes 196612

commit v23 on v22

--- a/solution.py
+++ b/solution.py
@@ -561,16 +561,13 @@
     diagonal = turn(first, 4, 2)
     first_sibling = swap(first, "row", 1)
     mine = [held, turn(held, 2, 4), turn(held, 4, 2), swap(held, "row", 6)]
-    sources = [source[None] for source in (first, second)]
-    near, = bands(gram_rows, sources, 1, staged, row_shape, surface_rows)
-    near, second = lax.optimization_barrier((near, second))
     second_sibling = swap(second, "row", 1)
     mine = jnp.concatenate(mine, axis=0)
-    near, diagonal, mine = lax.optimization_barrier((near, diagonal, mine))
+    diagonal, mine = lax.optimization_barrier((diagonal, mine))
     theirs = swap(mine, "row", 1)
-    late = [sibling, first_sibling, second_sibling, diagonal, swap(diagonal, "row", 1)]
+    late = [first, second, sibling, first_sibling, second_sibling, diagonal, swap(diagonal, "row", 1)]
     return decode(
-        lines, [mine, theirs], [0, 1, 2, 6, 3, 4, 5, 7], late, [own_rows, near], gram_rows, own, row_shape,
+        lines, [mine, theirs], [0, 1, 2, 6, 3, 4, 5, 7], late, [own_rows], gram_rows, own, row_shape,
         surface_rows, pupil, norm, staged,
     )
 

time: 53.6 us -> 55.1 us (1.028)
  Pallas kernels: 33.5 us -> 29.8 us
  starting transfers between devices: 16 us -> 18.6 us
  local copies, waits for them, and re-layouts: 0.23 us -> 1.78 us
  waiting for transfers between devices: 2.83 us -> 3.88 us
    pallas_call x1 -> x0, Pallas kernels: 4.07 us -> none  [bands(): pl.pallas_call(functools.partial(bands_kernel, row_shape, surface_rows, f...]
    ppermute x8, starting transfers between devices: 10.2 us -> 12.9 us  [swap(): lax.ppermute(block, axis, [(i, i ^ distance) for i in range(lax.axis_size...]
    unnamed x8 -> x16, local copies, waits for them, and re-layouts: 0.23 us -> 1.78 us
    ppermute x8, waiting for transfers between devices: 2.04 us -> 3.07 us  [swap(): lax.ppermute(block, axis, [(i, i ^ distance) for i in range(lax.axis_size...]
  transfers between devices with their start and end apart: 13 -> 13, of which waited for: 4 -> 3; matrix products, arithmetic and copies ran while one was open for 1% -> 1% of each run, Pallas kernels for 30% -> 22%
where the time goes in v23:
time: 55.1 us; the launch traced here: 54.9 us
  Pallas kernels  29.8 us (54%)
  starting transfers between devices  18.6 us (34%)
  waiting for transfers between devices  3.88 us (7%)
  local copies, waits for them, and re-layouts  1.78 us (3%)
  other arithmetic  0.71 us (1%)
    pallas_call x1, Pallas kernels, decode(): pl.pallas_call(functools.partial(decode_kernel, row_shape, surface_rows,...  15.3 us
    ppermute x8, starting transfers between devices, swap(): lax.ppermute(block, axis, [(i, i ^ distance) for i in range(lax.axis_size...  12.9 us
    pallas_call x1, Pallas kernels, gram(): pl.pallas_call(functools.partial(gram_kernel, row_shape, surface_rows), g...  12 us
    ppermute x5, starting transfers between devices, turn(): lax.ppermute(block, 'row', [(i, i ^ (odd if i % 2 else even)) for i in ra...  5.74 us
    ppermute x8, waiting for transfers between devices, swap(): lax.ppermute(block, axis, [(i, i ^ distance) for i in range(lax.axis_size...  3.07 us
    pallas_call x1, Pallas kernels, pack(): pl.pallas_call(pack_kernel, out_shape=[jax.ShapeDtypeStruct((mirrors * ro...  2.57 us
    unnamed x16, local copies, waits for them, and re-layouts  1.78 us
  transfers between devices with their start and end apart: 13, of which 3 were waited for; matrix products, arithmetic and copies ran while one was open for 1% of the time, Pallas kernels for 22%

profile of v23, /device:TPU:0, one launch (start us, length us, event | category | flops | bytes accessed | tf_op | source)
XLA Modules:
  0.0 54.9 jit_solution(15751027189254275380)
XLA Ops:
  0.0 2.6 %pack_influence.1 = (bf16[2592,128]{1,0:T(8,128)(2,1)}, s32[8,256]{1,0:T(8,128)}) custom-call(bf16[3,4,144,192]{3,2,1,0:T(8,128)(2,1)} %bitcast.8, s32[3,1,4]{2,1,0:T(1,128)} %bitcast.12, s32[3,1,160]{2,1,0:T(1,128)} %bitcast.11, s32[1,2,80]{2,1,0:T(2,128)} %valid_ref.1), custom_call_target="tpu_custom_call" | custom-call | bytes 995328 | tf_op jit(solution)/shard_map/pack_influence/pallas_call | solution.py:65
  2.6 3.0 %collective-permute-start = (s32[8,256]{1,0:T(8,128)}, s32[8,256]{1,0:T(8,128)S(1)}, u32[]{:S(2)}, u32[]{:S(2)}) collective-permute-start(s32[8,256]{1,0:T(8,128)} %get-tuple-element.18), channel_id=1, source_target_pairs={{0,8},{8,0},{16,24},{24,16},{1,9},{9,1},{17,25},{25,17},{2,10},{10... | collective-permute-start | bytes 24584 | tf_op jit(solution)/shard_map/ppermute | solution.py:518
  5.6 0.0 collective-permute-start.4
  5.6 1.5 %collective-permute-start.3 = (bf16[2592,128]{1,0:T(8,128)(2,1)}, bf16[2592,128]{1,0:T(8,128)(2,1)}, u32[]{:S(2)}, u32[]{:S(2)}) collective-permute-start(bf16[2592,128]{1,0:T(8,128)(2,1)} %get-tuple-element.21.packed_ref), channel_id=1, source_target_pairs={{0,4},{1,3},{2,6},{3,1},{4,0},{5,7},{6,2},{7,5},{8,12},{9,11},{10,... | collective-permute-start | bytes 1990664 | tf_op jit(solution)/shard_map/ppermute | solution.py:522
  7.1 1.5 %collective-permute-start.2 = (bf16[2592,128]{1,0:T(8,128)(2,1)}, bf16[2592,128]{1,0:T(8,128)(2,1)}, u32[]{:S(2)}, u32[]{:S(2)}) collective-permute-start(bf16[2592,128]{1,0:T(8,128)(2,1)} %get-tuple-element.21.packed_ref), channel_id=1, source_target_pairs={{0,2},{1,5},{2,0},{3,7},{4,6},{5,1},{6,4},{7,3},{8,10},{9,13},{10,... | collective-permute-start | bytes 1990664 | tf_op jit(solution)/shard_map/ppermute | solution.py:522
  8.6 0.0 collective-permute-done
  8.6 0.7 %pad_add_fusion.2.refs_0_ = s32[2,8,256]{2,1,0:T(8,128)S(1)} fusion(s32[1,8,256]{2,1,0:T(8,128)S(1)} %bitcast.10, s32[1,8,256]{2,1,0:T(8,128)} %bitcast.9), kind=kLoop, calls=%fused_computation.3 | loop fusion | flops 4096 | bytes 32768 | tf_op jit(solution)/shard_map/stack | solution.py:551
  9.3 0.0 copy-start.5
  9.3 2.6 %collective-permute-start.1 = (s32[2,8,256]{2,1,0:T(8,128)S(1)}, s32[2,8,256]{2,1,0:T(8,128)S(1)}, u32[]{:S(2)}, u32[]{:S(2)}) collective-permute-start(s32[2,8,256]{2,1,0:T(8,128)S(1)} %pad_add_fusion.2.refs_0_), channel_id=1, source_target_pairs={{0,16},{8,24},{16,0},{24,8},{1,17},{9,25},{17,1},{25,9},{2,18},{10... | collective-permute-start | bytes 49160 | tf_op jit(solution)/shard_map/ppermute | solution.py:518
  11.9 12.0 %gram_rows.1 = (bf16[6912,224]{1,0:T(8,128)(2,1)}, bf16[1,12,192,224]{3,2,1,0:T(8,128)(2,1)}) custom-call(s32[3,48,48]{2,1,0:T(8,128)} %table_ref.1, s32[16,128]{1,0:T(8,128)} %bitcast.13, bf16[2592,128]{1,0:T(8,128)(2,1)} %get-tuple-element.21.packed_ref), custom_call_target="tpu_custom_call" | custom-call | flops 6341787648 | bytes 3096576 | tf_op jit(solution)/shard_map/gram_rows/pallas_call | solution.py:194
  23.9 0.0 collective-permute-done.1.refs_1_
  23.9 0.0 copy-done.5
  23.9 0.0 copy-start.7
  24.0 0.0 collective-permute-done.4.refs_6_
  24.0 0.0 collective-permute-done.3.refs_5_
  24.0 0.0 collective-permute-done.2.refs_4_
  24.0 0.9 %collective-permute-start.5 = (bf16[2592,128]{1,0:T(8,128)(2,1)}, bf16[2592,128]{1,0:T(8,128)(2,1)S(1)}, u32[]{:S(2)}, u32[]{:S(2)}) collective-permute-start(bf16[2592,128]{1,0:T(8,128)(2,1)} %collective-permute-done.2.refs_4_), channel_id=1, source_target_pairs={{0,4},{1,3},{2,6},{3,1},{4,0},{5,7},{6,2},{7,5},{8,12},{9,11},{10,... | collective-permute-start | bytes 1990664 | tf_op jit(solution)/shard_map/ppermute | solution.py:522
  24.8 1.6 %collective-permute-start.8 = (s32[1,4,8,128]{3,2,1,0:T(8,128)S(1)}, s32[1,4,8,128]{3,2,1,0:T(8,128)S(1)}, u32[]{:S(2)}, u32[]{:S(2)}) collective-permute-start(s32[1,4,8,128]{3,2,1,0:T(8,128)S(1)} %fusion), channel_id=1, source_target_pairs={{0,6},{1,7},{2,4},{3,5},{4,2},{5,3},{6,0},{7,1},{8,14},{9,15},{10,... | collective-permute-start | bytes 49160 | tf_op jit(solution)/shard_map/ppermute | solution.py:518
  26.5 1.5 %collective-permute-start.7 = (s32[1,4,8,128]{3,2,1,0:T(8,128)S(1)}, s32[1,4,8,128]{3,2,1,0:T(8,128)S(1)}, u32[]{:S(2)}, u32[]{:S(2)}) collective-permute-start(s32[1,4,8,128]{3,2,1,0:T(8,128)S(1)} %fusion), channel_id=1, source_target_pairs={{0,4},{1,3},{2,6},{3,1},{4,0},{5,7},{6,2},{7,5},{8,12},{9,11},{10,... | collective-permute-start | bytes 49160 | tf_op jit(solution)/shard_map/ppermute | solution.py:522
  28.0 0.4 collective-permute-start.6
  28.3 0.0 collective-permute-start.10
  28.3 1.4 %collective-permute-done.8 = s32[1,4,8,128]{3,2,1,0:T(8,128)S(1)} collective-permute-done((s32[1,4,8,128]{3,2,1,0:T(8,128)S(1)}, s32[1,4,8,128]{3,2,1,0:T(8,128)S(1)}, u32[]{:S(2)}, u32[]{:S(2)}) %collective-permute-start.8) | collective-permute-done | bytes 16416 | tf_op jit(solution)/shard_map/ppermute | solution.py:518
  29.7 5.1 %collective-permute-start.11 = (bf16[2592,128]{1,0:T(8,128)(2,1)}, bf16[2592,128]{1,0:T(8,128)(2,1)S(1)}, u32[]{:S(2)}, u32[]{:S(2)}) collective-permute-start(bf16[2592,128]{1,0:T(8,128)(2,1)} %collective-permute-done.3.refs_5_), channel_id=1, source_target_pairs={{0,1},{1,0},{2,3},{3,2},{4,5},{5,4},{6,7},{7,6},{8,9},{9,8},{10,11... | collective-permute-start | bytes 1990664 | tf_op jit(solution)/shard_map/ppermute | solution.py:518
  34.8 0.8 %collective-permute-done.7 = s32[1,4,8,128]{3,2,1,0:T(8,128)S(1)} collective-permute-done((s32[1,4,8,128]{3,2,1,0:T(8,128)S(1)}, s32[1,4,8,128]{3,2,1,0:T(8,128)S(1)}, u32[]{:S(2)}, u32[]{:S(2)}) %collective-permute-start.7) | collective-permute-done | bytes 16416 | tf_op jit(solution)/shard_map/ppermute | solution.py:522
  35.6 0.0 collective-permute-done.6
  35.7 0.0 copy-start.4
  35.7 0.0 collective-permute-done.5.refs_9_
  35.7 0.0 copy-start
  35.7 0.9 %copy-done = bf16[2592,128]{1,0:T(8,128)(2,1)} copy-done((bf16[2592,128]{1,0:T(8,128)(2,1)}, bf16[2592,128]{1,0:T(8,128)(2,1)S(1)}, u32[]{:S(2)}) %copy-start) | copy-done | bytes 663576
  36.6 0.0 collective-permute-start.12
  36.6 0.5 collective-permute-start.9
  37.1 0.0 collective-permute-done.11.refs_8_
  37.1 0.0 copy-start.2
  37.1 0.0 collective-permute-done.10.refs_7_
  37.1 0.0 copy-start.1
  37.1 1.7 %collective-permute-done.9.refs_3_ = s32[4,4,8,128]{3,2,1,0:T(8,128)S(1)} collective-permute-done((s32[4,4,8,128]{3,2,1,0:T(8,128)S(1)}, s32[4,4,8,128]{3,2,1,0:T(8,128)S(1)}, u32[]{:S(2)}, u32[]{:S(2)}) %collective-permute-start.9) | collective-permute-done | bytes 65568 | tf_op jit(solution)/shard_map/ppermute | solution.py:518
  38.8 0.0 copy-start.6
  38.8 0.0 collective-permute-done.12.refs_10_
  38.8 0.0 copy-done.2
  38.8 0.0 copy-done.1
  38.8 0.0 copy-start.3
  38.8 0.9 %copy-done.3 = bf16[2592,128]{1,0:T(8,128)(2,1)} copy-done((bf16[2592,128]{1,0:T(8,128)(2,1)}, bf16[2592,128]{1,0:T(8,128)(2,1)S(1)}, u32[]{:S(2)}) %copy-start.3) | copy-done | bytes 663576
  39.7 0.0 copy-done.7
  39.7 0.0 copy-done.4
  39.7 0.0 copy-done.6
  39.7 15.3 %decode.1 = bf16[216,4,2560]{2,1,0:T(4,128)(2,1)} custom-call(s32[2,8,256]{2,1,0:T(8,128)} %copy-done.5, s32[2,8,256]{2,1,0:T(8,128)} %copy-done.7, s32[4,4,8,128]{3,2,1,0:T(8,128)} %copy-done.4, s32[4,4,8,128]{3,2,1,0:T(8,128)} %copy-done.6, bf16[2592,128]{1,0:T(8,128)(2,1)} %collective-permute-done.2.refs_4_, ...), custom_call_target="tpu_custom_call" | custom-call | flops 2642411520 | bytes 4423680 | tf_op jit(solution)/shard_map/decode/pallas_call | solution.py:491
  (2 shorter events, 0.0 us)
Async XLA Ops:
  2.6 6.0 %collective-permute-start = (s32[8,256]{1,0:T(8,128)}, s32[8,256]{1,0:T(8,128)S(1)}, u32[]{:S(2)}, u32[]{:S(2)}) collective-permute-start(s32[8,256]{1,0:T(8,128)} %get-tuple-element.18), channel_id=1, source_target_pairs={{0,8},{8,0},{16,24},{24,16},{1,9},{9,1},{17,25},{25,17},{2,10},{10... | collective-permute-start | bytes 24584 | tf_op jit(solution)/shard_map/ppermute | solution.py:518
  5.6 18.4 %collective-permute-start.4 = (bf16[2592,128]{1,0:T(8,128)(2,1)}, bf16[2592,128]{1,0:T(8,128)(2,1)}, u32[]{:S(2)}, u32[]{:S(2)}) collective-permute-start(bf16[2592,128]{1,0:T(8,128)(2,1)} %get-tuple-element.21.packed_ref), channel_id=1, source_target_pairs={{0,1},{1,0},{2,3},{3,2},{4,5},{5,4},{6,7},{7,6},{8,9},{9,8},{10,11... | collective-permute-start | bytes 1990664 | tf_op jit(solution)/shard_map/ppermute | solution.py:518
  5.6 18.4 %collective-permute-start.3 = (bf16[2592,128]{1,0:T(8,128)(2,1)}, bf16[2592,128]{1,0:T(8,128)(2,1)}, u32[]{:S(2)}, u32[]{:S(2)}) collective-permute-start(bf16[2592,128]{1,0:T(8,128)(2,1)} %get-tuple-element.21.packed_ref), channel_id=1, source_target_pairs={{0,4},{1,3},{2,6},{3,1},{4,0},{5,7},{6,2},{7,5},{8,12},{9,11},{10,... | collective-permute-start | bytes 1990664 | tf_op jit(solution)/shard_map/ppermute | solution.py:522
  7.1 16.9 %collective-permute-start.2 = (bf16[2592,128]{1,0:T(8,128)(2,1)}, bf16[2592,128]{1,0:T(8,128)(2,1)}, u32[]{:S(2)}, u32[]{:S(2)}) collective-permute-start(bf16[2592,128]{1,0:T(8,128)(2,1)} %get-tuple-element.21.packed_ref), channel_id=1, source_target_pairs={{0,2},{1,5},{2,0},{3,7},{4,6},{5,1},{6,4},{7,3},{8,10},{9,13},{10,... | collective-permute-start | bytes 1990664 | tf_op jit(solution)/shard_map/ppermute | solution.py:522
  9.3 14.6 %copy-start.5 = (s32[2,8,256]{2,1,0:T(8,128)}, s32[2,8,256]{2,1,0:T(8,128)S(1)}, u32[]{:S(2)}) copy-start(s32[2,8,256]{2,1,0:T(8,128)S(1)} %pad_add_fusion.2.refs_0_) | copy-start | bytes 49156
  9.3 14.6 %collective-permute-start.1 = (s32[2,8,256]{2,1,0:T(8,128)S(1)}, s32[2,8,256]{2,1,0:T(8,128)S(1)}, u32[]{:S(2)}, u32[]{:S(2)}) collective-permute-start(s32[2,8,256]{2,1,0:T(8,128)S(1)} %pad_add_fusion.2.refs_0_), channel_id=1, source_target_pairs={{0,16},{8,24},{16,0},{24,8},{1,17},{9,25},{17,1},{25,9},{2,18},{10... | collective-permute-start | bytes 49160 | tf_op jit(solution)/shard_map/ppermute | solution.py:518
  23.9 15.7 %copy-start.7 = (s32[2,8,256]{2,1,0:T(8,128)}, s32[2,8,256]{2,1,0:T(8,128)S(1)}, u32[]{:S(2)}) copy-start(s32[2,8,256]{2,1,0:T(8,128)S(1)} %collective-permute-done.1.refs_1_) | copy-start | bytes 49156
  24.0 11.7 %collective-permute-start.5 = (bf16[2592,128]{1,0:T(8,128)(2,1)}, bf16[2592,128]{1,0:T(8,128)(2,1)S(1)}, u32[]{:S(2)}, u32[]{:S(2)}) collective-permute-start(bf16[2592,128]{1,0:T(8,128)(2,1)} %collective-permute-done.2.refs_4_), channel_id=1, source_target_pairs={{0,4},{1,3},{2,6},{3,1},{4,0},{5,7},{6,2},{7,5},{8,12},{9,11},{10,... | collective-permute-start | bytes 1990664 | tf_op jit(solution)/shard_map/ppermute | solution.py:522
  24.8 4.9 %collective-permute-start.8 = (s32[1,4,8,128]{3,2,1,0:T(8,128)S(1)}, s32[1,4,8,128]{3,2,1,0:T(8,128)S(1)}, u32[]{:S(2)}, u32[]{:S(2)}) collective-permute-start(s32[1,4,8,128]{3,2,1,0:T(8,128)S(1)} %fusion), channel_id=1, source_target_pairs={{0,6},{1,7},{2,4},{3,5},{4,2},{5,3},{6,0},{7,1},{8,14},{9,15},{10,... | collective-permute-start | bytes 49160 | tf_op jit(solution)/shard_map/ppermute | solution.py:518
  26.5 9.2 %collective-permute-start.7 = (s32[1,4,8,128]{3,2,1,0:T(8,128)S(1)}, s32[1,4,8,128]{3,2,1,0:T(8,128)S(1)}, u32[]{:S(2)}, u32[]{:S(2)}) collective-permute-start(s32[1,4,8,128]{3,2,1,0:T(8,128)S(1)} %fusion), channel_id=1, source_target_pairs={{0,4},{1,3},{2,6},{3,1},{4,0},{5,7},{6,2},{7,5},{8,12},{9,11},{10,... | collective-permute-start | bytes 49160 | tf_op jit(solution)/shard_map/ppermute | solution.py:522
  28.0 7.7 %collective-permute-start.6 = (s32[1,4,8,128]{3,2,1,0:T(8,128)S(1)}, s32[1,4,8,128]{3,2,1,0:T(8,128)S(1)}, u32[]{:S(2)}, u32[]{:S(2)}) collective-permute-start(s32[1,4,8,128]{3,2,1,0:T(8,128)S(1)} %fusion), channel_id=1, source_target_pairs={{0,2},{1,5},{2,0},{3,7},{4,6},{5,1},{6,4},{7,3},{8,10},{9,13},{10,... | collective-permute-start | bytes 49160 | tf_op jit(solution)/shard_map/ppermute | solution.py:522
  28.3 8.8 %collective-permute-start.10 = (bf16[2592,128]{1,0:T(8,128)(2,1)}, bf16[2592,128]{1,0:T(8,128)(2,1)S(1)}, u32[]{:S(2)}, u32[]{:S(2)}) collective-permute-start(bf16[2592,128]{1,0:T(8,128)(2,1)} %collective-permute-done.2.refs_4_), channel_id=1, source_target_pairs={{0,1},{1,0},{2,3},{3,2},{4,5},{5,4},{6,7},{7,6},{8,9},{9,8},{10,11... | collective-permute-start | bytes 1990664 | tf_op jit(solution)/shard_map/ppermute | solution.py:518
  29.7 7.4 %collective-permute-start.11 = (bf16[2592,128]{1,0:T(8,128)(2,1)}, bf16[2592,128]{1,0:T(8,128)(2,1)S(1)}, u32[]{:S(2)}, u32[]{:S(2)}) collective-permute-start(bf16[2592,128]{1,0:T(8,128)(2,1)} %collective-permute-done.3.refs_5_), channel_id=1, source_target_pairs={{0,1},{1,0},{2,3},{3,2},{4,5},{5,4},{6,7},{7,6},{8,9},{9,8},{10,11... | collective-permute-start | bytes 1990664 | tf_op jit(solution)/shard_map/ppermute | solution.py:518
  35.7 4.0 %copy-start.4 = (s32[4,4,8,128]{3,2,1,0:T(8,128)}, s32[4,4,8,128]{3,2,1,0:T(8,128)S(1)}, u32[]{:S(2)}) copy-start(s32[4,4,8,128]{3,2,1,0:T(8,128)S(1)} %pad_add_fusion.refs_2_) | copy-start | bytes 196612
  35.7 0.9 %copy-start = (bf16[2592,128]{1,0:T(8,128)(2,1)}, bf16[2592,128]{1,0:T(8,128)(2,1)S(1)}, u32[]{:S(2)}) copy-start(bf16[2592,128]{1,0:T(8,128)(2,1)S(1)} %collective-permute-done.5.refs_9_) | copy-start | bytes 1990660
  36.6 2.2 %collective-permute-start.12 = (bf16[2592,128]{1,0:T(8,128)(2,1)S(1)}, bf16[2592,128]{1,0:T(8,128)(2,1)S(1)}, u32[]{:S(2)}, u32[]{:S(2)}) collective-permute-start(bf16[2592,128]{1,0:T(8,128)(2,1)S(1)} %collective-permute-done.5.refs_9_), channel_id=1, source_target_pairs={{0,1},{1,0},{2,3},{3,2},{4,5},{5,4},{6,7},{7,6},{8,9},{9,8},{10,11... | collective-permute-start | bytes 1990664 | tf_op jit(solution)/shard_map/ppermute | solution.py:518
  36.6 2.2 %collective-permute-start.9 = (s32[4,4,8,128]{3,2,1,0:T(8,128)S(1)}, s32[4,4,8,128]{3,2,1,0:T(8,128)S(1)}, u32[]{:S(2)}, u32[]{:S(2)}) collective-permute-start(s32[4,4,8,128]{3,2,1,0:T(8,128)S(1)} %pad_add_fusion.refs_2_), channel_id=1, source_target_pairs={{0,1},{1,0},{2,3},{3,2},{4,5},{5,4},{6,7},{7,6},{8,9},{9,8},{10,11... | collective-permute-start | bytes 196616 | tf_op jit(solution)/shard_map/ppermute | solution.py:518
  37.1 1.7 %copy-start.2 = (bf16[2592,128]{1,0:T(8,128)(2,1)}, bf16[2592,128]{1,0:T(8,128)(2,1)S(1)}, u32[]{:S(2)}) copy-start(bf16[2592,128]{1,0:T(8,128)(2,1)S(1)} %collective-permute-done.11.refs_8_) | copy-start | bytes 1990660
  37.1 1.7 %copy-start.1 = (bf16[2592,128]{1,0:T(8,128)(2,1)}, bf16[2592,128]{1,0:T(8,128)(2,1)S(1)}, u32[]{:S(2)}) copy-start(bf16[2592,128]{1,0:T(8,128)(2,1)S(1)} %collective-permute-done.10.refs_7_) | copy-start | bytes 1990660
  38.8 0.9 %copy-start.6 = (s32[4,4,8,128]{3,2,1,0:T(8,128)}, s32[4,4,8,128]{3,2,1,0:T(8,128)S(1)}, u32[]{:S(2)}) copy-start(s32[4,4,8,128]{3,2,1,0:T(8,128)S(1)} %collective-permute-done.9.refs_3_) | copy-start | bytes 196612
  38.8 0.9 %copy-start.3 = (bf16[2592,128]{1,0:T(8,128)(2,1)}, bf16[2592,128]{1,0:T(8,128)(2,1)S(1)}, u32[]{:S(2)}) copy-start(bf16[2592,128]{1,0:T(8,128)(2,1)S(1)} %collective-permute-done.12.refs_10_) | copy-start | bytes 1990660
